TPU v7x, 32 devices: a whole 2x2x4 slice. The times are simulated.
32 devices in a mesh: prow: 4 (over x, core), pcol: 8 (over z, y).
Axes of the slice: x: 2, y: 2, z: 4, core: 2. Of those that a mesh axis runs over, the one named last changes fastest.
Arguments:
- matrix: float32 [8192, 5120], P('prow', 'pcol'), may hold values from -6 to 6
- pivots: int32 [512], replicated, may hold values from 0 to 8191, as said below
- lower_inverse: float32 [512, 512], replicated, as said below
- upper_inverse: float32 [512, 512], replicated, as said below
Outputs:
- factored: float32 [8192, 5120], P('prow', 'pcol')
Inputs may be any that keep to these rules, and one draw needn't show every extreme that they name: The 512 pivots are distinct. `lower_inverse`: unit diagonal, zeros above it. `upper_inverse`: zeros below the diagonal, a positive diagonal.
All inputs are finite; a program needn't handle non-finite values.
Results may differ from a plain program's by a relative error of at most 0.00005.
Values sent between devices are 32-bit elements; how exact they have to be, the bound alone decides.
No kernel may reach another device: no remote copies, remote signals or barrier semaphores. Data moves between devices by JAX's collectives and lax.ppermute only.
A program may use at most 128 MiB of HBM per device.

v0:
```python
import jax
import jax.numpy as jnp
from jax import lax
from jax.sharding import PartitionSpec as P


def from_root(array, axis, root):
    mine = lax.axis_index(axis) == root
    return lax.psum(jnp.where(mine, array, jnp.zeros_like(array)), axis)


def row_sources(pivots, panel_width):
    below = pivots >= panel_width
    vac_rank = jnp.cumsum(below.astype(jnp.int32)) - 1
    slot_ids = jnp.arange(panel_width, dtype=jnp.int32)
    chosen_top = jnp.any(pivots[:, None] == slot_ids[None, :], axis=0)
    freed_rows = jnp.logical_not(chosen_top)
    freed_rank = jnp.cumsum(freed_rows.astype(jnp.int32)) - 1
    pairing = freed_rows[None, :] & (freed_rank[None, :] == vac_rank[:, None])
    source_rows = jnp.sum(jnp.where(pairing, slot_ids[None, :], 0), axis=1)
    return (below, source_rows)


def local(matrix, pivots, lower_inverse, upper_inverse):
    row_dev, col_dev = matrix.shape
    panel_width = pivots.shape[0]
    row_start = lax.axis_index("prow") * row_dev
    col_start = lax.axis_index("pcol") * col_dev
    global_rows = row_start + jnp.arange(row_dev, dtype=jnp.int32)
    global_cols = col_start + jnp.arange(col_dev, dtype=jnp.int32)
    below, source_rows = row_sources(pivots, panel_width)
    owned_rows = pivots - row_start
    inside = (owned_rows >= 0) & (owned_rows < row_dev)
    picked = jnp.take(matrix, jnp.clip(owned_rows, 0, row_dev - 1), axis=0)
    picked = jnp.where(inside[:, None], picked, 0.0)
    top_orig = matrix[:panel_width]
    new_top = lax.psum(picked, "prow")
    old_top = from_root(top_orig, "prow", 0)
    matches = (global_rows[:, None] == pivots[None, :]) & below[None, :]
    displaced = jnp.any(matches, axis=1)
    sources = jnp.sum(jnp.where(matches, source_rows[None, :], 0), axis=1)
    from_old = jnp.take(old_top, sources, axis=0)
    top_rows = global_rows < panel_width
    from_top = jnp.concatenate([new_top, matrix[panel_width:]], axis=0)
    swapped = jnp.where(
        top_rows[:, None], from_top, jnp.where(displaced[:, None], from_old, matrix)
    )
    u_rows = jnp.dot(lower_inverse, new_top, precision=lax.Precision.HIGHEST)
    panel_local = swapped[:, :panel_width]
    raw_panel = jnp.where(top_rows[:, None], 0.0, panel_local)
    spread = from_root(raw_panel, "pcol", 0)
    combined = jnp.dot(upper_inverse, u_rows, precision=lax.Precision.HIGHEST)
    update = jnp.dot(spread, combined, precision=lax.Precision.HIGHEST)
    lower_part = lax.cond(
        lax.axis_index("pcol") == 0,
        lambda: jnp.dot(raw_panel, upper_inverse, precision=lax.Precision.HIGHEST),
        lambda: jnp.zeros((row_dev, panel_width), jnp.float32),
    )
    panel_cols = global_cols < panel_width
    upper_full = jnp.concatenate(
        [u_rows, jnp.zeros((row_dev - panel_width, col_dev), jnp.float32)], axis=0
    )
    lower_full = jnp.concatenate(
        [lower_part, jnp.zeros((row_dev, col_dev - panel_width), jnp.float32)], axis=1
    )
    upper_band = jnp.where(panel_cols[None, :], swapped, upper_full)
    lower_band = jnp.where(panel_cols[None, :], lower_full, swapped - update)
    return jnp.where(top_rows[:, None], upper_band, lower_band)


def solution(mesh):
    return jax.shard_map(
        local,
        mesh=mesh,
        in_specs=(P("prow", "pcol"), P(), P(), P()),
        out_specs=P("prow", "pcol"),
        check_vma=False,
    )
```

profile of v0, /device:TPU:10, one launch (start us, length us, event | category | flops | bytes accessed | tf_op | source)
XLA Modules:
  0.0 297.1 jit_solution(10919722459428369984)
XLA Ops:
  6.5 0.8 convert_bitcast_fusion
  7.3 5.9 %copy.26 = f32[2048,640]{0,1:T(8,128)} copy(f32[2048,640]{1,0:T(8,128)} %param.6) | data formatting | bytes 10485760 | tf_op args[0]
  13.2 4.7 %gather_fusion = f32[512,640]{1,0:T(8,128)S(1)} fusion(f32[2048,640]{1,0:T(8,128)} %param.6, s32[1024]{0:T(1024)S(1)} %pad_clamp_fusion), kind=kCustom, calls=%fused_computation | custom fusion | bytes 2623488 | tf_op jit(solution)/shard_map/jit(_take)/gather | solution.py:34
  17.9 1.5 copy.25
  19.4 3.7 %slice_select_fusion.1 = (f32[512,640]{0,1:T(8,128)}, f32[512,640]{0,1:T(8,128)}) fusion(f32[2048,640]{0,1:T(8,128)} %copy.26, pred[]{:T(512)S(6)} %eq.58, f32[512,640]{0,1:T(8,128)} %copy.25, pred[512]{0:T(512)(128)(4,1)S(1)} %get-tuple-element.31, pred[512]{0:T(512)(128)(4,1)S(1)} %get-tuple-element.30), kind=kLoop, calls=%fused_computation.9 | loop fusion | flops 983040 | bytes 5243905 | tf_op jit(solution)/shard_map/jit(_where)/select_n | solution.py:9
  23.2 0.2 fusion.1
  23.5 4.3 %slice.34 = f32[1536,640]{0,1:T(8,128)} slice(f32[2048,640]{0,1:T(8,128)} %copy.26), slice={[512:2048], [0:640]} | slice | bytes 7864320 | tf_op jit(solution)/shard_map/slice | solution.py:44
  27.8 0.3 reduce-window.24
  28.1 0.1 slice.26
  28.2 0.1 slice_reduce_fusion
  28.3 0.3 reduce-window.16
  28.6 0.1 slice.24
  28.7 0.1 slice_reduce_fusion.1
  28.8 0.1 add_bitcast_fusion
  28.9 0.4 select_reduce_fusion.1
  29.3 1.1 fusion
  30.4 1.3 select_reduce_fusion
  31.8 51.9 %all-reduce.9.cloned.1.call-done = (f32[512,640]{0,1:T(8,128)}, f32[512,640]{0,1:T(8,128)}) async-done(((f32[512,640]{0,1:T(8,128)}, f32[512,640]{0,1:T(8,128)}), (f32[512,640]{0,1:T(8,128)}, f32[512,640]{0,1:T(8,128)})) %all-reduce.9.cloned.1.call-update) | async-done | bytes 2621456 | tf_op jit(solution)/shard_map/psum | solution.py:37
  83.7 1.7 copy.28
  85.4 9.3 %gather_fusion.1 = f32[2048,640]{1,0:T(8,128)} fusion(f32[512,640]{1,0:T(8,128)S(1)} %copy.28, s32[2048]{0:T(1024)S(1)} %broadcast_clamp_fusion), kind=kCustom, calls=%fused_computation.1 | custom fusion | bytes 10493952 | tf_op jit(solution)/shard_map/jit(_take)/gather | solution.py:42
  94.8 6.2 %copy.29 = f32[2048,640]{0,1:T(8,128)} copy(f32[2048,640]{1,0:T(8,128)} %gather_fusion.1) | data formatting | bytes 10485760 | tf_op jit(solution)/shard_map/jit(_take)/gather | solution.py:42
  100.9 7.0 %maximum_select_fusion = f32[2048,640]{0,1:T(8,128)S(1)} fusion(f32[1536,640]{0,1:T(8,128)} %slice.34, f32[512,640]{0,1:T(8,128)S(1)} %copy-done.2, f32[2048,640]{0,1:T(8,128)} %copy.26, f32[2048,640]{0,1:T(8,128)} %copy.29, pred[2048]{0:T(1024)(128)(4,1)S(1)} %compare_and_fusion.1, pred[2048]{0:T(1024)(128)(4,1)S(1)} %fusion, ...), kind=kLoop, calls=%fused_computation.2 | loop fusion | flops 5242880 | bytes 20977664 | tf_op jit(solution)/shard_map/jit(_where)/select_n | solution.py:45
  107.9 4.8 %broadcast_select_fusion = (f32[2048,512]{0,1:T(8,128)}, f32[2048,512]{0,1:T(8,128)}) fusion(pred[]{:T(512)S(6)} %eq.59, f32[2048,640]{0,1:T(8,128)S(1)} %maximum_select_fusion, pred[2048]{0:T(1024)(128)(4,1)S(1)} %broadcast_compare_fusion), kind=kLoop, calls=%fused_computation.8 | loop fusion | flops 2097152 | bytes 12584961 | tf_op jit(solution)/shard_map/jit(_where)/select_n | solution.py:9
  112.8 0.1 copy-done.1
  112.9 1.2 copy-done.3
  114.1 2.8 conditional.1
  114.1 2.8 concatenate.6.clone
  116.9 3.6 %fusion.4 = f32[640,512]{1,0:T(8,128)S(1)} fusion(f32[512,640]{0,1:T(8,128)} %get-tuple-element.22, f32[512,512]{1,0:T(8,128)S(1)} %copy-done), kind=kOutput, calls=%fused_computation.34 | convolution fusion | flops 2013265920 | bytes 3670016 | tf_op jit(solution)/shard_map/dot_general | solution.py:48
  120.4 3.3 %fusion.5 = f32[640,512]{1,0:T(8,128)} fusion(f32[640,512]{1,0:T(8,128)S(1)} %fusion.4, f32[512,512]{1,0:T(8,128)S(1)} %copy-done.3), kind=kOutput, calls=%fused_computation.35 | convolution fusion | flops 2013265920 | bytes 3670016 | tf_op jit(solution)/shard_map/dot_general | solution.py:52
  123.8 144.7 %all-reduce.7.cloned.1.call-done = f32[2048,512]{0,1:T(8,128)} async-done(((f32[2048,512]{0,1:T(8,128)}), f32[2048,512]{0,1:T(8,128)}) %all-reduce.7.cloned.1.call-update) | async-done | bytes 4194320 | tf_op jit(solution)/shard_map/psum | solution.py:9
  268.5 15.9 %select_select_fusion = f32[2048,640]{0,1:T(8,128)} fusion(f32[2048,640]{0,1:T(8,128)} %get-tuple-element.21, f32[2048,640]{0,1:T(8,128)} %copy-done.1, f32[512,640]{0,1:T(8,128)S(1)} %bitcast.19, f32[2048,512]{0,1:T(8,128)} %all-reduce.7.cloned.1.call-done, f32[640,512]{1,0:T(8,128)} %fusion.5, pred[640]{0:T(1024)(128)(4,1)S(1)} %add_compare_fusion, ...), kind=kOutput, calls=%fused_computation.3 | convolution fusion | flops 8058306560 | bytes 22547072 | tf_op jit(solution)/shard_map/dot_general | solution.py:53
  284.3 5.9 %copy.34 = f32[2048,640]{1,0:T(8,128)} copy(f32[2048,640]{0,1:T(8,128)} %select_select_fusion) | data formatting | bytes 10485760 | tf_op jit(solution)/shard_map/jit(_where)/select_n | solution.py:68
  (24 shorter events, 0.2 us)
Async XLA Ops:
  6.5 110.3 %copy-start = (f32[512,512]{1,0:T(8,128)S(1)}, f32[512,512]{1,0:T(8,128)}, u32[]{:S(2)}) copy-start(f32[512,512]{1,0:T(8,128)} %param.8) | copy-start | bytes 3145732
  6.5 77.2 %all-reduce.9.cloned.1.call-start = ((), (), s32[]{:S(2)}) async-start(), calls=%async_computation.1 | async-start | bytes 5242880 | tf_op jit(solution)/shard_map/psum | solution.py:37
  19.4 3.8 %copy-start.4 = (s32[512]{0:T(512)S(1)}, s32[512]{0:T(512)}, u32[]{:S(2)}) copy-start(s32[512]{0:T(512)} %param.7) | copy-start | bytes 6148
  23.1 245.3 %all-reduce.7.cloned.1.call-start = ((), (), s32[]{:S(2)}) async-start(), calls=%async_computation | async-start | bytes 8388608 | tf_op jit(solution)/shard_map/psum | solution.py:9
  94.8 6.2 %copy-start.2 = (f32[512,640]{0,1:T(8,128)S(1)}, f32[512,640]{0,1:T(8,128)}, u32[]{:S(2)}) copy-start(f32[512,640]{0,1:T(8,128)} %get-tuple-element.22) | copy-start | bytes 3932164
  107.9 4.9 %copy-start.1 = (f32[2048,640]{0,1:T(8,128)}, f32[2048,640]{0,1:T(8,128)S(1)}, u32[]{:S(2)}) copy-start(f32[2048,640]{0,1:T(8,128)S(1)} %maximum_select_fusion) | copy-start | bytes 15728644
  112.9 1.2 copy-start.3
Sparse Core Ops, SparseCore 0:
  23.3 60.4 all-reduce.8
  113.0 155.4 all-reduce.6
where the time goes:
time: 301 us; the launch traced here: 297 us
  waiting for transfers between devices  197 us (65%)
  local copies, waits for them, and re-layouts  43.9 us (15%)
  matrix products  22.8 us (8%)
  other arithmetic  20.2 us (7%)
  between operations  13.5 us (4%)
    psum x1, waiting for transfers between devices, from_root(): return lax.psum(jnp.where(mine, array, jnp.zeros_like(array)), axis)  145 us
    psum x1, waiting for transfers between devices, local(): new_top = lax.psum(picked, 'prow')  51.9 us
    dot_general x1, matrix products, local(): update = jnp.dot(spread, combined, precision=lax.Precision.HIGHEST)  15.9 us
    gather x2, local copies, waits for them, and re-layouts, local(): from_old = jnp.take(old_top, sources, axis=0)  15.5 us
    select_n x2, other arithmetic, from_root(): return lax.psum(jnp.where(mine, array, jnp.zeros_like(array)), axis)  8.55 us
    unnamed x11, local copies, waits for them, and re-layouts  7.16 us
    select_n x1, other arithmetic, local(): jnp.where(top_rows[:, None], from_top, jnp.where(displaced[:, None], from...  6.99 us
    gather x2, local copies, waits for them, and re-layouts, local(): picked = jnp.take(matrix, jnp.clip(owned_rows, 0, row_dev - 1), axis=0)  6.19 us
  transfers between devices with their start and end apart: 2, of which 2 were waited for; matrix products, arithmetic and copies ran while one was open for 6% of the time, Pallas kernels for 0%

commit v1 on v0

v1 whole, which is shorter than its diff:
```python
import functools

import jax
import jax.numpy as jnp
from jax import lax
from jax.experimental import pallas as pl
from jax.experimental.pallas import tpu as pltpu
from jax.sharding import PartitionSpec as P

HIGHEST = lax.Precision.HIGHEST
VMEM = pl.BlockSpec(memory_space=pltpu.VMEM)
SMEM = pl.BlockSpec(memory_space=pltpu.SMEM)
ANY = pl.BlockSpec(memory_space=pl.ANY)
LANES = 128
PICK, FROM, ROW, COUNT = 0, 1, 2, 3


def call(kernel, out, ins, outs, scratch=(), vmem=40 << 20, flops=0, moved=0):
    return pl.pallas_call(
        kernel,
        out_shape=out,
        in_specs=ins,
        out_specs=outs,
        scratch_shapes=list(scratch),
        compiler_params=pltpu.CompilerParams(vmem_limit_bytes=vmem),
        cost_estimate=pl.CostEstimate(
            flops=flops, bytes_accessed=moved, transcendentals=0
        ),
    )


def index_kernel(where_ref, pivots_ref, table_ref, owner_ref, *, row_dev):
    nb = pivots_ref.shape[1]
    start = where_ref[0] * row_dev
    first = where_ref[0] == 0
    down = lax.broadcasted_iota(jnp.int32, (nb, nb), 0)
    across = lax.broadcasted_iota(jnp.int32, (nb, nb), 1)
    piv_row = jnp.broadcast_to(pivots_ref[...], (nb, nb))

    def column(full):
        return jnp.sum(jnp.where(down == across, full, 0.0), axis=1, keepdims=True)

    piv_f = piv_row.astype(jnp.float32)
    piv_col = jnp.broadcast_to(column(piv_f), (nb, nb))
    upto = (down <= across).astype(jnp.bfloat16)
    below = (piv_row >= nb).astype(jnp.float32)
    vacancy = jnp.dot(
        below[:8].astype(jnp.bfloat16), upto, preferred_element_type=jnp.float32
    )[:1]
    taken = jnp.max((piv_row == down).astype(jnp.float32), axis=1, keepdims=True)
    freed = jnp.broadcast_to(1.0 - taken, (nb, LANES))
    rank = jnp.dot(
        (across <= down).astype(jnp.bfloat16),
        freed.astype(jnp.bfloat16),
        preferred_element_type=jnp.float32,
    )[:, :1]
    down_f = down.astype(jnp.float32)
    pair = (rank == vacancy) & (freed[:, :1] > 0.5)
    source = jnp.sum(jnp.where(pair, down_f, 0.0), axis=0, keepdims=True)
    source_col = jnp.broadcast_to(column(jnp.broadcast_to(source, (nb, nb))), (nb, nb))

    own_row = (pivots_ref[...] >= start) & (pivots_ref[...] < start + row_dev)
    pick = jnp.where(own_row, pivots_ref[...] - start, source.astype(jnp.int32))
    moved_row = (own_row & (pivots_ref[...] >= nb)).astype(jnp.float32)
    start_f = start.astype(jnp.float32)
    moved_col = (
        (piv_col >= start_f) & (piv_col < start_f + row_dev) & (piv_col >= nb)
    )
    order = jnp.sum(
        jnp.where(piv_f < piv_col, jnp.broadcast_to(moved_row, (nb, nb)), 0.0),
        axis=1,
        keepdims=True,
    )
    placed = moved_col & (order == across.astype(jnp.float32))
    origin = jnp.where(first, source_col, down_f)
    listed_from = jnp.sum(jnp.where(placed, origin, 0.0), axis=0, keepdims=True)
    listed_row = jnp.sum(
        jnp.where(placed, piv_col - start_f, 0.0), axis=0, keepdims=True
    )
    count = jnp.sum(moved_row, axis=1, keepdims=True)
    table_ref[...] = jnp.zeros_like(table_ref)
    table_ref[PICK : PICK + 1, :] = pick
    table_ref[FROM : FROM + 1, :] = listed_from.astype(jnp.int32)
    table_ref[ROW : ROW + 1, :] = listed_row.astype(jnp.int32)
    table_ref[COUNT : COUNT + 1, :] = jnp.broadcast_to(
        count.astype(jnp.int32), (1, nb)
    )
    owner_ref[...] = piv_col[:, :LANES].astype(jnp.int32) // row_dev


def gather_kernel(table_ref, matrix_ref, out_ref):
    nb = out_ref.shape[0]

    @pl.loop(0, nb, step=8)
    def _(base):
        for k in range(8):
            j = base + k
            out_ref[pl.ds(j, 1), :] = matrix_ref[pl.ds(table_ref[PICK, j], 1), :]


def merge_kernel(where_ref, owner_ref, held_ref, *refs, log, halves):
    arrived, (merged_ref, half_ref) = refs[: 2 if halves else 1], refs[-2:]
    me = where_ref[0]
    mine, theirs = me >> log, (me >> log) ^ 1
    odd = me & 1
    nb, cols = held_ref.shape
    half = nb // 2

    def merge(rows, piece):
        group = owner_ref[rows, :] >> log
        take = (group == theirs) | ((theirs == 0) & (group != mine))
        for q in range(cols // LANES):
            lane = slice(q * LANES, (q + 1) * LANES)
            merged_ref[rows, lane] = jnp.where(take, piece[:, lane], held_ref[rows, lane])

    low, high = slice(0, half), slice(half, nb)
    if halves:
        @pl.when(odd == 0)
        def _():
            merge(low, arrived[0])
            merge(high, arrived[1])

        @pl.when(odd == 1)
        def _():
            merge(low, arrived[1])
            merge(high, arrived[0])
    else:
        merge(slice(0, nb), arrived[0])

    @pl.when(odd == 0)
    def _():
        half_ref[...] = merged_ref[low, :]

    @pl.when(odd == 1)
    def _():
        half_ref[...] = merged_ref[high, :]


def factor_kernel(where_ref, top_in_ref, lower_ref, upper_ref, weights_ref, top_ref):
    nb, cols = top_in_ref.shape
    u = jnp.dot(
        lower_ref[...], top_in_ref[...], precision=HIGHEST,
        preferred_element_type=jnp.float32,
    )
    top_ref[...] = u
    weights_ref[...] = jnp.dot(
        upper_ref[...], u, precision=HIGHEST, preferred_element_type=jnp.float32
    )

    @pl.when(where_ref[1] == 0)
    def _():
        top_ref[:, :nb] = top_in_ref[:, :nb]
        weights_ref[:, :nb] = -upper_ref[...]


def final_kernel(
    where_ref, table_ref, choice_ref, displaced_ref, weights_ref, top_ref, matrix_ref,
    *refs, counts, chunk, extra, block,
):
    n_bufs = sum(counts)
    bufs = refs[:n_bufs]
    out_ref = refs[n_bufs]
    mat, pan, low, w_hi, w_lo, result, in_sem, mat_sem, out_sem = refs[n_bufs + 1 :]
    rows, cols = matrix_ref.shape
    nb = weights_ref.shape[0]
    first_row, first_col = where_ref[0] == 0, where_ref[1] == 0
    full = rows // (2 * chunk)

    load = pltpu.make_async_copy(matrix_ref, mat, mat_sem)
    load.start()

    def place(i, h):
        if i < full:
            return pan.at[pl.ds((2 * i + h) * chunk, chunk), :]
        return low.at[pl.ds((2 * (i - full) + h) * chunk, chunk), :]

    @pl.when(first_col)
    def _():
        pltpu.make_async_copy(matrix_ref.at[:, pl.ds(0, nb)], pan, in_sem).start()
        pltpu.make_async_copy(displaced_ref.at[:, pl.ds(0, nb)], low, in_sem).start()

    @pl.when(jnp.logical_not(first_col))
    def _():
        for i in range(full + extra):
            for h in range(2):
                for b in candidates(i, h, counts):
                    @pl.when(choice_ref[2 * i + h] == b)
                    def _():
                        pltpu.make_async_copy(bufs[b], place(i, h), in_sem).start()

    w = weights_ref[...]
    w_hi[...] = w.astype(jnp.bfloat16)
    w_lo[...] = (w - w_hi[...].astype(jnp.float32)).astype(jnp.bfloat16)

    pltpu.make_async_copy(matrix_ref.at[:, pl.ds(0, nb)], pan, in_sem).wait()
    pltpu.make_async_copy(displaced_ref.at[:, pl.ds(0, nb)], low, in_sem).wait()
    load.wait()

    count = table_ref[COUNT, 0]

    def swap(from_mat, from_pan):
        def body(k, _):
            to, at = table_ref[ROW, k], table_ref[FROM, k]
            mat[pl.ds(to, 1), :] = from_mat[pl.ds(at, 1), :]
            pan[pl.ds(to, 1), :] = from_pan[pl.ds(at, 1), :]
            return 0

        lax.fori_loop(0, count, body, 0)

    @pl.when(first_row)
    def _():
        swap(mat, pan)

    @pl.when(jnp.logical_not(first_row))
    def _():
        swap(displaced_ref, low)

    @pl.when(first_col)
    def _():
        mat[:, :nb] = jnp.zeros((rows, nb), jnp.float32)

    copies = []
    for b in range(rows // block):
        span = pl.ds(b * block, block)

        def update():
            p = pan[span, :]
            p_hi = p.astype(jnp.bfloat16)
            p_lo = (p - p_hi.astype(jnp.float32)).astype(jnp.bfloat16)
            dot = functools.partial(jnp.dot, preferred_element_type=jnp.float32)
            total = dot(p_lo, w_hi[...]) + dot(p_hi, w_lo[...]) + dot(p_hi, w_hi[...])
            result[span, :] = mat[span, :] - total

        if (b + 1) * block <= nb:
            pl.when(jnp.logical_not(first_row))(update)

            @pl.when(first_row)
            def _():
                result[span, :] = top_ref[span, :]
        else:
            update()
        copy = pltpu.make_async_copy(result.at[span, :], out_ref.at[span, :], out_sem)
        copy.start()
        copies.append(copy)
    for copy in copies:
        copy.wait()


def candidates(i, h, counts):
    n_feed, n_chain, n_cross, n_back = counts
    depth = n_chain - n_feed + 1
    chain, cross = n_feed, n_feed + n_chain
    back = cross + n_cross
    if h == 0:
        found = [i]
        for z in range(1, depth):
            found += [chain + i + z, cross + i + z]
    else:
        found = [back + i]
        for z in range(1, depth):
            found += [chain + i + z - 1, cross + i + z - 1]
    return found


def choice_table(n_cols, counts):
    n_feed, n_chain, n_cross, n_back = counts
    chain, cross = n_feed, n_feed + n_chain
    back = cross + n_cross
    table = []
    for p in range(n_cols):
        z, y = divmod(p, 2)
        row = []
        for i in range(n_feed):
            if z == 0:
                row += [i, back + i] if y else [0, 0]
            elif y:
                row += [chain + i + z, cross + i + z - 1]
            else:
                row += [cross + i + z, chain + i + z - 1]
        table.append(row)
    return table


def spread(pieces, col, n_cols):
    total, depth = len(pieces), n_cols // 2
    pass_feed = [(0, 1)]
    pass_chain = [(p, p + 2) for p in range(n_cols - 2)]
    pass_cross = [(p, p ^ 1) for p in range(2, n_cols)]
    pass_back = [(3, 1)]
    send = functools.partial(lax.ppermute, axis_name="pcol")
    feed, chain, cross, back = [], [], [], []
    for s in range(total + depth):
        if s < total + depth - 1:
            own = pieces[s][1] if s < total else pieces[0][1]
            if s == 0:
                entry = own
            else:
                entry = chain[s - 1]
                if s - 1 < total:
                    entry = jnp.where(col < 2, feed[s - 1], entry)
                if s < total:
                    entry = jnp.where(col == 0, own, entry)
        if s < total:
            feed.append(send(pieces[s][0], perm=pass_feed))
        if s >= 1:
            cross.append(send(chain[s - 1], perm=pass_cross))
        if s < total + depth - 1:
            chain.append(send(entry, perm=pass_chain))
        if 2 <= s < total + 2:
            back.append(send(cross[s - 2], perm=pass_back))
    return feed, chain, cross, back


def local(matrix, pivots, lower_inverse, upper_inverse, *, n_rows, n_cols, parts):
    row_dev, cols = matrix.shape
    nb = pivots.shape[0]
    f32 = jnp.float32
    row, col = lax.axis_index("prow"), lax.axis_index("pcol")
    here = jnp.stack([row, col]).astype(jnp.int32)

    table, owner = call(
        functools.partial(index_kernel, row_dev=row_dev),
        (jax.ShapeDtypeStruct((8, nb), jnp.int32), jax.ShapeDtypeStruct((nb, LANES), jnp.int32)),
        [SMEM, VMEM], (VMEM, VMEM),
    )(here, pivots.reshape(1, nb))

    slot = jax.ShapeDtypeStruct((nb, cols), f32)
    half_slot = jax.ShapeDtypeStruct((nb // 2, cols), f32)
    held = call(gather_kernel, slot, [SMEM, VMEM], VMEM)(table, matrix)
    displaced = held
    log = 0
    half = None
    while (1 << log) < n_rows:
        d = 1 << log
        far = [(p, p ^ d) for p in range(n_rows)]
        if log == 0:
            arrived = [lax.ppermute(held, "prow", far)]
            whole = arrived[0]
        else:
            near = [(p, p ^ 1) for p in range(n_rows)]
            one = lax.ppermute(half, "prow", far)
            two = lax.ppermute(one, "prow", near)
            arrived = [one, two]
            whole = jnp.concatenate(
                [jnp.where(row % 2 == 0, one, two), jnp.where(row % 2 == 0, two, one)], axis=0
            )
        held, half = call(
            functools.partial(merge_kernel, log=log, halves=log > 0),
            (slot, half_slot), [SMEM] + [VMEM] * (2 + len(arrived)), (VMEM, VMEM),
        )(here, owner, held, *arrived)
        displaced = jnp.where((row >> log) == 1, whole, displaced)
        log += 1

    weights, top = call(
        factor_kernel, (slot, slot), [SMEM, VMEM, VMEM, VMEM], (VMEM, VMEM),
        flops=4 * nb * nb * cols * 6,
    )(here, held, lower_inverse, upper_inverse)

    chunk = row_dev // (2 * parts)
    extra = nb // (2 * chunk)
    pieces = []
    for i in range(parts + extra):
        source, at = (matrix, i) if i < parts else (displaced, i - parts)
        pieces.append(tuple(
            lax.slice(source, ((2 * at + h) * chunk, 0), ((2 * at + h + 1) * chunk, nb))
            for h in range(2)
        ))
    sent = spread(pieces, col, n_cols)
    counts = tuple(len(group) for group in sent)
    bufs = [b for group in sent for b in group]
    choice = jnp.asarray(choice_table(n_cols, counts), jnp.int32)[col]

    block = 256
    return call(
        functools.partial(
            final_kernel, counts=counts, chunk=chunk, extra=extra, block=block
        ),
        jax.ShapeDtypeStruct(matrix.shape, f32),
        [SMEM, SMEM, SMEM, VMEM, VMEM, VMEM, ANY] + [ANY] * len(bufs),
        ANY,
        [
            pltpu.VMEM((row_dev, cols), f32),
            pltpu.VMEM((row_dev, nb), f32),
            pltpu.VMEM((nb, nb), f32),
            pltpu.VMEM((nb, cols), jnp.bfloat16),
            pltpu.VMEM((nb, cols), jnp.bfloat16),
            pltpu.VMEM((row_dev, cols), f32),
            pltpu.SemaphoreType.DMA,
            pltpu.SemaphoreType.DMA,
            pltpu.SemaphoreType.DMA,
        ],
        flops=2 * row_dev * nb * cols * 3,
        moved=4 * row_dev * (2 * cols + nb),
    )(here, table, choice, displaced, weights, top, matrix, *bufs)


def solution(mesh):
    n_rows, n_cols = mesh.shape["prow"], mesh.shape["pcol"]
    return jax.shard_map(
        functools.partial(local, n_rows=n_rows, n_cols=n_cols, parts=8),
        mesh=mesh,
        in_specs=(P("prow", "pcol"), P(), P(), P()),
        out_specs=P("prow", "pcol"),
        check_vma=False,
    )
```

time: 301 us -> 202 us (0.67)
  waiting for transfers between devices: 197 us -> 51.2 us
  starting transfers between devices: 0.04 us -> 95.7 us
  local copies, waits for them, and re-layouts: 43.9 us -> 16.9 us
  Pallas kernels: 0 us -> 26.2 us
  matrix products: 22.8 us -> 0 us
  between operations: 13.5 us -> 1.64 us
  other arithmetic: 20.2 us -> 8.63 us
    psum x2 -> x0, waiting for transfers between devices: 197 us -> none  [the longest x1 145 us: from_root(): return lax.psum(jnp.where(mine, array, jnp.zeros_like(array)), axis)]
    ppermute x0 -> x49, starting transfers between devices: none -> 95.7 us  [the longest x13 47 us: spread(): cross.append(send(chain[s - 1], perm=pass_cross))]
    ppermute x0 -> x49, waiting for transfers between devices: none -> 51.2 us  [the longest x13 40.6 us: spread(): chain.append(send(entry, perm=pass_chain))]
    pallas_call x0 -> x6, Pallas kernels: none -> 26.2 us  [the longest x1 13 us: local(): call(functools.partial(final_kernel, counts=counts, chunk=chunk, extra=ex...]
    dot_general x3 -> x0, matrix products: 22.8 us -> none  [the longest x1 15.9 us: local(): update = jnp.dot(spread, combined, precision=lax.Precision.HIGHEST)]
    gather x4 -> x0, local copies, waits for them, and re-layouts: 21.7 us -> none  [the longest x2 15.5 us: local(): from_old = jnp.take(old_top, sources, axis=0)]
    unnamed x11 -> x152, local copies, waits for them, and re-layouts: 7.16 us -> 15.1 us
    select_n x4 -> x12, other arithmetic: 15.6 us -> 8.55 us  [the longest x9 7.13 us: spread(): entry = jnp.where(col == 0, own, entry)]
  transfers between devices with their start and end apart: 2 -> 49, of which waited for: 2 -> 9; matrix products, arithmetic and copies ran while one was open for 6% -> 4% of each run, Pallas kernels for 0% -> 7%
where the time goes in v1:
time: 202 us; the launch traced here: 200 us
  starting transfers between devices  95.7 us (47%)
  waiting for transfers between devices  51.2 us (25%)
  Pallas kernels  26.2 us (13%)
  local copies, waits for them, and re-layouts  16.9 us (8%)
  other arithmetic  8.63 us (4%)
    ppermute x13, starting transfers between devices, spread(): cross.append(send(chain[s - 1], perm=pass_cross))  47 us
    ppermute x13, waiting for transfers between devices, spread(): chain.append(send(entry, perm=pass_chain))  40.6 us
    ppermute x13, starting transfers between devices, spread(): chain.append(send(entry, perm=pass_chain))  32.3 us
    unnamed x152, local copies, waits for them, and re-layouts  15.1 us
    pallas_call x1, Pallas kernels, local(): call(functools.partial(final_kernel, counts=counts, chunk=chunk, extra=ex...  13 us
    ppermute x10, starting transfers between devices, spread(): back.append(send(cross[s - 2], perm=pass_back))  8.15 us
    ppermute x10, starting transfers between devices, spread(): feed.append(send(pieces[s][0], perm=pass_feed))  7.6 us
    select_n x9, other arithmetic, spread(): entry = jnp.where(col == 0, own, entry)  7.13 us
  transfers between devices with their start and end apart: 49, of which 9 were waited for; matrix products, arithmetic and copies ran while one was open for 4% of the time, Pallas kernels for 7%

profile of v1, /device:TPU:10, one launch (start us, length us, event | category | flops | bytes accessed | tf_op | source)
XLA Modules:
  0.0 200.3 jit_solution(4110248744075479376)
XLA Ops:
  1.1 3.5 %collective-permute-start.13 = (f32[128,512]{1,0:T(8,128)S(1)}, f32[128,512]{1,0:T(8,128)S(1)}, u32[]{:S(2)}, u32[]{:S(2)}) collective-permute-start(f32[128,512]{1,0:T(8,128)S(1)} %get-tuple-element.33), channel_id=1, source_target_pairs={{0,2},{1,3},{2,4},{3,5},{4,6},{5,7},{8,10},{9,11},{10,12},{11,13},... | collective-permute-start | bytes 786440 | tf_op jit(solution)/shard_map/ppermute | solution.py:308
  5.3 5.8 %collective-permute-done.13.refs_10_ = f32[128,512]{1,0:T(8,128)S(1)} collective-permute-done((f32[128,512]{1,0:T(8,128)S(1)}, f32[128,512]{1,0:T(8,128)S(1)}, u32[]{:S(2)}, u32[]{:S(2)}) %collective-permute-start.13) | collective-permute-done | bytes 262176 | tf_op jit(solution)/shard_map/ppermute | solution.py:308
  12.2 3.5 %collective-permute-start.14 = (f32[128,512]{1,0:T(8,128)S(1)}, f32[128,512]{1,0:T(8,128)S(1)}, u32[]{:S(2)}, u32[]{:S(2)}) collective-permute-start(f32[128,512]{1,0:T(8,128)S(1)} %get-tuple-element.31), channel_id=1, source_target_pairs={{0,2},{1,3},{2,4},{3,5},{4,6},{5,7},{8,10},{9,11},{10,12},{11,13},... | collective-permute-start | bytes 786440 | tf_op jit(solution)/shard_map/ppermute | solution.py:308
  18.0 2.6 %copy-done = f32[2048,640]{1,0:T(8,128)S(1)} copy-done((f32[2048,640]{1,0:T(8,128)S(1)}, f32[2048,640]{1,0:T(8,128)}, u32[]{:S(2)}) %copy-start) | copy-done | bytes 5242904
  20.6 3.5 %shard_map.56.held_ref = f32[512,640]{1,0:T(8,128)S(1)} custom-call(s32[8,512]{1,0:T(8,128)S(1)} %get-tuple-element.12.table_ref, f32[2048,640]{1,0:T(8,128)S(1)} %copy-done), custom_call_target="tpu_custom_call" | custom-call | tf_op jit(solution)/shard_map/pallas_call | solution.py:329
  24.3 3.5 %collective-permute-start.15 = (f32[128,512]{1,0:T(8,128)S(1)}, f32[128,512]{1,0:T(8,128)S(1)}, u32[]{:S(2)}, u32[]{:S(2)}) collective-permute-start(f32[128,512]{1,0:T(8,128)S(1)} %get-tuple-element.29), channel_id=1, source_target_pairs={{0,2},{1,3},{2,4},{3,5},{4,6},{5,7},{8,10},{9,11},{10,12},{11,13},... | collective-permute-start | bytes 786440 | tf_op jit(solution)/shard_map/ppermute | solution.py:308
  28.5 8.3 %collective-permute-done.15.refs_12_ = f32[128,512]{1,0:T(8,128)S(1)} collective-permute-done((f32[128,512]{1,0:T(8,128)S(1)}, f32[128,512]{1,0:T(8,128)S(1)}, u32[]{:S(2)}, u32[]{:S(2)}) %collective-permute-start.15) | collective-permute-done | bytes 262176 | tf_op jit(solution)/shard_map/ppermute | solution.py:308
  39.5 7.4 %collective-permute-done.16.refs_13_ = f32[128,512]{1,0:T(8,128)S(1)} collective-permute-done((f32[128,512]{1,0:T(8,128)S(1)}, f32[128,512]{1,0:T(8,128)S(1)}, u32[]{:S(2)}, u32[]{:S(2)}) %collective-permute-start.16) | collective-permute-done | bytes 262176 | tf_op jit(solution)/shard_map/ppermute | solution.py:308
  47.0 2.2 %collective-permute-start.17 = (f32[128,512]{1,0:T(8,128)S(1)}, f32[128,512]{1,0:T(8,128)S(1)}, u32[]{:S(2)}, u32[]{:S(2)}) collective-permute-start(f32[128,512]{1,0:T(8,128)S(1)} %get-tuple-element.25), channel_id=1, source_target_pairs={{0,2},{1,3},{2,4},{3,5},{4,6},{5,7},{8,10},{9,11},{10,12},{11,13},... | collective-permute-start | bytes 786440 | tf_op jit(solution)/shard_map/ppermute | solution.py:308
  51.5 4.6 %collective-permute-done.17.refs_14_ = f32[128,512]{1,0:T(8,128)S(1)} collective-permute-done((f32[128,512]{1,0:T(8,128)S(1)}, f32[128,512]{1,0:T(8,128)S(1)}, u32[]{:S(2)}, u32[]{:S(2)}) %collective-permute-start.17) | collective-permute-done | bytes 262176 | tf_op jit(solution)/shard_map/ppermute | solution.py:308
  58.1 2.5 %collective-permute-start.18 = (f32[128,512]{1,0:T(8,128)S(1)}, f32[128,512]{1,0:T(8,128)S(1)}, u32[]{:S(2)}, u32[]{:S(2)}) collective-permute-start(f32[128,512]{1,0:T(8,128)S(1)} %get-tuple-element.23), channel_id=1, source_target_pairs={{0,2},{1,3},{2,4},{3,5},{4,6},{5,7},{8,10},{9,11},{10,12},{11,13},... | collective-permute-start | bytes 786440 | tf_op jit(solution)/shard_map/ppermute | solution.py:308
  61.3 5.4 %collective-permute-done.1.refs_0_ = f32[256,640]{1,0:T(8,128)S(1)} collective-permute-done((f32[256,640]{1,0:T(8,128)S(1)}, f32[256,640]{1,0:T(8,128)S(1)}, u32[]{:S(2)}, u32[]{:S(2)}) %collective-permute-start.1) | collective-permute-done | bytes 655392 | tf_op jit(solution)/shard_map/ppermute | solution.py:341
  66.7 2.1 %select_select_fusion.1 = (f32[128,512]{1,0:T(8,128)}, f32[128,512]{1,0:T(8,128)}) fusion(f32[128,512]{1,0:T(8,128)S(1)} %collective-permute-done.8.refs_5_, f32[128,512]{1,0:T(8,128)S(1)} %collective-permute-done.18.refs_15_, f32[2048,640]{1,0:T(8,128)} %matrix_ref.3, pred[]{:T(512)S(6)} %lt.14, pred[]{:T(512)S(6)} %eq.14), kind=kLoop, calls=%fused_computation.6 | loop fusion | flops 131072 | bytes 1572866 | tf_op jit(solution)/shard_map/jit(_where)/select_n | solution.py:302
  68.9 2.4 %collective-permute-start.19 = (f32[128,512]{1,0:T(8,128)}, f32[128,512]{1,0:T(8,128)}, u32[]{:S(2)}, u32[]{:S(2)}) collective-permute-start(f32[128,512]{1,0:T(8,128)} %get-tuple-element.21), channel_id=1, source_target_pairs={{0,2},{1,3},{2,4},{3,5},{4,6},{5,7},{8,10},{9,11},{10,12},{11,13},... | collective-permute-start | bytes 786440 | tf_op jit(solution)/shard_map/ppermute | solution.py:308
  72.6 8.4 %collective-permute-done.19.refs_16_ = f32[128,512]{1,0:T(8,128)} collective-permute-done((f32[128,512]{1,0:T(8,128)}, f32[128,512]{1,0:T(8,128)}, u32[]{:S(2)}, u32[]{:S(2)}) %collective-permute-start.19) | collective-permute-done | bytes 262176 | tf_op jit(solution)/shard_map/ppermute | solution.py:308
  86.3 6.0 %collective-permute-done.20.refs_17_ = f32[128,512]{1,0:T(8,128)S(1)} collective-permute-done((f32[128,512]{1,0:T(8,128)S(1)}, f32[128,512]{1,0:T(8,128)S(1)}, u32[]{:S(2)}, u32[]{:S(2)}) %collective-permute-start.20) | collective-permute-done | bytes 262176 | tf_op jit(solution)/shard_map/ppermute | solution.py:308
  92.4 2.3 %collective-permute-start.21 = (f32[128,512]{1,0:T(8,128)S(1)}, f32[128,512]{1,0:T(8,128)}, u32[]{:S(2)}, u32[]{:S(2)}) collective-permute-start(f32[128,512]{1,0:T(8,128)S(1)} %get-tuple-element.37), channel_id=1, source_target_pairs={{0,2},{1,3},{2,4},{3,5},{4,6},{5,7},{8,10},{9,11},{10,12},{11,13},... | collective-permute-start | bytes 786440 | tf_op jit(solution)/shard_map/ppermute | solution.py:308
  97.4 3.9 %collective-permute-start.27 = (f32[128,512]{1,0:T(8,128)S(1)}, f32[128,512]{1,0:T(8,128)S(1)}, u32[]{:S(2)}, u32[]{:S(2)}) collective-permute-start(f32[128,512]{1,0:T(8,128)S(1)} %copy-done.12), channel_id=1, source_target_pairs={{2,3},{3,2},{4,5},{5,4},{6,7},{7,6},{10,11},{11,10},{12,13},{13,12... | collective-permute-start | bytes 786440 | tf_op jit(solution)/shard_map/ppermute | solution.py:306
  107.8 4.4 %collective-permute-done.27.refs_24_ = f32[128,512]{1,0:T(8,128)S(1)} collective-permute-done((f32[128,512]{1,0:T(8,128)S(1)}, f32[128,512]{1,0:T(8,128)S(1)}, u32[]{:S(2)}, u32[]{:S(2)}) %collective-permute-start.27) | collective-permute-done | bytes 262176 | tf_op jit(solution)/shard_map/ppermute | solution.py:306
  112.2 4.1 %collective-permute-start.29 = (f32[128,512]{1,0:T(8,128)S(1)}, f32[128,512]{1,0:T(8,128)S(1)}, u32[]{:S(2)}, u32[]{:S(2)}) collective-permute-start(f32[128,512]{1,0:T(8,128)S(1)} %copy-done.21), channel_id=1, source_target_pairs={{2,3},{3,2},{4,5},{5,4},{6,7},{7,6},{10,11},{11,10},{12,13},{13,12... | collective-permute-start | bytes 786440 | tf_op jit(solution)/shard_map/ppermute | solution.py:306
  119.0 2.7 %collective-permute-start.30 = (f32[128,512]{1,0:T(8,128)S(1)}, f32[128,512]{1,0:T(8,128)S(1)}, u32[]{:S(2)}, u32[]{:S(2)}) collective-permute-start(f32[128,512]{1,0:T(8,128)S(1)} %copy-done.26), channel_id=1, source_target_pairs={{2,3},{3,2},{4,5},{5,4},{6,7},{7,6},{10,11},{11,10},{12,13},{13,12... | collective-permute-start | bytes 786440 | tf_op jit(solution)/shard_map/ppermute | solution.py:306
  123.4 3.1 %collective-permute-start.31 = (f32[128,512]{1,0:T(8,128)S(1)}, f32[128,512]{1,0:T(8,128)S(1)}, u32[]{:S(2)}, u32[]{:S(2)}) collective-permute-start(f32[128,512]{1,0:T(8,128)S(1)} %copy-done.31), channel_id=1, source_target_pairs={{2,3},{3,2},{4,5},{5,4},{6,7},{7,6},{10,11},{11,10},{12,13},{13,12... | collective-permute-start | bytes 786440 | tf_op jit(solution)/shard_map/ppermute | solution.py:306
  128.0 2.8 %collective-permute-start.23 = (f32[128,512]{1,0:T(8,128)S(1)}, f32[128,512]{1,0:T(8,128)S(1)}, u32[]{:S(2)}, u32[]{:S(2)}) collective-permute-start(f32[128,512]{1,0:T(8,128)S(1)} %broadcast_select_fusion.2), channel_id=1, source_target_pairs={{0,2},{1,3},{2,4},{3,5},{4,6},{5,7},{8,10},{9,11},{10,12},{11,13},... | collective-permute-start | bytes 786440 | tf_op jit(solution)/shard_map/ppermute | solution.py:308
  132.9 5.7 %collective-permute-start.32 = (f32[128,512]{1,0:T(8,128)}, f32[128,512]{1,0:T(8,128)}, u32[]{:S(2)}, u32[]{:S(2)}) collective-permute-start(f32[128,512]{1,0:T(8,128)} %collective-permute-done.19.refs_16_), channel_id=1, source_target_pairs={{2,3},{3,2},{4,5},{5,4},{6,7},{7,6},{10,11},{11,10},{12,13},{13,12... | collective-permute-start | bytes 786440 | tf_op jit(solution)/shard_map/ppermute | solution.py:306
  140.7 2.5 %collective-permute-start.33 = (f32[128,512]{1,0:T(8,128)S(1)}, f32[128,512]{1,0:T(8,128)}, u32[]{:S(2)}, u32[]{:S(2)}) collective-permute-start(f32[128,512]{1,0:T(8,128)S(1)} %collective-permute-done.20.refs_17_), channel_id=1, source_target_pairs={{2,3},{3,2},{4,5},{5,4},{6,7},{7,6},{10,11},{11,10},{12,13},{13,12... | collective-permute-start | bytes 786440 | tf_op jit(solution)/shard_map/ppermute | solution.py:306
  145.9 3.3 %collective-permute-start.34 = (f32[128,512]{1,0:T(8,128)}, f32[128,512]{1,0:T(8,128)}, u32[]{:S(2)}, u32[]{:S(2)}) collective-permute-start(f32[128,512]{1,0:T(8,128)} %collective-permute-done.21.refs_18_), channel_id=1, source_target_pairs={{2,3},{3,2},{4,5},{5,4},{6,7},{7,6},{10,11},{11,10},{12,13},{13,12... | collective-permute-start | bytes 786440 | tf_op jit(solution)/shard_map/ppermute | solution.py:306
  151.3 5.3 %collective-permute-start.35 = (f32[128,512]{1,0:T(8,128)}, f32[128,512]{1,0:T(8,128)}, u32[]{:S(2)}, u32[]{:S(2)}) collective-permute-start(f32[128,512]{1,0:T(8,128)} %collective-permute-done.22.refs_19_), channel_id=1, source_target_pairs={{2,3},{3,2},{4,5},{5,4},{6,7},{7,6},{10,11},{11,10},{12,13},{13,12... | collective-permute-start | bytes 786440 | tf_op jit(solution)/shard_map/ppermute | solution.py:306
  165.2 6.5 %collective-permute-start.36 = (f32[128,512]{1,0:T(8,128)S(1)}, f32[128,512]{1,0:T(8,128)S(1)}, u32[]{:S(2)}, u32[]{:S(2)}) collective-permute-start(f32[128,512]{1,0:T(8,128)S(1)} %copy-done.66), channel_id=1, source_target_pairs={{2,3},{3,2},{4,5},{5,4},{6,7},{7,6},{10,11},{11,10},{12,13},{13,12... | collective-permute-start | bytes 786440 | tf_op jit(solution)/shard_map/ppermute | solution.py:306
  172.5 2.5 %collective-permute-start.37 = (f32[128,512]{1,0:T(8,128)}, f32[128,512]{1,0:T(8,128)S(1)}, u32[]{:S(2)}, u32[]{:S(2)}) collective-permute-start(f32[128,512]{1,0:T(8,128)} %collective-permute-done.24.refs_21_), channel_id=1, source_target_pairs={{2,3},{3,2},{4,5},{5,4},{6,7},{7,6},{10,11},{11,10},{12,13},{13,12... | collective-permute-start | bytes 786440 | tf_op jit(solution)/shard_map/ppermute | solution.py:306
  175.0 3.5 %collective-permute-start.38 = (f32[128,512]{1,0:T(8,128)}, f32[128,512]{1,0:T(8,128)S(1)}, u32[]{:S(2)}, u32[]{:S(2)}) collective-permute-start(f32[128,512]{1,0:T(8,128)} %collective-permute-done.25.refs_22_), channel_id=1, source_target_pairs={{2,3},{3,2},{4,5},{5,4},{6,7},{7,6},{10,11},{11,10},{12,13},{13,12... | collective-permute-start | bytes 786440 | tf_op jit(solution)/shard_map/ppermute | solution.py:306
  178.8 5.8 %shard_map.59 = (f32[512,640]{1,0:T(8,128)S(1)}, f32[512,640]{1,0:T(8,128)S(1)}) custom-call(s32[2]{0:T(128)S(1)} %copy-done.72, f32[512,640]{1,0:T(8,128)S(1)} %get-tuple-element.16.top_in_ref, f32[512,512]{1,0:T(8,128)S(1)} %copy-done.74, f32[512,512]{1,0:T(8,128)S(1)} %copy-done.75), custom_call_target="tpu_custom_call" | custom-call | flops 4026531840 | tf_op jit(solution)/shard_map/pallas_call | solution.py:354
  187.1 13.0 %shard_map.60 = f32[2048,640]{1,0:T(8,128)} custom-call(s32[2]{0:T(128)S(1)} %copy-done.72, s32[8,512]{1,0:T(8,128)S(1)} %get-tuple-element.12.table_ref, s32[20]{0:T(128)S(1)} %dynamic-slice_bitcast_fusion.choice_ref, f32[512,640]{1,0:T(8,128)S(1)} %maximum_select_fusion.displaced_ref, f32[512,640]{1,0:T(8,128)} %copy-done.5, f32[512,640]{1,0:T(8,128)} %copy-done.6, ...), custom_call_target="tpu_custom_call" | custom-call | flops 4026531840 | bytes 14680064 | tf_op jit(solution)/shard_map/pallas_call | solution.py:374
  (239 shorter events, 55.3 us)
Async XLA Ops:
  12.2 12.0 %collective-permute-start.14 = (f32[128,512]{1,0:T(8,128)S(1)}, f32[128,512]{1,0:T(8,128)S(1)}, u32[]{:S(2)}, u32[]{:S(2)}) collective-permute-start(f32[128,512]{1,0:T(8,128)S(1)} %get-tuple-element.31), channel_id=1, source_target_pairs={{0,2},{1,3},{2,4},{3,5},{4,6},{5,7},{8,10},{9,11},{10,12},{11,13},... | collective-permute-start | bytes 786440 | tf_op jit(solution)/shard_map/ppermute | solution.py:308
  24.1 25.8 %collective-permute-start = (f32[512,640]{1,0:T(8,128)S(1)}, f32[512,640]{1,0:T(8,128)S(1)}, u32[]{:S(2)}, u32[]{:S(2)}) collective-permute-start(f32[512,640]{1,0:T(8,128)S(1)} %shard_map.56.held_ref), channel_id=1, source_target_pairs={{0,8},{8,0},{16,24},{24,16},{1,9},{9,1},{17,25},{25,17},{2,10},{10... | collective-permute-start | bytes 3932168 | tf_op jit(solution)/shard_map/ppermute | solution.py:337
  24.3 12.5 %collective-permute-start.15 = (f32[128,512]{1,0:T(8,128)S(1)}, f32[128,512]{1,0:T(8,128)S(1)}, u32[]{:S(2)}, u32[]{:S(2)}) collective-permute-start(f32[128,512]{1,0:T(8,128)S(1)} %get-tuple-element.29), channel_id=1, source_target_pairs={{0,2},{1,3},{2,4},{3,5},{4,6},{5,7},{8,10},{9,11},{10,12},{11,13},... | collective-permute-start | bytes 786440 | tf_op jit(solution)/shard_map/ppermute | solution.py:308
  51.0 15.7 %collective-permute-start.1 = (f32[256,640]{1,0:T(8,128)S(1)}, f32[256,640]{1,0:T(8,128)S(1)}, u32[]{:S(2)}, u32[]{:S(2)}) collective-permute-start(f32[256,640]{1,0:T(8,128)S(1)} %get-tuple-element.14), channel_id=1, source_target_pairs={{0,16},{8,24},{16,0},{24,8},{1,17},{9,25},{17,1},{25,9},{2,18},{10... | collective-permute-start | bytes 1966088 | tf_op jit(solution)/shard_map/ppermute | solution.py:341
  66.7 18.3 %collective-permute-start.2 = (f32[256,640]{1,0:T(8,128)S(1)}, f32[256,640]{1,0:T(8,128)S(1)}, u32[]{:S(2)}, u32[]{:S(2)}) collective-permute-start(f32[256,640]{1,0:T(8,128)S(1)} %collective-permute-done.1.refs_0_), channel_id=1, source_target_pairs={{0,8},{8,0},{16,24},{24,16},{1,9},{9,1},{17,25},{25,17},{2,10},{10... | collective-permute-start | bytes 1966088 | tf_op jit(solution)/shard_map/ppermute | solution.py:342
  68.9 12.2 %collective-permute-start.19 = (f32[128,512]{1,0:T(8,128)}, f32[128,512]{1,0:T(8,128)}, u32[]{:S(2)}, u32[]{:S(2)}) collective-permute-start(f32[128,512]{1,0:T(8,128)} %get-tuple-element.21), channel_id=1, source_target_pairs={{0,2},{1,3},{2,4},{3,5},{4,6},{5,7},{8,10},{9,11},{10,12},{11,13},... | collective-permute-start | bytes 786440 | tf_op jit(solution)/shard_map/ppermute | solution.py:308
  97.4 14.8 %collective-permute-start.27 = (f32[128,512]{1,0:T(8,128)S(1)}, f32[128,512]{1,0:T(8,128)S(1)}, u32[]{:S(2)}, u32[]{:S(2)}) collective-permute-start(f32[128,512]{1,0:T(8,128)S(1)} %copy-done.12), channel_id=1, source_target_pairs={{2,3},{3,2},{4,5},{5,4},{6,7},{7,6},{10,11},{11,10},{12,13},{13,12... | collective-permute-start | bytes 786440 | tf_op jit(solution)/shard_map/ppermute | solution.py:306
  101.3 15.6 %collective-permute-start.28 = (f32[128,512]{1,0:T(8,128)S(1)}, f32[128,512]{1,0:T(8,128)S(1)}, u32[]{:S(2)}, u32[]{:S(2)}) collective-permute-start(f32[128,512]{1,0:T(8,128)S(1)} %copy-done.16), channel_id=1, source_target_pairs={{2,3},{3,2},{4,5},{5,4},{6,7},{7,6},{10,11},{11,10},{12,13},{13,12... | collective-permute-start | bytes 786440 | tf_op jit(solution)/shard_map/ppermute | solution.py:306
  104.5 13.1 %collective-permute-start.22 = (f32[128,512]{1,0:T(8,128)S(1)}, f32[128,512]{1,0:T(8,128)}, u32[]{:S(2)}, u32[]{:S(2)}) collective-permute-start(f32[128,512]{1,0:T(8,128)S(1)} %get-tuple-element.35), channel_id=1, source_target_pairs={{0,2},{1,3},{2,4},{3,5},{4,6},{5,7},{8,10},{9,11},{10,12},{11,13},... | collective-permute-start | bytes 786440 | tf_op jit(solution)/shard_map/ppermute | solution.py:308
  106.4 12.6 %collective-permute-start.12 = (f32[128,512]{1,0:T(8,128)S(1)}, f32[128,512]{1,0:T(8,128)S(1)}, u32[]{:S(2)}, u32[]{:S(2)}) collective-permute-start(f32[128,512]{1,0:T(8,128)S(1)} %get-tuple-element.36), channel_id=1, source_target_pairs={{0,1},{8,9},{16,17},{24,25}} | collective-permute-start | bytes 786440 | tf_op jit(solution)/shard_map/ppermute | solution.py:304
  107.1 15.6 %collective-permute-start.39 = (f32[128,512]{1,0:T(8,128)S(1)}, f32[128,512]{1,0:T(8,128)S(1)}, u32[]{:S(2)}, u32[]{:S(2)}) collective-permute-start(f32[128,512]{1,0:T(8,128)S(1)} %collective-permute-done.26.refs_23_), channel_id=1, source_target_pairs={{3,1},{11,9},{19,17},{27,25}} | collective-permute-start | bytes 786440 | tf_op jit(solution)/shard_map/ppermute | solution.py:310
  112.2 14.3 %collective-permute-start.29 = (f32[128,512]{1,0:T(8,128)S(1)}, f32[128,512]{1,0:T(8,128)S(1)}, u32[]{:S(2)}, u32[]{:S(2)}) collective-permute-start(f32[128,512]{1,0:T(8,128)S(1)} %copy-done.21), channel_id=1, source_target_pairs={{2,3},{3,2},{4,5},{5,4},{6,7},{7,6},{10,11},{11,10},{12,13},{13,12... | collective-permute-start | bytes 786440 | tf_op jit(solution)/shard_map/ppermute | solution.py:306
  117.6 14.6 %collective-permute-start.41 = (f32[128,512]{1,0:T(8,128)S(1)}, f32[128,512]{1,0:T(8,128)S(1)}, u32[]{:S(2)}, u32[]{:S(2)}) collective-permute-start(f32[128,512]{1,0:T(8,128)S(1)} %collective-permute-done.28.refs_25_), channel_id=1, source_target_pairs={{3,1},{11,9},{19,17},{27,25}} | collective-permute-start | bytes 786440 | tf_op jit(solution)/shard_map/ppermute | solution.py:310
  119.0 11.8 %collective-permute-start.30 = (f32[128,512]{1,0:T(8,128)S(1)}, f32[128,512]{1,0:T(8,128)S(1)}, u32[]{:S(2)}, u32[]{:S(2)}) collective-permute-start(f32[128,512]{1,0:T(8,128)S(1)} %copy-done.26), channel_id=1, source_target_pairs={{2,3},{3,2},{4,5},{5,4},{6,7},{7,6},{10,11},{11,10},{12,13},{13,12... | collective-permute-start | bytes 786440 | tf_op jit(solution)/shard_map/ppermute | solution.py:306
  123.4 15.2 %collective-permute-start.31 = (f32[128,512]{1,0:T(8,128)S(1)}, f32[128,512]{1,0:T(8,128)S(1)}, u32[]{:S(2)}, u32[]{:S(2)}) collective-permute-start(f32[128,512]{1,0:T(8,128)S(1)} %copy-done.31), channel_id=1, source_target_pairs={{2,3},{3,2},{4,5},{5,4},{6,7},{7,6},{10,11},{11,10},{12,13},{13,12... | collective-permute-start | bytes 786440 | tf_op jit(solution)/shard_map/ppermute | solution.py:306
  126.6 13.4 %collective-permute-start.42 = (f32[128,512]{1,0:T(8,128)S(1)}, f32[128,512]{1,0:T(8,128)S(1)}, u32[]{:S(2)}, u32[]{:S(2)}) collective-permute-start(f32[128,512]{1,0:T(8,128)S(1)} %collective-permute-done.29.refs_26_), channel_id=1, source_target_pairs={{3,1},{11,9},{19,17},{27,25}} | collective-permute-start | bytes 786440 | tf_op jit(solution)/shard_map/ppermute | solution.py:310
  128.0 15.3 %collective-permute-start.23 = (f32[128,512]{1,0:T(8,128)S(1)}, f32[128,512]{1,0:T(8,128)S(1)}, u32[]{:S(2)}, u32[]{:S(2)}) collective-permute-start(f32[128,512]{1,0:T(8,128)S(1)} %broadcast_select_fusion.2), channel_id=1, source_target_pairs={{0,2},{1,3},{2,4},{3,5},{4,6},{5,7},{8,10},{9,11},{10,12},{11,13},... | collective-permute-start | bytes 786440 | tf_op jit(solution)/shard_map/ppermute | solution.py:308
  130.8 14.4 %collective-permute-start.43 = (f32[128,512]{1,0:T(8,128)S(1)}, f32[128,512]{1,0:T(8,128)S(1)}, u32[]{:S(2)}, u32[]{:S(2)}) collective-permute-start(f32[128,512]{1,0:T(8,128)S(1)} %collective-permute-done.30.refs_27_), channel_id=1, source_target_pairs={{3,1},{11,9},{19,17},{27,25}} | collective-permute-start | bytes 786440 | tf_op jit(solution)/shard_map/ppermute | solution.py:310
  132.9 16.3 %collective-permute-start.32 = (f32[128,512]{1,0:T(8,128)}, f32[128,512]{1,0:T(8,128)}, u32[]{:S(2)}, u32[]{:S(2)}) collective-permute-start(f32[128,512]{1,0:T(8,128)} %collective-permute-done.19.refs_16_), channel_id=1, source_target_pairs={{2,3},{3,2},{4,5},{5,4},{6,7},{7,6},{10,11},{11,10},{12,13},{13,12... | collective-permute-start | bytes 786440 | tf_op jit(solution)/shard_map/ppermute | solution.py:306
  138.6 12.0 %collective-permute-start.44 = (f32[128,512]{1,0:T(8,128)S(1)}, f32[128,512]{1,0:T(8,128)S(1)}, u32[]{:S(2)}, u32[]{:S(2)}) collective-permute-start(f32[128,512]{1,0:T(8,128)S(1)} %collective-permute-done.31.refs_28_), channel_id=1, source_target_pairs={{3,1},{11,9},{19,17},{27,25}} | collective-permute-start | bytes 786440 | tf_op jit(solution)/shard_map/ppermute | solution.py:310
  140.7 15.9 %collective-permute-start.33 = (f32[128,512]{1,0:T(8,128)S(1)}, f32[128,512]{1,0:T(8,128)}, u32[]{:S(2)}, u32[]{:S(2)}) collective-permute-start(f32[128,512]{1,0:T(8,128)S(1)} %collective-permute-done.20.refs_17_), channel_id=1, source_target_pairs={{2,3},{3,2},{4,5},{5,4},{6,7},{7,6},{10,11},{11,10},{12,13},{13,12... | collective-permute-start | bytes 786440 | tf_op jit(solution)/shard_map/ppermute | solution.py:306
  143.3 14.7 %collective-permute-start.24 = (f32[128,512]{1,0:T(8,128)S(1)}, f32[128,512]{1,0:T(8,128)}, u32[]{:S(2)}, u32[]{:S(2)}) collective-permute-start(f32[128,512]{1,0:T(8,128)S(1)} %collective-permute-done.23.refs_20_), channel_id=1, source_target_pairs={{0,2},{1,3},{2,4},{3,5},{4,6},{5,7},{8,10},{9,11},{10,12},{11,13},... | collective-permute-start | bytes 786440 | tf_op jit(solution)/shard_map/ppermute | solution.py:308
  145.9 18.6 %collective-permute-start.34 = (f32[128,512]{1,0:T(8,128)}, f32[128,512]{1,0:T(8,128)}, u32[]{:S(2)}, u32[]{:S(2)}) collective-permute-start(f32[128,512]{1,0:T(8,128)} %collective-permute-done.21.refs_18_), channel_id=1, source_target_pairs={{2,3},{3,2},{4,5},{5,4},{6,7},{7,6},{10,11},{11,10},{12,13},{13,12... | collective-permute-start | bytes 786440 | tf_op jit(solution)/shard_map/ppermute | solution.py:306
  149.2 16.0 %collective-permute-start.45 = (f32[128,512]{1,0:T(8,128)}, f32[128,512]{1,0:T(8,128)}, u32[]{:S(2)}, u32[]{:S(2)}) collective-permute-start(f32[128,512]{1,0:T(8,128)} %collective-permute-done.32.refs_29_), channel_id=1, source_target_pairs={{3,1},{11,9},{19,17},{27,25}} | collective-permute-start | bytes 786440 | tf_op jit(solution)/shard_map/ppermute | solution.py:310
  151.3 20.5 %collective-permute-start.35 = (f32[128,512]{1,0:T(8,128)}, f32[128,512]{1,0:T(8,128)}, u32[]{:S(2)}, u32[]{:S(2)}) collective-permute-start(f32[128,512]{1,0:T(8,128)} %collective-permute-done.22.refs_19_), channel_id=1, source_target_pairs={{2,3},{3,2},{4,5},{5,4},{6,7},{7,6},{10,11},{11,10},{12,13},{13,12... | collective-permute-start | bytes 786440 | tf_op jit(solution)/shard_map/ppermute | solution.py:306
  156.6 15.8 %collective-permute-start.46 = (f32[128,512]{1,0:T(8,128)}, f32[128,512]{1,0:T(8,128)}, u32[]{:S(2)}, u32[]{:S(2)}) collective-permute-start(f32[128,512]{1,0:T(8,128)} %collective-permute-done.33.refs_30_), channel_id=1, source_target_pairs={{3,1},{11,9},{19,17},{27,25}} | collective-permute-start | bytes 786440 | tf_op jit(solution)/shard_map/ppermute | solution.py:310
  158.0 17.0 %collective-permute-start.25 = (f32[128,512]{1,0:T(8,128)}, f32[128,512]{1,0:T(8,128)}, u32[]{:S(2)}, u32[]{:S(2)}) collective-permute-start(f32[128,512]{1,0:T(8,128)} %collective-permute-done.24.refs_21_), channel_id=1, source_target_pairs={{0,2},{1,3},{2,4},{3,5},{4,6},{5,7},{8,10},{9,11},{10,12},{11,13},... | collective-permute-start | bytes 786440 | tf_op jit(solution)/shard_map/ppermute | solution.py:308
  164.5 22.2 %collective-permute-start.47 = (f32[128,512]{1,0:T(8,128)}, f32[128,512]{1,0:T(8,128)S(1)}, u32[]{:S(2)}, u32[]{:S(2)}) collective-permute-start(f32[128,512]{1,0:T(8,128)} %collective-permute-done.34.refs_31_), channel_id=1, source_target_pairs={{3,1},{11,9},{19,17},{27,25}} | collective-permute-start | bytes 786440 | tf_op jit(solution)/shard_map/ppermute | solution.py:310
  165.2 21.5 %collective-permute-start.36 = (f32[128,512]{1,0:T(8,128)S(1)}, f32[128,512]{1,0:T(8,128)S(1)}, u32[]{:S(2)}, u32[]{:S(2)}) collective-permute-start(f32[128,512]{1,0:T(8,128)S(1)} %copy-done.66), channel_id=1, source_target_pairs={{2,3},{3,2},{4,5},{5,4},{6,7},{7,6},{10,11},{11,10},{12,13},{13,12... | collective-permute-start | bytes 786440 | tf_op jit(solution)/shard_map/ppermute | solution.py:306
  171.8 15.0 %collective-permute-start.48 = (f32[128,512]{1,0:T(8,128)}, f32[128,512]{1,0:T(8,128)S(1)}, u32[]{:S(2)}, u32[]{:S(2)}) collective-permute-start(f32[128,512]{1,0:T(8,128)} %collective-permute-done.35.refs_32_), channel_id=1, source_target_pairs={{3,1},{11,9},{19,17},{27,25}} | collective-permute-start | bytes 786440 | tf_op jit(solution)/shard_map/ppermute | solution.py:310
  172.5 14.3 %collective-permute-start.37 = (f32[128,512]{1,0:T(8,128)}, f32[128,512]{1,0:T(8,128)S(1)}, u32[]{:S(2)}, u32[]{:S(2)}) collective-permute-start(f32[128,512]{1,0:T(8,128)} %collective-permute-done.24.refs_21_), channel_id=1, source_target_pairs={{2,3},{3,2},{4,5},{5,4},{6,7},{7,6},{10,11},{11,10},{12,13},{13,12... | collective-permute-start | bytes 786440 | tf_op jit(solution)/shard_map/ppermute | solution.py:306
  175.0 11.8 %collective-permute-start.38 = (f32[128,512]{1,0:T(8,128)}, f32[128,512]{1,0:T(8,128)S(1)}, u32[]{:S(2)}, u32[]{:S(2)}) collective-permute-start(f32[128,512]{1,0:T(8,128)} %collective-permute-done.25.refs_22_), channel_id=1, source_target_pairs={{2,3},{3,2},{4,5},{5,4},{6,7},{7,6},{10,11},{11,10},{12,13},{13,12... | collective-permute-start | bytes 786440 | tf_op jit(solution)/shard_map/ppermute | solution.py:306
  (93 other events, 1175.9 us)

commit v2 on v1

v2 whole, which is shorter than its diff:
```python
import functools

import jax
import jax.numpy as jnp
from jax import lax
from jax.experimental import pallas as pl
from jax.experimental.pallas import tpu as pltpu
from jax.sharding import PartitionSpec as P

HIGHEST = lax.Precision.HIGHEST
VMEM = pl.BlockSpec(memory_space=pltpu.VMEM)
SMEM = pl.BlockSpec(memory_space=pltpu.SMEM)
ANY = pl.BlockSpec(memory_space=pl.ANY)
LANES = 128
PICK, FROM, ROW, COUNT = 0, 1, 2, 3


def call(kernel, out, ins, outs, scratch=(), vmem=40 << 20, flops=0, moved=0):
    return pl.pallas_call(
        kernel,
        out_shape=out,
        in_specs=ins,
        out_specs=outs,
        scratch_shapes=list(scratch),
        compiler_params=pltpu.CompilerParams(vmem_limit_bytes=vmem),
        cost_estimate=pl.CostEstimate(
            flops=flops, bytes_accessed=moved, transcendentals=0
        ),
    )


def index_kernel(where_ref, pivots_ref, table_ref, owner_ref, *, row_dev):
    nb = pivots_ref.shape[1]
    start = where_ref[0] * row_dev
    first = where_ref[0] == 0
    down = lax.broadcasted_iota(jnp.int32, (nb, nb), 0)
    across = lax.broadcasted_iota(jnp.int32, (nb, nb), 1)
    piv_row = jnp.broadcast_to(pivots_ref[...], (nb, nb))

    def column(full):
        return jnp.sum(jnp.where(down == across, full, 0.0), axis=1, keepdims=True)

    piv_f = piv_row.astype(jnp.float32)
    piv_col = jnp.broadcast_to(column(piv_f), (nb, nb))
    upto = (down <= across).astype(jnp.bfloat16)
    below = (piv_row >= nb).astype(jnp.float32)
    vacancy = jnp.dot(
        below[:8].astype(jnp.bfloat16), upto, preferred_element_type=jnp.float32
    )[:1]
    taken = jnp.max((piv_row == down).astype(jnp.float32), axis=1, keepdims=True)
    freed = jnp.broadcast_to(1.0 - taken, (nb, LANES))
    rank = jnp.dot(
        (across <= down).astype(jnp.bfloat16),
        freed.astype(jnp.bfloat16),
        preferred_element_type=jnp.float32,
    )[:, :1]
    down_f = down.astype(jnp.float32)
    pair = (rank == vacancy) & (freed[:, :1] > 0.5)
    source = jnp.sum(jnp.where(pair, down_f, 0.0), axis=0, keepdims=True)
    source_col = jnp.broadcast_to(column(jnp.broadcast_to(source, (nb, nb))), (nb, nb))

    own_row = (pivots_ref[...] >= start) & (pivots_ref[...] < start + row_dev)
    pick = jnp.where(own_row, pivots_ref[...] - start, source.astype(jnp.int32))
    moved_row = (own_row & (pivots_ref[...] >= nb)).astype(jnp.float32)
    start_f = start.astype(jnp.float32)
    moved_col = (
        (piv_col >= start_f) & (piv_col < start_f + row_dev) & (piv_col >= nb)
    )
    order = jnp.sum(
        jnp.where(piv_f < piv_col, jnp.broadcast_to(moved_row, (nb, nb)), 0.0),
        axis=1,
        keepdims=True,
    )
    placed = moved_col & (order == across.astype(jnp.float32))
    origin = jnp.where(first, source_col, down_f)
    listed_from = jnp.sum(jnp.where(placed, origin, 0.0), axis=0, keepdims=True)
    listed_row = jnp.sum(
        jnp.where(placed, piv_col - start_f, 0.0), axis=0, keepdims=True
    )
    count = jnp.sum(moved_row, axis=1, keepdims=True)
    table_ref[...] = jnp.zeros_like(table_ref)
    table_ref[PICK : PICK + 1, :] = pick
    table_ref[FROM : FROM + 1, :] = listed_from.astype(jnp.int32)
    table_ref[ROW : ROW + 1, :] = listed_row.astype(jnp.int32)
    table_ref[COUNT : COUNT + 1, :] = jnp.broadcast_to(
        count.astype(jnp.int32), (1, nb)
    )
    owner_ref[...] = piv_col[:, :LANES].astype(jnp.int32) // row_dev


def gather_kernel(table_ref, matrix_ref, out_ref):
    nb = out_ref.shape[0]

    @pl.loop(0, nb, step=8)
    def _(base):
        for k in range(8):
            j = base + k
            out_ref[pl.ds(j, 1), :] = matrix_ref[pl.ds(table_ref[PICK, j], 1), :]


def merge_kernel(where_ref, owner_ref, held_ref, *refs, log, halves):
    arrived, (merged_ref, half_ref) = refs[: 2 if halves else 1], refs[-2:]
    me = where_ref[0]
    mine, theirs = me >> log, (me >> log) ^ 1
    odd = me & 1
    nb, cols = held_ref.shape
    half = nb // 2

    def merge(rows, piece):
        group = owner_ref[rows, :] >> log
        take = (group == theirs) | ((theirs == 0) & (group != mine))
        for q in range(cols // LANES):
            lane = slice(q * LANES, (q + 1) * LANES)
            merged_ref[rows, lane] = jnp.where(take, piece[:, lane], held_ref[rows, lane])

    low, high = slice(0, half), slice(half, nb)
    if halves:
        @pl.when(odd == 0)
        def _():
            merge(low, arrived[0])
            merge(high, arrived[1])

        @pl.when(odd == 1)
        def _():
            merge(low, arrived[1])
            merge(high, arrived[0])
    else:
        merge(slice(0, nb), arrived[0])

    @pl.when(odd == 0)
    def _():
        half_ref[...] = merged_ref[low, :]

    @pl.when(odd == 1)
    def _():
        half_ref[...] = merged_ref[high, :]


def factor_kernel(where_ref, top_in_ref, lower_ref, upper_ref, weights_ref, top_ref):
    nb, cols = top_in_ref.shape
    u = jnp.dot(
        lower_ref[...], top_in_ref[...], precision=HIGHEST,
        preferred_element_type=jnp.float32,
    )
    top_ref[...] = u
    weights_ref[...] = jnp.dot(
        upper_ref[...], u, precision=HIGHEST, preferred_element_type=jnp.float32
    )

    @pl.when(where_ref[1] == 0)
    def _():
        top_ref[:, :nb] = top_in_ref[:, :nb]
        weights_ref[:, :nb] = -upper_ref[...]


def swap_kernel(where_ref, table_ref, displaced_ref, matrix_ref, swapped_ref, *pieces):
    nb = pieces[0].shape[1]
    size = pieces[0].shape[0]
    swapped_ref[...] = matrix_ref[...]

    def swap(origin):
        def body(k, _):
            to, at = table_ref[ROW, k], table_ref[FROM, k]
            swapped_ref[pl.ds(to, 1), :] = origin[pl.ds(at, 1), :]
            return 0

        lax.fori_loop(0, table_ref[COUNT, 0], body, 0)

    @pl.when(where_ref[0] == 0)
    def _():
        swap(matrix_ref)

    @pl.when(where_ref[0] > 0)
    def _():
        swap(displaced_ref)

    @pl.when(where_ref[1] == 0)
    def _():
        for p, piece in enumerate(pieces):
            piece[...] = swapped_ref[p * size : (p + 1) * size, :nb]


def pick_kernel(where_ref, *refs):
    options, out_ref, sem = refs[:-2], refs[-2], refs[-1]
    for p, option in enumerate(options):
        @pl.when(where_ref[1] == p)
        def _():
            copy = pltpu.make_async_copy(option, out_ref, sem)
            copy.start()
            copy.wait()


def final_kernel(where_ref, weights_ref, top_ref, swapped_ref, panel_ref, out_ref, w_hi, w_lo):
    nb = weights_ref.shape[0]
    block, cols = out_ref.shape
    step = pl.program_id(0)
    on_top = (where_ref[0] == 0) & ((step + 1) * block <= nb)

    @pl.when(step == 0)
    def _():
        w = weights_ref[...]
        hi = w.astype(jnp.bfloat16)
        w_hi[...] = hi
        w_lo[...] = (w - hi.astype(jnp.float32)).astype(jnp.bfloat16)

    @pl.when(on_top)
    def _():
        out_ref[...] = top_ref[pl.ds(pl.multiple_of(step * block, block), block), :]

    @pl.when(jnp.logical_not(on_top))
    def _():
        p = panel_ref[...]
        p_hi = p.astype(jnp.bfloat16)
        p_lo = (p - p_hi.astype(jnp.float32)).astype(jnp.bfloat16)
        dot = functools.partial(jnp.dot, preferred_element_type=jnp.float32)
        total = dot(p_lo, w_hi[...]) + dot(p_hi, w_lo[...]) + dot(p_hi, w_hi[...])
        keep = where_ref[1] > 0
        out_ref[:, :nb] = jnp.where(keep, swapped_ref[:, :nb], 0.0) - total[:, :nb]
        out_ref[:, nb:] = swapped_ref[:, nb:] - total[:, nb:]


def local(matrix, pivots, lower_inverse, upper_inverse, *, n_rows, n_cols):
    row_dev, cols = matrix.shape
    nb = pivots.shape[0]
    f32 = jnp.float32
    row, col = lax.axis_index("prow"), lax.axis_index("pcol")
    here = jnp.stack([row, col]).astype(jnp.int32)

    table, owner = call(
        functools.partial(index_kernel, row_dev=row_dev),
        (jax.ShapeDtypeStruct((8, nb), jnp.int32), jax.ShapeDtypeStruct((nb, LANES), jnp.int32)),
        [SMEM, VMEM], (VMEM, VMEM),
    )(here, pivots.reshape(1, nb))

    slot = jax.ShapeDtypeStruct((nb, cols), f32)
    half_slot = jax.ShapeDtypeStruct((nb // 2, cols), f32)
    held = call(gather_kernel, slot, [SMEM, VMEM], VMEM)(table, matrix)
    displaced = held
    log = 0
    half = None
    while (1 << log) < n_rows:
        d = 1 << log
        far = [(p, p ^ d) for p in range(n_rows)]
        if log == 0:
            arrived = [lax.ppermute(held, "prow", far)]
            whole = arrived[0]
        else:
            near = [(p, p ^ 1) for p in range(n_rows)]
            one = lax.ppermute(half, "prow", far)
            two = lax.ppermute(one, "prow", near)
            arrived = [one, two]
            whole = jnp.concatenate(
                [jnp.where(row % 2 == 0, one, two), jnp.where(row % 2 == 0, two, one)], axis=0
            )
        held, half = call(
            functools.partial(merge_kernel, log=log, halves=log > 0),
            (slot, half_slot), [SMEM] + [VMEM] * (2 + len(arrived)), (VMEM, VMEM),
        )(here, owner, held, *arrived)
        displaced = jnp.where((row >> log) == 1, whole, displaced)
        log += 1

    weights, top = call(
        factor_kernel, (slot, slot), [SMEM, VMEM, VMEM, VMEM], (VMEM, VMEM),
        flops=4 * nb * nb * cols * 6,
    )(here, held, lower_inverse, upper_inverse)

    size = row_dev // n_cols
    piece = jax.ShapeDtypeStruct((size, nb), f32)
    swapped, *pieces = call(
        swap_kernel, (jax.ShapeDtypeStruct(matrix.shape, f32),) + (piece,) * n_cols,
        [SMEM, SMEM, VMEM, VMEM], (VMEM,) * (1 + n_cols),
    )(here, table, displaced, matrix)
    parts = [pieces[0]] + [
        lax.ppermute(pieces[p], "pcol", [(0, p)]) for p in range(1, n_cols)
    ]
    mine = call(
        pick_kernel, piece, [SMEM] + [ANY] * n_cols, ANY, [pltpu.SemaphoreType.DMA]
    )(here, *parts)
    panel = lax.all_gather(mine, "pcol", axis=0, tiled=True)

    block = 256
    whole = pl.BlockSpec((nb, cols), lambda i: (0, 0))
    wide = pl.BlockSpec((block, cols), lambda i: (i, 0))
    return pl.pallas_call(
        final_kernel,
        grid=(row_dev // block,),
        out_shape=jax.ShapeDtypeStruct(matrix.shape, f32),
        in_specs=[SMEM, whole, whole, wide, pl.BlockSpec((block, nb), lambda i: (i, 0))],
        out_specs=wide,
        scratch_shapes=[pltpu.VMEM((nb, cols), jnp.bfloat16)] * 2,
        compiler_params=pltpu.CompilerParams(vmem_limit_bytes=40 << 20),
        cost_estimate=pl.CostEstimate(
            flops=2 * row_dev * nb * cols * 3,
            bytes_accessed=4 * row_dev * (2 * cols + nb),
            transcendentals=0,
        ),
    )(here, weights, top, swapped, panel)


def solution(mesh):
    n_rows, n_cols = mesh.shape["prow"], mesh.shape["pcol"]
    return jax.shard_map(
        functools.partial(local, n_rows=n_rows, n_cols=n_cols),
        mesh=mesh,
        in_specs=(P("prow", "pcol"), P(), P(), P()),
        out_specs=P("prow", "pcol"),
        check_vma=False,
    )
```

time: 202 us -> 217 us (1.074)
  waiting for transfers between devices: 51.2 us -> 155 us
  starting transfers between devices: 95.7 us -> 6.05 us
  between operations: 1.64 us -> 13.6 us
  other arithmetic: 8.63 us -> 1.43 us
  local copies, waits for them, and re-layouts: 16.9 us -> 11.8 us
    all_gather x0 -> x1, waiting for transfers between devices: none -> 120 us  [local(): panel = lax.all_gather(mine, 'pcol', axis=0, tiled=True)]
    ppermute x46 -> x7, starting transfers between devices: 95.1 us -> 5.43 us  [local(): lax.ppermute(pieces[p], 'pcol', [(0, p)])]
    ppermute x46 -> x7, waiting for transfers between devices: 45.7 us -> 13.1 us  [local(): lax.ppermute(pieces[p], 'pcol', [(0, p)])]
    ppermute x1, waiting for transfers between devices: 5.43 us -> 16.2 us  [local(): one = lax.ppermute(half, 'prow', far)]
    select_n x10 -> x0, other arithmetic: 8.13 us -> none  [the longest x9 7.13 us: spread(): entry = jnp.where(col == 0, own, entry)]
    unnamed x152 -> x24, local copies, waits for them, and re-layouts: 15.1 us -> 11.8 us
    ppermute x1, waiting for transfers between devices: 0.01 us -> 3.02 us  [local(): arrived = [lax.ppermute(held, 'prow', far)]]
    ppermute x1, waiting for transfers between devices: 0.01 us -> 2.23 us  [local(): two = lax.ppermute(one, 'prow', near)]
  transfers between devices with their start and end apart: 49 -> 11, of which waited for: 9 -> 5; matrix products, arithmetic and copies ran while one was open for 4% -> 0% of each run, Pallas kernels for 7% -> 4%
where the time goes in v2:
time: 217 us; the launch traced here: 215 us
  waiting for transfers between devices  155 us (71%)
  Pallas kernels  27.6 us (13%)
  between operations  13.6 us (6%)
  local copies, waits for them, and re-layouts  11.8 us (5%)
  starting transfers between devices  6.05 us (3%)
    all_gather x1, waiting for transfers between devices, local(): panel = lax.all_gather(mine, 'pcol', axis=0, tiled=True)  120 us
    ppermute x1, waiting for transfers between devices, local(): one = lax.ppermute(half, 'prow', far)  16.2 us
    ppermute x7, waiting for transfers between devices, local(): lax.ppermute(pieces[p], 'pcol', [(0, p)])  13.1 us
    unnamed x24, local copies, waits for them, and re-layouts  11.8 us
    pallas_call x1, Pallas kernels, local(): pl.pallas_call(final_kernel, grid=(row_dev // block,), out_shape=jax.Shap...  8.21 us
    pallas_call x1, Pallas kernels, local(): call(factor_kernel, (slot, slot), [SMEM, VMEM, VMEM, VMEM], (VMEM, VMEM),...  5.85 us
    ppermute x7, starting transfers between devices, local(): lax.ppermute(pieces[p], 'pcol', [(0, p)])  5.43 us
  transfers between devices with their start and end apart: 11, of which 5 were waited for; matrix products, arithmetic and copies ran while one was open for 0% of the time, Pallas kernels for 4%

profile of v2, /device:TPU:10, one launch (start us, length us, event | category | flops | bytes accessed | tf_op | source)
XLA Modules:
  0.0 215.4 jit_solution(9308667951422887496)
XLA Ops:
  6.5 0.1 pad_add_fusion.where_ref
  6.6 0.7 copy-done.9
  7.3 1.5 shard_map.46
  8.8 2.5 %copy-done = f32[2048,640]{1,0:T(8,128)S(1)} copy-done((f32[2048,640]{1,0:T(8,128)S(1)}, f32[2048,640]{1,0:T(8,128)}, u32[]{:S(2)}) %copy-start) | copy-done | bytes 5242904
  11.3 3.5 %shard_map.47.held_ref = f32[512,640]{1,0:T(8,128)S(1)} custom-call(s32[8,512]{1,0:T(8,128)S(1)} %get-tuple-element.22.table_ref, f32[2048,640]{1,0:T(8,128)S(1)} %copy-done), custom_call_target="tpu_custom_call" | custom-call | tf_op jit(solution)/shard_map/pallas_call | solution.py:237
  14.8 0.1 collective-permute-start
  14.9 3.0 %collective-permute-done.refs_0_ = f32[512,640]{1,0:T(8,128)S(1)} collective-permute-done((f32[512,640]{1,0:T(8,128)S(1)}, f32[512,640]{1,0:T(8,128)S(1)}, u32[]{:S(2)}, u32[]{:S(2)}) %collective-permute-start) | collective-permute-done | bytes 1310752 | tf_op jit(solution)/shard_map/ppermute | solution.py:245
  17.9 0.8 shard_map.48
  18.7 1.1 copy-done.4
  19.8 0.5 collective-permute-start.1
  20.4 16.2 %collective-permute-done.1.refs_0_ = f32[256,640]{1,0:T(8,128)S(1)} collective-permute-done((f32[256,640]{1,0:T(8,128)S(1)}, f32[256,640]{1,0:T(8,128)S(1)}, u32[]{:S(2)}, u32[]{:S(2)}) %collective-permute-start.1) | collective-permute-done | bytes 655392 | tf_op jit(solution)/shard_map/ppermute | solution.py:249
  36.6 2.2 %collective-permute-done.2.refs_1_ = f32[256,640]{1,0:T(8,128)} collective-permute-done((f32[256,640]{1,0:T(8,128)S(1)}, f32[256,640]{1,0:T(8,128)}, u32[]{:S(2)}, u32[]{:S(2)}) %collective-permute-start.2) | collective-permute-done | bytes 655392 | tf_op jit(solution)/shard_map/ppermute | solution.py:250
  38.8 1.2 broadcast_select_fusion.1
  40.0 0.2 maximum_select_fusion.displaced_ref
  40.2 0.5 copy-done.7
  40.7 4.1 %shard_map.51 = (f32[2048,640]{1,0:T(8,128)S(1)}, f32[256,512]{1,0:T(8,128)S(1)}, f32[256,512]{1,0:T(8,128)S(1)}, f32[256,512]{1,0:T(8,128)S(1)}, f32[256,512]{1...) custom-call(s32[2]{0:T(128)S(1)} %copy-done.7, ...), custom_call_target="tpu_custom_call" | custom-call | tf_op jit(solution)/shard_map/pallas_call | solution.py:269
  44.8 2.3 %copy-done.1 = f32[2048,640]{1,0:T(8,128)} copy-done((f32[2048,640]{1,0:T(8,128)}, f32[2048,640]{1,0:T(8,128)S(1)}, u32[]{:S(2)}) %copy-start.1) | copy-done | bytes 5242904
  47.1 0.7 collective-permute-start.3
  47.8 1.3 collective-permute-start.4
  49.1 0.7 collective-permute-start.5
  49.8 0.7 collective-permute-start.6
  50.5 0.7 collective-permute-start.7
  51.2 0.7 collective-permute-start.8
  51.9 13.1 %collective-permute-done.4.refs_2_ = f32[256,512]{1,0:T(8,128)S(1)} collective-permute-done((f32[256,512]{1,0:T(8,128)S(1)}, f32[256,512]{1,0:T(8,128)S(1)}, u32[]{:S(2)}, u32[]{:S(2)}) %collective-permute-start.4) | collective-permute-done | bytes 524320 | tf_op jit(solution)/shard_map/ppermute | solution.py:274
  65.0 0.7 collective-permute-start.9
  65.8 1.4 shard_map.52
  67.2 2.3 %shard_map.49 = (f32[512,640]{1,0:T(8,128)S(1)}, f32[256,640]{1,0:T(8,128)}) custom-call(s32[2]{0:T(128)S(1)} %copy-done.8, s32[512,128]{1,0:T(8,128)S(1)} %get-tuple-element.21.owner_ref, f32[512,640]{1,0:T(8,128)S(1)} %copy-done.5, f32[256,640]{1,0:T(8,128)S(1)} %collective-permute-done.1.refs_0_, f32[256,640]{1,0:T(8,128)} %collective-permute-done.2.refs_1_), custom_call_target="tpu_custom_call" | custom-call | tf_op jit(solution)/shard_map/pallas_call | solution.py:255
  69.5 5.9 %shard_map.50 = (f32[512,640]{1,0:T(8,128)S(1)}, f32[512,640]{1,0:T(8,128)S(1)}) custom-call(s32[2]{0:T(128)S(1)} %copy-done.8, f32[512,640]{1,0:T(8,128)S(1)} %get-tuple-element.25.top_in_ref, f32[512,512]{1,0:T(8,128)S(1)} %copy-done.10, f32[512,512]{1,0:T(8,128)S(1)} %copy-done.11), custom_call_target="tpu_custom_call" | custom-call | flops 4026531840 | tf_op jit(solution)/shard_map/pallas_call | solution.py:262
  75.4 120.3 %all-gather.2.cloned.1.call-done.panel_ref = f32[2048,512]{1,0:T(8,128)} async-done(((f32[256,512]{1,0:T(8,128)}), f32[2048,512]{1,0:T(8,128)}) %all-gather.2.cloned.1.call-update) | async-done | bytes 4194320 | tf_op jit(solution)/shard_map/all_gather | solution.py:279
  195.7 2.5 %copy-done.2 = f32[2048,640]{1,0:T(8,128)S(1)} copy-done((f32[2048,640]{1,0:T(8,128)S(1)}, f32[2048,640]{1,0:T(8,128)}, u32[]{:S(2)}) %copy-start.2) | copy-done | bytes 5242904
  198.2 2.2 %copy-done.3 = f32[2048,512]{1,0:T(8,128)S(1)} copy-done((f32[2048,512]{1,0:T(8,128)S(1)}, f32[2048,512]{1,0:T(8,128)}, u32[]{:S(2)}) %copy-start.3) | copy-done | bytes 4194328
  200.4 8.2 %shard_map.53 = f32[2048,640]{1,0:T(8,128)} custom-call(s32[2]{0:T(128)S(1)} %copy-done.8, f32[512,640]{1,0:T(8,128)S(1)} %get-tuple-element.26.weights_ref, f32[512,640]{1,0:T(8,128)S(1)} %get-tuple-element.27.top_ref, f32[2048,640]{1,0:T(8,128)S(1)} %copy-done.2, f32[2048,512]{1,0:T(8,128)S(1)} %copy-done.3), custom_call_target="tpu_custom_call" | custom-call | flops 4026531840 | bytes 14680064 | tf_op jit(solution)/shard_map/pallas_call | solution.py:284
  (26 shorter events, 0.1 us)
Async XLA Ops:
  6.5 189.2 %all-gather.2.cloned.1.call-start = ((), (), s32[]{:S(2)}) async-start(), calls=%async_computation | async-start | bytes 4718592 | tf_op jit(solution)/shard_map/all_gather | solution.py:279
  6.6 11.3 %copy-start.6 = (s32[2]{0:T(128)}, s32[2]{0:T(128)S(1)}, u32[]{:S(2)}) copy-start(s32[2]{0:T(128)S(1)} %pad_add_fusion.where_ref) | copy-start | bytes 28
  6.6 0.7 copy-start.9
  8.8 2.5 %copy-start = (f32[2048,640]{1,0:T(8,128)S(1)}, f32[2048,640]{1,0:T(8,128)}, u32[]{:S(2)}) copy-start(f32[2048,640]{1,0:T(8,128)} %matrix_ref.3) | copy-start | bytes 15728644
  14.8 3.1 %collective-permute-start = (f32[512,640]{1,0:T(8,128)S(1)}, f32[512,640]{1,0:T(8,128)S(1)}, u32[]{:S(2)}, u32[]{:S(2)}) collective-permute-start(f32[512,640]{1,0:T(8,128)S(1)} %shard_map.47.held_ref), channel_id=1, source_target_pairs={{0,8},{8,0},{16,24},{24,16},{1,9},{9,1},{17,25},{25,17},{2,10},{10... | collective-permute-start | bytes 3932168 | tf_op jit(solution)/shard_map/ppermute | solution.py:245
  18.7 1.1 copy-start.4
  19.8 16.8 %collective-permute-start.1 = (f32[256,640]{1,0:T(8,128)S(1)}, f32[256,640]{1,0:T(8,128)S(1)}, u32[]{:S(2)}, u32[]{:S(2)}) collective-permute-start(f32[256,640]{1,0:T(8,128)S(1)} %get-tuple-element.24), channel_id=1, source_target_pairs={{0,16},{8,24},{16,0},{24,8},{1,17},{9,25},{17,1},{25,9},{2,18},{10... | collective-permute-start | bytes 1966088 | tf_op jit(solution)/shard_map/ppermute | solution.py:249
  36.6 2.2 %collective-permute-start.2 = (f32[256,640]{1,0:T(8,128)S(1)}, f32[256,640]{1,0:T(8,128)}, u32[]{:S(2)}, u32[]{:S(2)}) collective-permute-start(f32[256,640]{1,0:T(8,128)S(1)} %collective-permute-done.1.refs_0_), channel_id=1, source_target_pairs={{0,8},{8,0},{16,24},{24,16},{1,9},{9,1},{17,25},{25,17},{2,10},{10... | collective-permute-start | bytes 1966088 | tf_op jit(solution)/shard_map/ppermute | solution.py:250
  40.0 0.7 copy-start.7
  44.7 2.4 %copy-start.1 = (f32[2048,640]{1,0:T(8,128)}, f32[2048,640]{1,0:T(8,128)S(1)}, u32[]{:S(2)}) copy-start(f32[2048,640]{1,0:T(8,128)S(1)} %get-tuple-element.28.swapped_ref) | copy-start | bytes 15728644
  47.1 4.1 %collective-permute-start.3 = (f32[256,512]{1,0:T(8,128)S(1)}, f32[256,512]{1,0:T(8,128)S(1)}, u32[]{:S(2)}, u32[]{:S(2)}) collective-permute-start(f32[256,512]{1,0:T(8,128)S(1)} %get-tuple-element.30), channel_id=1, source_target_pairs={{0,1},{8,9},{16,17},{24,25}} | collective-permute-start | bytes 1572872 | tf_op jit(solution)/shard_map/ppermute | solution.py:274
  47.8 17.2 %collective-permute-start.4 = (f32[256,512]{1,0:T(8,128)S(1)}, f32[256,512]{1,0:T(8,128)S(1)}, u32[]{:S(2)}, u32[]{:S(2)}) collective-permute-start(f32[256,512]{1,0:T(8,128)S(1)} %get-tuple-element.31), channel_id=1, source_target_pairs={{0,2},{8,10},{16,18},{24,26}} | collective-permute-start | bytes 1572872 | tf_op jit(solution)/shard_map/ppermute | solution.py:274
  49.1 16.6 %collective-permute-start.5 = (f32[256,512]{1,0:T(8,128)S(1)}, f32[256,512]{1,0:T(8,128)S(1)}, u32[]{:S(2)}, u32[]{:S(2)}) collective-permute-start(f32[256,512]{1,0:T(8,128)S(1)} %get-tuple-element.32), channel_id=1, source_target_pairs={{0,3},{8,11},{16,19},{24,27}} | collective-permute-start | bytes 1572872 | tf_op jit(solution)/shard_map/ppermute | solution.py:274
  49.8 15.9 %collective-permute-start.6 = (f32[256,512]{1,0:T(8,128)S(1)}, f32[256,512]{1,0:T(8,128)S(1)}, u32[]{:S(2)}, u32[]{:S(2)}) collective-permute-start(f32[256,512]{1,0:T(8,128)S(1)} %get-tuple-element.33), channel_id=1, source_target_pairs={{0,4},{8,12},{16,20},{24,28}} | collective-permute-start | bytes 1572872 | tf_op jit(solution)/shard_map/ppermute | solution.py:274
  50.5 15.2 %collective-permute-start.7 = (f32[256,512]{1,0:T(8,128)S(1)}, f32[256,512]{1,0:T(8,128)S(1)}, u32[]{:S(2)}, u32[]{:S(2)}) collective-permute-start(f32[256,512]{1,0:T(8,128)S(1)} %get-tuple-element.34), channel_id=1, source_target_pairs={{0,5},{8,13},{16,21},{24,29}} | collective-permute-start | bytes 1572872 | tf_op jit(solution)/shard_map/ppermute | solution.py:274
  51.2 14.5 %collective-permute-start.8 = (f32[256,512]{1,0:T(8,128)S(1)}, f32[256,512]{1,0:T(8,128)S(1)}, u32[]{:S(2)}, u32[]{:S(2)}) collective-permute-start(f32[256,512]{1,0:T(8,128)S(1)} %get-tuple-element.35), channel_id=1, source_target_pairs={{0,6},{8,14},{16,22},{24,30}} | collective-permute-start | bytes 1572872 | tf_op jit(solution)/shard_map/ppermute | solution.py:274
  65.0 0.7 collective-permute-start.9
  65.8 1.4 copy-start.5
  65.8 1.4 copy-start.8
  67.2 2.3 %copy-start.10 = (f32[512,512]{1,0:T(8,128)S(1)}, f32[512,512]{1,0:T(8,128)}, u32[]{:S(2)}) copy-start(f32[512,512]{1,0:T(8,128)} %lower_ref.1) | copy-start | bytes 3145732
  67.2 2.3 %copy-start.11 = (f32[512,512]{1,0:T(8,128)S(1)}, f32[512,512]{1,0:T(8,128)}, u32[]{:S(2)}) copy-start(f32[512,512]{1,0:T(8,128)} %upper_ref.1) | copy-start | bytes 3145732
  195.7 2.5 %copy-start.2 = (f32[2048,640]{1,0:T(8,128)S(1)}, f32[2048,640]{1,0:T(8,128)}, u32[]{:S(2)}) copy-start(f32[2048,640]{1,0:T(8,128)} %copy-done.1) | copy-start | bytes 15728644
  198.2 2.2 %copy-start.3 = (f32[2048,512]{1,0:T(8,128)S(1)}, f32[2048,512]{1,0:T(8,128)}, u32[]{:S(2)}) copy-start(f32[2048,512]{1,0:T(8,128)} %all-gather.2.cloned.1.call-done.panel_ref) | copy-start | bytes 12582916
Sparse Core Ops, SparseCore 0:
  67.3 128.3 all-gather.1

commit v3 on v1

v3 whole, which is shorter than its diff:
```python
import functools

import jax
import jax.numpy as jnp
from jax import lax
from jax.experimental import pallas as pl
from jax.experimental.pallas import tpu as pltpu
from jax.sharding import PartitionSpec as P

HIGHEST = lax.Precision.HIGHEST
VMEM = pl.BlockSpec(memory_space=pltpu.VMEM)
SMEM = pl.BlockSpec(memory_space=pltpu.SMEM)
ANY = pl.BlockSpec(memory_space=pl.ANY)
LANES = 128
PICK, FROM, ROW, COUNT, TOP = 0, 1, 2, 3, 4


def call(kernel, out, ins, outs, scratch=(), vmem=16 << 20, flops=0, moved=0):
    return pl.pallas_call(
        kernel,
        out_shape=out,
        in_specs=ins,
        out_specs=outs,
        scratch_shapes=list(scratch),
        compiler_params=pltpu.CompilerParams(vmem_limit_bytes=vmem),
        cost_estimate=pl.CostEstimate(
            flops=flops, bytes_accessed=moved, transcendentals=0
        ),
    )


def index_kernel(where_ref, pivots_ref, table_ref, owner_ref, *, row_dev):
    nb = pivots_ref.shape[1]
    start = where_ref[0] * row_dev
    first = where_ref[0] == 0
    down = lax.broadcasted_iota(jnp.int32, (nb, nb), 0)
    across = lax.broadcasted_iota(jnp.int32, (nb, nb), 1)
    piv_row = jnp.broadcast_to(pivots_ref[...], (nb, nb))

    def column(full):
        return jnp.sum(jnp.where(down == across, full, 0.0), axis=1, keepdims=True)

    piv_f = piv_row.astype(jnp.float32)
    piv_col = jnp.broadcast_to(column(piv_f), (nb, nb))
    upto = (down <= across).astype(jnp.bfloat16)
    below = (piv_row >= nb).astype(jnp.float32)
    vacancy = jnp.dot(
        below[:8].astype(jnp.bfloat16), upto, preferred_element_type=jnp.float32
    )[:1]
    taken = jnp.max((piv_row == down).astype(jnp.float32), axis=1, keepdims=True)
    freed = jnp.broadcast_to(1.0 - taken, (nb, LANES))
    rank = jnp.dot(
        (across <= down).astype(jnp.bfloat16),
        freed.astype(jnp.bfloat16),
        preferred_element_type=jnp.float32,
    )[:, :1]
    down_f = down.astype(jnp.float32)
    pair = (rank == vacancy) & (freed[:, :1] > 0.5)
    source = jnp.sum(jnp.where(pair, down_f, 0.0), axis=0, keepdims=True)
    source_col = jnp.broadcast_to(column(jnp.broadcast_to(source, (nb, nb))), (nb, nb))

    own_row = (pivots_ref[...] >= start) & (pivots_ref[...] < start + row_dev)
    pick = jnp.where(own_row, pivots_ref[...] - start, source.astype(jnp.int32))
    moved_row = (own_row & (pivots_ref[...] >= nb)).astype(jnp.float32)
    start_f = start.astype(jnp.float32)
    moved_col = (
        (piv_col >= start_f) & (piv_col < start_f + row_dev) & (piv_col >= nb)
    )
    order = jnp.sum(
        jnp.where(piv_f < piv_col, jnp.broadcast_to(moved_row, (nb, nb)), 0.0),
        axis=1,
        keepdims=True,
    )
    placed = moved_col & (order == across.astype(jnp.float32))
    origin = jnp.where(first, source_col, down_f)
    listed_from = jnp.sum(jnp.where(placed, origin, 0.0), axis=0, keepdims=True)
    listed_row = jnp.sum(
        jnp.where(placed, piv_col - start_f, 0.0), axis=0, keepdims=True
    )
    listed_top = jnp.sum(jnp.where(placed, source_col, 0.0), axis=0, keepdims=True)
    count = jnp.sum(moved_row, axis=1, keepdims=True)
    table_ref[...] = jnp.zeros_like(table_ref)
    table_ref[PICK : PICK + 1, :] = pick
    table_ref[FROM : FROM + 1, :] = listed_from.astype(jnp.int32)
    table_ref[ROW : ROW + 1, :] = listed_row.astype(jnp.int32)
    table_ref[TOP : TOP + 1, :] = listed_top.astype(jnp.int32)
    table_ref[COUNT : COUNT + 1, :] = jnp.broadcast_to(
        count.astype(jnp.int32), (1, nb)
    )
    owner_ref[...] = piv_col[:, :LANES].astype(jnp.int32) // row_dev


def gather_kernel(table_ref, matrix_ref, out_ref):
    nb = out_ref.shape[0]

    @pl.loop(0, nb, step=8)
    def _(base):
        for k in range(8):
            j = base + k
            out_ref[pl.ds(j, 1), :] = matrix_ref[pl.ds(table_ref[PICK, j], 1), :]


def merge_kernel(where_ref, owner_ref, held_ref, *refs, log, halves):
    arrived, (merged_ref, half_ref) = refs[: 2 if halves else 1], refs[-2:]
    me = where_ref[0]
    mine, theirs = me >> log, (me >> log) ^ 1
    odd = me & 1
    nb, cols = held_ref.shape
    half = nb // 2

    def merge(rows, piece):
        group = owner_ref[rows, :] >> log
        take = (group == theirs) | ((theirs == 0) & (group != mine))
        for q in range(cols // LANES):
            lane = slice(q * LANES, (q + 1) * LANES)
            merged_ref[rows, lane] = jnp.where(take, piece[:, lane], held_ref[rows, lane])

    low, high = slice(0, half), slice(half, nb)
    if halves:
        @pl.when(odd == 0)
        def _():
            merge(low, arrived[0])
            merge(high, arrived[1])

        @pl.when(odd == 1)
        def _():
            merge(low, arrived[1])
            merge(high, arrived[0])
    else:
        merge(slice(0, nb), arrived[0])

    @pl.when(odd == 0)
    def _():
        half_ref[...] = merged_ref[low, :]

    @pl.when(odd == 1)
    def _():
        half_ref[...] = merged_ref[high, :]


def factor_kernel(where_ref, top_in_ref, lower_ref, upper_ref, weights_ref, top_ref):
    nb, cols = top_in_ref.shape
    u = jnp.dot(
        lower_ref[...], top_in_ref[...], precision=HIGHEST,
        preferred_element_type=jnp.float32,
    )
    top_ref[...] = u
    weights_ref[...] = jnp.dot(
        upper_ref[...], u, precision=HIGHEST, preferred_element_type=jnp.float32
    )

    @pl.when(where_ref[1] == 0)
    def _():
        top_ref[:, :nb] = top_in_ref[:, :nb]
        weights_ref[:, :nb] = -upper_ref[...]


def fetch(choice_ref, bufs, place, sem, n_cols, parts, pairs):
    for i in range(pairs):
        for h in range(2):
            for b in sorted({arrival(p, i, h, n_cols, parts) for p in range(1, n_cols)}):
                @pl.when(choice_ref[2 * i + h] == b)
                def _():
                    pltpu.make_async_copy(bufs[b], place(i, h), sem).start()


def old_top_kernel(where_ref, choice_ref, matrix_ref, *refs, used, n_cols, parts, pairs):
    bufs, top_ref, sem = dict(zip(used, refs)), refs[-2], refs[-1]
    nb = top_ref.shape[0]
    chunk = nb // (2 * pairs)
    from_matrix = pltpu.make_async_copy(
        matrix_ref.at[pl.ds(0, nb), pl.ds(0, nb)], top_ref, sem
    )

    @pl.when(where_ref[0] == 0)
    def _():
        @pl.when(where_ref[1] == 0)
        def _():
            from_matrix.start()

        @pl.when(where_ref[1] > 0)
        def _():
            fetch(
                choice_ref, bufs,
                lambda i, h: top_ref.at[pl.ds((2 * i + h) * chunk, chunk), :],
                sem, n_cols, parts, pairs,
            )

        from_matrix.wait()


def final_kernel(
    where_ref, table_ref, choice_ref, displaced_ref, weights_ref, top_ref, matrix_ref,
    *refs, n_bufs, n_tops, n_cols, parts, block,
):
    bufs, tops, out_ref = refs[:n_bufs], refs[n_bufs : n_bufs + n_tops], refs[n_bufs + n_tops]
    mat, pan, low, w_hi, w_lo, result, in_sem, low_sem, mat_sem, out_sem = refs[
        n_bufs + n_tops + 1 :
    ]
    rows, cols = matrix_ref.shape
    nb = weights_ref.shape[0]
    half = nb // 2
    chunk = rows // (2 * parts)
    row = where_ref[0]
    first_row, first_col = row == 0, where_ref[1] == 0

    load = pltpu.make_async_copy(matrix_ref, mat, mat_sem)
    load.start()
    whole_panel = pltpu.make_async_copy(matrix_ref.at[:, pl.ds(0, nb)], pan, in_sem)

    @pl.when(first_col)
    def _():
        whole_panel.start()

    @pl.when(jnp.logical_not(first_col))
    def _():
        fetch(
            choice_ref, bufs, lambda i, h: pan.at[pl.ds((2 * i + h) * chunk, chunk), :],
            in_sem, n_cols, parts, parts,
        )

    @pl.when(row == 1)
    def _():
        pltpu.make_async_copy(tops[0], low, low_sem).start()

    for log in range(1, (n_tops + 1) // 2):
        for odd in range(2):
            @pl.when(((row >> log) == 1) & ((row & 1) == odd))
            def _():
                for part, ref in enumerate(tops[2 * log - 1 : 2 * log + 1]):
                    at = half * (part ^ odd)
                    pltpu.make_async_copy(ref, low.at[pl.ds(at, half), :], low_sem).start()

    w = weights_ref[...]
    w_hi[...] = w.astype(jnp.bfloat16)
    w_lo[...] = (w - w_hi[...].astype(jnp.float32)).astype(jnp.bfloat16)

    whole_panel.wait()
    load.wait()
    count = table_ref[COUNT, 0]

    def swap(from_mat, from_pan):
        def body(k, _):
            to = table_ref[ROW, k]
            mat[pl.ds(to, 1), :] = from_mat[pl.ds(table_ref[FROM, k], 1), :]
            pan[pl.ds(to, 1), :] = from_pan[pl.ds(table_ref[TOP, k], 1), :]
            return 0

        lax.fori_loop(0, count, body, 0)

    @pl.when(first_row)
    def _():
        swap(mat, pan)

    @pl.when(jnp.logical_not(first_row))
    def _():
        pltpu.make_async_copy(tops[0], low, low_sem).wait()
        swap(displaced_ref, low)

    @pl.when(first_col)
    def _():
        mat[:, :nb] = jnp.zeros((rows, nb), jnp.float32)

    copies = []
    for b in range(rows // block):
        span = pl.ds(b * block, block)

        def update():
            p = pan[span, :]
            p_hi = p.astype(jnp.bfloat16)
            p_lo = (p - p_hi.astype(jnp.float32)).astype(jnp.bfloat16)
            dot = functools.partial(jnp.dot, preferred_element_type=jnp.float32)
            total = dot(p_lo, w_hi[...]) + dot(p_hi, w_lo[...]) + dot(p_hi, w_hi[...])
            result[span, :] = mat[span, :] - total

        if (b + 1) * block <= nb:
            pl.when(jnp.logical_not(first_row))(update)

            @pl.when(first_row)
            def _():
                result[span, :] = top_ref[span, :]
        else:
            update()
        copy = pltpu.make_async_copy(result.at[span, :], out_ref.at[span, :], out_sem)
        copy.start()
        copies.append(copy)
    for copy in copies:
        copy.wait()


LAG = 2


def steps(n_cols, parts):
    depth = n_cols // 2
    return parts + LAG * (depth - 1), max(2 * parts, parts + LAG * depth)


def arrival(p, i, h, n_cols, parts):
    z, y = divmod(p, 2)
    cross = steps(n_cols, parts)[0]
    if z == 0:
        return cross + i + h * parts
    if y == 0:
        return cross + i + LAG * (z + 1) if h == 0 else i + LAG * (z - 1)
    return i + LAG * z if h == 0 else cross + i + LAG * z


def spread(pieces, col, n_cols, riders):
    parts = len(pieces)
    n_chain, n_cross = steps(n_cols, parts)
    along = [(p, p + 2) for p in range(n_cols - 2)]
    across = [(0, 1)] + [(p, p ^ 1) for p in range(2, n_cols)]
    chain, cross = [], []
    waiting = [(rider, next(rider)(chain, cross)) for rider in riders]
    for s in range(n_cross):
        ahead = pieces[min(s, parts - 1)][1]
        aside = pieces[s][0] if s < parts else pieces[min(s - parts, parts - 1)][1]
        if s >= LAG:
            came = chain[s - LAG] if s - LAG < n_chain else chain[-1]
            due = [k for k, (_, (at, _)) in enumerate(waiting) if at == s]
            tied = [waiting[k][1][1] for k in due]
            (came, fed), tied = lax.optimization_barrier(((came, cross[s - LAG]), tied))
            ahead = jnp.where(col == 0, ahead, jnp.where(col == 1, fed, came))
            aside = jnp.where(col == 0, aside, came)
        if s < n_chain:
            chain.append(lax.ppermute(ahead, "pcol", along))
        cross.append(lax.ppermute(aside, "pcol", across))
        if s >= LAG:
            for k, values in zip(due, tied):
                rider = waiting[k][0]
                waiting[k] = (rider, resume(rider, values, chain, cross))
    results = []
    for rider, (at, values) in waiting:
        while at != DONE:
            at, values = resume(rider, values, chain, cross)
        results.append(values)
    return chain, cross, results


DONE = -1


def resume(rider, values, chain, cross):
    return rider.send(values)(chain, cross)


def give(at, values):
    return lambda chain, cross: (at, values)


def local(matrix, pivots, lower_inverse, upper_inverse, *, n_rows, n_cols, parts):
    row_dev, cols = matrix.shape
    nb = pivots.shape[0]
    f32 = jnp.float32
    row, col = lax.axis_index("prow"), lax.axis_index("pcol")
    here = jnp.stack([row, col]).astype(jnp.int32)
    odd = row % 2 == 1

    chunk = row_dev // (2 * parts)
    flat = [
        lax.slice(matrix, (k * chunk, 0), ((k + 1) * chunk, nb)) for k in range(2 * parts)
    ]
    flat = flat[:2] + list(lax.optimization_barrier(tuple(flat[2:])))
    choice = jnp.asarray(
        [
            [0] * (2 * parts) if p == 0 else
            [arrival(p, i, h, n_cols, parts) for i in range(parts) for h in range(2)]
            for p in range(n_cols)
        ],
        jnp.int32,
    )[col]

    pairs = nb // (2 * chunk)
    used = sorted({
        arrival(p, i, h, n_cols, parts)
        for p in range(1, n_cols) for i in range(pairs) for h in range(2)
    })
    n_chain = steps(n_cols, parts)[0]
    last = max(b - n_chain if b >= n_chain else b for b in used)

    def both_halves(one, two):
        return jnp.concatenate([jnp.where(odd, two, one), jnp.where(odd, one, two)], axis=0)

    def old_top_rider():
        at = last + LAG

        def start(chain, cross):
            return at, [chain[b] if b < n_chain else cross[b - n_chain] for b in used]

        arrived = yield give(at - 1, ())
        arrived = yield start
        old_top = call(
            functools.partial(
                old_top_kernel, used=used, n_cols=n_cols, parts=parts, pairs=pairs
            ),
            jax.ShapeDtypeStruct((nb, nb), f32),
            [SMEM, SMEM, ANY] + [ANY] * len(used), ANY, [pltpu.SemaphoreType.DMA],
            vmem=4 << 20,
        )(here, choice, matrix, *arrived)
        tops = []
        log = 0
        while (1 << log) < n_rows:
            d = 1 << log
            far = [(p, p + d) for p in range(d)]
            if log == 0:
                at += 2
                whole = yield give(at, lax.ppermute(old_top, "prow", far))
                tops.append(whole)
            else:
                half = jnp.where(odd, old_top[nb // 2 :], old_top[: nb // 2])
                at += 3
                one = yield give(at, lax.ppermute(half, "prow", far))
                two = lax.ppermute(one, "prow", [(p, p ^ 1) for p in range(d, 2 * d)])
                tops += [one, two]
                whole = both_halves(one, two)
            old_top = jnp.where((row >> log) == 1, whole, old_top)
            log += 1
        yield give(DONE, tops)

    slot = jax.ShapeDtypeStruct((nb, cols), f32)
    half_slot = jax.ShapeDtypeStruct((nb // 2, cols), f32)

    def exchange_rider():
        table, owner = yield give(2, call(
            functools.partial(index_kernel, row_dev=row_dev),
            (jax.ShapeDtypeStruct((8, nb), jnp.int32), jax.ShapeDtypeStruct((nb, LANES), jnp.int32)),
            [SMEM, VMEM], (VMEM, VMEM),
        )(here, pivots.reshape(1, nb)))
        held = yield give(3, call(gather_kernel, slot, [SMEM, VMEM], VMEM)(table, matrix))
        at = 5
        displaced = held
        log = 0
        half = None
        while (1 << log) < n_rows:
            d = 1 << log
            far = [(p, p ^ d) for p in range(n_rows)]
            if log == 0:
                whole = yield give(at, lax.ppermute(held, "prow", far))
                arrived = [whole]
            else:
                near = [(p, p ^ 1) for p in range(n_rows)]
                one = yield give(at + 4, lax.ppermute(half, "prow", far))
                at += 5
                two = yield give(at, lax.ppermute(one, "prow", near))
                arrived = [one, two]
                whole = both_halves(one, two)
            held, half = call(
                functools.partial(merge_kernel, log=log, halves=log > 0),
                (slot, half_slot), [SMEM] + [VMEM] * (2 + len(arrived)), (VMEM, VMEM),
            )(here, owner, held, *arrived)
            displaced = jnp.where((row >> log) == 1, whole, displaced)
            log += 1
        held, displaced = yield give(at + 1, (held, displaced))
        weights, top = yield give(at + 2, call(
            factor_kernel, (slot, slot), [SMEM, VMEM, VMEM, VMEM], (VMEM, VMEM),
            flops=4 * nb * nb * cols * 6,
        )(here, held, lower_inverse, upper_inverse))
        yield give(DONE, (table, displaced, weights, top))

    chain, cross, (tops, (table, displaced, weights, top)) = spread(
        [(flat[2 * i], flat[2 * i + 1]) for i in range(parts)], col, n_cols,
        [old_top_rider(), exchange_rider()],
    )
    bufs = chain + cross

    return call(
        functools.partial(
            final_kernel, n_bufs=len(bufs), n_tops=len(tops), n_cols=n_cols, parts=parts,
            block=256,
        ),
        jax.ShapeDtypeStruct(matrix.shape, f32),
        [SMEM, SMEM, SMEM, VMEM, VMEM, VMEM, ANY] + [ANY] * (len(bufs) + len(tops)),
        ANY,
        [
            pltpu.VMEM((row_dev, cols), f32),
            pltpu.VMEM((row_dev, nb), f32),
            pltpu.VMEM((nb, nb), f32),
            pltpu.VMEM((nb, cols), jnp.bfloat16),
            pltpu.VMEM((nb, cols), jnp.bfloat16),
            pltpu.VMEM((row_dev, cols), f32),
        ] + [pltpu.SemaphoreType.DMA] * 4,
        vmem=30 << 20,
        flops=2 * row_dev * nb * cols * 3,
        moved=4 * row_dev * (2 * cols + nb),
    )(here, table, choice, displaced, weights, top, matrix, *bufs, *tops)


def solution(mesh):
    n_rows, n_cols = mesh.shape["prow"], mesh.shape["pcol"]
    return jax.shard_map(
        functools.partial(local, n_rows=n_rows, n_cols=n_cols, parts=8),
        mesh=mesh,
        in_specs=(P("prow", "pcol"), P(), P(), P()),
        out_specs=P("prow", "pcol"),
        check_vma=False,
    )
```

time: 202 us -> 168 us (0.83)
  waiting for transfers between devices: 51.2 us -> 27.3 us
  starting transfers between devices: 95.7 us -> 90.4 us
  local copies, waits for them, and re-layouts: 16.9 us -> 13.8 us
    ppermute x49 -> x36, waiting for transfers between devices: 51.2 us -> 27.3 us  [the longest x16 16.3 us: spread(): cross.append(lax.ppermute(aside, 'pcol', across))]
    unnamed x152 -> x120, local copies, waits for them, and re-layouts: 15.1 us -> 9.3 us
    ppermute x49 -> x36, starting transfers between devices: 95.7 us -> 90.4 us  [the longest x16 44.3 us: spread(): cross.append(lax.ppermute(aside, 'pcol', across))]
    slice x1, local copies, waits for them, and re-layouts: 1.08 us -> 3.84 us  [local(): lax.slice(matrix, (k * chunk, 0), ((k + 1) * chunk, nb))]
    select_n x12 -> x15, other arithmetic: 8.55 us -> 7.17 us  [the longest x10 3.1 us: spread(): aside = jnp.where(col == 0, aside, came)]
    pallas_call x6 -> x7, Pallas kernels: 26.2 us -> 25.5 us  [the longest x1 10.8 us: local(): call(functools.partial(final_kernel, n_bufs=len(bufs), n_tops=len(tops),...]
  transfers between devices with their start and end apart: 49 -> 36, of which waited for: 9 -> 13; matrix products, arithmetic and copies ran while one was open for 4% -> 4% of each run, Pallas kernels for 7% -> 9%
where the time goes in v3:
time: 168 us; the launch traced here: 166 us
  starting transfers between devices  90.4 us (54%)
  waiting for transfers between devices  27.3 us (16%)
  Pallas kernels  25.5 us (15%)
  local copies, waits for them, and re-layouts  13.8 us (8%)
  other arithmetic  7.25 us (4%)
    ppermute x16, starting transfers between devices, spread(): cross.append(lax.ppermute(aside, 'pcol', across))  44.3 us
    ppermute x14, starting transfers between devices, spread(): chain.append(lax.ppermute(ahead, 'pcol', along))  41.3 us
    ppermute x16, waiting for transfers between devices, spread(): cross.append(lax.ppermute(aside, 'pcol', across))  16.3 us
    ppermute x14, waiting for transfers between devices, spread(): chain.append(lax.ppermute(ahead, 'pcol', along))  11 us
    pallas_call x1, Pallas kernels, local(): call(functools.partial(final_kernel, n_bufs=len(bufs), n_tops=len(tops),...  10.8 us
    unnamed x120, local copies, waits for them, and re-layouts  9.3 us
    pallas_call x1, Pallas kernels, exchange_rider(): call(factor_kernel, (slot, slot), [SMEM, VMEM, VMEM, VMEM], (VMEM, VMEM),...  5.87 us
    slice x1, local copies, waits for them, and re-layouts, local(): lax.slice(matrix, (k * chunk, 0), ((k + 1) * chunk, nb))  3.84 us
  transfers between devices with their start and end apart: 36, of which 13 were waited for; matrix products, arithmetic and copies ran while one was open for 4% of the time, Pallas kernels for 9%

profile of v3, /device:TPU:10, one launch (start us, length us, event | category | flops | bytes accessed | tf_op | source)
XLA Modules:
  0.0 165.5 jit_solution(5922821083673757848)
XLA Ops:
  0.0 3.8 %fusion = (f32[128,512]{1,0:T(8,128)}, f32[128,512]{1,0:T(8,128)}, f32[128,512]{1,0:T(8,128)}, f32[128,512]{1,0:T(8,128)}, f32[128,512]{1,0:T(8,128)}, /*index=5...) fusion(f32[2048,640]{1,0:T(8,128)} %matrix_ref.5), kind=kLoop, calls=%fused_computation.33 | loop fusion | bytes 8388608 | tf_op jit(solution)/shard_map/slice | solution.py:362
  3.9 3.4 %collective-permute-start.1 = (f32[128,512]{1,0:T(8,128)S(1)}, f32[128,512]{1,0:T(8,128)S(1)}, u32[]{:S(2)}, u32[]{:S(2)}) collective-permute-start(f32[128,512]{1,0:T(8,128)S(1)} %get-tuple-element.171), channel_id=1, source_target_pairs={{0,1},{2,3},{3,2},{4,5},{5,4},{6,7},{7,6},{8,9},{10,11},{11,10},{1... | collective-permute-start | bytes 786440 | tf_op jit(solution)/shard_map/ppermute | solution.py:328
  7.3 3.5 %collective-permute-start = (f32[128,512]{1,0:T(8,128)S(1)}, f32[128,512]{1,0:T(8,128)S(1)}, u32[]{:S(2)}, u32[]{:S(2)}) collective-permute-start(f32[128,512]{1,0:T(8,128)S(1)} %get-tuple-element.172), channel_id=1, source_target_pairs={{0,2},{1,3},{2,4},{3,5},{4,6},{5,7},{8,10},{9,11},{10,12},{11,13},... | collective-permute-start | bytes 786440 | tf_op jit(solution)/shard_map/ppermute | solution.py:327
  10.8 2.4 %collective-permute-start.3 = (f32[128,512]{1,0:T(8,128)S(1)}, f32[128,512]{1,0:T(8,128)S(1)}, u32[]{:S(2)}, u32[]{:S(2)}) collective-permute-start(f32[128,512]{1,0:T(8,128)S(1)} %get-tuple-element.88), channel_id=1, source_target_pairs={{0,1},{2,3},{3,2},{4,5},{5,4},{6,7},{7,6},{8,9},{10,11},{11,10},{1... | collective-permute-start | bytes 786440 | tf_op jit(solution)/shard_map/ppermute | solution.py:328
  13.2 3.5 %collective-permute-start.2 = (f32[128,512]{1,0:T(8,128)S(1)}, f32[128,512]{1,0:T(8,128)}, u32[]{:S(2)}, u32[]{:S(2)}) collective-permute-start(f32[128,512]{1,0:T(8,128)S(1)} %get-tuple-element.87), channel_id=1, source_target_pairs={{0,2},{1,3},{2,4},{3,5},{4,6},{5,7},{8,10},{9,11},{10,12},{11,13},... | collective-permute-start | bytes 786440 | tf_op jit(solution)/shard_map/ppermute | solution.py:327
  19.1 2.6 %copy-done = f32[2048,640]{1,0:T(8,128)S(1)} copy-done((f32[2048,640]{1,0:T(8,128)S(1)}, f32[2048,640]{1,0:T(8,128)}, u32[]{:S(2)}) %copy-start) | copy-done | bytes 5242904
  21.7 3.5 %shard_map.56.held_ref = f32[512,640]{1,0:T(8,128)S(1)} custom-call(s32[8,512]{1,0:T(8,128)S(1)} %get-tuple-element.83.table_ref, f32[2048,640]{1,0:T(8,128)S(1)} %copy-done), custom_call_target="tpu_custom_call" | custom-call | tf_op jit(solution)/shard_map/pallas_call | solution.py:430
  25.6 3.6 %collective-permute-start.15 = (f32[128,512]{1,0:T(8,128)S(1)}, f32[128,512]{1,0:T(8,128)S(1)}, u32[]{:S(2)}, u32[]{:S(2)}) collective-permute-start(f32[128,512]{1,0:T(8,128)S(1)} %get-tuple-element.192), channel_id=1, source_target_pairs={{0,1},{2,3},{3,2},{4,5},{5,4},{6,7},{7,6},{8,9},{10,11},{11,10},{1... | collective-permute-start | bytes 786440 | tf_op jit(solution)/shard_map/ppermute | solution.py:328
  32.3 2.4 %collective-permute-start.5 = (f32[128,512]{1,0:T(8,128)S(1)}, f32[128,512]{1,0:T(8,128)S(1)}, u32[]{:S(2)}, u32[]{:S(2)}) collective-permute-start(f32[128,512]{1,0:T(8,128)S(1)} %get-tuple-element.198), channel_id=1, source_target_pairs={{0,1},{2,3},{3,2},{4,5},{5,4},{6,7},{7,6},{8,9},{10,11},{11,10},{1... | collective-permute-start | bytes 786440 | tf_op jit(solution)/shard_map/ppermute | solution.py:328
  34.7 4.5 %collective-permute-start.4 = (f32[128,512]{1,0:T(8,128)S(1)}, f32[128,512]{1,0:T(8,128)S(1)}, u32[]{:S(2)}, u32[]{:S(2)}) collective-permute-start(f32[128,512]{1,0:T(8,128)S(1)} %get-tuple-element.199), channel_id=1, source_target_pairs={{0,2},{1,3},{2,4},{3,5},{4,6},{5,7},{8,10},{9,11},{10,12},{11,13},... | collective-permute-start | bytes 786440 | tf_op jit(solution)/shard_map/ppermute | solution.py:327
  42.1 2.3 %collective-permute-start.16 = (f32[128,512]{1,0:T(8,128)S(1)}, f32[128,512]{1,0:T(8,128)S(1)}, u32[]{:S(2)}, u32[]{:S(2)}) collective-permute-start(f32[128,512]{1,0:T(8,128)S(1)} %get-tuple-element.191), channel_id=1, source_target_pairs={{0,2},{1,3},{2,4},{3,5},{4,6},{5,7},{8,10},{9,11},{10,12},{11,13},... | collective-permute-start | bytes 786440 | tf_op jit(solution)/shard_map/ppermute | solution.py:327
  45.9 3.1 %collective-permute-start.8 = (f32[128,512]{1,0:T(8,128)S(1)}, f32[128,512]{1,0:T(8,128)S(1)}, u32[]{:S(2)}, u32[]{:S(2)}) collective-permute-start(f32[128,512]{1,0:T(8,128)S(1)} %get-tuple-element.196), channel_id=1, source_target_pairs={{0,1},{2,3},{3,2},{4,5},{5,4},{6,7},{7,6},{8,9},{10,11},{11,10},{1... | collective-permute-start | bytes 786440 | tf_op jit(solution)/shard_map/ppermute | solution.py:328
  49.0 3.3 %collective-permute-start.7 = (f32[128,512]{1,0:T(8,128)S(1)}, f32[128,512]{1,0:T(8,128)S(1)}, u32[]{:S(2)}, u32[]{:S(2)}) collective-permute-start(f32[128,512]{1,0:T(8,128)S(1)} %get-tuple-element.197), channel_id=1, source_target_pairs={{0,2},{1,3},{2,4},{3,5},{4,6},{5,7},{8,10},{9,11},{10,12},{11,13},... | collective-permute-start | bytes 786440 | tf_op jit(solution)/shard_map/ppermute | solution.py:327
  55.3 2.7 %collective-permute-done.7.refs_5_ = f32[128,512]{1,0:T(8,128)S(1)} collective-permute-done((f32[128,512]{1,0:T(8,128)S(1)}, f32[128,512]{1,0:T(8,128)S(1)}, u32[]{:S(2)}, u32[]{:S(2)}) %collective-permute-start.7) | collective-permute-done | bytes 262176 | tf_op jit(solution)/shard_map/ppermute | solution.py:327
  58.1 3.0 %collective-permute-start.10 = (f32[128,512]{1,0:T(8,128)S(1)}, f32[128,512]{1,0:T(8,128)S(1)}, u32[]{:S(2)}, u32[]{:S(2)}) collective-permute-start(f32[128,512]{1,0:T(8,128)S(1)} %get-tuple-element.194), channel_id=1, source_target_pairs={{0,1},{2,3},{3,2},{4,5},{5,4},{6,7},{7,6},{8,9},{10,11},{11,10},{1... | collective-permute-start | bytes 786440 | tf_op jit(solution)/shard_map/ppermute | solution.py:328
  61.2 3.5 %collective-permute-start.9 = (f32[128,512]{1,0:T(8,128)S(1)}, f32[128,512]{1,0:T(8,128)S(1)}, u32[]{:S(2)}, u32[]{:S(2)}) collective-permute-start(f32[128,512]{1,0:T(8,128)S(1)} %get-tuple-element.195), channel_id=1, source_target_pairs={{0,2},{1,3},{2,4},{3,5},{4,6},{5,7},{8,10},{9,11},{10,12},{11,13},... | collective-permute-start | bytes 786440 | tf_op jit(solution)/shard_map/ppermute | solution.py:327
  67.0 3.3 %collective-permute-start.18 = (f32[128,512]{1,0:T(8,128)S(1)}, f32[128,512]{1,0:T(8,128)S(1)}, u32[]{:S(2)}, u32[]{:S(2)}) collective-permute-start(f32[128,512]{1,0:T(8,128)S(1)} %get-tuple-element.189), channel_id=1, source_target_pairs={{0,2},{1,3},{2,4},{3,5},{4,6},{5,7},{8,10},{9,11},{10,12},{11,13},... | collective-permute-start | bytes 786440 | tf_op jit(solution)/shard_map/ppermute | solution.py:327
  70.7 2.4 %collective-permute-done.19.refs_14_.refs_20_ = f32[128,512]{1,0:T(8,128)S(1)} collective-permute-done((f32[128,512]{1,0:T(8,128)S(1)}, f32[128,512]{1,0:T(8,128)S(1)}, u32[]{:S(2)}, u32[]{:S(2)}) %collective-permute-start.19) | collective-permute-done | bytes 262176 | tf_op jit(solution)/shard_map/ppermute | solution.py:328
  77.4 3.3 %collective-permute-start.21 = (f32[128,512]{1,0:T(8,128)}, f32[128,512]{1,0:T(8,128)}, u32[]{:S(2)}, u32[]{:S(2)}) collective-permute-start(f32[128,512]{1,0:T(8,128)} %get-tuple-element.184), channel_id=1, source_target_pairs={{0,2},{1,3},{2,4},{3,5},{4,6},{5,7},{8,10},{9,11},{10,12},{11,13},... | collective-permute-start | bytes 786440 | tf_op jit(solution)/shard_map/ppermute | solution.py:327
  80.8 2.5 %collective-permute-start.20 = (f32[128,512]{1,0:T(8,128)}, f32[128,512]{1,0:T(8,128)}, u32[]{:S(2)}, u32[]{:S(2)}) collective-permute-start(f32[128,512]{1,0:T(8,128)} %get-tuple-element.185), channel_id=1, source_target_pairs={{0,1},{2,3},{3,2},{4,5},{5,4},{6,7},{7,6},{8,9},{10,11},{11,10},{1... | collective-permute-start | bytes 786440 | tf_op jit(solution)/shard_map/ppermute | solution.py:328
  84.0 2.9 %collective-permute-start.12 = (f32[128,512]{1,0:T(8,128)}, f32[128,512]{1,0:T(8,128)S(1)}, u32[]{:S(2)}, u32[]{:S(2)}) collective-permute-start(f32[128,512]{1,0:T(8,128)} %get-tuple-element.186), channel_id=1, source_target_pairs={{0,2},{1,3},{2,4},{3,5},{4,6},{5,7},{8,10},{9,11},{10,12},{11,13},... | collective-permute-start | bytes 786440 | tf_op jit(solution)/shard_map/ppermute | solution.py:327
  86.9 2.5 %collective-permute-start.13 = (f32[128,512]{1,0:T(8,128)}, f32[128,512]{1,0:T(8,128)S(1)}, u32[]{:S(2)}, u32[]{:S(2)}) collective-permute-start(f32[128,512]{1,0:T(8,128)} %get-tuple-element.187), channel_id=1, source_target_pairs={{0,1},{2,3},{3,2},{4,5},{5,4},{6,7},{7,6},{8,9},{10,11},{11,10},{1... | collective-permute-start | bytes 786440 | tf_op jit(solution)/shard_map/ppermute | solution.py:328
  92.4 2.3 %shard_map.58 = (f32[512,640]{1,0:T(8,128)S(1)}, f32[256,640]{1,0:T(8,128)}) custom-call(s32[2]{0:T(128)S(1)} %copy-done.35, s32[512,128]{1,0:T(8,128)S(1)} %copy-done.33, f32[512,640]{1,0:T(8,128)S(1)} %copy-done.30, f32[256,640]{1,0:T(8,128)S(1)} %collective-permute-done.11.refs_0_, f32[256,640]{1,0:T(8,128)} %collective-permute-done.22.refs_1_), custom_call_target="tpu_custom_call" | custom-call | tf_op jit(solution)/shard_map/pallas_call | solution.py:448
  99.5 3.3 %collective-permute-start.27 = (f32[128,512]{1,0:T(8,128)S(1)}, f32[128,512]{1,0:T(8,128)S(1)}, u32[]{:S(2)}, u32[]{:S(2)}) collective-permute-start(f32[128,512]{1,0:T(8,128)S(1)} %get-tuple-element.182), channel_id=1, source_target_pairs={{0,1},{2,3},{3,2},{4,5},{5,4},{6,7},{7,6},{8,9},{10,11},{11,10},{1... | collective-permute-start | bytes 786440 | tf_op jit(solution)/shard_map/ppermute | solution.py:328
  102.8 3.2 %collective-permute-start.25 = (f32[128,512]{1,0:T(8,128)S(1)}, f32[128,512]{1,0:T(8,128)S(1)}, u32[]{:S(2)}, u32[]{:S(2)}) collective-permute-start(f32[128,512]{1,0:T(8,128)S(1)} %get-tuple-element.183), channel_id=1, source_target_pairs={{0,2},{1,3},{2,4},{3,5},{4,6},{5,7},{8,10},{9,11},{10,12},{11,13},... | collective-permute-start | bytes 786440 | tf_op jit(solution)/shard_map/ppermute | solution.py:327
  107.7 4.4 %collective-permute-done.25.refs_11_ = f32[128,512]{1,0:T(8,128)S(1)} collective-permute-done((f32[128,512]{1,0:T(8,128)S(1)}, f32[128,512]{1,0:T(8,128)S(1)}, u32[]{:S(2)}, u32[]{:S(2)}) %collective-permute-start.25) | collective-permute-done | bytes 262176 | tf_op jit(solution)/shard_map/ppermute | solution.py:327
  120.6 4.1 %collective-permute-start.24 = (f32[128,512]{1,0:T(8,128)S(1)}, f32[128,512]{1,0:T(8,128)S(1)}, u32[]{:S(2)}, u32[]{:S(2)}) collective-permute-start(f32[128,512]{1,0:T(8,128)S(1)} %get-tuple-element.181), channel_id=1, source_target_pairs={{0,1},{2,3},{3,2},{4,5},{5,4},{6,7},{7,6},{8,9},{10,11},{11,10},{1... | collective-permute-start | bytes 786440 | tf_op jit(solution)/shard_map/ppermute | solution.py:328
  126.2 5.9 %shard_map.59 = (f32[512,640]{1,0:T(8,128)S(1)}, f32[512,640]{1,0:T(8,128)S(1)}) custom-call(s32[2]{0:T(128)S(1)} %copy-done.36, f32[512,640]{1,0:T(8,128)S(1)} %get-tuple-element.125.top_in_ref, f32[512,512]{1,0:T(8,128)S(1)} %copy-done.38, f32[512,512]{1,0:T(8,128)S(1)} %copy-done.39), custom_call_target="tpu_custom_call" | custom-call | flops 4026531840 | tf_op jit(solution)/shard_map/pallas_call | solution.py:455
  138.0 3.9 %collective-permute-start.33 = (f32[128,512]{1,0:T(8,128)S(1)}, f32[128,512]{1,0:T(8,128)S(1)}, u32[]{:S(2)}, u32[]{:S(2)}) collective-permute-start(f32[128,512]{1,0:T(8,128)S(1)} %get-tuple-element.175), channel_id=1, source_target_pairs={{0,1},{2,3},{3,2},{4,5},{5,4},{6,7},{7,6},{8,9},{10,11},{11,10},{1... | collective-permute-start | bytes 786440 | tf_op jit(solution)/shard_map/ppermute | solution.py:328
  144.4 4.7 %collective-permute-done.33.refs_29_ = f32[128,512]{1,0:T(8,128)S(1)} collective-permute-done((f32[128,512]{1,0:T(8,128)S(1)}, f32[128,512]{1,0:T(8,128)S(1)}, u32[]{:S(2)}, u32[]{:S(2)}) %collective-permute-start.33) | collective-permute-done | bytes 262176 | tf_op jit(solution)/shard_map/ppermute | solution.py:328
  149.1 5.4 %collective-permute-done.32.refs_28_ = f32[128,512]{1,0:T(8,128)S(1)} collective-permute-done((f32[128,512]{1,0:T(8,128)S(1)}, f32[128,512]{1,0:T(8,128)S(1)}, u32[]{:S(2)}, u32[]{:S(2)}) %collective-permute-start.32) | collective-permute-done | bytes 262176 | tf_op jit(solution)/shard_map/ppermute | solution.py:328
  154.5 10.8 %shard_map.61 = f32[2048,640]{1,0:T(8,128)} custom-call(s32[2]{0:T(128)S(1)} %copy-done.36, s32[8,512]{1,0:T(8,128)S(1)} %get-tuple-element.83.table_ref, s32[16]{0:T(128)S(1)} %dynamic-slice_bitcast_fusion.choice_ref, f32[512,640]{1,0:T(8,128)S(1)} %maximum_select_fusion.displaced_ref, f32[512,640]{1,0:T(8,128)S(1)} %get-tuple-element.128.weights_ref, ...), custom_call_target="tpu_custom_call" | custom-call | flops 4026531840 | bytes 14680064 | tf_op jit(solution)/shard_map/pallas_call | solution.py:467
  (186 shorter events, 48.2 us)
Async XLA Ops:
  3.9 15.3 %collective-permute-start.1 = (f32[128,512]{1,0:T(8,128)S(1)}, f32[128,512]{1,0:T(8,128)S(1)}, u32[]{:S(2)}, u32[]{:S(2)}) collective-permute-start(f32[128,512]{1,0:T(8,128)S(1)} %get-tuple-element.171), channel_id=1, source_target_pairs={{0,1},{2,3},{3,2},{4,5},{5,4},{6,7},{7,6},{8,9},{10,11},{11,10},{1... | collective-permute-start | bytes 786440 | tf_op jit(solution)/shard_map/ppermute | solution.py:328
  7.3 11.8 %collective-permute-start = (f32[128,512]{1,0:T(8,128)S(1)}, f32[128,512]{1,0:T(8,128)S(1)}, u32[]{:S(2)}, u32[]{:S(2)}) collective-permute-start(f32[128,512]{1,0:T(8,128)S(1)} %get-tuple-element.172), channel_id=1, source_target_pairs={{0,2},{1,3},{2,4},{3,5},{4,6},{5,7},{8,10},{9,11},{10,12},{11,13},... | collective-permute-start | bytes 786440 | tf_op jit(solution)/shard_map/ppermute | solution.py:327
  10.8 14.5 %collective-permute-start.3 = (f32[128,512]{1,0:T(8,128)S(1)}, f32[128,512]{1,0:T(8,128)S(1)}, u32[]{:S(2)}, u32[]{:S(2)}) collective-permute-start(f32[128,512]{1,0:T(8,128)S(1)} %get-tuple-element.88), channel_id=1, source_target_pairs={{0,1},{2,3},{3,2},{4,5},{5,4},{6,7},{7,6},{8,9},{10,11},{11,10},{1... | collective-permute-start | bytes 786440 | tf_op jit(solution)/shard_map/ppermute | solution.py:328
  13.2 12.1 %collective-permute-start.2 = (f32[128,512]{1,0:T(8,128)S(1)}, f32[128,512]{1,0:T(8,128)}, u32[]{:S(2)}, u32[]{:S(2)}) collective-permute-start(f32[128,512]{1,0:T(8,128)S(1)} %get-tuple-element.87), channel_id=1, source_target_pairs={{0,2},{1,3},{2,4},{3,5},{4,6},{5,7},{8,10},{9,11},{10,12},{11,13},... | collective-permute-start | bytes 786440 | tf_op jit(solution)/shard_map/ppermute | solution.py:327
  25.3 19.9 %collective-permute-start.6 = (f32[512,640]{1,0:T(8,128)S(1)}, f32[512,640]{1,0:T(8,128)S(1)}, u32[]{:S(2)}, u32[]{:S(2)}) collective-permute-start(f32[512,640]{1,0:T(8,128)S(1)} %shard_map.56.held_ref), channel_id=1, source_target_pairs={{0,8},{8,0},{16,24},{24,16},{1,9},{9,1},{17,25},{25,17},{2,10},{10... | collective-permute-start | bytes 3932168 | tf_op jit(solution)/shard_map/ppermute | solution.py:439
  25.6 13.6 %collective-permute-start.15 = (f32[128,512]{1,0:T(8,128)S(1)}, f32[128,512]{1,0:T(8,128)S(1)}, u32[]{:S(2)}, u32[]{:S(2)}) collective-permute-start(f32[128,512]{1,0:T(8,128)S(1)} %get-tuple-element.192), channel_id=1, source_target_pairs={{0,1},{2,3},{3,2},{4,5},{5,4},{6,7},{7,6},{8,9},{10,11},{11,10},{1... | collective-permute-start | bytes 786440 | tf_op jit(solution)/shard_map/ppermute | solution.py:328
  29.1 10.7 %collective-permute-start.14 = (f32[128,512]{1,0:T(8,128)S(1)}, f32[128,512]{1,0:T(8,128)S(1)}, u32[]{:S(2)}, u32[]{:S(2)}) collective-permute-start(f32[128,512]{1,0:T(8,128)S(1)} %get-tuple-element.193), channel_id=1, source_target_pairs={{0,2},{1,3},{2,4},{3,5},{4,6},{5,7},{8,10},{9,11},{10,12},{11,13},... | collective-permute-start | bytes 786440 | tf_op jit(solution)/shard_map/ppermute | solution.py:327
  32.3 12.1 %collective-permute-start.5 = (f32[128,512]{1,0:T(8,128)S(1)}, f32[128,512]{1,0:T(8,128)S(1)}, u32[]{:S(2)}, u32[]{:S(2)}) collective-permute-start(f32[128,512]{1,0:T(8,128)S(1)} %get-tuple-element.198), channel_id=1, source_target_pairs={{0,1},{2,3},{3,2},{4,5},{5,4},{6,7},{7,6},{8,9},{10,11},{11,10},{1... | collective-permute-start | bytes 786440 | tf_op jit(solution)/shard_map/ppermute | solution.py:328
  34.7 10.5 %collective-permute-start.4 = (f32[128,512]{1,0:T(8,128)S(1)}, f32[128,512]{1,0:T(8,128)S(1)}, u32[]{:S(2)}, u32[]{:S(2)}) collective-permute-start(f32[128,512]{1,0:T(8,128)S(1)} %get-tuple-element.199), channel_id=1, source_target_pairs={{0,2},{1,3},{2,4},{3,5},{4,6},{5,7},{8,10},{9,11},{10,12},{11,13},... | collective-permute-start | bytes 786440 | tf_op jit(solution)/shard_map/ppermute | solution.py:327
  39.9 12.4 %collective-permute-start.17 = (f32[128,512]{1,0:T(8,128)S(1)}, f32[128,512]{1,0:T(8,128)S(1)}, u32[]{:S(2)}, u32[]{:S(2)}) collective-permute-start(f32[128,512]{1,0:T(8,128)S(1)} %get-tuple-element.190), channel_id=1, source_target_pairs={{0,1},{2,3},{3,2},{4,5},{5,4},{6,7},{7,6},{8,9},{10,11},{11,10},{1... | collective-permute-start | bytes 786440 | tf_op jit(solution)/shard_map/ppermute | solution.py:328
  42.1 10.3 %collective-permute-start.16 = (f32[128,512]{1,0:T(8,128)S(1)}, f32[128,512]{1,0:T(8,128)S(1)}, u32[]{:S(2)}, u32[]{:S(2)}) collective-permute-start(f32[128,512]{1,0:T(8,128)S(1)} %get-tuple-element.191), channel_id=1, source_target_pairs={{0,2},{1,3},{2,4},{3,5},{4,6},{5,7},{8,10},{9,11},{10,12},{11,13},... | collective-permute-start | bytes 786440 | tf_op jit(solution)/shard_map/ppermute | solution.py:327
  45.9 9.4 %collective-permute-start.8 = (f32[128,512]{1,0:T(8,128)S(1)}, f32[128,512]{1,0:T(8,128)S(1)}, u32[]{:S(2)}, u32[]{:S(2)}) collective-permute-start(f32[128,512]{1,0:T(8,128)S(1)} %get-tuple-element.196), channel_id=1, source_target_pairs={{0,1},{2,3},{3,2},{4,5},{5,4},{6,7},{7,6},{8,9},{10,11},{11,10},{1... | collective-permute-start | bytes 786440 | tf_op jit(solution)/shard_map/ppermute | solution.py:328
  49.0 9.0 %collective-permute-start.7 = (f32[128,512]{1,0:T(8,128)S(1)}, f32[128,512]{1,0:T(8,128)S(1)}, u32[]{:S(2)}, u32[]{:S(2)}) collective-permute-start(f32[128,512]{1,0:T(8,128)S(1)} %get-tuple-element.197), channel_id=1, source_target_pairs={{0,2},{1,3},{2,4},{3,5},{4,6},{5,7},{8,10},{9,11},{10,12},{11,13},... | collective-permute-start | bytes 786440 | tf_op jit(solution)/shard_map/ppermute | solution.py:327
  53.3 17.5 %collective-permute-start.11 = (f32[256,640]{1,0:T(8,128)S(1)}, f32[256,640]{1,0:T(8,128)S(1)}, u32[]{:S(2)}, u32[]{:S(2)}) collective-permute-start(f32[256,640]{1,0:T(8,128)S(1)} %get-tuple-element.101), channel_id=1, source_target_pairs={{0,16},{8,24},{16,0},{24,8},{1,17},{9,25},{17,1},{25,9},{2,18},{10... | collective-permute-start | bytes 1966088 | tf_op jit(solution)/shard_map/ppermute | solution.py:443
  58.1 12.2 %collective-permute-start.10 = (f32[128,512]{1,0:T(8,128)S(1)}, f32[128,512]{1,0:T(8,128)S(1)}, u32[]{:S(2)}, u32[]{:S(2)}) collective-permute-start(f32[128,512]{1,0:T(8,128)S(1)} %get-tuple-element.194), channel_id=1, source_target_pairs={{0,1},{2,3},{3,2},{4,5},{5,4},{6,7},{7,6},{8,9},{10,11},{11,10},{1... | collective-permute-start | bytes 786440 | tf_op jit(solution)/shard_map/ppermute | solution.py:328
  61.2 9.6 %collective-permute-start.9 = (f32[128,512]{1,0:T(8,128)S(1)}, f32[128,512]{1,0:T(8,128)S(1)}, u32[]{:S(2)}, u32[]{:S(2)}) collective-permute-start(f32[128,512]{1,0:T(8,128)S(1)} %get-tuple-element.195), channel_id=1, source_target_pairs={{0,2},{1,3},{2,4},{3,5},{4,6},{5,7},{8,10},{9,11},{10,12},{11,13},... | collective-permute-start | bytes 786440 | tf_op jit(solution)/shard_map/ppermute | solution.py:327
  70.7 18.8 %collective-permute-start.22 = (f32[256,640]{1,0:T(8,128)S(1)}, f32[256,640]{1,0:T(8,128)}, u32[]{:S(2)}, u32[]{:S(2)}) collective-permute-start(f32[256,640]{1,0:T(8,128)S(1)} %collective-permute-done.11.refs_0_), channel_id=1, source_target_pairs={{0,8},{8,0},{16,24},{24,16},{1,9},{9,1},{17,25},{25,17},{2,10},{10... | collective-permute-start | bytes 1966088 | tf_op jit(solution)/shard_map/ppermute | solution.py:445
  77.4 12.0 %collective-permute-start.21 = (f32[128,512]{1,0:T(8,128)}, f32[128,512]{1,0:T(8,128)}, u32[]{:S(2)}, u32[]{:S(2)}) collective-permute-start(f32[128,512]{1,0:T(8,128)} %get-tuple-element.184), channel_id=1, source_target_pairs={{0,2},{1,3},{2,4},{3,5},{4,6},{5,7},{8,10},{9,11},{10,12},{11,13},... | collective-permute-start | bytes 786440 | tf_op jit(solution)/shard_map/ppermute | solution.py:327
  80.8 8.7 %collective-permute-start.20 = (f32[128,512]{1,0:T(8,128)}, f32[128,512]{1,0:T(8,128)}, u32[]{:S(2)}, u32[]{:S(2)}) collective-permute-start(f32[128,512]{1,0:T(8,128)} %get-tuple-element.185), channel_id=1, source_target_pairs={{0,1},{2,3},{3,2},{4,5},{5,4},{6,7},{7,6},{8,9},{10,11},{11,10},{1... | collective-permute-start | bytes 786440 | tf_op jit(solution)/shard_map/ppermute | solution.py:328
  84.0 12.5 %collective-permute-start.12 = (f32[128,512]{1,0:T(8,128)}, f32[128,512]{1,0:T(8,128)S(1)}, u32[]{:S(2)}, u32[]{:S(2)}) collective-permute-start(f32[128,512]{1,0:T(8,128)} %get-tuple-element.186), channel_id=1, source_target_pairs={{0,2},{1,3},{2,4},{3,5},{4,6},{5,7},{8,10},{9,11},{10,12},{11,13},... | collective-permute-start | bytes 786440 | tf_op jit(solution)/shard_map/ppermute | solution.py:327
  86.9 9.6 %collective-permute-start.13 = (f32[128,512]{1,0:T(8,128)}, f32[128,512]{1,0:T(8,128)S(1)}, u32[]{:S(2)}, u32[]{:S(2)}) collective-permute-start(f32[128,512]{1,0:T(8,128)} %get-tuple-element.187), channel_id=1, source_target_pairs={{0,1},{2,3},{3,2},{4,5},{5,4},{6,7},{7,6},{8,9},{10,11},{11,10},{1... | collective-permute-start | bytes 786440 | tf_op jit(solution)/shard_map/ppermute | solution.py:328
  98.6 13.5 %collective-permute-start.28 = (f32[512,512]{1,0:T(8,128)S(1)}, f32[512,512]{1,0:T(8,128)S(1)}, u32[]{:S(2)}, u32[]{:S(2)}) collective-permute-start(f32[512,512]{1,0:T(8,128)S(1)} %shard_map.60), channel_id=1, source_target_pairs={{0,8},{1,9},{2,10},{3,11},{4,12},{5,13},{6,14},{7,15}} | collective-permute-start | bytes 3145736 | tf_op jit(solution)/shard_map/ppermute | solution.py:408
  102.8 9.4 %collective-permute-start.25 = (f32[128,512]{1,0:T(8,128)S(1)}, f32[128,512]{1,0:T(8,128)S(1)}, u32[]{:S(2)}, u32[]{:S(2)}) collective-permute-start(f32[128,512]{1,0:T(8,128)S(1)} %get-tuple-element.183), channel_id=1, source_target_pairs={{0,2},{1,3},{2,4},{3,5},{4,6},{5,7},{8,10},{9,11},{10,12},{11,13},... | collective-permute-start | bytes 786440 | tf_op jit(solution)/shard_map/ppermute | solution.py:327
  114.7 17.4 %collective-permute-start.31 = (f32[128,512]{1,0:T(8,128)S(1)}, f32[128,512]{1,0:T(8,128)S(1)}, u32[]{:S(2)}, u32[]{:S(2)}) collective-permute-start(f32[128,512]{1,0:T(8,128)S(1)} %get-tuple-element.178), channel_id=1, source_target_pairs={{0,1},{2,3},{3,2},{4,5},{5,4},{6,7},{7,6},{8,9},{10,11},{11,10},{1... | collective-permute-start | bytes 786440 | tf_op jit(solution)/shard_map/ppermute | solution.py:328
  116.6 15.5 %collective-permute-start.29 = (f32[128,512]{1,0:T(8,128)S(1)}, f32[128,512]{1,0:T(8,128)S(1)}, u32[]{:S(2)}, u32[]{:S(2)}) collective-permute-start(f32[128,512]{1,0:T(8,128)S(1)} %get-tuple-element.179), channel_id=1, source_target_pairs={{0,2},{1,3},{2,4},{3,5},{4,6},{5,7},{8,10},{9,11},{10,12},{11,13},... | collective-permute-start | bytes 786440 | tf_op jit(solution)/shard_map/ppermute | solution.py:327
  118.7 13.4 %collective-permute-start.23 = (f32[128,512]{1,0:T(8,128)S(1)}, f32[128,512]{1,0:T(8,128)S(1)}, u32[]{:S(2)}, u32[]{:S(2)}) collective-permute-start(f32[128,512]{1,0:T(8,128)S(1)} %get-tuple-element.180), channel_id=1, source_target_pairs={{0,2},{1,3},{2,4},{3,5},{4,6},{5,7},{8,10},{9,11},{10,12},{11,13},... | collective-permute-start | bytes 786440 | tf_op jit(solution)/shard_map/ppermute | solution.py:327
  120.6 11.5 %collective-permute-start.24 = (f32[128,512]{1,0:T(8,128)S(1)}, f32[128,512]{1,0:T(8,128)S(1)}, u32[]{:S(2)}, u32[]{:S(2)}) collective-permute-start(f32[128,512]{1,0:T(8,128)S(1)} %get-tuple-element.181), channel_id=1, source_target_pairs={{0,1},{2,3},{3,2},{4,5},{5,4},{6,7},{7,6},{8,9},{10,11},{11,10},{1... | collective-permute-start | bytes 786440 | tf_op jit(solution)/shard_map/ppermute | solution.py:328
  124.7 11.4 %collective-permute-start.34 = (f32[256,512]{1,0:T(8,128)S(1)}, f32[256,512]{1,0:T(8,128)S(1)}, u32[]{:S(2)}, u32[]{:S(2)}) collective-permute-start(f32[256,512]{1,0:T(8,128)S(1)} %slice_select_fusion), channel_id=1, source_target_pairs={{0,16},{8,24},{1,17},{9,25},{2,18},{10,26},{3,19},{11,27},{4,20},{... | collective-permute-start | bytes 1572872 | tf_op jit(solution)/shard_map/ppermute | solution.py:413
  132.2 9.7 %collective-permute-start.26 = (f32[128,512]{1,0:T(8,128)S(1)}, f32[128,512]{1,0:T(8,128)S(1)}, u32[]{:S(2)}, u32[]{:S(2)}) collective-permute-start(f32[128,512]{1,0:T(8,128)S(1)} %get-tuple-element.176), channel_id=1, source_target_pairs={{0,2},{1,3},{2,4},{3,5},{4,6},{5,7},{8,10},{9,11},{10,12},{11,13},... | collective-permute-start | bytes 786440 | tf_op jit(solution)/shard_map/ppermute | solution.py:327
  136.1 18.4 %collective-permute-start.35 = (f32[256,512]{1,0:T(8,128)S(1)}, f32[256,512]{1,0:T(8,128)S(1)}, u32[]{:S(2)}, u32[]{:S(2)}) collective-permute-start(f32[256,512]{1,0:T(8,128)S(1)} %collective-permute-done.34.refs_31_), channel_id=1, source_target_pairs={{16,24},{24,16},{17,25},{25,17},{18,26},{26,18},{19,27},{27,19},{2... | collective-permute-start | bytes 1572872 | tf_op jit(solution)/shard_map/ppermute | solution.py:414
  138.0 11.1 %collective-permute-start.33 = (f32[128,512]{1,0:T(8,128)S(1)}, f32[128,512]{1,0:T(8,128)S(1)}, u32[]{:S(2)}, u32[]{:S(2)}) collective-permute-start(f32[128,512]{1,0:T(8,128)S(1)} %get-tuple-element.175), channel_id=1, source_target_pairs={{0,1},{2,3},{3,2},{4,5},{5,4},{6,7},{7,6},{8,9},{10,11},{11,10},{1... | collective-permute-start | bytes 786440 | tf_op jit(solution)/shard_map/ppermute | solution.py:328
  142.5 12.1 %collective-permute-start.32 = (f32[128,512]{1,0:T(8,128)S(1)}, f32[128,512]{1,0:T(8,128)S(1)}, u32[]{:S(2)}, u32[]{:S(2)}) collective-permute-start(f32[128,512]{1,0:T(8,128)S(1)} %broadcast_select_fusion.4), channel_id=1, source_target_pairs={{0,1},{2,3},{3,2},{4,5},{5,4},{6,7},{7,6},{8,9},{10,11},{11,10},{1... | collective-permute-start | bytes 786440 | tf_op jit(solution)/shard_map/ppermute | solution.py:328
  (64 other events, 453.2 us)

commit v4 on v3

--- a/solution.py
+++ b/solution.py
@@ -155,43 +155,40 @@
         weights_ref[:, :nb] = -upper_ref[...]
 
 
-def fetch(choice_ref, bufs, place, sem, n_cols, parts, pairs):
-    for i in range(pairs):
-        for h in range(2):
-            for b in sorted({arrival(p, i, h, n_cols, parts) for p in range(1, n_cols)}):
-                @pl.when(choice_ref[2 * i + h] == b)
-                def _():
-                    pltpu.make_async_copy(bufs[b], place(i, h), sem).start()
-
-
-def old_top_kernel(where_ref, choice_ref, matrix_ref, *refs, used, n_cols, parts, pairs):
-    bufs, top_ref, sem = dict(zip(used, refs)), refs[-2], refs[-1]
+def old_top_kernel(where_ref, matrix_ref, near_ref, far_ref, top_ref, sem):
     nb = top_ref.shape[0]
-    chunk = nb // (2 * pairs)
     from_matrix = pltpu.make_async_copy(
         matrix_ref.at[pl.ds(0, nb), pl.ds(0, nb)], top_ref, sem
     )
 
     @pl.when(where_ref[0] == 0)
     def _():
-        @pl.when(where_ref[1] == 0)
+        fetch_panel(where_ref, matrix_ref, [near_ref, far_ref], top_ref, sem)
+        from_matrix.wait()
+
+
+def fetch_panel(where_ref, matrix_ref, bufs, out_ref, sem):
+    rows, nb = out_ref.shape
+    half = rows // len(bufs)
+    col = where_ref[1]
+
+    @pl.when(col == 0)
+    def _():
+        pltpu.make_async_copy(
+            matrix_ref.at[pl.ds(0, rows), pl.ds(0, nb)], out_ref, sem
+        ).start()
+
+    for y in range(2):
+        @pl.when((col > 0) & ((col & 1) == y))
         def _():
-            from_matrix.start()
-
-        @pl.when(where_ref[1] > 0)
-        def _():
-            fetch(
-                choice_ref, bufs,
-                lambda i, h: top_ref.at[pl.ds((2 * i + h) * chunk, chunk), :],
-                sem, n_cols, parts, pairs,
-            )
-
-        from_matrix.wait()
+            for k, buf in enumerate(bufs):
+                at = half * (k if y else k ^ 1)
+                pltpu.make_async_copy(buf, out_ref.at[pl.ds(at, half), :], sem).start()
 
 
 def final_kernel(
-    where_ref, table_ref, choice_ref, displaced_ref, weights_ref, top_ref, matrix_ref,
-    *refs, n_bufs, n_tops, n_cols, parts, block,
+    where_ref, table_ref, displaced_ref, weights_ref, top_ref, matrix_ref,
+    *refs, n_bufs, n_tops, block,
 ):
     bufs, tops, out_ref = refs[:n_bufs], refs[n_bufs : n_bufs + n_tops], refs[n_bufs + n_tops]
     mat, pan, low, w_hi, w_lo, result, in_sem, low_sem, mat_sem, out_sem = refs[
@@ -200,7 +197,6 @@
     rows, cols = matrix_ref.shape
     nb = weights_ref.shape[0]
     half = nb // 2
-    chunk = rows // (2 * parts)
     row = where_ref[0]
     first_row, first_col = row == 0, where_ref[1] == 0
 
@@ -208,16 +204,7 @@
     load.start()
     whole_panel = pltpu.make_async_copy(matrix_ref.at[:, pl.ds(0, nb)], pan, in_sem)
 
-    @pl.when(first_col)
-    def _():
-        whole_panel.start()
-
-    @pl.when(jnp.logical_not(first_col))
-    def _():
-        fetch(
-            choice_ref, bufs, lambda i, h: pan.at[pl.ds((2 * i + h) * chunk, chunk), :],
-            in_sem, n_cols, parts, parts,
-        )
+    fetch_panel(where_ref, matrix_ref, bufs, pan, in_sem)
 
     @pl.when(row == 1)
     def _():
@@ -288,147 +275,48 @@
         copy.wait()
 
 
-LAG = 2
-
-
-def steps(n_cols, parts):
-    depth = n_cols // 2
-    return parts + LAG * (depth - 1), max(2 * parts, parts + LAG * depth)
-
-
-def arrival(p, i, h, n_cols, parts):
-    z, y = divmod(p, 2)
-    cross = steps(n_cols, parts)[0]
-    if z == 0:
-        return cross + i + h * parts
-    if y == 0:
-        return cross + i + LAG * (z + 1) if h == 0 else i + LAG * (z - 1)
-    return i + LAG * z if h == 0 else cross + i + LAG * z
-
-
-def spread(pieces, col, n_cols, riders):
-    parts = len(pieces)
-    n_chain, n_cross = steps(n_cols, parts)
-    along = [(p, p + 2) for p in range(n_cols - 2)]
-    across = [(0, 1)] + [(p, p ^ 1) for p in range(2, n_cols)]
-    chain, cross = [], []
-    waiting = [(rider, next(rider)(chain, cross)) for rider in riders]
-    for s in range(n_cross):
-        ahead = pieces[min(s, parts - 1)][1]
-        aside = pieces[s][0] if s < parts else pieces[min(s - parts, parts - 1)][1]
-        if s >= LAG:
-            came = chain[s - LAG] if s - LAG < n_chain else chain[-1]
-            due = [k for k, (_, (at, _)) in enumerate(waiting) if at == s]
-            tied = [waiting[k][1][1] for k in due]
-            (came, fed), tied = lax.optimization_barrier(((came, cross[s - LAG]), tied))
-            ahead = jnp.where(col == 0, ahead, jnp.where(col == 1, fed, came))
-            aside = jnp.where(col == 0, aside, came)
-        if s < n_chain:
-            chain.append(lax.ppermute(ahead, "pcol", along))
-        cross.append(lax.ppermute(aside, "pcol", across))
-        if s >= LAG:
-            for k, values in zip(due, tied):
-                rider = waiting[k][0]
-                waiting[k] = (rider, resume(rider, values, chain, cross))
-    results = []
-    for rider, (at, values) in waiting:
-        while at != DONE:
-            at, values = resume(rider, values, chain, cross)
-        results.append(values)
-    return chain, cross, results
-
-
-DONE = -1
-
-
-def resume(rider, values, chain, cross):
-    return rider.send(values)(chain, cross)
-
-
-def give(at, values):
-    return lambda chain, cross: (at, values)
-
-
-def local(matrix, pivots, lower_inverse, upper_inverse, *, n_rows, n_cols, parts):
+def tie(*values):
+    return lax.optimization_barrier(values)
+
+
+def local(matrix, pivots, lower_inverse, upper_inverse, *, n_rows, n_cols, groups):
     row_dev, cols = matrix.shape
     nb = pivots.shape[0]
     f32 = jnp.float32
     row, col = lax.axis_index("prow"), lax.axis_index("pcol")
     here = jnp.stack([row, col]).astype(jnp.int32)
     odd = row % 2 == 1
-
-    chunk = row_dev // (2 * parts)
-    flat = [
-        lax.slice(matrix, (k * chunk, 0), ((k + 1) * chunk, nb)) for k in range(2 * parts)
-    ]
-    flat = flat[:2] + list(lax.optimization_barrier(tuple(flat[2:])))
-    choice = jnp.asarray(
-        [
-            [0] * (2 * parts) if p == 0 else
-            [arrival(p, i, h, n_cols, parts) for i in range(parts) for h in range(2)]
-            for p in range(n_cols)
-        ],
-        jnp.int32,
-    )[col]
-
-    pairs = nb // (2 * chunk)
-    used = sorted({
-        arrival(p, i, h, n_cols, parts)
-        for p in range(1, n_cols) for i in range(pairs) for h in range(2)
-    })
-    n_chain = steps(n_cols, parts)[0]
-    last = max(b - n_chain if b >= n_chain else b for b in used)
-
-    def both_halves(one, two):
-        return jnp.concatenate([jnp.where(odd, two, one), jnp.where(odd, one, two)], axis=0)
-
-    def old_top_rider():
-        at = last + LAG
-
-        def start(chain, cross):
-            return at, [chain[b] if b < n_chain else cross[b - n_chain] for b in used]
-
-        arrived = yield give(at - 1, ())
-        arrived = yield start
-        old_top = call(
-            functools.partial(
-                old_top_kernel, used=used, n_cols=n_cols, parts=parts, pairs=pairs
-            ),
-            jax.ShapeDtypeStruct((nb, nb), f32),
-            [SMEM, SMEM, ANY] + [ANY] * len(used), ANY, [pltpu.SemaphoreType.DMA],
-            vmem=4 << 20,
-        )(here, choice, matrix, *arrived)
-        tops = []
-        log = 0
-        while (1 << log) < n_rows:
-            d = 1 << log
-            far = [(p, p + d) for p in range(d)]
-            if log == 0:
-                at += 2
-                whole = yield give(at, lax.ppermute(old_top, "prow", far))
-                tops.append(whole)
-            else:
-                half = jnp.where(odd, old_top[nb // 2 :], old_top[: nb // 2])
-                at += 3
-                one = yield give(at, lax.ppermute(half, "prow", far))
-                two = lax.ppermute(one, "prow", [(p, p ^ 1) for p in range(d, 2 * d)])
-                tops += [one, two]
-                whole = both_halves(one, two)
-            old_top = jnp.where((row >> log) == 1, whole, old_top)
-            log += 1
-        yield give(DONE, tops)
-
     slot = jax.ShapeDtypeStruct((nb, cols), f32)
     half_slot = jax.ShapeDtypeStruct((nb // 2, cols), f32)
 
-    def exchange_rider():
-        table, owner = yield give(2, call(
+    depth = n_cols // 2
+    half_rows = row_dev // (2 * groups)
+    piece_rows = half_rows // depth
+    lanes = [[z * 2 + y for z in range(depth)] for y in range(2)]
+    across = [(0, 1)] + [(p, p ^ 1) for p in range(2, n_cols)]
+
+    def panel_rows(start, size):
+        return lax.slice(matrix, (start, 0), (start + size, nb))
+
+    def scatter(line):
+        pieces = [line[z * piece_rows : (z + 1) * piece_rows] for z in range(depth)]
+        mine = pieces[0]
+        for z in range(1, depth):
+            came = lax.ppermute(pieces[z], "pcol", [(0, 2 * z), (1, 2 * z + 1)])
+            mine = jnp.where(col // 2 == z, came, mine)
+        return mine
+
+    def gather(piece):
+        return lax.all_gather(piece, "pcol", axis=0, tiled=True, axis_index_groups=lanes)
+
+    def exchange():
+        table, owner = call(
             functools.partial(index_kernel, row_dev=row_dev),
             (jax.ShapeDtypeStruct((8, nb), jnp.int32), jax.ShapeDtypeStruct((nb, LANES), jnp.int32)),
             [SMEM, VMEM], (VMEM, VMEM),
-        )(here, pivots.reshape(1, nb)))
-        held = yield give(3, call(gather_kernel, slot, [SMEM, VMEM], VMEM)(table, matrix))
-        at = 5
+        )(here, pivots.reshape(1, nb))
+        held = call(gather_kernel, slot, [SMEM, VMEM], VMEM)(table, matrix)
+        (held,) = yield (held,)
         displaced = held
         log = 0
         half = None
@@ -436,13 +324,13 @@
             d = 1 << log
             far = [(p, p ^ d) for p in range(n_rows)]
             if log == 0:
-                whole = yield give(at, lax.ppermute(held, "prow", far))
+                (whole,) = yield (lax.ppermute(held, "prow", far),)
                 arrived = [whole]
             else:
                 near = [(p, p ^ 1) for p in range(n_rows)]
-                one = yield give(at + 4, lax.ppermute(half, "prow", far))
-                at += 5
-                two = yield give(at, lax.ppermute(one, "prow", near))
+                (one,) = yield (lax.ppermute(half, "prow", far),)
+                (one,) = yield (one,)
+                (two,) = yield (lax.ppermute(one, "prow", near),)
                 arrived = [one, two]
                 whole = both_halves(one, two)
             held, half = call(
@@ -451,26 +339,75 @@
             )(here, owner, held, *arrived)
             displaced = jnp.where((row >> log) == 1, whole, displaced)
             log += 1
-        held, displaced = yield give(at + 1, (held, displaced))
-        weights, top = yield give(at + 2, call(
+        weights, top = call(
             factor_kernel, (slot, slot), [SMEM, VMEM, VMEM, VMEM], (VMEM, VMEM),
             flops=4 * nb * nb * cols * 6,
-        )(here, held, lower_inverse, upper_inverse))
-        yield give(DONE, (table, displaced, weights, top))
-
-    chain, cross, (tops, (table, displaced, weights, top)) = spread(
-        [(flat[2 * i], flat[2 * i + 1]) for i in range(parts)], col, n_cols,
-        [old_top_rider(), exchange_rider()],
-    )
-    bufs = chain + cross
+        )(here, held, lower_inverse, upper_inverse)
+        return table, displaced, weights, top
+
+    def both_halves(one, two):
+        return jnp.concatenate([jnp.where(odd, two, one), jnp.where(odd, one, two)], axis=0)
+
+    def spread_top():
+        (near, far_half) = yield None
+        old_top = call(
+            old_top_kernel, jax.ShapeDtypeStruct((nb, nb), f32),
+            [SMEM, ANY, ANY, ANY], ANY, [pltpu.SemaphoreType.DMA], vmem=4 << 20,
+        )(here, matrix, near, far_half)
+        tops = []
+        log = 0
+        while (1 << log) < n_rows:
+            d = 1 << log
+            far = [(p, p + d) for p in range(d)]
+            if log == 0:
+                (whole,) = yield (lax.ppermute(old_top, "prow", far),)
+                tops.append(whole)
+            else:
+                half = jnp.where(odd, old_top[nb // 2 :], old_top[: nb // 2])
+                (one,) = yield (lax.ppermute(half, "prow", far),)
+                two = lax.ppermute(one, "prow", [(p, p ^ 1) for p in range(d, 2 * d)])
+                tops += [one, two]
+                whole = both_halves(one, two)
+            old_top = jnp.where((row >> log) == 1, whole, old_top)
+            log += 1
+        return tops
+
+    rows_side, top_side = Rider(exchange()), Rider(spread_top())
+    fed = lax.ppermute(panel_rows(0, half_rows), "pcol", [(0, 1)])
+    mine, along, other = None, [], []
+    for g in range(groups + 2):
+        if g == 3:
+            top_side.value = (along[0], other[0])
+        line, crossed = along[g - 2] if g > 1 else None, other[g - 3] if g > 3 else None
+        bundle = (fed, mine, line, crossed, rows_side.value, top_side.value)
+        fed, mine, line, crossed, rows_side.value, top_side.value = tie(*bundle)
+        if g > 3:
+            other[g - 3] = crossed
+        if g > 1:
+            other.append(lax.ppermute(line, "pcol", across))
+        if 0 < g <= groups:
+            along.append(gather(mine))
+        if g < groups:
+            run = jnp.where(
+                col == 0, panel_rows((2 * g + 1) * half_rows, half_rows), fed
+            )
+            if g + 1 < groups:
+                run, ahead = tie(run, panel_rows(2 * (g + 1) * half_rows, half_rows))
+            mine = scatter(run)
+            fed = lax.ppermute(ahead, "pcol", [(0, 1)]) if g + 1 < groups else None
+        else:
+            mine = None
+        rows_side.go()
+        if g >= 3:
+            top_side.go()
+    table, displaced, weights, top = rows_side.finish()
+    tops = top_side.finish()
+    bufs = [b for pair in zip(along, other) for b in pair]
 
     return call(
-        functools.partial(
-            final_kernel, n_bufs=len(bufs), n_tops=len(tops), n_cols=n_cols, parts=parts,
-            block=256,
-        ),
+        functools.partial(final_kernel, n_bufs=len(bufs), n_tops=len(tops), block=256),
         jax.ShapeDtypeStruct(matrix.shape, f32),
-        [SMEM, SMEM, SMEM, VMEM, VMEM, VMEM, ANY] + [ANY] * (len(bufs) + len(tops)),
+        [SMEM, SMEM, VMEM, VMEM, VMEM, ANY] + [ANY] * (len(bufs) + len(tops)),
         ANY,
         [
             pltpu.VMEM((row_dev, cols), f32),
@@ -483,13 +420,31 @@
         vmem=30 << 20,
         flops=2 * row_dev * nb * cols * 3,
         moved=4 * row_dev * (2 * cols + nb),
-    )(here, table, choice, displaced, weights, top, matrix, *bufs, *tops)
+    )(here, table, displaced, weights, top, matrix, *bufs, *tops)
+
+
+class Rider:
+    def __init__(self, stages):
+        self.stages, self.result = stages, None
+        self.value = next(stages)
+
+    def go(self):
+        if self.result is None:
+            try:
+                self.value = self.stages.send(self.value)
+            except StopIteration as end:
+                self.value, self.result = None, end.value
+
+    def finish(self):
+        while self.result is None:
+            self.go()
+        return self.result
 
 
 def solution(mesh):
     n_rows, n_cols = mesh.shape["prow"], mesh.shape["pcol"]
     return jax.shard_map(
-        functools.partial(local, n_rows=n_rows, n_cols=n_cols, parts=8),
+        functools.partial(local, n_rows=n_rows, n_cols=n_cols, groups=4),
         mesh=mesh,
         in_specs=(P("prow", "pcol"), P(), P(), P()),
         out_specs=P("prow", "pcol"),

time: 168 us -> 175 us (1.042)
  blocking collectives: 0 us -> 79.9 us
  starting transfers between devices: 90.4 us -> 32 us
  waiting for transfers between devices: 27.3 us -> 14 us
  local copies, waits for them, and re-layouts: 13.8 us -> 8.87 us
  other arithmetic: 7.25 us -> 9.91 us
    all_gather x0 -> x4, blocking collectives: none -> 79.9 us  [gather(): lax.all_gather(piece, 'pcol', axis=0, tiled=True, axis_index_groups=lanes)]
    ppermute x36 -> x26, starting transfers between devices: 90.4 us -> 32 us  [the longest x12 11.9 us: scatter(): came = lax.ppermute(pieces[z], 'pcol', [(0, 2 * z), (1, 2 * z + 1)])]
    ppermute x36 -> x26, waiting for transfers between devices: 27.3 us -> 14 us  [the longest x12 14 us: scatter(): came = lax.ppermute(pieces[z], 'pcol', [(0, 2 * z), (1, 2 * z + 1)])]
    unnamed x120 -> x46, local copies, waits for them, and re-layouts: 9.3 us -> 4.55 us
    select_n x14 -> x11, other arithmetic: 5.91 us -> 8.66 us  [the longest x4 3.62 us: local(): jnp.where(col == 0, panel_rows((2 * g + 1) * half_rows, half_rows), fed)]
    slice x1 -> x5, local copies, waits for them, and re-layouts: 3.84 us -> 4.31 us  [the longest x1 2.71 us: panel_rows(): return lax.slice(matrix, (start, 0), (start + size, nb))]
  transfers between devices with their start and end apart: 36 -> 26, of which waited for: 13 -> 2; matrix products, arithmetic and copies ran while one was open for 4% -> 5% of each run, Pallas kernels for 9% -> 9%
where the time goes in v4:
time: 175 us; the launch traced here: 172 us
  blocking collectives  79.9 us (46%)
  starting transfers between devices  32 us (18%)
  Pallas kernels  26.4 us (15%)
  waiting for transfers between devices  14 us (8%)
  other arithmetic  9.91 us (6%)
  local copies, waits for them, and re-layouts  8.87 us (5%)
    all_gather x4, blocking collectives, gather(): lax.all_gather(piece, 'pcol', axis=0, tiled=True, axis_index_groups=lanes)  79.9 us
    ppermute x12, waiting for transfers between devices, scatter(): came = lax.ppermute(pieces[z], 'pcol', [(0, 2 * z), (1, 2 * z + 1)])  14 us
    ppermute x12, starting transfers between devices, scatter(): came = lax.ppermute(pieces[z], 'pcol', [(0, 2 * z), (1, 2 * z + 1)])  11.9 us
    ppermute x4, starting transfers between devices, local(): other.append(lax.ppermute(line, 'pcol', across))  11 us
    pallas_call x1, Pallas kernels, local(): call(functools.partial(final_kernel, n_bufs=len(bufs), n_tops=len(tops),...  10.6 us
    pallas_call x1, Pallas kernels, exchange(): call(factor_kernel, (slot, slot), [SMEM, VMEM, VMEM, VMEM], (VMEM, VMEM),...  5.89 us
    unnamed x46, local copies, waits for them, and re-layouts  4.55 us
    pallas_call x2, Pallas kernels, exchange(): call(functools.partial(merge_kernel, log=log, halves=log > 0), (slot, hal...  4.24 us
  transfers between devices with their start and end apart: 26, of which 2 were waited for; matrix products, arithmetic and copies ran while one was open for 5% of the time, Pallas kernels for 9%

profile of v4, /device:TPU:10, one launch (start us, length us, event | category | flops | bytes accessed | tf_op | source)
XLA Modules:
  0.0 171.9 jit_solution(9915390338536542457)
XLA Ops:
  0.0 2.7 %fusion.2 = (f32[256,512]{1,0:T(8,128)}, f32[256,512]{1,0:T(8,128)}, f32[256,512]{1,0:T(8,128)}, f32[256,512]{1,0:T(8,128)S(1)}) fusion(f32[2048,640]{1,0:T(8,128)} %matrix_ref.5), kind=kLoop, calls=%fused_computation.16 | loop fusion | bytes 4194304 | tf_op jit(solution)/shard_map/slice | solution.py:299
  3.5 1.6 shard_map.46
  5.2 2.6 %copy-done = f32[2048,640]{1,0:T(8,128)S(1)} copy-done((f32[2048,640]{1,0:T(8,128)S(1)}, f32[2048,640]{1,0:T(8,128)}, u32[]{:S(2)}) %copy-start) | copy-done | bytes 5242904
  7.7 3.5 %shard_map.47.held_ref = f32[512,640]{1,0:T(8,128)S(1)} custom-call(s32[8,512]{1,0:T(8,128)S(1)} %get-tuple-element.41.table_ref, f32[2048,640]{1,0:T(8,128)S(1)} %copy-done), custom_call_target="tpu_custom_call" | custom-call | tf_op jit(solution)/shard_map/pallas_call | solution.py:318
  12.5 1.5 collective-permute-start.1
  14.7 1.3 collective-permute-start.4
  16.0 1.3 collective-permute-start.3
  17.3 1.3 collective-permute-start.2
  18.6 11.9 %collective-permute-done.4 = f32[64,512]{1,0:T(8,128)S(1)} collective-permute-done((f32[64,512]{1,0:T(8,128)}, f32[64,512]{1,0:T(8,128)S(1)}, u32[]{:S(2)}, u32[]{:S(2)}) %collective-permute-start.4) | collective-permute-done | bytes 131104 | tf_op jit(solution)/shard_map/ppermute | solution.py:305
  30.7 1.3 slice_select_fusion.2
  32.7 1.7 %shard_map.48 = (f32[512,640]{1,0:T(8,128)S(1)}, f32[256,640]{1,0:T(8,128)S(1)}) custom-call(s32[2]{0:T(128)S(1)} %pad_add_fusion.where_ref, s32[512,128]{1,0:T(8,128)S(1)} %get-tuple-element.50.owner_ref, f32[512,640]{1,0:T(8,128)S(1)} %shard_map.47.held_ref, f32[512,640]{1,0:T(8,128)} %collective-permute-done.5.refs_0_), custom_call_target="tpu_custom_call" | custom-call | tf_op jit(solution)/shard_map/pallas_call | solution.py:336
  35.1 1.3 collective-permute-start.9
  37.9 27.1 %all_gather.12.near_ref.refs_0_ = f32[256,512]{1,0:T(8,128)S(1)} all-gather(f32[64,512]{1,0:T(8,128)S(1)} %select_select_fusion.2), channel_id=1, replica_groups={{0,2,4,6},{1,3,5,7},{8,10,12,14},{9,11,13,15},{16,18,20,22},{17,19,21,2..., dimensions={0}, use_global_device_ids=true | all-gather | bytes 655360 | tf_op jit(solution)/shard_map/all_gather | solution.py:310
  66.9 1.9 %collective-permute-start.15 = (f32[256,512]{1,0:T(8,128)S(1)}, f32[256,512]{1,0:T(8,128)S(1)}, u32[]{:S(2)}, u32[]{:S(2)}) collective-permute-start(f32[256,512]{1,0:T(8,128)S(1)} %all_gather.12.near_ref.refs_0_), channel_id=1, source_target_pairs={{0,1},{2,3},{3,2},{4,5},{5,4},{6,7},{7,6},{8,9},{10,11},{11,10},{1... | collective-permute-start | bytes 1572872 | tf_op jit(solution)/shard_map/ppermute | solution.py:387
  68.9 1.3 collective-permute-start.14
  71.5 19.9 %all_gather.13.refs_2_ = f32[256,512]{1,0:T(8,128)} all-gather(f32[64,512]{1,0:T(8,128)S(1)} %select_select_fusion.1), channel_id=1, replica_groups={{0,2,4,6},{1,3,5,7},{8,10,12,14},{9,11,13,15},{16,18,20,22},{17,19,21,2..., dimensions={0}, use_global_device_ids=true | all-gather | bytes 655360 | tf_op jit(solution)/shard_map/all_gather | solution.py:310
  93.0 1.6 collective-permute-start.21
  95.5 1.3 collective-permute-start.18
  96.8 3.7 %collective-permute-start.19 = (f32[256,512]{1,0:T(8,128)}, f32[256,512]{1,0:T(8,128)S(1)}, u32[]{:S(2)}, u32[]{:S(2)}) collective-permute-start(f32[256,512]{1,0:T(8,128)} %all_gather.13.refs_2_), channel_id=1, source_target_pairs={{0,1},{2,3},{3,2},{4,5},{5,4},{6,7},{7,6},{8,9},{10,11},{11,10},{1... | collective-permute-start | bytes 1572872 | tf_op jit(solution)/shard_map/ppermute | solution.py:387
  101.2 2.0 %collective-permute-done.18 = f32[64,512]{1,0:T(8,128)S(1)} collective-permute-done((f32[64,512]{1,0:T(8,128)S(1)}, f32[64,512]{1,0:T(8,128)S(1)}, u32[]{:S(2)}, u32[]{:S(2)}) %collective-permute-start.18) | collective-permute-done | bytes 131104 | tf_op jit(solution)/shard_map/ppermute | solution.py:305
  104.5 17.3 %all_gather.14.refs_4_ = f32[256,512]{1,0:T(8,128)S(1)} all-gather(f32[64,512]{1,0:T(8,128)} %select_select_fusion), channel_id=1, replica_groups={{0,2,4,6},{1,3,5,7},{8,10,12,14},{9,11,13,15},{16,18,20,22},{17,19,21,2..., dimensions={0}, use_global_device_ids=true | all-gather | bytes 655360 | tf_op jit(solution)/shard_map/all_gather | solution.py:310
  121.9 1.7 fusion.1
  123.6 2.0 %collective-permute-start.22 = (f32[256,512]{1,0:T(8,128)S(1)}, f32[256,512]{1,0:T(8,128)}, u32[]{:S(2)}, u32[]{:S(2)}) collective-permute-start(f32[256,512]{1,0:T(8,128)S(1)} %all_gather.14.refs_4_), channel_id=1, source_target_pairs={{0,1},{2,3},{3,2},{4,5},{5,4},{6,7},{7,6},{8,9},{10,11},{11,10},{1... | collective-permute-start | bytes 1572872 | tf_op jit(solution)/shard_map/ppermute | solution.py:387
  125.6 1.4 broadcast_select_fusion
  127.9 1.3 collective-permute-start.23
  129.2 15.5 %all_gather.15.refs_6_ = f32[256,512]{1,0:T(8,128)S(1)} all-gather(f32[64,512]{1,0:T(8,128)} %fusion.1), channel_id=1, replica_groups={{0,2,4,6},{1,3,5,7},{8,10,12,14},{9,11,13,15},{16,18,20,22},{17,19,21,2..., dimensions={0}, use_global_device_ids=true | all-gather | bytes 655360 | tf_op jit(solution)/shard_map/all_gather | solution.py:310
  144.8 1.2 broadcast_select_fusion.2
  146.0 3.4 %collective-permute-start.24 = (f32[256,512]{1,0:T(8,128)S(1)}, f32[256,512]{1,0:T(8,128)S(1)}, u32[]{:S(2)}, u32[]{:S(2)}) collective-permute-start(f32[256,512]{1,0:T(8,128)S(1)} %all_gather.15.refs_6_), channel_id=1, source_target_pairs={{0,1},{2,3},{3,2},{4,5},{5,4},{6,7},{7,6},{8,9},{10,11},{11,10},{1... | collective-permute-start | bytes 1572872 | tf_op jit(solution)/shard_map/ppermute | solution.py:387
  149.4 1.9 %collective-permute-start.25 = (f32[256,512]{1,0:T(8,128)}, f32[256,512]{1,0:T(8,128)S(1)}, u32[]{:S(2)}, u32[]{:S(2)}) collective-permute-start(f32[256,512]{1,0:T(8,128)} %collective-permute-done.23.refs_9_), channel_id=1, source_target_pairs={{16,24},{24,16},{17,25},{25,17},{18,26},{26,18},{19,27},{27,19},{2... | collective-permute-start | bytes 1572872 | tf_op jit(solution)/shard_map/ppermute | solution.py:368
  152.7 2.5 %shard_map.50 = (f32[512,640]{1,0:T(8,128)S(1)}, f32[256,640]{1,0:T(8,128)}) custom-call(s32[2]{0:T(128)S(1)} %copy-done.11, s32[512,128]{1,0:T(8,128)S(1)} %copy-done.6, f32[512,640]{1,0:T(8,128)S(1)} %copy-done.4, f32[256,640]{1,0:T(8,128)S(1)} %collective-permute-done.10.refs_0_, f32[256,640]{1,0:T(8,128)} %collective-permute-done.20.refs_1_), custom_call_target="tpu_custom_call" | custom-call | tf_op jit(solution)/shard_map/pallas_call | solution.py:336
  155.2 5.9 %shard_map.51 = (f32[512,640]{1,0:T(8,128)S(1)}, f32[512,640]{1,0:T(8,128)S(1)}) custom-call(s32[2]{0:T(128)S(1)} %copy-done.11, f32[512,640]{1,0:T(8,128)S(1)} %get-tuple-element.67.top_in_ref, f32[512,512]{1,0:T(8,128)S(1)} %copy-done.13, f32[512,512]{1,0:T(8,128)S(1)} %copy-done.14), custom_call_target="tpu_custom_call" | custom-call | flops 4026531840 | tf_op jit(solution)/shard_map/pallas_call | solution.py:342
  161.2 10.6 %shard_map.52 = f32[2048,640]{1,0:T(8,128)} custom-call(s32[2]{0:T(128)S(1)} %copy-done.11, s32[8,512]{1,0:T(8,128)S(1)} %get-tuple-element.41.table_ref, f32[512,640]{1,0:T(8,128)S(1)} %maximum_select_fusion.displaced_ref, f32[512,640]{1,0:T(8,128)S(1)} %get-tuple-element.68.weights_ref, f32[512,640]{1,0:T(8,128)S(1)} %get-tuple-element.69.top_ref, ...), custom_call_target="tpu_custom_call" | custom-call | flops 4026531840 | bytes 14680064 | tf_op jit(solution)/shard_map/pallas_call | solution.py:407
  (97 shorter events, 15.5 us)
Async XLA Ops:
  2.7 8.6 %collective-permute-start = (f32[256,512]{1,0:T(8,128)S(1)}, f32[256,512]{1,0:T(8,128)S(1)}, u32[]{:S(2)}, u32[]{:S(2)}) collective-permute-start(f32[256,512]{1,0:T(8,128)S(1)} %get-tuple-element.80), channel_id=1, source_target_pairs={{0,1},{8,9},{16,17},{24,25}} | collective-permute-start | bytes 1572872 | tf_op jit(solution)/shard_map/ppermute | solution.py:376
  3.5 29.2 %copy-start.9 = (s32[2]{0:T(128)}, s32[2]{0:T(128)S(1)}, u32[]{:S(2)}) copy-start(s32[2]{0:T(128)S(1)} %pad_add_fusion.where_ref) | copy-start | bytes 28
  5.1 27.5 %copy-start.5 = (s32[512,128]{1,0:T(8,128)}, s32[512,128]{1,0:T(8,128)S(1)}, u32[]{:S(2)}) copy-start(s32[512,128]{1,0:T(8,128)S(1)} %get-tuple-element.50.owner_ref) | copy-start | bytes 786436
  11.3 19.4 %collective-permute-start.5 = (f32[512,640]{1,0:T(8,128)S(1)}, f32[512,640]{1,0:T(8,128)}, u32[]{:S(2)}, u32[]{:S(2)}) collective-permute-start(f32[512,640]{1,0:T(8,128)S(1)} %shard_map.47.held_ref), channel_id=1, source_target_pairs={{0,8},{8,0},{16,24},{24,16},{1,9},{9,1},{17,25},{25,17},{2,10},{10... | collective-permute-start | bytes 3932168 | tf_op jit(solution)/shard_map/ppermute | solution.py:327
  12.5 18.2 %collective-permute-start.1 = (f32[256,512]{1,0:T(8,128)}, f32[256,512]{1,0:T(8,128)}, u32[]{:S(2)}, u32[]{:S(2)}) collective-permute-start(f32[256,512]{1,0:T(8,128)} %get-tuple-element.43), channel_id=1, source_target_pairs={{0,1},{8,9},{16,17},{24,25}} | collective-permute-start | bytes 1572872 | tf_op jit(solution)/shard_map/ppermute | solution.py:397
  14.0 78.3 %slice-start = ((s8[5242880]{0:T(1024)(128)(4,1)}), s8[1048576]{0:T(1024)(128)(4,1)S(1)}, s32[]{:S(2)}) async-start(s8[5242880]{0:T(1024)(128)(4,1)} %bitcast.3), calls=%async_computation | async-start | bytes 2097152
  14.7 15.8 %collective-permute-start.4 = (f32[64,512]{1,0:T(8,128)}, f32[64,512]{1,0:T(8,128)S(1)}, u32[]{:S(2)}, u32[]{:S(2)}) collective-permute-start(f32[64,512]{1,0:T(8,128)} %get-tuple-element.92), channel_id=1, source_target_pairs={{0,2},{1,3},{8,10},{9,11},{16,18},{17,19},{24,26},{25,27}} | collective-permute-start | bytes 393224 | tf_op jit(solution)/shard_map/ppermute | solution.py:305
  16.0 14.6 %collective-permute-start.3 = (f32[64,512]{1,0:T(8,128)}, f32[64,512]{1,0:T(8,128)}, u32[]{:S(2)}, u32[]{:S(2)}) collective-permute-start(f32[64,512]{1,0:T(8,128)} %get-tuple-element.93), channel_id=1, source_target_pairs={{0,4},{1,5},{8,12},{9,13},{16,20},{17,21},{24,28},{25,29}} | collective-permute-start | bytes 393224 | tf_op jit(solution)/shard_map/ppermute | solution.py:305
  17.3 13.3 %collective-permute-start.2 = (f32[64,512]{1,0:T(8,128)S(1)}, f32[64,512]{1,0:T(8,128)}, u32[]{:S(2)}, u32[]{:S(2)}) collective-permute-start(f32[64,512]{1,0:T(8,128)S(1)} %get-tuple-element.94), channel_id=1, source_target_pairs={{0,6},{1,7},{8,14},{9,15},{16,22},{17,23},{24,30},{25,31}} | collective-permute-start | bytes 393224 | tf_op jit(solution)/shard_map/ppermute | solution.py:305
  32.0 33.1 %collective-permute-start.6 = (f32[256,512]{1,0:T(8,128)S(1)}, f32[256,512]{1,0:T(8,128)S(1)}, u32[]{:S(2)}, u32[]{:S(2)}) collective-permute-start(f32[256,512]{1,0:T(8,128)S(1)} %copy-done.17), channel_id=1, source_target_pairs={{0,1},{8,9},{16,17},{24,25}} | collective-permute-start | bytes 1572872 | tf_op jit(solution)/shard_map/ppermute | solution.py:397
  32.7 59.6 %slice-start.1 = ((s8[5242880]{0:T(1024)(128)(4,1)}), s8[4194304]{0:T(1024)(128)(4,1)S(1)}, s32[]{:S(2)}) async-start(s8[5242880]{0:T(1024)(128)(4,1)} %bitcast.3), calls=%async_computation.1 | async-start | bytes 8388608
  34.4 31.7 %copy-start.3 = (f32[512,640]{1,0:T(8,128)}, f32[512,640]{1,0:T(8,128)S(1)}, u32[]{:S(2)}) copy-start(f32[512,640]{1,0:T(8,128)S(1)} %get-tuple-element.66.held_ref) | copy-start | bytes 3932164
  34.4 30.6 %collective-permute-start.10 = (f32[256,640]{1,0:T(8,128)S(1)}, f32[256,640]{1,0:T(8,128)S(1)}, u32[]{:S(2)}, u32[]{:S(2)}) collective-permute-start(f32[256,640]{1,0:T(8,128)S(1)} %get-tuple-element.52), channel_id=1, source_target_pairs={{0,16},{8,24},{16,0},{24,8},{1,17},{9,25},{17,1},{25,9},{2,18},{10... | collective-permute-start | bytes 1966088 | tf_op jit(solution)/shard_map/ppermute | solution.py:331
  35.1 29.9 %collective-permute-start.9 = (f32[64,512]{1,0:T(8,128)S(1)}, f32[64,512]{1,0:T(8,128)S(1)}, u32[]{:S(2)}, u32[]{:S(2)}) collective-permute-start(f32[64,512]{1,0:T(8,128)S(1)} %get-tuple-element.89), channel_id=1, source_target_pairs={{0,2},{1,3},{8,10},{9,11},{16,18},{17,19},{24,26},{25,27}} | collective-permute-start | bytes 393224 | tf_op jit(solution)/shard_map/ppermute | solution.py:305
  36.4 28.6 %collective-permute-start.8 = (f32[64,512]{1,0:T(8,128)S(1)}, f32[64,512]{1,0:T(8,128)S(1)}, u32[]{:S(2)}, u32[]{:S(2)}) collective-permute-start(f32[64,512]{1,0:T(8,128)S(1)} %get-tuple-element.90), channel_id=1, source_target_pairs={{0,4},{1,5},{8,12},{9,13},{16,20},{17,21},{24,28},{25,29}} | collective-permute-start | bytes 393224 | tf_op jit(solution)/shard_map/ppermute | solution.py:305
  37.1 29.1 %copy-start.16 = (f32[256,512]{1,0:T(8,128)S(1)}, f32[256,512]{1,0:T(8,128)}, u32[]{:S(2)}) copy-start(f32[256,512]{1,0:T(8,128)} %get-tuple-element.54) | copy-start | bytes 1572868
  37.1 27.9 %collective-permute-start.7 = (f32[64,512]{1,0:T(8,128)S(1)}, f32[64,512]{1,0:T(8,128)S(1)}, u32[]{:S(2)}, u32[]{:S(2)}) collective-permute-start(f32[64,512]{1,0:T(8,128)S(1)} %get-tuple-element.91), channel_id=1, source_target_pairs={{0,6},{1,7},{8,14},{9,15},{16,22},{17,23},{24,30},{25,31}} | collective-permute-start | bytes 393224 | tf_op jit(solution)/shard_map/ppermute | solution.py:305
  66.2 25.9 %collective-permute-start.11 = (f32[256,512]{1,0:T(8,128)S(1)}, f32[256,512]{1,0:T(8,128)S(1)}, u32[]{:S(2)}, u32[]{:S(2)}) collective-permute-start(f32[256,512]{1,0:T(8,128)S(1)} %copy-done.16), channel_id=1, source_target_pairs={{0,1},{8,9},{16,17},{24,25}} | collective-permute-start | bytes 1572872 | tf_op jit(solution)/shard_map/ppermute | solution.py:397
  66.9 25.2 %collective-permute-start.15 = (f32[256,512]{1,0:T(8,128)S(1)}, f32[256,512]{1,0:T(8,128)S(1)}, u32[]{:S(2)}, u32[]{:S(2)}) collective-permute-start(f32[256,512]{1,0:T(8,128)S(1)} %all_gather.12.near_ref.refs_0_), channel_id=1, source_target_pairs={{0,1},{2,3},{3,2},{4,5},{5,4},{6,7},{7,6},{8,9},{10,11},{11,10},{1... | collective-permute-start | bytes 1572872 | tf_op jit(solution)/shard_map/ppermute | solution.py:387
  68.9 22.6 %collective-permute-start.14 = (f32[64,512]{1,0:T(8,128)S(1)}, f32[64,512]{1,0:T(8,128)S(1)}, u32[]{:S(2)}, u32[]{:S(2)}) collective-permute-start(f32[64,512]{1,0:T(8,128)S(1)} %get-tuple-element.86), channel_id=1, source_target_pairs={{0,2},{1,3},{8,10},{9,11},{16,18},{17,19},{24,26},{25,27}} | collective-permute-start | bytes 393224 | tf_op jit(solution)/shard_map/ppermute | solution.py:305
  70.2 21.3 %collective-permute-start.13 = (f32[64,512]{1,0:T(8,128)S(1)}, f32[64,512]{1,0:T(8,128)S(1)}, u32[]{:S(2)}, u32[]{:S(2)}) collective-permute-start(f32[64,512]{1,0:T(8,128)S(1)} %get-tuple-element.87), channel_id=1, source_target_pairs={{0,4},{1,5},{8,12},{9,13},{16,20},{17,21},{24,28},{25,29}} | collective-permute-start | bytes 393224 | tf_op jit(solution)/shard_map/ppermute | solution.py:305
  70.8 20.6 %collective-permute-start.12 = (f32[64,512]{1,0:T(8,128)S(1)}, f32[64,512]{1,0:T(8,128)S(1)}, u32[]{:S(2)}, u32[]{:S(2)}) collective-permute-start(f32[64,512]{1,0:T(8,128)S(1)} %get-tuple-element.88), channel_id=1, source_target_pairs={{0,6},{1,7},{8,14},{9,15},{16,22},{17,23},{24,30},{25,31}} | collective-permute-start | bytes 393224 | tf_op jit(solution)/shard_map/ppermute | solution.py:305
  92.2 31.4 %collective-permute-start.20 = (f32[256,640]{1,0:T(8,128)S(1)}, f32[256,640]{1,0:T(8,128)}, u32[]{:S(2)}, u32[]{:S(2)}) collective-permute-start(f32[256,640]{1,0:T(8,128)S(1)} %collective-permute-done.10.refs_0_), channel_id=1, source_target_pairs={{0,8},{8,0},{16,24},{24,16},{1,9},{9,1},{17,25},{25,17},{2,10},{10... | collective-permute-start | bytes 1966088 | tf_op jit(solution)/shard_map/ppermute | solution.py:333
  93.0 30.6 %collective-permute-start.21 = (f32[512,512]{1,0:T(8,128)}, f32[512,512]{1,0:T(8,128)}, u32[]{:S(2)}, u32[]{:S(2)}) collective-permute-start(f32[512,512]{1,0:T(8,128)} %shard_map.49), channel_id=1, source_target_pairs={{0,8},{1,9},{2,10},{3,11},{4,12},{5,13},{6,14},{7,15}} | collective-permute-start | bytes 3145736 | tf_op jit(solution)/shard_map/ppermute | solution.py:363
  95.5 7.7 %collective-permute-start.18 = (f32[64,512]{1,0:T(8,128)S(1)}, f32[64,512]{1,0:T(8,128)S(1)}, u32[]{:S(2)}, u32[]{:S(2)}) collective-permute-start(f32[64,512]{1,0:T(8,128)S(1)} %get-tuple-element.83), channel_id=1, source_target_pairs={{0,2},{1,3},{8,10},{9,11},{16,18},{17,19},{24,26},{25,27}} | collective-permute-start | bytes 393224 | tf_op jit(solution)/shard_map/ppermute | solution.py:305
  96.8 26.7 %collective-permute-start.19 = (f32[256,512]{1,0:T(8,128)}, f32[256,512]{1,0:T(8,128)S(1)}, u32[]{:S(2)}, u32[]{:S(2)}) collective-permute-start(f32[256,512]{1,0:T(8,128)} %all_gather.13.refs_2_), channel_id=1, source_target_pairs={{0,1},{2,3},{3,2},{4,5},{5,4},{6,7},{7,6},{8,9},{10,11},{11,10},{1... | collective-permute-start | bytes 1572872 | tf_op jit(solution)/shard_map/ppermute | solution.py:387
  100.5 21.4 %collective-permute-start.17 = (f32[64,512]{1,0:T(8,128)}, f32[64,512]{1,0:T(8,128)S(1)}, u32[]{:S(2)}, u32[]{:S(2)}) collective-permute-start(f32[64,512]{1,0:T(8,128)} %get-tuple-element.84), channel_id=1, source_target_pairs={{0,4},{1,5},{8,12},{9,13},{16,20},{17,21},{24,28},{25,29}} | collective-permute-start | bytes 393224 | tf_op jit(solution)/shard_map/ppermute | solution.py:305
  103.9 18.0 %collective-permute-start.16 = (f32[64,512]{1,0:T(8,128)}, f32[64,512]{1,0:T(8,128)S(1)}, u32[]{:S(2)}, u32[]{:S(2)}) collective-permute-start(f32[64,512]{1,0:T(8,128)} %get-tuple-element.85), channel_id=1, source_target_pairs={{0,6},{1,7},{8,14},{9,15},{16,22},{17,23},{24,30},{25,31}} | collective-permute-start | bytes 393224 | tf_op jit(solution)/shard_map/ppermute | solution.py:305
  123.6 22.4 %collective-permute-start.22 = (f32[256,512]{1,0:T(8,128)S(1)}, f32[256,512]{1,0:T(8,128)}, u32[]{:S(2)}, u32[]{:S(2)}) collective-permute-start(f32[256,512]{1,0:T(8,128)S(1)} %all_gather.14.refs_4_), channel_id=1, source_target_pairs={{0,1},{2,3},{3,2},{4,5},{5,4},{6,7},{7,6},{8,9},{10,11},{11,10},{1... | collective-permute-start | bytes 1572872 | tf_op jit(solution)/shard_map/ppermute | solution.py:387
  127.9 18.0 %collective-permute-start.23 = (f32[256,512]{1,0:T(8,128)}, f32[256,512]{1,0:T(8,128)}, u32[]{:S(2)}, u32[]{:S(2)}) collective-permute-start(f32[256,512]{1,0:T(8,128)} %slice_select_fusion), channel_id=1, source_target_pairs={{0,16},{8,24},{1,17},{9,25},{2,18},{10,26},{3,19},{11,27},{4,20},{... | collective-permute-start | bytes 1572872 | tf_op jit(solution)/shard_map/ppermute | solution.py:367
  146.0 15.2 %collective-permute-start.24 = (f32[256,512]{1,0:T(8,128)S(1)}, f32[256,512]{1,0:T(8,128)S(1)}, u32[]{:S(2)}, u32[]{:S(2)}) collective-permute-start(f32[256,512]{1,0:T(8,128)S(1)} %all_gather.15.refs_6_), channel_id=1, source_target_pairs={{0,1},{2,3},{3,2},{4,5},{5,4},{6,7},{7,6},{8,9},{10,11},{11,10},{1... | collective-permute-start | bytes 1572872 | tf_op jit(solution)/shard_map/ppermute | solution.py:387
  149.4 11.8 %collective-permute-start.25 = (f32[256,512]{1,0:T(8,128)}, f32[256,512]{1,0:T(8,128)S(1)}, u32[]{:S(2)}, u32[]{:S(2)}) collective-permute-start(f32[256,512]{1,0:T(8,128)} %collective-permute-done.23.refs_9_), channel_id=1, source_target_pairs={{16,24},{24,16},{17,25},{25,17},{18,26},{26,18},{19,27},{27,19},{2... | collective-permute-start | bytes 1572872 | tf_op jit(solution)/shard_map/ppermute | solution.py:368
  (17 other events, 84.2 us)

commit v5 on v3

--- a/solution.py
+++ b/solution.py
@@ -12,7 +12,8 @@
 SMEM = pl.BlockSpec(memory_space=pltpu.SMEM)
 ANY = pl.BlockSpec(memory_space=pl.ANY)
 LANES = 128
-PICK, FROM, ROW, COUNT, TOP = 0, 1, 2, 3, 4
+PICK, FROM, ROW, BOUND, TOP = 0, 1, 2, 3, 4
+BLOCK = 256
 
 
 def call(kernel, out, ins, outs, scratch=(), vmem=16 << 20, flops=0, moved=0):
@@ -78,15 +79,14 @@
         jnp.where(placed, piv_col - start_f, 0.0), axis=0, keepdims=True
     )
     listed_top = jnp.sum(jnp.where(placed, source_col, 0.0), axis=0, keepdims=True)
-    count = jnp.sum(moved_row, axis=1, keepdims=True)
+    early = moved_col & (piv_col - start_f < (across.astype(jnp.float32) + 1.0) * BLOCK)
+    bound = jnp.sum(jnp.where(early, 1.0, 0.0), axis=0, keepdims=True)
     table_ref[...] = jnp.zeros_like(table_ref)
     table_ref[PICK : PICK + 1, :] = pick
     table_ref[FROM : FROM + 1, :] = listed_from.astype(jnp.int32)
     table_ref[ROW : ROW + 1, :] = listed_row.astype(jnp.int32)
     table_ref[TOP : TOP + 1, :] = listed_top.astype(jnp.int32)
-    table_ref[COUNT : COUNT + 1, :] = jnp.broadcast_to(
-        count.astype(jnp.int32), (1, nb)
-    )
+    table_ref[BOUND : BOUND + 1, :] = bound.astype(jnp.int32)
     owner_ref[...] = piv_col[:, :LANES].astype(jnp.int32) // row_dev
 
 
@@ -138,86 +138,112 @@
         half_ref[...] = merged_ref[high, :]
 
 
-def factor_kernel(where_ref, top_in_ref, lower_ref, upper_ref, weights_ref, top_ref):
-    nb, cols = top_in_ref.shape
-    u = jnp.dot(
-        lower_ref[...], top_in_ref[...], precision=HIGHEST,
-        preferred_element_type=jnp.float32,
-    )
+def split(x):
+    hi = x.astype(jnp.bfloat16)
+    return hi, (x - hi.astype(jnp.float32)).astype(jnp.bfloat16)
+
+
+def product(a, b):
+    dot = functools.partial(jnp.dot, preferred_element_type=jnp.float32)
+    return dot(a[1], b[0]) + dot(a[0], b[1]) + dot(a[0], b[0])
+
+
+def factor_kernel(
+    where_ref, owner_ref, held_ref, one_ref, two_ref, before_ref, lower_ref, upper_ref,
+    weights_ref, top_ref, displaced_ref, new_top, *, log,
+):
+    me = where_ref[0]
+    mine, theirs = me >> log, (me >> log) ^ 1
+    nb, cols = held_ref.shape
+    half = nb // 2
+
+    def merge(rows, piece):
+        group = owner_ref[rows, :] >> log
+        take = (group == theirs) | ((theirs == 0) & (group != mine))
+        for q in range(cols // LANES):
+            lane = slice(q * LANES, (q + 1) * LANES)
+            new_top[rows, lane] = jnp.where(take, piece[:, lane], held_ref[rows, lane])
+
+        @pl.when(mine == 1)
+        def _():
+            displaced_ref[rows, :] = piece[...]
+
+    @pl.when(mine != 1)
+    def _():
+        displaced_ref[...] = before_ref[...]
+
+    for odd, (first, second) in enumerate([(one_ref, two_ref), (two_ref, one_ref)]):
+        @pl.when((me & 1) == odd)
+        def _():
+            merge(slice(0, half), first)
+            merge(slice(half, nb), second)
+
+    u = product(split(lower_ref[...]), split(new_top[...]))
     top_ref[...] = u
-    weights_ref[...] = jnp.dot(
-        upper_ref[...], u, precision=HIGHEST, preferred_element_type=jnp.float32
-    )
+    weights_ref[...] = product(split(upper_ref[...]), split(u))
 
     @pl.when(where_ref[1] == 0)
     def _():
-        top_ref[:, :nb] = top_in_ref[:, :nb]
+        top_ref[:, :nb] = new_top[:, :nb]
         weights_ref[:, :nb] = -upper_ref[...]
 
 
-def fetch(choice_ref, bufs, place, sem, n_cols, parts, pairs):
-    for i in range(pairs):
-        for h in range(2):
-            for b in sorted({arrival(p, i, h, n_cols, parts) for p in range(1, n_cols)}):
-                @pl.when(choice_ref[2 * i + h] == b)
-                def _():
-                    pltpu.make_async_copy(bufs[b], place(i, h), sem).start()
-
-
-def old_top_kernel(where_ref, choice_ref, matrix_ref, *refs, used, n_cols, parts, pairs):
+def chunk_span(k, rows, chunk):
+    start = k * chunk
+    size = min(chunk, rows - start)
+    return start, size, chunk - size
+
+
+def fetch(where_ref, choice_ref, matrix_ref, bufs, out_ref, sem_of, n_cols, parts, chunk):
+    rows, nb = out_ref.shape
+    for k in range(-(-rows // chunk)):
+        start, size, skip = chunk_span(k, matrix_ref.shape[0], chunk)
+        size = min(size, rows - start)
+        to = out_ref.at[pl.ds(start, size), :]
+
+        @pl.when(where_ref[1] == 0)
+        def _():
+            pltpu.make_async_copy(
+                matrix_ref.at[pl.ds(start, size), pl.ds(0, nb)], to, sem_of(k)
+            ).start()
+
+        for b in sorted({arrival(p, k // 2, k % 2, n_cols, parts) for p in range(1, n_cols)}):
+            @pl.when((where_ref[1] > 0) & (choice_ref[k] == b))
+            def _():
+                pltpu.make_async_copy(
+                    bufs[b].at[pl.ds(skip, size), :], to, sem_of(k)
+                ).start()
+
+
+def old_top_kernel(where_ref, choice_ref, matrix_ref, *refs, used, n_cols, parts, chunk):
     bufs, top_ref, sem = dict(zip(used, refs)), refs[-2], refs[-1]
     nb = top_ref.shape[0]
-    chunk = nb // (2 * pairs)
-    from_matrix = pltpu.make_async_copy(
-        matrix_ref.at[pl.ds(0, nb), pl.ds(0, nb)], top_ref, sem
-    )
 
     @pl.when(where_ref[0] == 0)
     def _():
-        @pl.when(where_ref[1] == 0)
-        def _():
-            from_matrix.start()
-
-        @pl.when(where_ref[1] > 0)
-        def _():
-            fetch(
-                choice_ref, bufs,
-                lambda i, h: top_ref.at[pl.ds((2 * i + h) * chunk, chunk), :],
-                sem, n_cols, parts, pairs,
-            )
-
-        from_matrix.wait()
+        fetch(
+            where_ref, choice_ref, matrix_ref, bufs, top_ref, lambda k: sem,
+            n_cols, parts, chunk,
+        )
+        pltpu.make_async_copy(
+            matrix_ref.at[pl.ds(0, nb), pl.ds(0, nb)], top_ref, sem
+        ).wait()
 
 
 def final_kernel(
     where_ref, table_ref, choice_ref, displaced_ref, weights_ref, top_ref, matrix_ref,
-    *refs, n_bufs, n_tops, n_cols, parts, block,
+    *refs, n_bufs, n_tops, n_cols, parts, chunk,
 ):
     bufs, tops, out_ref = refs[:n_bufs], refs[n_bufs : n_bufs + n_tops], refs[n_bufs + n_tops]
-    mat, pan, low, w_hi, w_lo, result, in_sem, low_sem, mat_sem, out_sem = refs[
+    mat, pan, low, w_hi, w_lo, result, pan_sem, low_sem, mat_sem, out_sem = refs[
         n_bufs + n_tops + 1 :
     ]
     rows, cols = matrix_ref.shape
     nb = weights_ref.shape[0]
     half = nb // 2
-    chunk = rows // (2 * parts)
     row = where_ref[0]
     first_row, first_col = row == 0, where_ref[1] == 0
-
-    load = pltpu.make_async_copy(matrix_ref, mat, mat_sem)
-    load.start()
-    whole_panel = pltpu.make_async_copy(matrix_ref.at[:, pl.ds(0, nb)], pan, in_sem)
-
-    @pl.when(first_col)
-    def _():
-        whole_panel.start()
-
-    @pl.when(jnp.logical_not(first_col))
-    def _():
-        fetch(
-            choice_ref, bufs, lambda i, h: pan.at[pl.ds((2 * i + h) * chunk, chunk), :],
-            in_sem, n_cols, parts, parts,
-        )
+    blocks = [pl.ds(b * BLOCK, BLOCK) for b in range(rows // BLOCK)]
 
     @pl.when(row == 1)
     def _():
@@ -231,55 +257,68 @@
                     at = half * (part ^ odd)
                     pltpu.make_async_copy(ref, low.at[pl.ds(at, half), :], low_sem).start()
 
-    w = weights_ref[...]
-    w_hi[...] = w.astype(jnp.bfloat16)
-    w_lo[...] = (w - w_hi[...].astype(jnp.float32)).astype(jnp.bfloat16)
-
-    whole_panel.wait()
-    load.wait()
-    count = table_ref[COUNT, 0]
-
-    def swap(from_mat, from_pan):
+    loads = [
+        pltpu.make_async_copy(matrix_ref.at[span, :], mat.at[span, :], mat_sem.at[b])
+        for b, span in enumerate(blocks)
+    ]
+    loads[0].start()
+    fetch(
+        where_ref, choice_ref, matrix_ref, bufs, pan, lambda k: pan_sem.at[k],
+        n_cols, parts, chunk,
+    )
+    for load in loads[1:]:
+        load.start()
+
+    w_hi[...], w_lo[...] = split(weights_ref[...])
+
+    @pl.when(jnp.logical_not(first_row))
+    def _():
+        pltpu.make_async_copy(tops[0], low, low_sem).wait()
+
+    def swap(from_mat, from_pan, low_k, high_k):
         def body(k, _):
             to = table_ref[ROW, k]
             mat[pl.ds(to, 1), :] = from_mat[pl.ds(table_ref[FROM, k], 1), :]
             pan[pl.ds(to, 1), :] = from_pan[pl.ds(table_ref[TOP, k], 1), :]
             return 0
 
-        lax.fori_loop(0, count, body, 0)
-
-    @pl.when(first_row)
-    def _():
-        swap(mat, pan)
-
-    @pl.when(jnp.logical_not(first_row))
-    def _():
-        pltpu.make_async_copy(tops[0], low, low_sem).wait()
-        swap(displaced_ref, low)
-
-    @pl.when(first_col)
-    def _():
-        mat[:, :nb] = jnp.zeros((rows, nb), jnp.float32)
+        lax.fori_loop(low_k, high_k, body, 0)
 
     copies = []
-    for b in range(rows // block):
-        span = pl.ds(b * block, block)
+    ready = 0
+    for b, span in enumerate(blocks):
+        loads[b].wait()
+        while ready < 2 * parts and ready * chunk < (b + 1) * BLOCK:
+            start, size, _ = chunk_span(ready, rows, chunk)
+            to = pan.at[pl.ds(start, size), :]
+            pltpu.make_async_copy(
+                matrix_ref.at[pl.ds(start, size), pl.ds(0, nb)], to, pan_sem.at[ready]
+            ).wait()
+            ready += 1
+        low_k = table_ref[BOUND, b - 1] if b else 0
+        high_k = table_ref[BOUND, b]
+
+        @pl.when(jnp.logical_not(first_row))
+        def _():
+            swap(displaced_ref, low, low_k, high_k)
 
         def update():
-            p = pan[span, :]
-            p_hi = p.astype(jnp.bfloat16)
-            p_lo = (p - p_hi.astype(jnp.float32)).astype(jnp.bfloat16)
-            dot = functools.partial(jnp.dot, preferred_element_type=jnp.float32)
-            total = dot(p_lo, w_hi[...]) + dot(p_hi, w_lo[...]) + dot(p_hi, w_hi[...])
-            result[span, :] = mat[span, :] - total
-
-        if (b + 1) * block <= nb:
+            total = product(split(pan[span, :]), (w_hi[...], w_lo[...]))
+            kept = jnp.where(first_col, 0.0, mat[span, :nb])
+            result[span, :nb] = kept - total[:, :nb]
+            result[span, nb:] = mat[span, nb:] - total[:, nb:]
+
+        if (b + 1) * BLOCK <= nb:
             pl.when(jnp.logical_not(first_row))(update)
 
             @pl.when(first_row)
             def _():
                 result[span, :] = top_ref[span, :]
         else:
+            @pl.when(first_row)
+            def _():
+                swap(mat, pan, low_k, high_k)
+
             update()
         copy = pltpu.make_async_copy(result.at[span, :], out_ref.at[span, :], out_sem)
         copy.start()
@@ -357,10 +396,9 @@
     here = jnp.stack([row, col]).astype(jnp.int32)
     odd = row % 2 == 1
 
-    chunk = row_dev // (2 * parts)
-    flat = [
-        lax.slice(matrix, (k * chunk, 0), ((k + 1) * chunk, nb)) for k in range(2 * parts)
-    ]
+    chunk = -(-row_dev // (16 * parts)) * 8
+    firsts = [k * chunk - chunk_span(k, row_dev, chunk)[2] for k in range(2 * parts)]
+    flat = [lax.slice(matrix, (k, 0), (k + chunk, nb)) for k in firsts]
     flat = flat[:2] + list(lax.optimization_barrier(tuple(flat[2:])))
     choice = jnp.asarray(
         [
@@ -371,7 +409,7 @@
         jnp.int32,
     )[col]
 
-    pairs = nb // (2 * chunk)
+    pairs = -(-nb // (2 * chunk))
     used = sorted({
         arrival(p, i, h, n_cols, parts)
         for p in range(1, n_cols) for i in range(pairs) for h in range(2)
@@ -392,7 +430,7 @@
         arrived = yield start
         old_top = call(
             functools.partial(
-                old_top_kernel, used=used, n_cols=n_cols, parts=parts, pairs=pairs
+                old_top_kernel, used=used, n_cols=n_cols, parts=parts, chunk=chunk
             ),
             jax.ShapeDtypeStruct((nb, nb), f32),
             [SMEM, SMEM, ANY] + [ANY] * len(used), ANY, [pltpu.SemaphoreType.DMA],
@@ -444,18 +482,20 @@
                 at += 5
                 two = yield give(at, lax.ppermute(one, "prow", near))
                 arrived = [one, two]
-                whole = both_halves(one, two)
+                whole = None if 2 << log == n_rows else both_halves(one, two)
+            if 2 << log == n_rows:
+                break
             held, half = call(
                 functools.partial(merge_kernel, log=log, halves=log > 0),
                 (slot, half_slot), [SMEM] + [VMEM] * (2 + len(arrived)), (VMEM, VMEM),
             )(here, owner, held, *arrived)
-            displaced = jnp.where((row >> log) == 1, whole, displaced)
+            displaced = jnp.where((row >> log) == 1, whole, displaced) if log else whole
             log += 1
-        held, displaced = yield give(at + 1, (held, displaced))
-        weights, top = yield give(at + 2, call(
-            factor_kernel, (slot, slot), [SMEM, VMEM, VMEM, VMEM], (VMEM, VMEM),
-            flops=4 * nb * nb * cols * 6,
-        )(here, held, lower_inverse, upper_inverse))
+        weights, top, displaced = yield give(at + 2, call(
+            functools.partial(factor_kernel, log=log), (slot,) * 3,
+            [SMEM] + [VMEM] * 7, (VMEM,) * 3, [pltpu.VMEM((nb, cols), f32)], vmem=24 << 20,
+            flops=4 * nb * nb * cols * 3,
+        )(here, owner, held, *arrived, displaced, lower_inverse, upper_inverse))
         yield give(DONE, (table, displaced, weights, top))
 
     chain, cross, (tops, (table, displaced, weights, top)) = spread(
@@ -467,7 +507,7 @@
     return call(
         functools.partial(
             final_kernel, n_bufs=len(bufs), n_tops=len(tops), n_cols=n_cols, parts=parts,
-            block=256,
+            chunk=chunk,
         ),
         jax.ShapeDtypeStruct(matrix.shape, f32),
         [SMEM, SMEM, SMEM, VMEM, VMEM, VMEM, ANY] + [ANY] * (len(bufs) + len(tops)),
@@ -479,7 +519,11 @@
             pltpu.VMEM((nb, cols), jnp.bfloat16),
             pltpu.VMEM((nb, cols), jnp.bfloat16),
             pltpu.VMEM((row_dev, cols), f32),
-        ] + [pltpu.SemaphoreType.DMA] * 4,
+            pltpu.SemaphoreType.DMA((2 * parts,)),
+            pltpu.SemaphoreType.DMA,
+            pltpu.SemaphoreType.DMA((row_dev // BLOCK,)),
+            pltpu.SemaphoreType.DMA,
+        ],
         vmem=30 << 20,
         flops=2 * row_dev * nb * cols * 3,
         moved=4 * row_dev * (2 * cols + nb),
@@ -489,7 +533,7 @@
 def solution(mesh):
     n_rows, n_cols = mesh.shape["prow"], mesh.shape["pcol"]
     return jax.shard_map(
-        functools.partial(local, n_rows=n_rows, n_cols=n_cols, parts=8),
+        functools.partial(local, n_rows=n_rows, n_cols=n_cols, parts=6),
         mesh=mesh,
         in_specs=(P("prow", "pcol"), P(), P(), P()),
         out_specs=P("prow", "pcol"),

time: 168 us -> 207 us (1.23)
  waiting for transfers between devices: 27.3 us -> 52.8 us
  local copies, waits for them, and re-layouts: 13.8 us -> 26.4 us
  Pallas kernels: 25.5 us -> 29.2 us
    ppermute x14 -> x12, waiting for transfers between devices: 11 us -> 25.1 us  [spread(): chain.append(lax.ppermute(ahead, 'pcol', along))]
    unnamed x120 -> x148, local copies, waits for them, and re-layouts: 9.3 us -> 21.8 us
    ppermute x16 -> x14, waiting for transfers between devices: 16.3 us -> 27.8 us  [spread(): cross.append(lax.ppermute(aside, 'pcol', across))]
    pallas_call x1, Pallas kernels: 10.8 us -> 14.8 us  [local(): call(functools.partial(final_kernel, n_bufs=len(bufs), n_tops=len(tops),...]
    select_n x3 -> x0, other arithmetic: 3.79 us -> none  [the longest x1 2.18 us: spread(): ahead = jnp.where(col == 0, ahead, jnp.where(col == 1, fed, came))]
    select_n x10 -> x8, other arithmetic: 3.1 us -> 5.79 us  [spread(): aside = jnp.where(col == 0, aside, came)]
    ppermute x16 -> x14, starting transfers between devices: 44.3 us -> 42.4 us  [spread(): cross.append(lax.ppermute(aside, 'pcol', across))]
    ppermute x14 -> x12, starting transfers between devices: 41.3 us -> 41.9 us  [spread(): chain.append(lax.ppermute(ahead, 'pcol', along))]
  transfers between devices with their start and end apart: 36 -> 32, of which waited for: 13 -> 16; matrix products, arithmetic and copies ran while one was open for 4% -> 3% of each run, Pallas kernels for 9% -> 7%
where the time goes in v5:
time: 207 us; the launch traced here: 205 us
  starting transfers between devices  89.3 us (43%)
  waiting for transfers between devices  52.8 us (26%)
  Pallas kernels  29.2 us (14%)
  local copies, waits for them, and re-layouts  26.4 us (13%)
  other arithmetic  6.16 us (3%)
    ppermute x14, starting transfers between devices, spread(): cross.append(lax.ppermute(aside, 'pcol', across))  42.4 us
    ppermute x12, starting transfers between devices, spread(): chain.append(lax.ppermute(ahead, 'pcol', along))  41.9 us
    ppermute x14, waiting for transfers between devices, spread(): cross.append(lax.ppermute(aside, 'pcol', across))  27.8 us
    ppermute x12, waiting for transfers between devices, spread(): chain.append(lax.ppermute(ahead, 'pcol', along))  25.1 us
    unnamed x148, local copies, waits for them, and re-layouts  21.8 us
    pallas_call x1, Pallas kernels, local(): call(functools.partial(final_kernel, n_bufs=len(bufs), n_tops=len(tops),...  14.8 us
    pallas_call x1, Pallas kernels, exchange_rider(): call(functools.partial(factor_kernel, log=log), (slot,) * 3, [SMEM] + [VM...  6.86 us
    select_n x8, other arithmetic, spread(): aside = jnp.where(col == 0, aside, came)  5.79 us
  transfers between devices with their start and end apart: 32, of which 16 were waited for; matrix products, arithmetic and copies ran while one was open for 3% of the time, Pallas kernels for 7%

profile of v5, /device:TPU:10, one launch (start us, length us, event | category | flops | bytes accessed | tf_op | source)
XLA Modules:
  0.0 205.2 jit_solution(2251475683669012820)
XLA Ops:
  0.0 3.9 %fusion = (f32[176,512]{1,0:T(8,128)S(1)}, f32[176,512]{1,0:T(8,128)}, f32[176,512]{1,0:T(8,128)}, f32[176,512]{1,0:T(8,128)}, f32[176,512]{1,0:T(8,128)}, /*ind...) fusion(f32[2048,640]{1,0:T(8,128)} %matrix_ref.5), kind=kLoop, calls=%fused_computation.26 | loop fusion | bytes 8650752 | tf_op jit(solution)/shard_map/slice | solution.py:401
  3.9 3.4 %collective-permute-start.1 = (f32[176,512]{1,0:T(8,128)S(1)}, f32[176,512]{1,0:T(8,128)S(1)}, u32[]{:S(2)}, u32[]{:S(2)}) collective-permute-start(f32[176,512]{1,0:T(8,128)S(1)} %get-tuple-element.149), channel_id=1, source_target_pairs={{0,1},{2,3},{3,2},{4,5},{5,4},{6,7},{7,6},{8,9},{10,11},{11,10},{1... | collective-permute-start | bytes 1081352 | tf_op jit(solution)/shard_map/ppermute | solution.py:367
  7.4 3.5 %collective-permute-start = (f32[176,512]{1,0:T(8,128)S(1)}, f32[176,512]{1,0:T(8,128)S(1)}, u32[]{:S(2)}, u32[]{:S(2)}) collective-permute-start(f32[176,512]{1,0:T(8,128)S(1)} %get-tuple-element.150), channel_id=1, source_target_pairs={{0,2},{1,3},{2,4},{3,5},{4,6},{5,7},{8,10},{9,11},{10,12},{11,13},... | collective-permute-start | bytes 1081352 | tf_op jit(solution)/shard_map/ppermute | solution.py:366
  13.3 3.5 %collective-permute-start.10 = (f32[176,512]{1,0:T(8,128)}, f32[176,512]{1,0:T(8,128)S(1)}, u32[]{:S(2)}, u32[]{:S(2)}) collective-permute-start(f32[176,512]{1,0:T(8,128)} %get-tuple-element.89), channel_id=1, source_target_pairs={{0,2},{1,3},{2,4},{3,5},{4,6},{5,7},{8,10},{9,11},{10,12},{11,13},... | collective-permute-start | bytes 1081352 | tf_op jit(solution)/shard_map/ppermute | solution.py:366
  23.1 3.5 %shard_map.56.held_ref = f32[512,640]{1,0:T(8,128)S(1)} custom-call(s32[8,512]{1,0:T(8,128)S(1)} %get-tuple-element.74.table_ref, f32[2048,640]{1,0:T(8,128)S(1)} %copy-done), custom_call_target="tpu_custom_call" | custom-call | tf_op jit(solution)/shard_map/pallas_call | solution.py:468
  29.6 3.5 %collective-permute-start.2 = (f32[176,512]{1,0:T(8,128)S(1)}, f32[176,512]{1,0:T(8,128)S(1)}, u32[]{:S(2)}, u32[]{:S(2)}) collective-permute-start(f32[176,512]{1,0:T(8,128)S(1)} %get-tuple-element.172), channel_id=1, source_target_pairs={{0,2},{1,3},{2,4},{3,5},{4,6},{5,7},{8,10},{9,11},{10,12},{11,13},... | collective-permute-start | bytes 1081352 | tf_op jit(solution)/shard_map/ppermute | solution.py:366
  33.3 3.6 %collective-permute-start.13 = (f32[176,512]{1,0:T(8,128)S(1)}, f32[176,512]{1,0:T(8,128)S(1)}, u32[]{:S(2)}, u32[]{:S(2)}) collective-permute-start(f32[176,512]{1,0:T(8,128)S(1)} %get-tuple-element.167), channel_id=1, source_target_pairs={{0,1},{2,3},{3,2},{4,5},{5,4},{6,7},{7,6},{8,9},{10,11},{11,10},{1... | collective-permute-start | bytes 1081352 | tf_op jit(solution)/shard_map/ppermute | solution.py:367
  36.8 3.5 %collective-permute-start.12 = (f32[176,512]{1,0:T(8,128)S(1)}, f32[176,512]{1,0:T(8,128)S(1)}, u32[]{:S(2)}, u32[]{:S(2)}) collective-permute-start(f32[176,512]{1,0:T(8,128)S(1)} %get-tuple-element.168), channel_id=1, source_target_pairs={{0,2},{1,3},{2,4},{3,5},{4,6},{5,7},{8,10},{9,11},{10,12},{11,13},... | collective-permute-start | bytes 1081352 | tf_op jit(solution)/shard_map/ppermute | solution.py:366
  42.9 3.4 %collective-permute-start.5 = (f32[176,512]{1,0:T(8,128)S(1)}, f32[176,512]{1,0:T(8,128)S(1)}, u32[]{:S(2)}, u32[]{:S(2)}) collective-permute-start(f32[176,512]{1,0:T(8,128)S(1)} %get-tuple-element.169), channel_id=1, source_target_pairs={{0,1},{2,3},{3,2},{4,5},{5,4},{6,7},{7,6},{8,9},{10,11},{11,10},{1... | collective-permute-start | bytes 1081352 | tf_op jit(solution)/shard_map/ppermute | solution.py:367
  46.3 3.5 %collective-permute-start.4 = (f32[176,512]{1,0:T(8,128)S(1)}, f32[176,512]{1,0:T(8,128)S(1)}, u32[]{:S(2)}, u32[]{:S(2)}) collective-permute-start(f32[176,512]{1,0:T(8,128)S(1)} %get-tuple-element.170), channel_id=1, source_target_pairs={{0,2},{1,3},{2,4},{3,5},{4,6},{5,7},{8,10},{9,11},{10,12},{11,13},... | collective-permute-start | bytes 1081352 | tf_op jit(solution)/shard_map/ppermute | solution.py:366
  50.6 3.5 %collective-permute-start.16 = (f32[176,512]{1,0:T(8,128)S(1)}, f32[176,512]{1,0:T(8,128)S(1)}, u32[]{:S(2)}, u32[]{:S(2)}) collective-permute-start(f32[176,512]{1,0:T(8,128)S(1)} %get-tuple-element.165), channel_id=1, source_target_pairs={{0,1},{2,3},{3,2},{4,5},{5,4},{6,7},{7,6},{8,9},{10,11},{11,10},{1... | collective-permute-start | bytes 1081352 | tf_op jit(solution)/shard_map/ppermute | solution.py:367
  54.1 3.5 %collective-permute-start.15 = (f32[176,512]{1,0:T(8,128)S(1)}, f32[176,512]{1,0:T(8,128)S(1)}, u32[]{:S(2)}, u32[]{:S(2)}) collective-permute-start(f32[176,512]{1,0:T(8,128)S(1)} %get-tuple-element.166), channel_id=1, source_target_pairs={{0,2},{1,3},{2,4},{3,5},{4,6},{5,7},{8,10},{9,11},{10,12},{11,13},... | collective-permute-start | bytes 1081352 | tf_op jit(solution)/shard_map/ppermute | solution.py:366
  60.3 2.8 %collective-permute-done.16.refs_13_.refs_17_ = f32[176,512]{1,0:T(8,128)S(1)} collective-permute-done((f32[176,512]{1,0:T(8,128)S(1)}, f32[176,512]{1,0:T(8,128)S(1)}, u32[]{:S(2)}, u32[]{:S(2)}) %collective-permute-start.16) | collective-permute-done | bytes 360480 | tf_op jit(solution)/shard_map/ppermute | solution.py:367
  66.7 3.4 %collective-permute-start.18 = (f32[176,512]{1,0:T(8,128)S(1)}, f32[176,512]{1,0:T(8,128)S(1)}, u32[]{:S(2)}, u32[]{:S(2)}) collective-permute-start(f32[176,512]{1,0:T(8,128)S(1)} %get-tuple-element.161), channel_id=1, source_target_pairs={{0,1},{2,3},{3,2},{4,5},{5,4},{6,7},{7,6},{8,9},{10,11},{11,10},{1... | collective-permute-start | bytes 1081352 | tf_op jit(solution)/shard_map/ppermute | solution.py:367
  70.1 3.5 %collective-permute-start.17 = (f32[176,512]{1,0:T(8,128)S(1)}, f32[176,512]{1,0:T(8,128)S(1)}, u32[]{:S(2)}, u32[]{:S(2)}) collective-permute-start(f32[176,512]{1,0:T(8,128)S(1)} %get-tuple-element.162), channel_id=1, source_target_pairs={{0,2},{1,3},{2,4},{3,5},{4,6},{5,7},{8,10},{9,11},{10,12},{11,13},... | collective-permute-start | bytes 1081352 | tf_op jit(solution)/shard_map/ppermute | solution.py:366
  73.6 3.5 %collective-permute-start.6 = (f32[176,512]{1,0:T(8,128)S(1)}, f32[176,512]{1,0:T(8,128)S(1)}, u32[]{:S(2)}, u32[]{:S(2)}) collective-permute-start(f32[176,512]{1,0:T(8,128)S(1)} %get-tuple-element.163), channel_id=1, source_target_pairs={{0,2},{1,3},{2,4},{3,5},{4,6},{5,7},{8,10},{9,11},{10,12},{11,13},... | collective-permute-start | bytes 1081352 | tf_op jit(solution)/shard_map/ppermute | solution.py:366
  79.7 3.7 %collective-permute-done.17.refs_7_ = f32[176,512]{1,0:T(8,128)S(1)} collective-permute-done((f32[176,512]{1,0:T(8,128)S(1)}, f32[176,512]{1,0:T(8,128)S(1)}, u32[]{:S(2)}, u32[]{:S(2)}) %collective-permute-start.17) | collective-permute-done | bytes 360480 | tf_op jit(solution)/shard_map/ppermute | solution.py:366
  83.3 5.5 %collective-permute-done.6.refs_6_ = f32[176,512]{1,0:T(8,128)S(1)} collective-permute-done((f32[176,512]{1,0:T(8,128)S(1)}, f32[176,512]{1,0:T(8,128)S(1)}, u32[]{:S(2)}, u32[]{:S(2)}) %collective-permute-start.6) | collective-permute-done | bytes 360480 | tf_op jit(solution)/shard_map/ppermute | solution.py:366
  92.5 3.5 %collective-permute-start.23 = (f32[176,512]{1,0:T(8,128)}, f32[176,512]{1,0:T(8,128)S(1)}, u32[]{:S(2)}, u32[]{:S(2)}) collective-permute-start(f32[176,512]{1,0:T(8,128)} %get-tuple-element.158), channel_id=1, source_target_pairs={{0,2},{1,3},{2,4},{3,5},{4,6},{5,7},{8,10},{9,11},{10,12},{11,13},... | collective-permute-start | bytes 1081352 | tf_op jit(solution)/shard_map/ppermute | solution.py:366
  96.0 3.6 %collective-permute-start.9 = (f32[176,512]{1,0:T(8,128)}, f32[176,512]{1,0:T(8,128)S(1)}, u32[]{:S(2)}, u32[]{:S(2)}) collective-permute-start(f32[176,512]{1,0:T(8,128)} %get-tuple-element.160), channel_id=1, source_target_pairs={{0,1},{2,3},{3,2},{4,5},{5,4},{6,7},{7,6},{8,9},{10,11},{11,10},{1... | collective-permute-start | bytes 1081352 | tf_op jit(solution)/shard_map/ppermute | solution.py:367
  104.7 3.7 %collective-permute-done.9.refs_16_.refs_20_ = f32[176,512]{1,0:T(8,128)S(1)} collective-permute-done((f32[176,512]{1,0:T(8,128)}, f32[176,512]{1,0:T(8,128)S(1)}, u32[]{:S(2)}, u32[]{:S(2)}) %collective-permute-start.9) | collective-permute-done | bytes 360480 | tf_op jit(solution)/shard_map/ppermute | solution.py:367
  126.0 3.5 %collective-permute-start.8 = (f32[176,512]{1,0:T(8,128)S(1)}, f32[176,512]{1,0:T(8,128)S(1)}, u32[]{:S(2)}, u32[]{:S(2)}) collective-permute-start(f32[176,512]{1,0:T(8,128)S(1)} %copy-done.71), channel_id=1, source_target_pairs={{0,2},{1,3},{2,4},{3,5},{4,6},{5,7},{8,10},{9,11},{10,12},{11,13},... | collective-permute-start | bytes 1081352 | tf_op jit(solution)/shard_map/ppermute | solution.py:366
  129.5 6.3 %collective-permute-done.8.refs_8_ = f32[176,512]{1,0:T(8,128)S(1)} collective-permute-done((f32[176,512]{1,0:T(8,128)S(1)}, f32[176,512]{1,0:T(8,128)S(1)}, u32[]{:S(2)}, u32[]{:S(2)}) %collective-permute-start.8) | collective-permute-done | bytes 360480 | tf_op jit(solution)/shard_map/ppermute | solution.py:366
  139.2 3.5 %collective-permute-start.25 = (f32[176,512]{1,0:T(8,128)}, f32[176,512]{1,0:T(8,128)}, u32[]{:S(2)}, u32[]{:S(2)}) collective-permute-start(f32[176,512]{1,0:T(8,128)} %get-tuple-element.152), channel_id=1, source_target_pairs={{0,2},{1,3},{2,4},{3,5},{4,6},{5,7},{8,10},{9,11},{10,12},{11,13},... | collective-permute-start | bytes 1081352 | tf_op jit(solution)/shard_map/ppermute | solution.py:366
  142.8 3.9 %collective-permute-done.26.refs_23_ = f32[176,512]{1,0:T(8,128)} collective-permute-done((f32[176,512]{1,0:T(8,128)}, f32[176,512]{1,0:T(8,128)}, u32[]{:S(2)}, u32[]{:S(2)}) %collective-permute-start.26) | collective-permute-done | bytes 360480 | tf_op jit(solution)/shard_map/ppermute | solution.py:367
  150.8 3.6 %collective-permute-start.21 = (f32[176,512]{1,0:T(8,128)}, f32[176,512]{1,0:T(8,128)S(1)}, u32[]{:S(2)}, u32[]{:S(2)}) collective-permute-start(f32[176,512]{1,0:T(8,128)} %get-tuple-element.155), channel_id=1, source_target_pairs={{0,2},{1,3},{2,4},{3,5},{4,6},{5,7},{8,10},{9,11},{10,12},{11,13},... | collective-permute-start | bytes 1081352 | tf_op jit(solution)/shard_map/ppermute | solution.py:366
  154.4 3.6 %collective-permute-start.22 = (f32[176,512]{1,0:T(8,128)}, f32[176,512]{1,0:T(8,128)S(1)}, u32[]{:S(2)}, u32[]{:S(2)}) collective-permute-start(f32[176,512]{1,0:T(8,128)} %get-tuple-element.156), channel_id=1, source_target_pairs={{0,1},{2,3},{3,2},{4,5},{5,4},{6,7},{7,6},{8,9},{10,11},{11,10},{1... | collective-permute-start | bytes 1081352 | tf_op jit(solution)/shard_map/ppermute | solution.py:367
  159.4 6.9 %shard_map.58 = (f32[512,640]{1,0:T(8,128)S(1)}, f32[512,640]{1,0:T(8,128)S(1)}, f32[512,640]{1,0:T(8,128)S(1)}) custom-call(s32[2]{0:T(128)S(1)} %copy-done.54, s32[512,128]{1,0:T(8,128)S(1)} %copy-done.51, f32[512,640]{1,0:T(8,128)S(1)} %copy-done.59, f32[256,640]{1,0:T(8,128)} %collective-permute-done.19.one_ref, ...), custom_call_target="tpu_custom_call" | custom-call | flops 2013265920 | tf_op jit(solution)/shard_map/pallas_call | solution.py:494
  171.9 3.6 %collective-permute-start.27 = (f32[176,512]{1,0:T(8,128)S(1)}, f32[176,512]{1,0:T(8,128)S(1)}, u32[]{:S(2)}, u32[]{:S(2)}) collective-permute-start(f32[176,512]{1,0:T(8,128)S(1)} %get-tuple-element.154), channel_id=1, source_target_pairs={{0,1},{2,3},{3,2},{4,5},{5,4},{6,7},{7,6},{8,9},{10,11},{11,10},{1... | collective-permute-start | bytes 1081352 | tf_op jit(solution)/shard_map/ppermute | solution.py:367
  175.5 7.2 %collective-permute-done.29.refs_25_ = f32[176,512]{1,0:T(8,128)S(1)} collective-permute-done((f32[176,512]{1,0:T(8,128)S(1)}, f32[176,512]{1,0:T(8,128)S(1)}, u32[]{:S(2)}, u32[]{:S(2)}) %collective-permute-start.29) | collective-permute-done | bytes 360480 | tf_op jit(solution)/shard_map/ppermute | solution.py:367
  182.8 7.3 %collective-permute-done.27.refs_24_ = f32[176,512]{1,0:T(8,128)S(1)} collective-permute-done((f32[176,512]{1,0:T(8,128)S(1)}, f32[176,512]{1,0:T(8,128)S(1)}, u32[]{:S(2)}, u32[]{:S(2)}) %collective-permute-start.27) | collective-permute-done | bytes 360480 | tf_op jit(solution)/shard_map/ppermute | solution.py:367
  190.3 14.8 %shard_map.60 = f32[2048,640]{1,0:T(8,128)} custom-call(s32[2]{0:T(128)S(1)} %copy-done.54, s32[8,512]{1,0:T(8,128)S(1)} %get-tuple-element.74.table_ref, s32[12]{0:T(128)S(1)} %copy-done.56, f32[512,640]{1,0:T(8,128)S(1)} %get-tuple-element.111.displaced_ref, f32[512,640]{1,0:T(8,128)S(1)} %get-tuple-element.112.weights_ref, ...), custom_call_target="tpu_custom_call" | custom-call | flops 4026531840 | bytes 14680064 | tf_op jit(solution)/shard_map/pallas_call | solution.py:507
  (200 shorter events, 64.2 us)
Async XLA Ops:
  3.9 14.7 %collective-permute-start.1 = (f32[176,512]{1,0:T(8,128)S(1)}, f32[176,512]{1,0:T(8,128)S(1)}, u32[]{:S(2)}, u32[]{:S(2)}) collective-permute-start(f32[176,512]{1,0:T(8,128)S(1)} %get-tuple-element.149), channel_id=1, source_target_pairs={{0,1},{2,3},{3,2},{4,5},{5,4},{6,7},{7,6},{8,9},{10,11},{11,10},{1... | collective-permute-start | bytes 1081352 | tf_op jit(solution)/shard_map/ppermute | solution.py:367
  7.4 13.2 %collective-permute-start = (f32[176,512]{1,0:T(8,128)S(1)}, f32[176,512]{1,0:T(8,128)S(1)}, u32[]{:S(2)}, u32[]{:S(2)}) collective-permute-start(f32[176,512]{1,0:T(8,128)S(1)} %get-tuple-element.150), channel_id=1, source_target_pairs={{0,2},{1,3},{2,4},{3,5},{4,6},{5,7},{8,10},{9,11},{10,12},{11,13},... | collective-permute-start | bytes 1081352 | tf_op jit(solution)/shard_map/ppermute | solution.py:366
  10.9 15.8 %collective-permute-start.11 = (f32[176,512]{1,0:T(8,128)}, f32[176,512]{1,0:T(8,128)S(1)}, u32[]{:S(2)}, u32[]{:S(2)}) collective-permute-start(f32[176,512]{1,0:T(8,128)} %get-tuple-element.90), channel_id=1, source_target_pairs={{0,1},{2,3},{3,2},{4,5},{5,4},{6,7},{7,6},{8,9},{10,11},{11,10},{1... | collective-permute-start | bytes 1081352 | tf_op jit(solution)/shard_map/ppermute | solution.py:367
  13.3 13.6 %collective-permute-start.10 = (f32[176,512]{1,0:T(8,128)}, f32[176,512]{1,0:T(8,128)S(1)}, u32[]{:S(2)}, u32[]{:S(2)}) collective-permute-start(f32[176,512]{1,0:T(8,128)} %get-tuple-element.89), channel_id=1, source_target_pairs={{0,2},{1,3},{2,4},{3,5},{4,6},{5,7},{8,10},{9,11},{10,12},{11,13},... | collective-permute-start | bytes 1081352 | tf_op jit(solution)/shard_map/ppermute | solution.py:366
  26.9 23.4 %collective-permute-start.14 = (f32[512,640]{1,0:T(8,128)S(1)}, f32[512,640]{1,0:T(8,128)}, u32[]{:S(2)}, u32[]{:S(2)}) collective-permute-start(f32[512,640]{1,0:T(8,128)S(1)} %shard_map.56.held_ref), channel_id=1, source_target_pairs={{0,8},{8,0},{16,24},{24,16},{1,9},{9,1},{17,25},{25,17},{2,10},{10... | collective-permute-start | bytes 3932168 | tf_op jit(solution)/shard_map/ppermute | solution.py:477
  27.0 13.3 %collective-permute-start.3 = (f32[176,512]{1,0:T(8,128)S(1)}, f32[176,512]{1,0:T(8,128)S(1)}, u32[]{:S(2)}, u32[]{:S(2)}) collective-permute-start(f32[176,512]{1,0:T(8,128)S(1)} %get-tuple-element.171), channel_id=1, source_target_pairs={{0,1},{2,3},{3,2},{4,5},{5,4},{6,7},{7,6},{8,9},{10,11},{11,10},{1... | collective-permute-start | bytes 1081352 | tf_op jit(solution)/shard_map/ppermute | solution.py:367
  29.6 13.1 %collective-permute-start.2 = (f32[176,512]{1,0:T(8,128)S(1)}, f32[176,512]{1,0:T(8,128)S(1)}, u32[]{:S(2)}, u32[]{:S(2)}) collective-permute-start(f32[176,512]{1,0:T(8,128)S(1)} %get-tuple-element.172), channel_id=1, source_target_pairs={{0,2},{1,3},{2,4},{3,5},{4,6},{5,7},{8,10},{9,11},{10,12},{11,13},... | collective-permute-start | bytes 1081352 | tf_op jit(solution)/shard_map/ppermute | solution.py:366
  33.3 16.5 %collective-permute-start.13 = (f32[176,512]{1,0:T(8,128)S(1)}, f32[176,512]{1,0:T(8,128)S(1)}, u32[]{:S(2)}, u32[]{:S(2)}) collective-permute-start(f32[176,512]{1,0:T(8,128)S(1)} %get-tuple-element.167), channel_id=1, source_target_pairs={{0,1},{2,3},{3,2},{4,5},{5,4},{6,7},{7,6},{8,9},{10,11},{11,10},{1... | collective-permute-start | bytes 1081352 | tf_op jit(solution)/shard_map/ppermute | solution.py:367
  36.8 13.4 %collective-permute-start.12 = (f32[176,512]{1,0:T(8,128)S(1)}, f32[176,512]{1,0:T(8,128)S(1)}, u32[]{:S(2)}, u32[]{:S(2)}) collective-permute-start(f32[176,512]{1,0:T(8,128)S(1)} %get-tuple-element.168), channel_id=1, source_target_pairs={{0,2},{1,3},{2,4},{3,5},{4,6},{5,7},{8,10},{9,11},{10,12},{11,13},... | collective-permute-start | bytes 1081352 | tf_op jit(solution)/shard_map/ppermute | solution.py:366
  42.9 14.7 %collective-permute-start.5 = (f32[176,512]{1,0:T(8,128)S(1)}, f32[176,512]{1,0:T(8,128)S(1)}, u32[]{:S(2)}, u32[]{:S(2)}) collective-permute-start(f32[176,512]{1,0:T(8,128)S(1)} %get-tuple-element.169), channel_id=1, source_target_pairs={{0,1},{2,3},{3,2},{4,5},{5,4},{6,7},{7,6},{8,9},{10,11},{11,10},{1... | collective-permute-start | bytes 1081352 | tf_op jit(solution)/shard_map/ppermute | solution.py:367
  46.3 11.6 %collective-permute-start.4 = (f32[176,512]{1,0:T(8,128)S(1)}, f32[176,512]{1,0:T(8,128)S(1)}, u32[]{:S(2)}, u32[]{:S(2)}) collective-permute-start(f32[176,512]{1,0:T(8,128)S(1)} %get-tuple-element.170), channel_id=1, source_target_pairs={{0,2},{1,3},{2,4},{3,5},{4,6},{5,7},{8,10},{9,11},{10,12},{11,13},... | collective-permute-start | bytes 1081352 | tf_op jit(solution)/shard_map/ppermute | solution.py:366
  50.6 12.5 %collective-permute-start.16 = (f32[176,512]{1,0:T(8,128)S(1)}, f32[176,512]{1,0:T(8,128)S(1)}, u32[]{:S(2)}, u32[]{:S(2)}) collective-permute-start(f32[176,512]{1,0:T(8,128)S(1)} %get-tuple-element.165), channel_id=1, source_target_pairs={{0,1},{2,3},{3,2},{4,5},{5,4},{6,7},{7,6},{8,9},{10,11},{11,10},{1... | collective-permute-start | bytes 1081352 | tf_op jit(solution)/shard_map/ppermute | solution.py:367
  54.1 11.1 %collective-permute-start.15 = (f32[176,512]{1,0:T(8,128)S(1)}, f32[176,512]{1,0:T(8,128)S(1)}, u32[]{:S(2)}, u32[]{:S(2)}) collective-permute-start(f32[176,512]{1,0:T(8,128)S(1)} %get-tuple-element.166), channel_id=1, source_target_pairs={{0,2},{1,3},{2,4},{3,5},{4,6},{5,7},{8,10},{9,11},{10,12},{11,13},... | collective-permute-start | bytes 1081352 | tf_op jit(solution)/shard_map/ppermute | solution.py:366
  59.7 20.0 %collective-permute-start.19 = (f32[256,640]{1,0:T(8,128)S(1)}, f32[256,640]{1,0:T(8,128)}, u32[]{:S(2)}, u32[]{:S(2)}) collective-permute-start(f32[256,640]{1,0:T(8,128)S(1)} %get-tuple-element.102), channel_id=1, source_target_pairs={{0,16},{8,24},{16,0},{24,8},{1,17},{9,25},{17,1},{25,9},{2,18},{10... | collective-permute-start | bytes 1966088 | tf_op jit(solution)/shard_map/ppermute | solution.py:481
  66.7 13.0 %collective-permute-start.18 = (f32[176,512]{1,0:T(8,128)S(1)}, f32[176,512]{1,0:T(8,128)S(1)}, u32[]{:S(2)}, u32[]{:S(2)}) collective-permute-start(f32[176,512]{1,0:T(8,128)S(1)} %get-tuple-element.161), channel_id=1, source_target_pairs={{0,1},{2,3},{3,2},{4,5},{5,4},{6,7},{7,6},{8,9},{10,11},{11,10},{1... | collective-permute-start | bytes 1081352 | tf_op jit(solution)/shard_map/ppermute | solution.py:367
  70.1 13.2 %collective-permute-start.17 = (f32[176,512]{1,0:T(8,128)S(1)}, f32[176,512]{1,0:T(8,128)S(1)}, u32[]{:S(2)}, u32[]{:S(2)}) collective-permute-start(f32[176,512]{1,0:T(8,128)S(1)} %get-tuple-element.162), channel_id=1, source_target_pairs={{0,2},{1,3},{2,4},{3,5},{4,6},{5,7},{8,10},{9,11},{10,12},{11,13},... | collective-permute-start | bytes 1081352 | tf_op jit(solution)/shard_map/ppermute | solution.py:366
  73.6 15.3 %collective-permute-start.6 = (f32[176,512]{1,0:T(8,128)S(1)}, f32[176,512]{1,0:T(8,128)S(1)}, u32[]{:S(2)}, u32[]{:S(2)}) collective-permute-start(f32[176,512]{1,0:T(8,128)S(1)} %get-tuple-element.163), channel_id=1, source_target_pairs={{0,2},{1,3},{2,4},{3,5},{4,6},{5,7},{8,10},{9,11},{10,12},{11,13},... | collective-permute-start | bytes 1081352 | tf_op jit(solution)/shard_map/ppermute | solution.py:366
  77.1 11.8 %collective-permute-start.7 = (f32[176,512]{1,0:T(8,128)S(1)}, f32[176,512]{1,0:T(8,128)S(1)}, u32[]{:S(2)}, u32[]{:S(2)}) collective-permute-start(f32[176,512]{1,0:T(8,128)S(1)} %get-tuple-element.164), channel_id=1, source_target_pairs={{0,1},{2,3},{3,2},{4,5},{5,4},{6,7},{7,6},{8,9},{10,11},{11,10},{1... | collective-permute-start | bytes 1081352 | tf_op jit(solution)/shard_map/ppermute | solution.py:367
  90.3 12.9 %collective-permute-start.24 = (f32[176,512]{1,0:T(8,128)}, f32[176,512]{1,0:T(8,128)S(1)}, u32[]{:S(2)}, u32[]{:S(2)}) collective-permute-start(f32[176,512]{1,0:T(8,128)} %get-tuple-element.157), channel_id=1, source_target_pairs={{0,1},{2,3},{3,2},{4,5},{5,4},{6,7},{7,6},{8,9},{10,11},{11,10},{1... | collective-permute-start | bytes 1081352 | tf_op jit(solution)/shard_map/ppermute | solution.py:367
  92.5 11.4 %collective-permute-start.23 = (f32[176,512]{1,0:T(8,128)}, f32[176,512]{1,0:T(8,128)S(1)}, u32[]{:S(2)}, u32[]{:S(2)}) collective-permute-start(f32[176,512]{1,0:T(8,128)} %get-tuple-element.158), channel_id=1, source_target_pairs={{0,2},{1,3},{2,4},{3,5},{4,6},{5,7},{8,10},{9,11},{10,12},{11,13},... | collective-permute-start | bytes 1081352 | tf_op jit(solution)/shard_map/ppermute | solution.py:366
  96.0 12.4 %collective-permute-start.9 = (f32[176,512]{1,0:T(8,128)}, f32[176,512]{1,0:T(8,128)S(1)}, u32[]{:S(2)}, u32[]{:S(2)}) collective-permute-start(f32[176,512]{1,0:T(8,128)} %get-tuple-element.160), channel_id=1, source_target_pairs={{0,1},{2,3},{3,2},{4,5},{5,4},{6,7},{7,6},{8,9},{10,11},{11,10},{1... | collective-permute-start | bytes 1081352 | tf_op jit(solution)/shard_map/ppermute | solution.py:367
  99.6 36.1 %collective-permute-start.20 = (f32[256,640]{1,0:T(8,128)}, f32[256,640]{1,0:T(8,128)}, u32[]{:S(2)}, u32[]{:S(2)}) collective-permute-start(f32[256,640]{1,0:T(8,128)} %collective-permute-done.19.one_ref), channel_id=1, source_target_pairs={{0,8},{8,0},{16,24},{24,16},{1,9},{9,1},{17,25},{25,17},{2,10},{10... | collective-permute-start | bytes 1966088 | tf_op jit(solution)/shard_map/ppermute | solution.py:483
  125.2 23.7 %collective-permute-start.28 = (f32[512,512]{1,0:T(8,128)S(1)}, f32[512,512]{1,0:T(8,128)S(1)}, u32[]{:S(2)}, u32[]{:S(2)}) collective-permute-start(f32[512,512]{1,0:T(8,128)S(1)} %shard_map.59), channel_id=1, source_target_pairs={{0,8},{1,9},{2,10},{3,11},{4,12},{5,13},{6,14},{7,15}} | collective-permute-start | bytes 3145736 | tf_op jit(solution)/shard_map/ppermute | solution.py:446
  126.0 9.8 %collective-permute-start.8 = (f32[176,512]{1,0:T(8,128)S(1)}, f32[176,512]{1,0:T(8,128)S(1)}, u32[]{:S(2)}, u32[]{:S(2)}) collective-permute-start(f32[176,512]{1,0:T(8,128)S(1)} %copy-done.71), channel_id=1, source_target_pairs={{0,2},{1,3},{2,4},{3,5},{4,6},{5,7},{8,10},{9,11},{10,12},{11,13},... | collective-permute-start | bytes 1081352 | tf_op jit(solution)/shard_map/ppermute | solution.py:366
  137.1 9.6 %collective-permute-start.26 = (f32[176,512]{1,0:T(8,128)}, f32[176,512]{1,0:T(8,128)}, u32[]{:S(2)}, u32[]{:S(2)}) collective-permute-start(f32[176,512]{1,0:T(8,128)} %get-tuple-element.151), channel_id=1, source_target_pairs={{0,1},{2,3},{3,2},{4,5},{5,4},{6,7},{7,6},{8,9},{10,11},{11,10},{1... | collective-permute-start | bytes 1081352 | tf_op jit(solution)/shard_map/ppermute | solution.py:367
  139.2 9.6 %collective-permute-start.25 = (f32[176,512]{1,0:T(8,128)}, f32[176,512]{1,0:T(8,128)}, u32[]{:S(2)}, u32[]{:S(2)}) collective-permute-start(f32[176,512]{1,0:T(8,128)} %get-tuple-element.152), channel_id=1, source_target_pairs={{0,2},{1,3},{2,4},{3,5},{4,6},{5,7},{8,10},{9,11},{10,12},{11,13},... | collective-permute-start | bytes 1081352 | tf_op jit(solution)/shard_map/ppermute | solution.py:366
  149.2 17.1 %collective-permute-start.30 = (f32[256,512]{1,0:T(8,128)S(1)}, f32[256,512]{1,0:T(8,128)S(1)}, u32[]{:S(2)}, u32[]{:S(2)}) collective-permute-start(f32[256,512]{1,0:T(8,128)S(1)} %slice_select_fusion), channel_id=1, source_target_pairs={{0,16},{8,24},{1,17},{9,25},{2,18},{10,26},{3,19},{11,27},{4,20},{... | collective-permute-start | bytes 1572872 | tf_op jit(solution)/shard_map/ppermute | solution.py:451
  150.8 15.6 %collective-permute-start.21 = (f32[176,512]{1,0:T(8,128)}, f32[176,512]{1,0:T(8,128)S(1)}, u32[]{:S(2)}, u32[]{:S(2)}) collective-permute-start(f32[176,512]{1,0:T(8,128)} %get-tuple-element.155), channel_id=1, source_target_pairs={{0,2},{1,3},{2,4},{3,5},{4,6},{5,7},{8,10},{9,11},{10,12},{11,13},... | collective-permute-start | bytes 1081352 | tf_op jit(solution)/shard_map/ppermute | solution.py:366
  154.4 11.9 %collective-permute-start.22 = (f32[176,512]{1,0:T(8,128)}, f32[176,512]{1,0:T(8,128)S(1)}, u32[]{:S(2)}, u32[]{:S(2)}) collective-permute-start(f32[176,512]{1,0:T(8,128)} %get-tuple-element.156), channel_id=1, source_target_pairs={{0,1},{2,3},{3,2},{4,5},{5,4},{6,7},{7,6},{8,9},{10,11},{11,10},{1... | collective-permute-start | bytes 1081352 | tf_op jit(solution)/shard_map/ppermute | solution.py:367
  166.4 23.7 %collective-permute-start.31 = (f32[256,512]{1,0:T(8,128)S(1)}, f32[256,512]{1,0:T(8,128)S(1)}, u32[]{:S(2)}, u32[]{:S(2)}) collective-permute-start(f32[256,512]{1,0:T(8,128)S(1)} %collective-permute-done.30.refs_27_), channel_id=1, source_target_pairs={{16,24},{24,16},{17,25},{25,17},{18,26},{26,18},{19,27},{27,19},{2... | collective-permute-start | bytes 1572872 | tf_op jit(solution)/shard_map/ppermute | solution.py:452
  169.7 13.1 %collective-permute-start.29 = (f32[176,512]{1,0:T(8,128)S(1)}, f32[176,512]{1,0:T(8,128)S(1)}, u32[]{:S(2)}, u32[]{:S(2)}) collective-permute-start(f32[176,512]{1,0:T(8,128)S(1)} %get-tuple-element.153), channel_id=1, source_target_pairs={{0,1},{2,3},{3,2},{4,5},{5,4},{6,7},{7,6},{8,9},{10,11},{11,10},{1... | collective-permute-start | bytes 1081352 | tf_op jit(solution)/shard_map/ppermute | solution.py:367
  171.9 18.2 %collective-permute-start.27 = (f32[176,512]{1,0:T(8,128)S(1)}, f32[176,512]{1,0:T(8,128)S(1)}, u32[]{:S(2)}, u32[]{:S(2)}) collective-permute-start(f32[176,512]{1,0:T(8,128)S(1)} %get-tuple-element.154), channel_id=1, source_target_pairs={{0,1},{2,3},{3,2},{4,5},{5,4},{6,7},{7,6},{8,9},{10,11},{11,10},{1... | collective-permute-start | bytes 1081352 | tf_op jit(solution)/shard_map/ppermute | solution.py:367
  (74 other events, 1078.4 us)

commit v6 on v4

--- a/solution.py
+++ b/solution.py
@@ -12,6 +12,7 @@
 SMEM = pl.BlockSpec(memory_space=pltpu.SMEM)
 ANY = pl.BlockSpec(memory_space=pl.ANY)
 LANES = 128
+PCOL = ("along", "side")
 PICK, FROM, ROW, COUNT, TOP = 0, 1, 2, 3, 4
 
 
@@ -283,7 +284,7 @@
     row_dev, cols = matrix.shape
     nb = pivots.shape[0]
     f32 = jnp.float32
-    row, col = lax.axis_index("prow"), lax.axis_index("pcol")
+    row, col = lax.axis_index("prow"), lax.axis_index(PCOL)
     here = jnp.stack([row, col]).astype(jnp.int32)
     odd = row % 2 == 1
     slot = jax.ShapeDtypeStruct((nb, cols), f32)
@@ -292,7 +293,6 @@
     depth = n_cols // 2
     half_rows = row_dev // (2 * groups)
     piece_rows = half_rows // depth
-    lanes = [[z * 2 + y for z in range(depth)] for y in range(2)]
     across = [(0, 1)] + [(p, p ^ 1) for p in range(2, n_cols)]
 
     def panel_rows(start, size):
@@ -302,12 +302,12 @@
         pieces = [line[z * piece_rows : (z + 1) * piece_rows] for z in range(depth)]
         mine = pieces[0]
         for z in range(1, depth):
-            came = lax.ppermute(pieces[z], "pcol", [(0, 2 * z), (1, 2 * z + 1)])
+            came = lax.ppermute(pieces[z], PCOL, [(0, 2 * z), (1, 2 * z + 1)])
             mine = jnp.where(col // 2 == z, came, mine)
         return mine
 
     def gather(piece):
-        return lax.all_gather(piece, "pcol", axis=0, tiled=True, axis_index_groups=lanes)
+        return lax.all_gather(piece, "along", axis=0, tiled=True)
 
     def exchange():
         table, owner = call(
@@ -373,7 +373,7 @@
         return tops
 
     rows_side, top_side = Rider(exchange()), Rider(spread_top())
-    fed = lax.ppermute(panel_rows(0, half_rows), "pcol", [(0, 1)])
+    fed = lax.ppermute(panel_rows(0, half_rows), PCOL, [(0, 1)])
     mine, along, other = None, [], []
     for g in range(groups + 2):
         if g == 3:
@@ -384,7 +384,7 @@
         if g > 3:
             other[g - 3] = crossed
         if g > 1:
-            other.append(lax.ppermute(line, "pcol", across))
+            other.append(lax.ppermute(line, PCOL, across))
         if 0 < g <= groups:
             along.append(gather(mine))
         if g < groups:
@@ -394,7 +394,7 @@
             if g + 1 < groups:
                 run, ahead = tie(run, panel_rows(2 * (g + 1) * half_rows, half_rows))
             mine = scatter(run)
-            fed = lax.ppermute(ahead, "pcol", [(0, 1)]) if g + 1 < groups else None
+            fed = lax.ppermute(ahead, PCOL, [(0, 1)]) if g + 1 < groups else None
         else:
             mine = None
         rows_side.go()
@@ -443,10 +443,13 @@
 
 def solution(mesh):
     n_rows, n_cols = mesh.shape["prow"], mesh.shape["pcol"]
+    lines = jax.sharding.Mesh(
+        mesh.devices.reshape(n_rows, n_cols // 2, 2), ("prow",) + PCOL
+    )
     return jax.shard_map(
         functools.partial(local, n_rows=n_rows, n_cols=n_cols, groups=4),
-        mesh=mesh,
-        in_specs=(P("prow", "pcol"), P(), P(), P()),
-        out_specs=P("prow", "pcol"),
+        mesh=lines,
+        in_specs=(P("prow", PCOL), P(), P(), P()),
+        out_specs=P("prow", PCOL),
         check_vma=False,
     )

time: 175 us -> 175 us (level)
  no operation moved by 1% of the time
where the time goes in v6:
time: 175 us; the launch traced here: 172 us
  blocking collectives  79.9 us (46%)
  starting transfers between devices  32 us (18%)
  Pallas kernels  26.2 us (15%)
  waiting for transfers between devices  14 us (8%)
  other arithmetic  9.85 us (6%)
  local copies, waits for them, and re-layouts  8.93 us (5%)
    all_gather x4, blocking collectives, gather(): return lax.all_gather(piece, 'along', axis=0, tiled=True)  79.9 us
    ppermute x12, waiting for transfers between devices, scatter(): came = lax.ppermute(pieces[z], PCOL, [(0, 2 * z), (1, 2 * z + 1)])  14 us
    ppermute x12, starting transfers between devices, scatter(): came = lax.ppermute(pieces[z], PCOL, [(0, 2 * z), (1, 2 * z + 1)])  11.9 us
    ppermute x4, starting transfers between devices, local(): other.append(lax.ppermute(line, PCOL, across))  11 us
    pallas_call x1, Pallas kernels, local(): call(functools.partial(final_kernel, n_bufs=len(bufs), n_tops=len(tops),...  10.4 us
    pallas_call x1, Pallas kernels, exchange(): call(factor_kernel, (slot, slot), [SMEM, VMEM, VMEM, VMEM], (VMEM, VMEM),...  5.85 us
    unnamed x46, local copies, waits for them, and re-layouts  4.61 us
    pallas_call x2, Pallas kernels, exchange(): call(functools.partial(merge_kernel, log=log, halves=log > 0), (slot, hal...  4.23 us
  transfers between devices with their start and end apart: 26, of which 2 were waited for; matrix products, arithmetic and copies ran while one was open for 5% of the time, Pallas kernels for 9%

profile of v6, /device:TPU:10, one launch (start us, length us, event | category | flops | bytes accessed | tf_op | source)
XLA Modules:
  0.0 171.7 jit_solution(14896392517186102343)
XLA Ops:
  0.0 2.7 %fusion.2 = (f32[256,512]{1,0:T(8,128)}, f32[256,512]{1,0:T(8,128)}, f32[256,512]{1,0:T(8,128)}, f32[256,512]{1,0:T(8,128)S(1)}) fusion(f32[2048,640]{1,0:T(8,128)} %matrix_ref.5), kind=kLoop, calls=%fused_computation.16 | loop fusion | bytes 4194304 | tf_op jit(solution)/shard_map/slice | solution.py:299
  3.5 1.6 shard_map.46
  5.2 2.6 %copy-done = f32[2048,640]{1,0:T(8,128)S(1)} copy-done((f32[2048,640]{1,0:T(8,128)S(1)}, f32[2048,640]{1,0:T(8,128)}, u32[]{:S(2)}) %copy-start) | copy-done | bytes 5242904
  7.7 3.5 %shard_map.47.held_ref = f32[512,640]{1,0:T(8,128)S(1)} custom-call(s32[8,512]{1,0:T(8,128)S(1)} %get-tuple-element.41.table_ref, f32[2048,640]{1,0:T(8,128)S(1)} %copy-done), custom_call_target="tpu_custom_call" | custom-call | tf_op jit(solution)/shard_map/pallas_call | solution.py:318
  12.5 1.5 collective-permute-start.1
  14.7 1.3 collective-permute-start.4
  16.0 1.3 collective-permute-start.3
  17.3 1.3 collective-permute-start.2
  18.6 11.9 %collective-permute-done.4 = f32[64,512]{1,0:T(8,128)S(1)} collective-permute-done((f32[64,512]{1,0:T(8,128)}, f32[64,512]{1,0:T(8,128)S(1)}, u32[]{:S(2)}, u32[]{:S(2)}) %collective-permute-start.4) | collective-permute-done | bytes 131104 | tf_op jit(solution)/shard_map/ppermute | solution.py:305
  30.7 1.3 slice_select_fusion.2
  32.7 1.7 shard_map.48
  35.1 1.3 collective-permute-start.9
  37.9 27.1 %all_gather.12.near_ref.refs_0_ = f32[256,512]{1,0:T(8,128)S(1)} all-gather(f32[64,512]{1,0:T(8,128)S(1)} %select_select_fusion.2), channel_id=1, replica_groups=mesh['prow'=4,'along'=4,'side'=2] {'along'}, dimensions={0}, use_global_device_ids=true | all-gather | bytes 655360 | tf_op jit(solution)/shard_map/all_gather | solution.py:310
  66.9 1.9 %collective-permute-start.15 = (f32[256,512]{1,0:T(8,128)S(1)}, f32[256,512]{1,0:T(8,128)S(1)}, u32[]{:S(2)}, u32[]{:S(2)}) collective-permute-start(f32[256,512]{1,0:T(8,128)S(1)} %all_gather.12.near_ref.refs_0_), channel_id=1, source_target_pairs={{0,1},{2,3},{3,2},{4,5},{5,4},{6,7},{7,6},{8,9},{10,11},{11,10},{1... | collective-permute-start | bytes 1572872 | tf_op jit(solution)/shard_map/ppermute | solution.py:387
  68.9 1.3 collective-permute-start.14
  71.5 19.9 %all_gather.13.refs_2_ = f32[256,512]{1,0:T(8,128)} all-gather(f32[64,512]{1,0:T(8,128)S(1)} %select_select_fusion.1), channel_id=1, replica_groups=mesh['prow'=4,'along'=4,'side'=2] {'along'}, dimensions={0}, use_global_device_ids=true | all-gather | bytes 655360 | tf_op jit(solution)/shard_map/all_gather | solution.py:310
  92.9 1.6 collective-permute-start.21
  95.5 1.3 collective-permute-start.18
  96.8 3.7 %collective-permute-start.19 = (f32[256,512]{1,0:T(8,128)}, f32[256,512]{1,0:T(8,128)S(1)}, u32[]{:S(2)}, u32[]{:S(2)}) collective-permute-start(f32[256,512]{1,0:T(8,128)} %all_gather.13.refs_2_), channel_id=1, source_target_pairs={{0,1},{2,3},{3,2},{4,5},{5,4},{6,7},{7,6},{8,9},{10,11},{11,10},{1... | collective-permute-start | bytes 1572872 | tf_op jit(solution)/shard_map/ppermute | solution.py:387
  101.2 2.0 %collective-permute-done.18 = f32[64,512]{1,0:T(8,128)S(1)} collective-permute-done((f32[64,512]{1,0:T(8,128)S(1)}, f32[64,512]{1,0:T(8,128)S(1)}, u32[]{:S(2)}, u32[]{:S(2)}) %collective-permute-start.18) | collective-permute-done | bytes 131104 | tf_op jit(solution)/shard_map/ppermute | solution.py:305
  104.5 17.3 %all_gather.14.refs_4_ = f32[256,512]{1,0:T(8,128)S(1)} all-gather(f32[64,512]{1,0:T(8,128)} %select_select_fusion), channel_id=1, replica_groups=mesh['prow'=4,'along'=4,'side'=2] {'along'}, dimensions={0}, use_global_device_ids=true | all-gather | bytes 655360 | tf_op jit(solution)/shard_map/all_gather | solution.py:310
  121.9 1.7 fusion.1
  123.6 2.0 %collective-permute-start.22 = (f32[256,512]{1,0:T(8,128)S(1)}, f32[256,512]{1,0:T(8,128)}, u32[]{:S(2)}, u32[]{:S(2)}) collective-permute-start(f32[256,512]{1,0:T(8,128)S(1)} %all_gather.14.refs_4_), channel_id=1, source_target_pairs={{0,1},{2,3},{3,2},{4,5},{5,4},{6,7},{7,6},{8,9},{10,11},{11,10},{1... | collective-permute-start | bytes 1572872 | tf_op jit(solution)/shard_map/ppermute | solution.py:387
  125.6 1.4 broadcast_select_fusion
  127.9 1.3 collective-permute-start.23
  129.2 15.5 %all_gather.15.refs_6_ = f32[256,512]{1,0:T(8,128)S(1)} all-gather(f32[64,512]{1,0:T(8,128)} %fusion.1), channel_id=1, replica_groups=mesh['prow'=4,'along'=4,'side'=2] {'along'}, dimensions={0}, use_global_device_ids=true | all-gather | bytes 655360 | tf_op jit(solution)/shard_map/all_gather | solution.py:310
  144.8 1.2 broadcast_select_fusion.2
  146.0 3.4 %collective-permute-start.24 = (f32[256,512]{1,0:T(8,128)S(1)}, f32[256,512]{1,0:T(8,128)S(1)}, u32[]{:S(2)}, u32[]{:S(2)}) collective-permute-start(f32[256,512]{1,0:T(8,128)S(1)} %all_gather.15.refs_6_), channel_id=1, source_target_pairs={{0,1},{2,3},{3,2},{4,5},{5,4},{6,7},{7,6},{8,9},{10,11},{11,10},{1... | collective-permute-start | bytes 1572872 | tf_op jit(solution)/shard_map/ppermute | solution.py:387
  149.4 1.9 %collective-permute-start.25 = (f32[256,512]{1,0:T(8,128)}, f32[256,512]{1,0:T(8,128)S(1)}, u32[]{:S(2)}, u32[]{:S(2)}) collective-permute-start(f32[256,512]{1,0:T(8,128)} %collective-permute-done.23.refs_9_), channel_id=1, source_target_pairs={{16,24},{24,16},{17,25},{25,17},{18,26},{26,18},{19,27},{27,19},{2... | collective-permute-start | bytes 1572872 | tf_op jit(solution)/shard_map/ppermute | solution.py:368
  152.7 2.5 %shard_map.50 = (f32[512,640]{1,0:T(8,128)S(1)}, f32[256,640]{1,0:T(8,128)}) custom-call(s32[2]{0:T(128)S(1)} %copy-done.11, s32[512,128]{1,0:T(8,128)S(1)} %copy-done.6, f32[512,640]{1,0:T(8,128)S(1)} %copy-done.4, f32[256,640]{1,0:T(8,128)S(1)} %collective-permute-done.10.refs_0_, f32[256,640]{1,0:T(8,128)} %collective-permute-done.20.refs_1_), custom_call_target="tpu_custom_call" | custom-call | tf_op jit(solution)/shard_map/pallas_call | solution.py:336
  155.2 5.8 %shard_map.51 = (f32[512,640]{1,0:T(8,128)S(1)}, f32[512,640]{1,0:T(8,128)S(1)}) custom-call(s32[2]{0:T(128)S(1)} %copy-done.11, f32[512,640]{1,0:T(8,128)S(1)} %get-tuple-element.67.top_in_ref, f32[512,512]{1,0:T(8,128)S(1)} %copy-done.13, f32[512,512]{1,0:T(8,128)S(1)} %copy-done.14), custom_call_target="tpu_custom_call" | custom-call | flops 4026531840 | tf_op jit(solution)/shard_map/pallas_call | solution.py:342
  161.1 10.4 %shard_map.52 = f32[2048,640]{1,0:T(8,128)} custom-call(s32[2]{0:T(128)S(1)} %copy-done.11, s32[8,512]{1,0:T(8,128)S(1)} %get-tuple-element.41.table_ref, f32[512,640]{1,0:T(8,128)S(1)} %maximum_select_fusion.displaced_ref, f32[512,640]{1,0:T(8,128)S(1)} %get-tuple-element.68.weights_ref, f32[512,640]{1,0:T(8,128)S(1)} %get-tuple-element.69.top_ref, ...), custom_call_target="tpu_custom_call" | custom-call | flops 4026531840 | bytes 14680064 | tf_op jit(solution)/shard_map/pallas_call | solution.py:407
  (97 shorter events, 15.5 us)
Async XLA Ops:
  2.7 8.6 %collective-permute-start = (f32[256,512]{1,0:T(8,128)S(1)}, f32[256,512]{1,0:T(8,128)S(1)}, u32[]{:S(2)}, u32[]{:S(2)}) collective-permute-start(f32[256,512]{1,0:T(8,128)S(1)} %get-tuple-element.80), channel_id=1, source_target_pairs={{0,1},{8,9},{16,17},{24,25}} | collective-permute-start | bytes 1572872 | tf_op jit(solution)/shard_map/ppermute | solution.py:376
  3.5 29.2 %copy-start.9 = (s32[2]{0:T(128)}, s32[2]{0:T(128)S(1)}, u32[]{:S(2)}) copy-start(s32[2]{0:T(128)S(1)} %pad_add_fusion.where_ref) | copy-start | bytes 28
  5.1 27.6 %copy-start.5 = (s32[512,128]{1,0:T(8,128)}, s32[512,128]{1,0:T(8,128)S(1)}, u32[]{:S(2)}) copy-start(s32[512,128]{1,0:T(8,128)S(1)} %get-tuple-element.50.owner_ref) | copy-start | bytes 786436
  11.3 19.4 %collective-permute-start.5 = (f32[512,640]{1,0:T(8,128)S(1)}, f32[512,640]{1,0:T(8,128)}, u32[]{:S(2)}, u32[]{:S(2)}) collective-permute-start(f32[512,640]{1,0:T(8,128)S(1)} %shard_map.47.held_ref), channel_id=1, source_target_pairs={{0,8},{8,0},{16,24},{24,16},{1,9},{9,1},{17,25},{25,17},{2,10},{10... | collective-permute-start | bytes 3932168 | tf_op jit(solution)/shard_map/ppermute | solution.py:327
  12.5 18.2 %collective-permute-start.1 = (f32[256,512]{1,0:T(8,128)}, f32[256,512]{1,0:T(8,128)}, u32[]{:S(2)}, u32[]{:S(2)}) collective-permute-start(f32[256,512]{1,0:T(8,128)} %get-tuple-element.43), channel_id=1, source_target_pairs={{0,1},{8,9},{16,17},{24,25}} | collective-permute-start | bytes 1572872 | tf_op jit(solution)/shard_map/ppermute | solution.py:397
  14.0 78.3 %slice-start = ((s8[5242880]{0:T(1024)(128)(4,1)}), s8[1048576]{0:T(1024)(128)(4,1)S(1)}, s32[]{:S(2)}) async-start(s8[5242880]{0:T(1024)(128)(4,1)} %bitcast.3), calls=%async_computation | async-start | bytes 2097152
  14.7 15.8 %collective-permute-start.4 = (f32[64,512]{1,0:T(8,128)}, f32[64,512]{1,0:T(8,128)S(1)}, u32[]{:S(2)}, u32[]{:S(2)}) collective-permute-start(f32[64,512]{1,0:T(8,128)} %get-tuple-element.92), channel_id=1, source_target_pairs={{0,2},{1,3},{8,10},{9,11},{16,18},{17,19},{24,26},{25,27}} | collective-permute-start | bytes 393224 | tf_op jit(solution)/shard_map/ppermute | solution.py:305
  16.0 14.6 %collective-permute-start.3 = (f32[64,512]{1,0:T(8,128)}, f32[64,512]{1,0:T(8,128)}, u32[]{:S(2)}, u32[]{:S(2)}) collective-permute-start(f32[64,512]{1,0:T(8,128)} %get-tuple-element.93), channel_id=1, source_target_pairs={{0,4},{1,5},{8,12},{9,13},{16,20},{17,21},{24,28},{25,29}} | collective-permute-start | bytes 393224 | tf_op jit(solution)/shard_map/ppermute | solution.py:305
  17.3 13.3 %collective-permute-start.2 = (f32[64,512]{1,0:T(8,128)S(1)}, f32[64,512]{1,0:T(8,128)}, u32[]{:S(2)}, u32[]{:S(2)}) collective-permute-start(f32[64,512]{1,0:T(8,128)S(1)} %get-tuple-element.94), channel_id=1, source_target_pairs={{0,6},{1,7},{8,14},{9,15},{16,22},{17,23},{24,30},{25,31}} | collective-permute-start | bytes 393224 | tf_op jit(solution)/shard_map/ppermute | solution.py:305
  32.0 33.0 %collective-permute-start.6 = (f32[256,512]{1,0:T(8,128)S(1)}, f32[256,512]{1,0:T(8,128)S(1)}, u32[]{:S(2)}, u32[]{:S(2)}) collective-permute-start(f32[256,512]{1,0:T(8,128)S(1)} %copy-done.17), channel_id=1, source_target_pairs={{0,1},{8,9},{16,17},{24,25}} | collective-permute-start | bytes 1572872 | tf_op jit(solution)/shard_map/ppermute | solution.py:397
  32.7 59.5 %slice-start.1 = ((s8[5242880]{0:T(1024)(128)(4,1)}), s8[4194304]{0:T(1024)(128)(4,1)S(1)}, s32[]{:S(2)}) async-start(s8[5242880]{0:T(1024)(128)(4,1)} %bitcast.3), calls=%async_computation.1 | async-start | bytes 8388608
  34.4 31.7 %copy-start.3 = (f32[512,640]{1,0:T(8,128)}, f32[512,640]{1,0:T(8,128)S(1)}, u32[]{:S(2)}) copy-start(f32[512,640]{1,0:T(8,128)S(1)} %get-tuple-element.66.held_ref) | copy-start | bytes 3932164
  34.4 30.6 %collective-permute-start.10 = (f32[256,640]{1,0:T(8,128)S(1)}, f32[256,640]{1,0:T(8,128)S(1)}, u32[]{:S(2)}, u32[]{:S(2)}) collective-permute-start(f32[256,640]{1,0:T(8,128)S(1)} %get-tuple-element.52), channel_id=1, source_target_pairs={{0,16},{8,24},{16,0},{24,8},{1,17},{9,25},{17,1},{25,9},{2,18},{10... | collective-permute-start | bytes 1966088 | tf_op jit(solution)/shard_map/ppermute | solution.py:331
  35.1 29.9 %collective-permute-start.9 = (f32[64,512]{1,0:T(8,128)S(1)}, f32[64,512]{1,0:T(8,128)S(1)}, u32[]{:S(2)}, u32[]{:S(2)}) collective-permute-start(f32[64,512]{1,0:T(8,128)S(1)} %get-tuple-element.89), channel_id=1, source_target_pairs={{0,2},{1,3},{8,10},{9,11},{16,18},{17,19},{24,26},{25,27}} | collective-permute-start | bytes 393224 | tf_op jit(solution)/shard_map/ppermute | solution.py:305
  36.4 28.6 %collective-permute-start.8 = (f32[64,512]{1,0:T(8,128)S(1)}, f32[64,512]{1,0:T(8,128)S(1)}, u32[]{:S(2)}, u32[]{:S(2)}) collective-permute-start(f32[64,512]{1,0:T(8,128)S(1)} %get-tuple-element.90), channel_id=1, source_target_pairs={{0,4},{1,5},{8,12},{9,13},{16,20},{17,21},{24,28},{25,29}} | collective-permute-start | bytes 393224 | tf_op jit(solution)/shard_map/ppermute | solution.py:305
  37.0 29.1 %copy-start.16 = (f32[256,512]{1,0:T(8,128)S(1)}, f32[256,512]{1,0:T(8,128)}, u32[]{:S(2)}) copy-start(f32[256,512]{1,0:T(8,128)} %get-tuple-element.54) | copy-start | bytes 1572868
  37.1 27.9 %collective-permute-start.7 = (f32[64,512]{1,0:T(8,128)S(1)}, f32[64,512]{1,0:T(8,128)S(1)}, u32[]{:S(2)}, u32[]{:S(2)}) collective-permute-start(f32[64,512]{1,0:T(8,128)S(1)} %get-tuple-element.91), channel_id=1, source_target_pairs={{0,6},{1,7},{8,14},{9,15},{16,22},{17,23},{24,30},{25,31}} | collective-permute-start | bytes 393224 | tf_op jit(solution)/shard_map/ppermute | solution.py:305
  66.2 25.9 %collective-permute-start.11 = (f32[256,512]{1,0:T(8,128)S(1)}, f32[256,512]{1,0:T(8,128)S(1)}, u32[]{:S(2)}, u32[]{:S(2)}) collective-permute-start(f32[256,512]{1,0:T(8,128)S(1)} %copy-done.16), channel_id=1, source_target_pairs={{0,1},{8,9},{16,17},{24,25}} | collective-permute-start | bytes 1572872 | tf_op jit(solution)/shard_map/ppermute | solution.py:397
  66.9 25.2 %collective-permute-start.15 = (f32[256,512]{1,0:T(8,128)S(1)}, f32[256,512]{1,0:T(8,128)S(1)}, u32[]{:S(2)}, u32[]{:S(2)}) collective-permute-start(f32[256,512]{1,0:T(8,128)S(1)} %all_gather.12.near_ref.refs_0_), channel_id=1, source_target_pairs={{0,1},{2,3},{3,2},{4,5},{5,4},{6,7},{7,6},{8,9},{10,11},{11,10},{1... | collective-permute-start | bytes 1572872 | tf_op jit(solution)/shard_map/ppermute | solution.py:387
  68.9 22.6 %collective-permute-start.14 = (f32[64,512]{1,0:T(8,128)S(1)}, f32[64,512]{1,0:T(8,128)S(1)}, u32[]{:S(2)}, u32[]{:S(2)}) collective-permute-start(f32[64,512]{1,0:T(8,128)S(1)} %get-tuple-element.86), channel_id=1, source_target_pairs={{0,2},{1,3},{8,10},{9,11},{16,18},{17,19},{24,26},{25,27}} | collective-permute-start | bytes 393224 | tf_op jit(solution)/shard_map/ppermute | solution.py:305
  70.2 21.3 %collective-permute-start.13 = (f32[64,512]{1,0:T(8,128)S(1)}, f32[64,512]{1,0:T(8,128)S(1)}, u32[]{:S(2)}, u32[]{:S(2)}) collective-permute-start(f32[64,512]{1,0:T(8,128)S(1)} %get-tuple-element.87), channel_id=1, source_target_pairs={{0,4},{1,5},{8,12},{9,13},{16,20},{17,21},{24,28},{25,29}} | collective-permute-start | bytes 393224 | tf_op jit(solution)/shard_map/ppermute | solution.py:305
  70.8 20.6 %collective-permute-start.12 = (f32[64,512]{1,0:T(8,128)S(1)}, f32[64,512]{1,0:T(8,128)S(1)}, u32[]{:S(2)}, u32[]{:S(2)}) collective-permute-start(f32[64,512]{1,0:T(8,128)S(1)} %get-tuple-element.88), channel_id=1, source_target_pairs={{0,6},{1,7},{8,14},{9,15},{16,22},{17,23},{24,30},{25,31}} | collective-permute-start | bytes 393224 | tf_op jit(solution)/shard_map/ppermute | solution.py:305
  92.1 31.4 %collective-permute-start.20 = (f32[256,640]{1,0:T(8,128)S(1)}, f32[256,640]{1,0:T(8,128)}, u32[]{:S(2)}, u32[]{:S(2)}) collective-permute-start(f32[256,640]{1,0:T(8,128)S(1)} %collective-permute-done.10.refs_0_), channel_id=1, source_target_pairs={{0,8},{8,0},{16,24},{24,16},{1,9},{9,1},{17,25},{25,17},{2,10},{10... | collective-permute-start | bytes 1966088 | tf_op jit(solution)/shard_map/ppermute | solution.py:333
  92.9 30.6 %collective-permute-start.21 = (f32[512,512]{1,0:T(8,128)}, f32[512,512]{1,0:T(8,128)}, u32[]{:S(2)}, u32[]{:S(2)}) collective-permute-start(f32[512,512]{1,0:T(8,128)} %shard_map.49), channel_id=1, source_target_pairs={{0,8},{1,9},{2,10},{3,11},{4,12},{5,13},{6,14},{7,15}} | collective-permute-start | bytes 3145736 | tf_op jit(solution)/shard_map/ppermute | solution.py:363
  95.5 7.7 %collective-permute-start.18 = (f32[64,512]{1,0:T(8,128)S(1)}, f32[64,512]{1,0:T(8,128)S(1)}, u32[]{:S(2)}, u32[]{:S(2)}) collective-permute-start(f32[64,512]{1,0:T(8,128)S(1)} %get-tuple-element.83), channel_id=1, source_target_pairs={{0,2},{1,3},{8,10},{9,11},{16,18},{17,19},{24,26},{25,27}} | collective-permute-start | bytes 393224 | tf_op jit(solution)/shard_map/ppermute | solution.py:305
  96.8 26.7 %collective-permute-start.19 = (f32[256,512]{1,0:T(8,128)}, f32[256,512]{1,0:T(8,128)S(1)}, u32[]{:S(2)}, u32[]{:S(2)}) collective-permute-start(f32[256,512]{1,0:T(8,128)} %all_gather.13.refs_2_), channel_id=1, source_target_pairs={{0,1},{2,3},{3,2},{4,5},{5,4},{6,7},{7,6},{8,9},{10,11},{11,10},{1... | collective-permute-start | bytes 1572872 | tf_op jit(solution)/shard_map/ppermute | solution.py:387
  100.5 21.4 %collective-permute-start.17 = (f32[64,512]{1,0:T(8,128)}, f32[64,512]{1,0:T(8,128)S(1)}, u32[]{:S(2)}, u32[]{:S(2)}) collective-permute-start(f32[64,512]{1,0:T(8,128)} %get-tuple-element.84), channel_id=1, source_target_pairs={{0,4},{1,5},{8,12},{9,13},{16,20},{17,21},{24,28},{25,29}} | collective-permute-start | bytes 393224 | tf_op jit(solution)/shard_map/ppermute | solution.py:305
  103.9 18.0 %collective-permute-start.16 = (f32[64,512]{1,0:T(8,128)}, f32[64,512]{1,0:T(8,128)S(1)}, u32[]{:S(2)}, u32[]{:S(2)}) collective-permute-start(f32[64,512]{1,0:T(8,128)} %get-tuple-element.85), channel_id=1, source_target_pairs={{0,6},{1,7},{8,14},{9,15},{16,22},{17,23},{24,30},{25,31}} | collective-permute-start | bytes 393224 | tf_op jit(solution)/shard_map/ppermute | solution.py:305
  123.6 22.4 %collective-permute-start.22 = (f32[256,512]{1,0:T(8,128)S(1)}, f32[256,512]{1,0:T(8,128)}, u32[]{:S(2)}, u32[]{:S(2)}) collective-permute-start(f32[256,512]{1,0:T(8,128)S(1)} %all_gather.14.refs_4_), channel_id=1, source_target_pairs={{0,1},{2,3},{3,2},{4,5},{5,4},{6,7},{7,6},{8,9},{10,11},{11,10},{1... | collective-permute-start | bytes 1572872 | tf_op jit(solution)/shard_map/ppermute | solution.py:387
  127.9 18.0 %collective-permute-start.23 = (f32[256,512]{1,0:T(8,128)}, f32[256,512]{1,0:T(8,128)}, u32[]{:S(2)}, u32[]{:S(2)}) collective-permute-start(f32[256,512]{1,0:T(8,128)} %slice_select_fusion), channel_id=1, source_target_pairs={{0,16},{8,24},{1,17},{9,25},{2,18},{10,26},{3,19},{11,27},{4,20},{... | collective-permute-start | bytes 1572872 | tf_op jit(solution)/shard_map/ppermute | solution.py:367
  146.0 15.1 %collective-permute-start.24 = (f32[256,512]{1,0:T(8,128)S(1)}, f32[256,512]{1,0:T(8,128)S(1)}, u32[]{:S(2)}, u32[]{:S(2)}) collective-permute-start(f32[256,512]{1,0:T(8,128)S(1)} %all_gather.15.refs_6_), channel_id=1, source_target_pairs={{0,1},{2,3},{3,2},{4,5},{5,4},{6,7},{7,6},{8,9},{10,11},{11,10},{1... | collective-permute-start | bytes 1572872 | tf_op jit(solution)/shard_map/ppermute | solution.py:387
  149.4 11.7 %collective-permute-start.25 = (f32[256,512]{1,0:T(8,128)}, f32[256,512]{1,0:T(8,128)S(1)}, u32[]{:S(2)}, u32[]{:S(2)}) collective-permute-start(f32[256,512]{1,0:T(8,128)} %collective-permute-done.23.refs_9_), channel_id=1, source_target_pairs={{16,24},{24,16},{17,25},{25,17},{18,26},{26,18},{19,27},{27,19},{2... | collective-permute-start | bytes 1572872 | tf_op jit(solution)/shard_map/ppermute | solution.py:368
  (17 other events, 84.0 us)

commit v7 on v4

--- a/solution.py
+++ b/solution.py
@@ -138,38 +138,70 @@
         half_ref[...] = merged_ref[high, :]
 
 
-def factor_kernel(where_ref, top_in_ref, lower_ref, upper_ref, weights_ref, top_ref):
-    nb, cols = top_in_ref.shape
-    u = jnp.dot(
-        lower_ref[...], top_in_ref[...], precision=HIGHEST,
-        preferred_element_type=jnp.float32,
-    )
+def split(x):
+    hi = x.astype(jnp.bfloat16)
+    return hi, (x - hi.astype(jnp.float32)).astype(jnp.bfloat16)
+
+
+def product(a, b):
+    dot = functools.partial(jnp.dot, preferred_element_type=jnp.float32)
+    return dot(a[1], b[0]) + dot(a[0], b[1]) + dot(a[0], b[0])
+
+
+def factor_kernel(
+    where_ref, owner_ref, held_ref, one_ref, two_ref, before_ref, lower_ref, upper_ref,
+    weights_ref, top_ref, displaced_ref, new_top, *, log,
+):
+    me = where_ref[0]
+    mine, theirs = me >> log, (me >> log) ^ 1
+    nb, cols = held_ref.shape
+    half = nb // 2
+
+    def merge(rows, piece):
+        group = owner_ref[rows, :] >> log
+        take = (group == theirs) | ((theirs == 0) & (group != mine))
+        for q in range(cols // LANES):
+            lane = slice(q * LANES, (q + 1) * LANES)
+            new_top[rows, lane] = jnp.where(take, piece[:, lane], held_ref[rows, lane])
+
+        @pl.when(mine == 1)
+        def _():
+            displaced_ref[rows, :] = piece[...]
+
+    @pl.when(mine != 1)
+    def _():
+        displaced_ref[...] = before_ref[...]
+
+    for odd, (first, second) in enumerate([(one_ref, two_ref), (two_ref, one_ref)]):
+        @pl.when((me & 1) == odd)
+        def _():
+            merge(slice(0, half), first)
+            merge(slice(half, nb), second)
+
+    u = product(split(lower_ref[...]), split(new_top[...]))
     top_ref[...] = u
-    weights_ref[...] = jnp.dot(
-        upper_ref[...], u, precision=HIGHEST, preferred_element_type=jnp.float32
-    )
+    weights_ref[...] = product(split(upper_ref[...]), split(u))
 
     @pl.when(where_ref[1] == 0)
     def _():
-        top_ref[:, :nb] = top_in_ref[:, :nb]
+        top_ref[:, :nb] = new_top[:, :nb]
         weights_ref[:, :nb] = -upper_ref[...]
 
 
-def old_top_kernel(where_ref, matrix_ref, near_ref, far_ref, top_ref, sem):
+def old_top_kernel(where_ref, matrix_ref, line_ref, cross_ref, top_ref, sem):
     nb = top_ref.shape[0]
-    from_matrix = pltpu.make_async_copy(
-        matrix_ref.at[pl.ds(0, nb), pl.ds(0, nb)], top_ref, sem
-    )
+    part = nb // 2
 
     @pl.when(where_ref[0] == 0)
     def _():
-        fetch_panel(where_ref, matrix_ref, [near_ref, far_ref], top_ref, sem)
-        from_matrix.wait()
-
-
-def fetch_panel(where_ref, matrix_ref, bufs, out_ref, sem):
+        fetch_panel(where_ref, matrix_ref, [(0, line_ref, 0, cross_ref, 0)], part, top_ref, sem)
+        pltpu.make_async_copy(
+            matrix_ref.at[pl.ds(0, nb), pl.ds(0, nb)], top_ref, sem
+        ).wait()
+
+
+def fetch_panel(where_ref, matrix_ref, items, part, out_ref, sem):
     rows, nb = out_ref.shape
-    half = rows // len(bufs)
     col = where_ref[1]
 
     @pl.when(col == 0)
@@ -181,14 +213,17 @@
     for y in range(2):
         @pl.when((col > 0) & ((col & 1) == y))
         def _():
-            for k, buf in enumerate(bufs):
-                at = half * (k if y else k ^ 1)
-                pltpu.make_async_copy(buf, out_ref.at[pl.ds(at, half), :], sem).start()
+            for row, line, line_at, cross, cross_at in items:
+                for k, (ref, at) in enumerate([(line, line_at), (cross, cross_at)]):
+                    to = row + part * (k if y else 1 - k)
+                    pltpu.make_async_copy(
+                        ref.at[pl.ds(at, part), :], out_ref.at[pl.ds(to, part), :], sem
+                    ).start()
 
 
 def final_kernel(
     where_ref, table_ref, displaced_ref, weights_ref, top_ref, matrix_ref,
-    *refs, n_bufs, n_tops, block,
+    *refs, n_bufs, n_tops, places, part, block,
 ):
     bufs, tops, out_ref = refs[:n_bufs], refs[n_bufs : n_bufs + n_tops], refs[n_bufs + n_tops]
     mat, pan, low, w_hi, w_lo, result, in_sem, low_sem, mat_sem, out_sem = refs[
@@ -204,7 +239,8 @@
     load.start()
     whole_panel = pltpu.make_async_copy(matrix_ref.at[:, pl.ds(0, nb)], pan, in_sem)
 
-    fetch_panel(where_ref, matrix_ref, bufs, pan, in_sem)
+    items = [(at, bufs[a], i, bufs[b], j) for at, a, i, b, j in places]
+    fetch_panel(where_ref, matrix_ref, items, part, pan, in_sem)
 
     @pl.when(row == 1)
     def _():
@@ -279,7 +315,7 @@
     return lax.optimization_barrier(values)
 
 
-def local(matrix, pivots, lower_inverse, upper_inverse, *, n_rows, n_cols, groups):
+def local(matrix, pivots, lower_inverse, upper_inverse, *, n_rows, n_cols):
     row_dev, cols = matrix.shape
     nb = pivots.shape[0]
     f32 = jnp.float32
@@ -289,25 +325,36 @@
     slot = jax.ShapeDtypeStruct((nb, cols), f32)
     half_slot = jax.ShapeDtypeStruct((nb // 2, cols), f32)
 
+    groups = row_dev // (2 * nb)
     depth = n_cols // 2
-    half_rows = row_dev // (2 * groups)
-    piece_rows = half_rows // depth
+    part = nb // 2
+    piece = 2 * part // depth
     lanes = [[z * 2 + y for z in range(depth)] for y in range(2)]
     across = [(0, 1)] + [(p, p ^ 1) for p in range(2, n_cols)]
 
-    def panel_rows(start, size):
-        return lax.slice(matrix, (start, 0), (start + size, nb))
-
-    def scatter(line):
-        pieces = [line[z * piece_rows : (z + 1) * piece_rows] for z in range(depth)]
-        mine = pieces[0]
-        for z in range(1, depth):
-            came = lax.ppermute(pieces[z], "pcol", [(0, 2 * z), (1, 2 * z + 1)])
-            mine = jnp.where(col // 2 == z, came, mine)
+    def panel(g, s, y):
+        start = 2 * nb * g + nb * s + part * (1 - y)
+        return lax.slice(matrix, (start, 0), (start + part, nb))
+
+    def feed(rows):
+        return lax.ppermute(rows, "pcol", [(0, 1)])
+
+    def scatter(run, s):
+        mine = None
+        for k in reversed(range(depth // 2)):
+            z = k + s * (depth // 2)
+            came = run[k * piece : (k + 1) * piece]
+            if z:
+                came = lax.ppermute(came, "pcol", [(0, 2 * z), (1, 2 * z + 1)])
+            mine = came if mine is None else jnp.where(col // 2 == z, came, mine)
         return mine
 
     def gather(piece):
         return lax.all_gather(piece, "pcol", axis=0, tiled=True, axis_index_groups=lanes)
+
+    def cross(line, g):
+        parts = [line] if g else [line[:part], line[part:]]
+        return [lax.ppermute(rows, "pcol", across) for rows in parts]
 
     def exchange():
         table, owner = call(
@@ -329,20 +376,23 @@
             else:
                 near = [(p, p ^ 1) for p in range(n_rows)]
                 (one,) = yield (lax.ppermute(half, "prow", far),)
-                (one,) = yield (one,)
                 (two,) = yield (lax.ppermute(one, "prow", near),)
                 arrived = [one, two]
-                whole = both_halves(one, two)
+                whole = None if 2 << log == n_rows else both_halves(one, two)
+            if 2 << log == n_rows:
+                break
             held, half = call(
                 functools.partial(merge_kernel, log=log, halves=log > 0),
                 (slot, half_slot), [SMEM] + [VMEM] * (2 + len(arrived)), (VMEM, VMEM),
             )(here, owner, held, *arrived)
-            displaced = jnp.where((row >> log) == 1, whole, displaced)
+            displaced = jnp.where((row >> log) == 1, whole, displaced) if log else whole
             log += 1
-        weights, top = call(
-            factor_kernel, (slot, slot), [SMEM, VMEM, VMEM, VMEM], (VMEM, VMEM),
-            flops=4 * nb * nb * cols * 6,
-        )(here, held, lower_inverse, upper_inverse)
+        held, arrived = yield held, arrived
+        weights, top, displaced = call(
+            functools.partial(factor_kernel, log=log), (slot,) * 3,
+            [SMEM] + [VMEM] * 7, (VMEM,) * 3, [pltpu.VMEM((nb, cols), f32)], vmem=24 << 20,
+            flops=4 * nb * nb * cols * 3,
+        )(here, owner, held, *arrived, displaced, lower_inverse, upper_inverse)
         return table, displaced, weights, top
 
     def both_halves(one, two):
@@ -373,39 +423,55 @@
         return tops
 
     rows_side, top_side = Rider(exchange()), Rider(spread_top())
-    fed = lax.ppermute(panel_rows(0, half_rows), "pcol", [(0, 1)])
-    mine, along, other = None, [], []
-    for g in range(groups + 2):
-        if g == 3:
-            top_side.value = (along[0], other[0])
-        line, crossed = along[g - 2] if g > 1 else None, other[g - 3] if g > 3 else None
-        bundle = (fed, mine, line, crossed, rows_side.value, top_side.value)
-        fed, mine, line, crossed, rows_side.value, top_side.value = tie(*bundle)
-        if g > 3:
-            other[g - 3] = crossed
-        if g > 1:
-            other.append(lax.ppermute(line, "pcol", across))
-        if 0 < g <= groups:
-            along.append(gather(mine))
-        if g < groups:
-            run = jnp.where(
-                col == 0, panel_rows((2 * g + 1) * half_rows, half_rows), fed
-            )
-            if g + 1 < groups:
-                run, ahead = tie(run, panel_rows(2 * (g + 1) * half_rows, half_rows))
-            mine = scatter(run)
-            fed = lax.ppermute(ahead, "pcol", [(0, 1)]) if g + 1 < groups else None
+    turns = [(g, s) for g in range(groups) for s in (1, 0)]
+    fed = feed(panel(0, 1, 1))
+    far_piece = near_piece = None
+    along, other = [], []
+    for t, (g, s) in enumerate(turns):
+        if s and g:
+            fed, far_piece, near_piece = tie(fed, far_piece, near_piece)
+        elif g:
+            fed, along[g - 1], rows_side.value = tie(fed, along[g - 1], rows_side.value)
         else:
-            mine = None
-        rows_side.go()
-        if g >= 3:
-            top_side.go()
+            fed, rows_side.value = tie(fed, rows_side.value)
+        run = jnp.where(col == 0, panel(g, s, 0), fed)
+        if t + 1 < len(turns):
+            run, ahead = tie(run, panel(*turns[t + 1], 1))
+            fed = feed(ahead)
+        if s and g:
+            along.append(gather(jnp.where(col // 2 < depth // 2, near_piece, far_piece)))
+        elif g:
+            other.append(cross(along[g - 1], g - 1))
+        if s:
+            far_piece = scatter(run, s)
+        else:
+            near_piece = scatter(run, s)
+        if g == 0 or s == 0:
+            rows_side.go()
+    far_piece, near_piece, rows_side.value = tie(far_piece, near_piece, rows_side.value)
+    along.append(gather(jnp.where(col // 2 < depth // 2, near_piece, far_piece)))
+    rows_side.go()
+    along[-1], other[0], rows_side.value = tie(along[-1], other[0], rows_side.value)
+    other.append(cross(along[-1], groups - 1))
+    top_side.value = (along[0], other[0][0])
+    top_side.go()
     table, displaced, weights, top = rows_side.finish()
     tops = top_side.finish()
-    bufs = [b for pair in zip(along, other) for b in pair]
+    bufs = along + [ref for refs in other for ref in refs]
+    places = [
+        (
+            2 * nb * g + nb * s, g, s * part,
+            groups + sum(map(len, other[:g])) + (s if len(other[g]) > 1 else 0),
+            0 if len(other[g]) > 1 else s * part,
+        )
+        for g in range(groups) for s in range(2)
+    ]
 
     return call(
-        functools.partial(final_kernel, n_bufs=len(bufs), n_tops=len(tops), block=256),
+        functools.partial(
+            final_kernel, n_bufs=len(bufs), n_tops=len(tops), places=places, part=part,
+            block=256,
+        ),
         jax.ShapeDtypeStruct(matrix.shape, f32),
         [SMEM, SMEM, VMEM, VMEM, VMEM, ANY] + [ANY] * (len(bufs) + len(tops)),
         ANY,
@@ -444,7 +510,7 @@
 def solution(mesh):
     n_rows, n_cols = mesh.shape["prow"], mesh.shape["pcol"]
     return jax.shard_map(
-        functools.partial(local, n_rows=n_rows, n_cols=n_cols, groups=4),
+        functools.partial(local, n_rows=n_rows, n_cols=n_cols),
         mesh=mesh,
         in_specs=(P("prow", "pcol"), P(), P(), P()),
         out_specs=P("prow", "pcol"),

time: 175 us -> 195 us (1.11)
  waiting for transfers between devices: 14 us -> 97.4 us
  blocking collectives: 79.9 us -> 0 us
  between operations: 0.79 us -> 13.9 us
  local copies, waits for them, and re-layouts: 8.87 us -> 21.5 us
  starting transfers between devices: 32 us -> 26.6 us
  Pallas kernels: 26.4 us -> 21.7 us
    all_gather x4 -> x0, blocking collectives: 79.9 us -> none  [gather(): lax.all_gather(piece, 'pcol', axis=0, tiled=True, axis_index_groups=lanes)]
    ppermute x20 -> x13, waiting for transfers between devices: 14 us -> 53.7 us  [the longest x6 33.7 us: scatter(): came = lax.ppermute(came, 'pcol', [(0, 2 * z), (1, 2 * z + 1)])]
    all_gather x0 -> x2, waiting for transfers between devices: none -> 20.6 us  [gather(): lax.all_gather(piece, 'pcol', axis=0, tiled=True, axis_index_groups=lanes)]
    ppermute x1, waiting for transfers between devices: 0.01 us -> 13.8 us  [spread_top(): one, = (yield (lax.ppermute(half, 'prow', far),))]
    unnamed x46 -> x44, local copies, waits for them, and re-layouts: 4.55 us -> 16.3 us
    ppermute x1, waiting for transfers between devices: 0.01 us -> 9.29 us  [exchange(): one, = (yield (lax.ppermute(half, 'prow', far),))]
    ppermute x20 -> x13, starting transfers between devices: 26.4 us -> 21.9 us  [the longest x3 9.49 us: cross(): return [lax.ppermute(rows, 'pcol', across) for rows in parts]]
    pallas_call x2 -> x1, Pallas kernels: 4.24 us -> 0.78 us  [exchange(): call(functools.partial(merge_kernel, log=log, halves=log > 0), (slot, hal...]
  transfers between devices with their start and end apart: 26 -> 21, of which waited for: 2 -> 8; matrix products, arithmetic and copies ran while one was open for 5% -> 6% of each run, Pallas kernels for 9% -> 6%
where the time goes in v7:
time: 195 us; the launch traced here: 193 us
  waiting for transfers between devices  97.4 us (50%)
  starting transfers between devices  26.6 us (14%)
  Pallas kernels  21.7 us (11%)
  local copies, waits for them, and re-layouts  21.5 us (11%)
  between operations  13.9 us (7%)
  other arithmetic  11.6 us (6%)
    ppermute x6, waiting for transfers between devices, scatter(): came = lax.ppermute(came, 'pcol', [(0, 2 * z), (1, 2 * z + 1)])  33.7 us
    all_gather x2, waiting for transfers between devices, gather(): lax.all_gather(piece, 'pcol', axis=0, tiled=True, axis_index_groups=lanes)  20.6 us
    ppermute x3, waiting for transfers between devices, cross(): return [lax.ppermute(rows, 'pcol', across) for rows in parts]  19.9 us
    unnamed x44, local copies, waits for them, and re-layouts  16.3 us
    ppermute x1, waiting for transfers between devices, spread_top(): one, = (yield (lax.ppermute(half, 'prow', far),))  13.8 us
    pallas_call x1, Pallas kernels, local(): call(functools.partial(final_kernel, n_bufs=len(bufs), n_tops=len(tops),...  9.79 us
    ppermute x3, starting transfers between devices, cross(): return [lax.ppermute(rows, 'pcol', across) for rows in parts]  9.49 us
    ppermute x1, waiting for transfers between devices, exchange(): one, = (yield (lax.ppermute(half, 'prow', far),))  9.29 us
  transfers between devices with their start and end apart: 21, of which 8 were waited for; matrix products, arithmetic and copies ran while one was open for 6% of the time, Pallas kernels for 6%

profile of v7, /device:TPU:10, one launch (start us, length us, event | category | flops | bytes accessed | tf_op | source)
XLA Modules:
  0.0 192.6 jit_solution(8241180961322108021)
XLA Ops:
  6.5 2.7 %fusion = (f32[256,512]{1,0:T(8,128)}, f32[256,512]{1,0:T(8,128)}, f32[256,512]{1,0:T(8,128)}, f32[256,512]{1,0:T(8,128)S(1)}) fusion(f32[2048,640]{1,0:T(8,128)} %matrix_ref.5), kind=kLoop, calls=%fused_computation.13 | loop fusion | bytes 4194304 | tf_op jit(solution)/shard_map/slice | solution.py:337
  9.2 1.5 collective-permute-start
  11.4 1.6 shard_map.46
  13.1 2.5 %copy-done = f32[2048,640]{1,0:T(8,128)S(1)} copy-done((f32[2048,640]{1,0:T(8,128)S(1)}, f32[2048,640]{1,0:T(8,128)}, u32[]{:S(2)}) %copy-start) | copy-done | bytes 5242904
  15.6 3.5 %shard_map.47.held_ref = f32[512,640]{1,0:T(8,128)S(1)} custom-call(s32[8,512]{1,0:T(8,128)S(1)} %get-tuple-element.37.table_ref, f32[2048,640]{1,0:T(8,128)S(1)} %copy-done), custom_call_target="tpu_custom_call" | custom-call | tf_op jit(solution)/shard_map/pallas_call | solution.py:365
  19.2 1.3 slice_select_fusion.2
  22.0 1.4 collective-permute-start.5
  23.4 1.4 collective-permute-start.4
  24.8 1.5 slice_select_fusion.3
  26.3 1.5 collective-permute-start.3
  30.8 26.2 %collective-permute-done.6 = f32[128,512]{1,0:T(8,128)} collective-permute-done((f32[128,512]{1,0:T(8,128)}, f32[128,512]{1,0:T(8,128)}, u32[]{:S(2)}, u32[]{:S(2)}) %collective-permute-start.6) | collective-permute-done | bytes 262176 | tf_op jit(solution)/shard_map/ppermute | solution.py:348
  62.5 1.5 collective-permute-start.9
  65.4 1.4 collective-permute-start.7
  66.8 9.3 %collective-permute-done.10.one_ref = f32[256,640]{1,0:T(8,128)S(1)} collective-permute-done((f32[256,640]{1,0:T(8,128)S(1)}, f32[256,640]{1,0:T(8,128)S(1)}, u32[]{:S(2)}, u32[]{:S(2)}) %collective-permute-start.10) | collective-permute-done | bytes 655392 | tf_op jit(solution)/shard_map/ppermute | solution.py:378
  76.1 20.5 %all-gather.3.cloned.1.call-done.line_ref.refs_0_ = f32[512,512]{1,0:T(8,128)} async-done(((f32[128,512]{1,0:T(8,128)}), f32[512,512]{1,0:T(8,128)}) %all-gather.3.cloned.1.call-update) | async-done | bytes 1048592 | tf_op jit(solution)/shard_map/all_gather | solution.py:353
  96.6 1.4 slice_select_fusion.1
  98.0 1.3 collective-permute-start.11
  101.1 7.5 %collective-permute-done.11 = f32[128,512]{1,0:T(8,128)S(1)} collective-permute-done((f32[128,512]{1,0:T(8,128)S(1)}, f32[128,512]{1,0:T(8,128)S(1)}, u32[]{:S(2)}, u32[]{:S(2)}) %collective-permute-start.11) | collective-permute-done | bytes 262176 | tf_op jit(solution)/shard_map/ppermute | solution.py:348
  109.5 3.1 %collective-permute-start.14 = (f32[256,512]{1,0:T(8,128)S(1)}, f32[256,512]{1,0:T(8,128)S(1)}, u32[]{:S(2)}, u32[]{:S(2)}) collective-permute-start(f32[256,512]{1,0:T(8,128)S(1)} %get-tuple-element.73), channel_id=1, source_target_pairs={{0,1},{2,3},{3,2},{4,5},{5,4},{6,7},{7,6},{8,9},{10,11},{11,10},{1... | collective-permute-start | bytes 1572872 | tf_op jit(solution)/shard_map/ppermute | solution.py:357
  112.6 2.8 %collective-permute-start.13 = (f32[256,512]{1,0:T(8,128)S(1)}, f32[256,512]{1,0:T(8,128)S(1)}, u32[]{:S(2)}, u32[]{:S(2)}) collective-permute-start(f32[256,512]{1,0:T(8,128)S(1)} %get-tuple-element.74), channel_id=1, source_target_pairs={{0,1},{2,3},{3,2},{4,5},{5,4},{6,7},{7,6},{8,9},{10,11},{11,10},{1... | collective-permute-start | bytes 1572872 | tf_op jit(solution)/shard_map/ppermute | solution.py:357
  115.4 10.9 %collective-permute-done.14.refs_3_ = f32[256,512]{1,0:T(8,128)S(1)} collective-permute-done((f32[256,512]{1,0:T(8,128)S(1)}, f32[256,512]{1,0:T(8,128)S(1)}, u32[]{:S(2)}, u32[]{:S(2)}) %collective-permute-start.14) | collective-permute-done | bytes 524320 | tf_op jit(solution)/shard_map/ppermute | solution.py:357
  127.1 9.1 %collective-permute-done.13.cross_ref.refs_2_ = f32[256,512]{1,0:T(8,128)S(1)} collective-permute-done((f32[256,512]{1,0:T(8,128)S(1)}, f32[256,512]{1,0:T(8,128)S(1)}, u32[]{:S(2)}, u32[]{:S(2)}) %collective-permute-start.13) | collective-permute-done | bytes 524320 | tf_op jit(solution)/shard_map/ppermute | solution.py:357
  136.3 2.5 %copy-done.1 = f32[2048,640]{1,0:T(8,128)S(1)} copy-done((f32[2048,640]{1,0:T(8,128)S(1)}, f32[2048,640]{1,0:T(8,128)}, u32[]{:S(2)}) %copy-start.1) | copy-done | bytes 5242904
  140.9 3.6 %collective-permute-start.15 = (f32[512,512]{1,0:T(8,128)}, f32[512,512]{1,0:T(8,128)S(1)}, u32[]{:S(2)}, u32[]{:S(2)}) collective-permute-start(f32[512,512]{1,0:T(8,128)} %all-gather.5.cloned.1.call-done.refs_1_), channel_id=1, source_target_pairs={{0,1},{2,3},{3,2},{4,5},{5,4},{6,7},{7,6},{8,9},{10,11},{11,10},{1... | collective-permute-start | bytes 3145736 | tf_op jit(solution)/shard_map/ppermute | solution.py:357
  144.5 1.4 broadcast_select_fusion
  146.1 1.4 collective-permute-start.17
  147.5 13.8 %collective-permute-done.17.refs_6_ = f32[256,512]{1,0:T(8,128)S(1)} collective-permute-done((f32[256,512]{1,0:T(8,128)S(1)}, f32[256,512]{1,0:T(8,128)S(1)}, u32[]{:S(2)}, u32[]{:S(2)}) %collective-permute-start.17) | collective-permute-done | bytes 524320 | tf_op jit(solution)/shard_map/ppermute | solution.py:417
  161.3 1.9 collective-permute-start.18
  163.2 1.3 copy-done.6
  164.5 1.3 copy-done.12
  170.5 5.4 %shard_map.49 = (f32[512,640]{1,0:T(8,128)S(1)}, f32[512,640]{1,0:T(8,128)S(1)}, f32[512,640]{1,0:T(8,128)S(1)}) custom-call(s32[2]{0:T(128)S(1)} %pad_add_fusion.where_ref, s32[512,128]{1,0:T(8,128)S(1)} %get-tuple-element.38.owner_ref, f32[512,640]{1,0:T(8,128)S(1)} %copy-done.12, f32[256,640]{1,0:T(8,128)S(1)} %copy-done.16, f32[256,640]{1,0:T(8,128)S(1)} %copy-done.18, ...), custom_call_target="tpu_custom_call" | custom-call | flops 2013265920 | tf_op jit(solution)/shard_map/pallas_call | solution.py:391
  175.9 9.8 %shard_map.51 = f32[2048,640]{1,0:T(8,128)} custom-call(s32[2]{0:T(128)S(1)} %pad_add_fusion.where_ref, s32[8,512]{1,0:T(8,128)S(1)} %get-tuple-element.37.table_ref, f32[512,640]{1,0:T(8,128)S(1)} %get-tuple-element.63.displaced_ref, f32[512,640]{1,0:T(8,128)S(1)} %get-tuple-element.64.weights_ref, f32[512,640]{1,0:T(8,128)S(1)} %get-tuple-element.65.top_ref, ...), custom_call_target="tpu_custom_call" | custom-call | flops 4026531840 | bytes 14680064 | tf_op jit(solution)/shard_map/pallas_call | solution.py:470
  (82 shorter events, 22.7 us)
Async XLA Ops:
  6.5 90.1 %all-gather.3.cloned.1.call-start = ((), (), s32[]{:S(2)}) async-start(), calls=%async_computation | async-start | bytes 1310720 | tf_op jit(solution)/shard_map/all_gather | solution.py:353
  9.2 9.9 %collective-permute-start = (f32[256,512]{1,0:T(8,128)S(1)}, f32[256,512]{1,0:T(8,128)}, u32[]{:S(2)}, u32[]{:S(2)}) collective-permute-start(f32[256,512]{1,0:T(8,128)S(1)} %get-tuple-element.72), channel_id=1, source_target_pairs={{0,1},{8,9},{16,17},{24,25}} | collective-permute-start | bytes 1572872 | tf_op jit(solution)/shard_map/ppermute | solution.py:340
  13.1 2.5 %copy-start = (f32[2048,640]{1,0:T(8,128)S(1)}, f32[2048,640]{1,0:T(8,128)}, u32[]{:S(2)}) copy-start(f32[2048,640]{1,0:T(8,128)} %matrix_ref.5) | copy-start | bytes 15728644
  19.1 5.7 %collective-permute-start.2 = (f32[512,640]{1,0:T(8,128)S(1)}, f32[512,640]{1,0:T(8,128)S(1)}, u32[]{:S(2)}, u32[]{:S(2)}) collective-permute-start(f32[512,640]{1,0:T(8,128)S(1)} %shard_map.47.held_ref), channel_id=1, source_target_pairs={{0,8},{8,0},{16,24},{24,16},{1,9},{9,1},{17,25},{25,17},{2,10},{10... | collective-permute-start | bytes 3932168 | tf_op jit(solution)/shard_map/ppermute | solution.py:374
  20.5 4.3 %collective-permute-start.1 = (f32[256,512]{1,0:T(8,128)}, f32[256,512]{1,0:T(8,128)S(1)}, u32[]{:S(2)}, u32[]{:S(2)}) collective-permute-start(f32[256,512]{1,0:T(8,128)} %get-tuple-element.40), channel_id=1, source_target_pairs={{0,1},{8,9},{16,17},{24,25}} | collective-permute-start | bytes 1572872 | tf_op jit(solution)/shard_map/ppermute | solution.py:340
  22.0 7.7 %collective-permute-start.5 = (f32[128,512]{1,0:T(8,128)}, f32[128,512]{1,0:T(8,128)}, u32[]{:S(2)}, u32[]{:S(2)}) collective-permute-start(f32[128,512]{1,0:T(8,128)} %get-tuple-element.77), channel_id=1, source_target_pairs={{0,6},{1,7},{8,14},{9,15},{16,22},{17,23},{24,30},{25,31}} | collective-permute-start | bytes 786440 | tf_op jit(solution)/shard_map/ppermute | solution.py:348
  23.4 6.3 %collective-permute-start.4 = (f32[128,512]{1,0:T(8,128)}, f32[128,512]{1,0:T(8,128)}, u32[]{:S(2)}, u32[]{:S(2)}) collective-permute-start(f32[128,512]{1,0:T(8,128)} %get-tuple-element.78), channel_id=1, source_target_pairs={{0,4},{1,5},{8,12},{9,13},{16,20},{17,21},{24,28},{25,29}} | collective-permute-start | bytes 786440 | tf_op jit(solution)/shard_map/ppermute | solution.py:348
  24.8 51.4 %copy-start.5 = (f32[512,640]{1,0:T(8,128)}, f32[512,640]{1,0:T(8,128)S(1)}, u32[]{:S(2)}) copy-start(f32[512,640]{1,0:T(8,128)S(1)} %collective-permute-done.2.refs_0_.before_ref) | copy-start | bytes 3932164
  26.3 31.7 %collective-permute-start.3 = (f32[256,512]{1,0:T(8,128)}, f32[256,512]{1,0:T(8,128)}, u32[]{:S(2)}, u32[]{:S(2)}) collective-permute-start(f32[256,512]{1,0:T(8,128)} %get-tuple-element.43), channel_id=1, source_target_pairs={{0,1},{8,9},{16,17},{24,25}} | collective-permute-start | bytes 1572872 | tf_op jit(solution)/shard_map/ppermute | solution.py:340
  28.4 28.5 %collective-permute-start.6 = (f32[128,512]{1,0:T(8,128)}, f32[128,512]{1,0:T(8,128)}, u32[]{:S(2)}, u32[]{:S(2)}) collective-permute-start(f32[128,512]{1,0:T(8,128)} %slice.69), channel_id=1, source_target_pairs={{0,2},{1,3},{8,10},{9,11},{16,18},{17,19},{24,26},{25,27}} | collective-permute-start | bytes 786440 | tf_op jit(solution)/shard_map/ppermute | solution.py:348
  58.8 77.5 %all-gather.5.cloned.1.call-start = ((), (), s32[]{:S(2)}) async-start(), calls=%async_computation.1 | async-start | bytes 1310720 | tf_op jit(solution)/shard_map/all_gather | solution.py:353
  60.7 15.5 %collective-permute-start.10 = (f32[256,640]{1,0:T(8,128)S(1)}, f32[256,640]{1,0:T(8,128)S(1)}, u32[]{:S(2)}, u32[]{:S(2)}) collective-permute-start(f32[256,640]{1,0:T(8,128)S(1)} %get-tuple-element.52), channel_id=1, source_target_pairs={{0,16},{8,24},{16,0},{24,8},{1,17},{9,25},{17,1},{25,9},{2,18},{10... | collective-permute-start | bytes 1966088 | tf_op jit(solution)/shard_map/ppermute | solution.py:378
  62.5 13.7 %collective-permute-start.9 = (f32[256,512]{1,0:T(8,128)}, f32[256,512]{1,0:T(8,128)}, u32[]{:S(2)}, u32[]{:S(2)}) collective-permute-start(f32[256,512]{1,0:T(8,128)} %get-tuple-element.48), channel_id=1, source_target_pairs={{0,1},{8,9},{16,17},{24,25}} | collective-permute-start | bytes 1572872 | tf_op jit(solution)/shard_map/ppermute | solution.py:340
  64.8 34.6 %collective-permute-start.8 = (f32[128,512]{1,0:T(8,128)}, f32[128,512]{1,0:T(8,128)S(1)}, u32[]{:S(2)}, u32[]{:S(2)}) collective-permute-start(f32[128,512]{1,0:T(8,128)} %get-tuple-element.75), channel_id=1, source_target_pairs={{0,6},{1,7},{8,14},{9,15},{16,22},{17,23},{24,30},{25,31}} | collective-permute-start | bytes 786440 | tf_op jit(solution)/shard_map/ppermute | solution.py:348
  65.4 34.6 %collective-permute-start.7 = (f32[128,512]{1,0:T(8,128)}, f32[128,512]{1,0:T(8,128)}, u32[]{:S(2)}, u32[]{:S(2)}) collective-permute-start(f32[128,512]{1,0:T(8,128)} %get-tuple-element.76), channel_id=1, source_target_pairs={{0,4},{1,5},{8,12},{9,13},{16,20},{17,21},{24,28},{25,29}} | collective-permute-start | bytes 786440 | tf_op jit(solution)/shard_map/ppermute | solution.py:348
  76.1 60.1 %copy-start.15 = (f32[256,640]{1,0:T(8,128)}, f32[256,640]{1,0:T(8,128)S(1)}, u32[]{:S(2)}) copy-start(f32[256,640]{1,0:T(8,128)S(1)} %collective-permute-done.10.one_ref) | copy-start | bytes 1966084
  96.6 12.8 %copy-start.2 = (f32[512,512]{1,0:T(8,128)S(1)}, f32[512,512]{1,0:T(8,128)}, u32[]{:S(2)}) copy-start(f32[512,512]{1,0:T(8,128)} %all-gather.3.cloned.1.call-done.line_ref.refs_0_) | copy-start | bytes 3145732
  96.6 12.0 %collective-permute-start.12 = (f32[256,640]{1,0:T(8,128)S(1)}, f32[256,640]{1,0:T(8,128)S(1)}, u32[]{:S(2)}, u32[]{:S(2)}) collective-permute-start(f32[256,640]{1,0:T(8,128)S(1)} %collective-permute-done.10.one_ref), channel_id=1, source_target_pairs={{0,8},{8,0},{16,24},{24,16},{1,9},{9,1},{17,25},{25,17},{2,10},{10... | collective-permute-start | bytes 1966088 | tf_op jit(solution)/shard_map/ppermute | solution.py:379
  98.0 10.5 %collective-permute-start.11 = (f32[128,512]{1,0:T(8,128)S(1)}, f32[128,512]{1,0:T(8,128)S(1)}, u32[]{:S(2)}, u32[]{:S(2)}) collective-permute-start(f32[128,512]{1,0:T(8,128)S(1)} %slice.81), channel_id=1, source_target_pairs={{0,2},{1,3},{8,10},{9,11},{16,18},{17,19},{24,26},{25,27}} | collective-permute-start | bytes 786440 | tf_op jit(solution)/shard_map/ppermute | solution.py:348
  108.6 4.0 %copy-start.17 = (f32[256,640]{1,0:T(8,128)}, f32[256,640]{1,0:T(8,128)S(1)}, u32[]{:S(2)}) copy-start(f32[256,640]{1,0:T(8,128)S(1)} %collective-permute-done.12.two_ref) | copy-start | bytes 1966084
  109.5 16.7 %collective-permute-start.14 = (f32[256,512]{1,0:T(8,128)S(1)}, f32[256,512]{1,0:T(8,128)S(1)}, u32[]{:S(2)}, u32[]{:S(2)}) collective-permute-start(f32[256,512]{1,0:T(8,128)S(1)} %get-tuple-element.73), channel_id=1, source_target_pairs={{0,1},{2,3},{3,2},{4,5},{5,4},{6,7},{7,6},{8,9},{10,11},{11,10},{1... | collective-permute-start | bytes 1572872 | tf_op jit(solution)/shard_map/ppermute | solution.py:357
  112.6 23.5 %collective-permute-start.13 = (f32[256,512]{1,0:T(8,128)S(1)}, f32[256,512]{1,0:T(8,128)S(1)}, u32[]{:S(2)}, u32[]{:S(2)}) collective-permute-start(f32[256,512]{1,0:T(8,128)S(1)} %get-tuple-element.74), channel_id=1, source_target_pairs={{0,1},{2,3},{3,2},{4,5},{5,4},{6,7},{7,6},{8,9},{10,11},{11,10},{1... | collective-permute-start | bytes 1572872 | tf_op jit(solution)/shard_map/ppermute | solution.py:357
  136.3 2.5 %copy-start.1 = (f32[2048,640]{1,0:T(8,128)S(1)}, f32[2048,640]{1,0:T(8,128)}, u32[]{:S(2)}) copy-start(f32[2048,640]{1,0:T(8,128)} %matrix_ref.5) | copy-start | bytes 15728644
  138.7 37.1 %slice-start = ((s8[5242880]{0:T(1024)(128)(4,1)}), s8[1048576]{0:T(1024)(128)(4,1)S(1)}, s32[]{:S(2)}) async-start(s8[5242880]{0:T(1024)(128)(4,1)} %bitcast.3), calls=%async_computation.2 | async-start | bytes 2097152
  140.1 4.4 %collective-permute-start.16 = (f32[512,512]{1,0:T(8,128)}, f32[512,512]{1,0:T(8,128)S(1)}, u32[]{:S(2)}, u32[]{:S(2)}) collective-permute-start(f32[512,512]{1,0:T(8,128)} %shard_map.50), channel_id=1, source_target_pairs={{0,8},{1,9},{2,10},{3,11},{4,12},{5,13},{6,14},{7,15}} | collective-permute-start | bytes 3145736 | tf_op jit(solution)/shard_map/ppermute | solution.py:413
  140.9 35.0 %slice-start.1 = ((s8[5242880]{0:T(1024)(128)(4,1)}), s8[4194304]{0:T(1024)(128)(4,1)S(1)}, s32[]{:S(2)}) async-start(s8[5242880]{0:T(1024)(128)(4,1)} %bitcast.3), calls=%async_computation.3 | async-start | bytes 8388608
  140.9 34.9 %collective-permute-start.15 = (f32[512,512]{1,0:T(8,128)}, f32[512,512]{1,0:T(8,128)S(1)}, u32[]{:S(2)}, u32[]{:S(2)}) collective-permute-start(f32[512,512]{1,0:T(8,128)} %all-gather.5.cloned.1.call-done.refs_1_), channel_id=1, source_target_pairs={{0,1},{2,3},{3,2},{4,5},{5,4},{6,7},{7,6},{8,9},{10,11},{11,10},{1... | collective-permute-start | bytes 3145736 | tf_op jit(solution)/shard_map/ppermute | solution.py:357
  146.0 29.9 %copy-start.4 = (f32[256,512]{1,0:T(8,128)S(1)}, f32[256,512]{1,0:T(8,128)}, u32[]{:S(2)}) copy-start(f32[256,512]{1,0:T(8,128)} %copy-done.3) | copy-start | bytes 1572868
  146.1 15.2 %collective-permute-start.17 = (f32[256,512]{1,0:T(8,128)S(1)}, f32[256,512]{1,0:T(8,128)S(1)}, u32[]{:S(2)}, u32[]{:S(2)}) collective-permute-start(f32[256,512]{1,0:T(8,128)S(1)} %slice_select_fusion), channel_id=1, source_target_pairs={{0,16},{8,24},{1,17},{9,25},{2,18},{10,26},{3,19},{11,27},{4,20},{... | collective-permute-start | bytes 1572872 | tf_op jit(solution)/shard_map/ppermute | solution.py:417
  161.3 14.6 %collective-permute-start.18 = (f32[256,512]{1,0:T(8,128)S(1)}, f32[256,512]{1,0:T(8,128)S(1)}, u32[]{:S(2)}, u32[]{:S(2)}) collective-permute-start(f32[256,512]{1,0:T(8,128)S(1)} %collective-permute-done.17.refs_6_), channel_id=1, source_target_pairs={{16,24},{24,16},{17,25},{25,17},{18,26},{26,18},{19,27},{27,19},{2... | collective-permute-start | bytes 1572872 | tf_op jit(solution)/shard_map/ppermute | solution.py:418
  170.5 5.4 %copy-start.7 = (f32[512,512]{1,0:T(8,128)S(1)}, f32[512,512]{1,0:T(8,128)}, u32[]{:S(2)}) copy-start(f32[512,512]{1,0:T(8,128)} %all-gather.5.cloned.1.call-done.refs_1_) | copy-start | bytes 3145732
  170.5 5.4 %copy-start.9 = (f32[256,512]{1,0:T(8,128)S(1)}, f32[256,512]{1,0:T(8,128)}, u32[]{:S(2)}) copy-start(f32[256,512]{1,0:T(8,128)} %copy-done.8) | copy-start | bytes 1572868
  (11 other events, 11.3 us)
Sparse Core Ops, SparseCore 0:
  58.9 37.6 all-gather.2
  109.6 26.6 all-gather.4

commit v8 on v3

--- a/solution.py
+++ b/solution.py
@@ -138,60 +138,69 @@
         half_ref[...] = merged_ref[high, :]
 
 
-def factor_kernel(where_ref, top_in_ref, lower_ref, upper_ref, weights_ref, top_ref):
-    nb, cols = top_in_ref.shape
-    u = jnp.dot(
-        lower_ref[...], top_in_ref[...], precision=HIGHEST,
-        preferred_element_type=jnp.float32,
-    )
+def split(x):
+    hi = x.astype(jnp.bfloat16)
+    return hi, (x - hi.astype(jnp.float32)).astype(jnp.bfloat16)
+
+
+def product(a, b):
+    dot = functools.partial(jnp.dot, preferred_element_type=jnp.float32)
+    return dot(a[1], b[0]) + dot(a[0], b[1]) + dot(a[0], b[0])
+
+
+def factor_kernel(
+    where_ref, owner_ref, held_ref, one_ref, two_ref, before_ref, lower_ref, upper_ref,
+    weights_ref, top_ref, displaced_ref, new_top, *, log,
+):
+    me = where_ref[0]
+    mine, theirs = me >> log, (me >> log) ^ 1
+    nb, cols = held_ref.shape
+    half = nb // 2
+
+    def merge(rows, piece):
+        group = owner_ref[rows, :] >> log
+        take = (group == theirs) | ((theirs == 0) & (group != mine))
+        for q in range(cols // LANES):
+            lane = slice(q * LANES, (q + 1) * LANES)
+            new_top[rows, lane] = jnp.where(take, piece[:, lane], held_ref[rows, lane])
+
+        @pl.when(mine == 1)
+        def _():
+            displaced_ref[rows, :] = piece[...]
+
+    @pl.when(mine != 1)
+    def _():
+        displaced_ref[...] = before_ref[...]
+
+    for odd, (first, second) in enumerate([(one_ref, two_ref), (two_ref, one_ref)]):
+        @pl.when((me & 1) == odd)
+        def _():
+            merge(slice(0, half), first)
+            merge(slice(half, nb), second)
+
+    u = product(split(lower_ref[...]), split(new_top[...]))
     top_ref[...] = u
-    weights_ref[...] = jnp.dot(
-        upper_ref[...], u, precision=HIGHEST, preferred_element_type=jnp.float32
-    )
+    weights_ref[...] = product(split(upper_ref[...]), split(u))
 
     @pl.when(where_ref[1] == 0)
     def _():
-        top_ref[:, :nb] = top_in_ref[:, :nb]
+        top_ref[:, :nb] = new_top[:, :nb]
         weights_ref[:, :nb] = -upper_ref[...]
 
 
-def fetch(choice_ref, bufs, place, sem, n_cols, parts, pairs):
-    for i in range(pairs):
-        for h in range(2):
-            for b in sorted({arrival(p, i, h, n_cols, parts) for p in range(1, n_cols)}):
-                @pl.when(choice_ref[2 * i + h] == b)
-                def _():
-                    pltpu.make_async_copy(bufs[b], place(i, h), sem).start()
-
-
-def old_top_kernel(where_ref, choice_ref, matrix_ref, *refs, used, n_cols, parts, pairs):
-    bufs, top_ref, sem = dict(zip(used, refs)), refs[-2], refs[-1]
-    nb = top_ref.shape[0]
-    chunk = nb // (2 * pairs)
-    from_matrix = pltpu.make_async_copy(
-        matrix_ref.at[pl.ds(0, nb), pl.ds(0, nb)], top_ref, sem
-    )
-
-    @pl.when(where_ref[0] == 0)
-    def _():
-        @pl.when(where_ref[1] == 0)
-        def _():
-            from_matrix.start()
-
-        @pl.when(where_ref[1] > 0)
-        def _():
-            fetch(
-                choice_ref, bufs,
-                lambda i, h: top_ref.at[pl.ds((2 * i + h) * chunk, chunk), :],
-                sem, n_cols, parts, pairs,
-            )
-
-        from_matrix.wait()
+def line_kernel(choice_ref, *refs, first, used, options):
+    bufs, out_ref = dict(zip(used, refs)), refs[-1]
+    chunk = bufs[used[0]].shape[0]
+    for k, names in enumerate(options):
+        for b in names:
+            @pl.when(choice_ref[first + k] == b)
+            def _():
+                out_ref[k * chunk : (k + 1) * chunk, :] = bufs[b][...]
 
 
 def final_kernel(
-    where_ref, table_ref, choice_ref, displaced_ref, weights_ref, top_ref, matrix_ref,
-    *refs, n_bufs, n_tops, n_cols, parts, block,
+    where_ref, table_ref, displaced_ref, weights_ref, top_ref, matrix_ref,
+    *refs, n_bufs, n_tops, parts, block,
 ):
     bufs, tops, out_ref = refs[:n_bufs], refs[n_bufs : n_bufs + n_tops], refs[n_bufs + n_tops]
     mat, pan, low, w_hi, w_lo, result, in_sem, low_sem, mat_sem, out_sem = refs[
@@ -208,16 +217,17 @@
     load.start()
     whole_panel = pltpu.make_async_copy(matrix_ref.at[:, pl.ds(0, nb)], pan, in_sem)
 
-    @pl.when(first_col)
-    def _():
-        whole_panel.start()
-
-    @pl.when(jnp.logical_not(first_col))
-    def _():
-        fetch(
-            choice_ref, bufs, lambda i, h: pan.at[pl.ds((2 * i + h) * chunk, chunk), :],
-            in_sem, n_cols, parts, parts,
-        )
+    at = 0
+    for buf in bufs:
+        count = buf.shape[0] // (2 * chunk)
+        for h in range(2):
+            for k in range(count):
+                to = (2 * (at + k) + 1 - h) * chunk
+                pltpu.make_async_copy(
+                    buf.at[pl.ds((h * count + k) * chunk, chunk), :],
+                    pan.at[pl.ds(to, chunk), :], in_sem,
+                ).start()
+        at += count
 
     @pl.when(row == 1)
     def _():
@@ -291,62 +301,52 @@
 LAG = 2
 
 
-def steps(n_cols, parts):
-    depth = n_cols // 2
-    return parts + LAG * (depth - 1), max(2 * parts, parts + LAG * depth)
-
-
-def arrival(p, i, h, n_cols, parts):
+def came_in(p, i, parts):
     z, y = divmod(p, 2)
-    cross = steps(n_cols, parts)[0]
     if z == 0:
-        return cross + i + h * parts
-    if y == 0:
-        return cross + i + LAG * (z + 1) if h == 0 else i + LAG * (z - 1)
-    return i + LAG * z if h == 0 else cross + i + LAG * z
+        return i + y * parts
+    return 2 * parts + i + LAG * (z - 1 + y)
 
 
 def spread(pieces, col, n_cols, riders):
     parts = len(pieces)
-    n_chain, n_cross = steps(n_cols, parts)
-    along = [(p, p + 2) for p in range(n_cols - 2)]
-    across = [(0, 1)] + [(p, p ^ 1) for p in range(2, n_cols)]
-    chain, cross = [], []
-    waiting = [(rider, next(rider)(chain, cross)) for rider in riders]
-    for s in range(n_cross):
+    n_chain = parts + LAG * (n_cols // 2 - 1)
+    onward = [(p, p + 2) for p in range(n_cols - 2)]
+    feed, chain = [], []
+    waiting = [(rider, next(rider)(feed, chain)) for rider in riders]
+    for s in range(n_chain):
         ahead = pieces[min(s, parts - 1)][1]
-        aside = pieces[s][0] if s < parts else pieces[min(s - parts, parts - 1)][1]
         if s >= LAG:
-            came = chain[s - LAG] if s - LAG < n_chain else chain[-1]
             due = [k for k, (_, (at, _)) in enumerate(waiting) if at == s]
             tied = [waiting[k][1][1] for k in due]
-            (came, fed), tied = lax.optimization_barrier(((came, cross[s - LAG]), tied))
-            ahead = jnp.where(col == 0, ahead, jnp.where(col == 1, fed, came))
-            aside = jnp.where(col == 0, aside, came)
-        if s < n_chain:
-            chain.append(lax.ppermute(ahead, "pcol", along))
-        cross.append(lax.ppermute(aside, "pcol", across))
+            fed = feed[min(s - LAG, parts - 1)]
+            (came, fed), tied = lax.optimization_barrier(((chain[s - LAG], fed), tied))
+            here = jnp.where(col == 1, fed, came)
+            ahead = jnp.where(col == 0, ahead, here) if s < parts else here
+        chain.append(lax.ppermute(ahead, "pcol", onward))
+        if s < parts:
+            feed.append(lax.ppermute(pieces[s][0], "pcol", [(0, 1)]))
         if s >= LAG:
             for k, values in zip(due, tied):
                 rider = waiting[k][0]
-                waiting[k] = (rider, resume(rider, values, chain, cross))
+                waiting[k] = (rider, resume(rider, values, feed, chain))
     results = []
     for rider, (at, values) in waiting:
         while at != DONE:
-            at, values = resume(rider, values, chain, cross)
+            at, values = resume(rider, values, feed, chain)
         results.append(values)
-    return chain, cross, results
+    return results
 
 
 DONE = -1
 
 
-def resume(rider, values, chain, cross):
-    return rider.send(values)(chain, cross)
+def resume(rider, values, feed, chain):
+    return rider.send(values)(feed, chain)
 
 
 def give(at, values):
-    return lambda chain, cross: (at, values)
+    return lambda feed, chain: (at, values)
 
 
 def local(matrix, pivots, lower_inverse, upper_inverse, *, n_rows, n_cols, parts):
@@ -362,61 +362,65 @@
         lax.slice(matrix, (k * chunk, 0), ((k + 1) * chunk, nb)) for k in range(2 * parts)
     ]
     flat = flat[:2] + list(lax.optimization_barrier(tuple(flat[2:])))
+    pairs = [(flat[2 * i], flat[2 * i + 1]) for i in range(parts)]
     choice = jnp.asarray(
-        [
-            [0] * (2 * parts) if p == 0 else
-            [arrival(p, i, h, n_cols, parts) for i in range(parts) for h in range(2)]
-            for p in range(n_cols)
-        ],
-        jnp.int32,
+        [[came_in(p, i, parts) for i in range(parts)] for p in range(n_cols)], jnp.int32
     )[col]
-
-    pairs = nb // (2 * chunk)
-    used = sorted({
-        arrival(p, i, h, n_cols, parts)
-        for p in range(1, n_cols) for i in range(pairs) for h in range(2)
-    })
-    n_chain = steps(n_cols, parts)[0]
-    last = max(b - n_chain if b >= n_chain else b for b in used)
+    count = parts // 2
+    sides = [[p, p + 1] for p in range(0, n_cols, 2)]
+
+    def line(first, feed, chain):
+        every = [piece for _, piece in pairs] + feed + [None] * (parts - len(feed)) + chain
+        options = [
+            sorted({came_in(p, i, parts) for p in range(n_cols)})
+            for i in range(first, first + count)
+        ]
+        used = sorted(set().union(*options))
+        return call(
+            functools.partial(line_kernel, first=first, used=used, options=options),
+            jax.ShapeDtypeStruct((count * chunk, nb), f32),
+            [SMEM] + [VMEM] * len(used), VMEM, vmem=20 << 20,
+        )(choice, *[every[b] for b in used])
+
+    def gather(rows):
+        return lax.all_gather(rows, "pcol", axis=0, tiled=True, axis_index_groups=sides)
+
+    def line_rider():
+        at = came_in(n_cols - 1, count - 1, parts) - 2 * parts + LAG
+        early = yield give(at, ())
+        early = yield lambda feed, chain: (at + 1, line(0, feed, chain))
+        yield give(DONE, gather(early))
+
+    def late_rider():
+        yield lambda feed, chain: (DONE - 1, ())
+        yield lambda feed, chain: (DONE, line(parts - count, feed, chain))
 
     def both_halves(one, two):
         return jnp.concatenate([jnp.where(odd, two, one), jnp.where(odd, one, two)], axis=0)
 
-    def old_top_rider():
-        at = last + LAG
-
-        def start(chain, cross):
-            return at, [chain[b] if b < n_chain else cross[b - n_chain] for b in used]
-
-        arrived = yield give(at - 1, ())
-        arrived = yield start
-        old_top = call(
-            functools.partial(
-                old_top_kernel, used=used, n_cols=n_cols, parts=parts, pairs=pairs
-            ),
-            jax.ShapeDtypeStruct((nb, nb), f32),
-            [SMEM, SMEM, ANY] + [ANY] * len(used), ANY, [pltpu.SemaphoreType.DMA],
-            vmem=4 << 20,
-        )(here, choice, matrix, *arrived)
+    def spread_top(panel):
+        own = [
+            panel[(h * count + i) * chunk : (h * count + i + 1) * chunk]
+            for i in range(nb // (2 * chunk)) for h in (1, 0)
+        ]
+        old_top = jnp.concatenate(own, axis=0)
         tops = []
         log = 0
         while (1 << log) < n_rows:
             d = 1 << log
             far = [(p, p + d) for p in range(d)]
             if log == 0:
-                at += 2
-                whole = yield give(at, lax.ppermute(old_top, "prow", far))
+                whole = lax.ppermute(old_top, "prow", far)
                 tops.append(whole)
             else:
                 half = jnp.where(odd, old_top[nb // 2 :], old_top[: nb // 2])
-                at += 3
-                one = yield give(at, lax.ppermute(half, "prow", far))
+                one = lax.ppermute(half, "prow", far)
                 two = lax.ppermute(one, "prow", [(p, p ^ 1) for p in range(d, 2 * d)])
                 tops += [one, two]
                 whole = both_halves(one, two)
             old_top = jnp.where((row >> log) == 1, whole, old_top)
             log += 1
-        yield give(DONE, tops)
+        return tops
 
     slot = jax.ShapeDtypeStruct((nb, cols), f32)
     half_slot = jax.ShapeDtypeStruct((nb // 2, cols), f32)
@@ -444,33 +448,36 @@
                 at += 5
                 two = yield give(at, lax.ppermute(one, "prow", near))
                 arrived = [one, two]
-                whole = both_halves(one, two)
+                whole = None if 2 << log == n_rows else both_halves(one, two)
+            if 2 << log == n_rows:
+                break
             held, half = call(
                 functools.partial(merge_kernel, log=log, halves=log > 0),
                 (slot, half_slot), [SMEM] + [VMEM] * (2 + len(arrived)), (VMEM, VMEM),
             )(here, owner, held, *arrived)
-            displaced = jnp.where((row >> log) == 1, whole, displaced)
+            displaced = jnp.where((row >> log) == 1, whole, displaced) if log else whole
             log += 1
-        held, displaced = yield give(at + 1, (held, displaced))
-        weights, top = yield give(at + 2, call(
-            factor_kernel, (slot, slot), [SMEM, VMEM, VMEM, VMEM], (VMEM, VMEM),
-            flops=4 * nb * nb * cols * 6,
-        )(here, held, lower_inverse, upper_inverse))
-        yield give(DONE, (table, displaced, weights, top))
-
-    chain, cross, (tops, (table, displaced, weights, top)) = spread(
-        [(flat[2 * i], flat[2 * i + 1]) for i in range(parts)], col, n_cols,
-        [old_top_rider(), exchange_rider()],
-    )
-    bufs = chain + cross
+        yield give(DONE, (table, owner, log, displaced, held, arrived))
+
+    early, late, (table, owner, log, displaced, held, arrived) = spread(
+        pairs, col, n_cols, [line_rider(), late_rider(), exchange_rider()]
+    )
+    bufs = [early, gather(late)]
+    _, held, arrived, early = lax.optimization_barrier((late, held, arrived, early))
+    tops = spread_top(early)
+    weights, top, displaced = call(
+        functools.partial(factor_kernel, log=log), (slot,) * 3,
+        [SMEM] + [VMEM] * 7, (VMEM,) * 3, [pltpu.VMEM((nb, cols), f32)], vmem=20 << 20,
+        flops=4 * nb * nb * cols * 3,
+    )(here, owner, held, *arrived, displaced, lower_inverse, upper_inverse)
 
     return call(
         functools.partial(
-            final_kernel, n_bufs=len(bufs), n_tops=len(tops), n_cols=n_cols, parts=parts,
+            final_kernel, n_bufs=len(bufs), n_tops=len(tops), parts=parts,
             block=256,
         ),
         jax.ShapeDtypeStruct(matrix.shape, f32),
-        [SMEM, SMEM, SMEM, VMEM, VMEM, VMEM, ANY] + [ANY] * (len(bufs) + len(tops)),
+        [SMEM, SMEM, VMEM, VMEM, VMEM, ANY] + [ANY] * (len(bufs) + len(tops)),
         ANY,
         [
             pltpu.VMEM((row_dev, cols), f32),
@@ -483,7 +490,7 @@
         vmem=30 << 20,
         flops=2 * row_dev * nb * cols * 3,
         moved=4 * row_dev * (2 * cols + nb),
-    )(here, table, choice, displaced, weights, top, matrix, *bufs, *tops)
+    )(here, table, displaced, weights, top, matrix, *bufs, *tops)
 
 
 def solution(mesh):

time: 168 us -> 196 us (1.17)
  starting transfers between devices: 90.4 us -> 49.4 us
  waiting for transfers between devices: 27.3 us -> 66.1 us
  local copies, waits for them, and re-layouts: 13.8 us -> 30.8 us
  between operations: 1.27 us -> 14.1 us
  Pallas kernels: 25.5 us -> 28 us
    ppermute x33 -> x25, starting transfers between devices: 89.7 us -> 48.6 us  [the longest x14 38.4 us: spread(): chain.append(lax.ppermute(ahead, 'pcol', onward))]
    ppermute x33 -> x25, waiting for transfers between devices: 27.3 us -> 53.7 us  [the longest x14 37.6 us: spread(): chain.append(lax.ppermute(ahead, 'pcol', onward))]
    unnamed x120 -> x92, local copies, waits for them, and re-layouts: 9.3 us -> 25.2 us
    all_gather x0 -> x2, waiting for transfers between devices: none -> 12.3 us  [gather(): lax.all_gather(rows, 'pcol', axis=0, tiled=True, axis_index_groups=sides)]
    pallas_call x2 -> x3, Pallas kernels: 6.44 us -> 10.7 us  [the longest x1 6.14 us: local(): call(functools.partial(factor_kernel, log=log), (slot,) * 3, [SMEM] + [VM...]
    select_n x15 -> x14, other arithmetic: 7.17 us -> 5.22 us  [the longest x6 2.6 us: spread(): here = jnp.where(col == 1, fed, came)]
  transfers between devices with their start and end apart: 36 -> 30, of which waited for: 13 -> 14; matrix products, arithmetic and copies ran while one was open for 4% -> 3% of each run, Pallas kernels for 9% -> 9%
where the time goes in v8:
time: 196 us; the launch traced here: 194 us
  waiting for transfers between devices  66.1 us (34%)
  starting transfers between devices  49.4 us (25%)
  local copies, waits for them, and re-layouts  30.8 us (16%)
  Pallas kernels  28 us (14%)
  between operations  14.1 us (7%)
  other arithmetic  5.37 us (3%)
    ppermute x14, starting transfers between devices, spread(): chain.append(lax.ppermute(ahead, 'pcol', onward))  38.4 us
    ppermute x14, waiting for transfers between devices, spread(): chain.append(lax.ppermute(ahead, 'pcol', onward))  37.6 us
    unnamed x92, local copies, waits for them, and re-layouts  25.2 us
    ppermute x1, waiting for transfers between devices, spread_top(): one = lax.ppermute(half, 'prow', far)  16.1 us
    all_gather x2, waiting for transfers between devices, gather(): lax.all_gather(rows, 'pcol', axis=0, tiled=True, axis_index_groups=sides)  12.3 us
    pallas_call x1, Pallas kernels, local(): call(functools.partial(final_kernel, n_bufs=len(bufs), n_tops=len(tops),...  10.6 us
    pallas_call x1, Pallas kernels, local(): call(functools.partial(factor_kernel, log=log), (slot,) * 3, [SMEM] + [VM...  6.14 us
    ppermute x8, starting transfers between devices, spread(): feed.append(lax.ppermute(pieces[s][0], 'pcol', [(0, 1)]))  6.09 us
  transfers between devices with their start and end apart: 30, of which 14 were waited for; matrix products, arithmetic and copies ran while one was open for 3% of the time, Pallas kernels for 9%

profile of v8, /device:TPU:10, one launch (start us, length us, event | category | flops | bytes accessed | tf_op | source)
XLA Modules:
  0.0 193.8 jit_solution(13051114538770643345)
XLA Ops:
  6.5 3.7 %fusion = (f32[128,512]{1,0:T(8,128)S(1)}, f32[128,512]{1,0:T(8,128)}, f32[128,512]{1,0:T(8,128)S(1)}, f32[128,512]{1,0:T(8,128)}, f32[128,512]{1,0:T(8,128)S(1)...) fusion(f32[2048,640]{1,0:T(8,128)} %matrix_ref.3), kind=kLoop, calls=%fused_computation.17 | loop fusion | bytes 8388608 | tf_op jit(solution)/shard_map/slice | solution.py:362
  10.9 3.5 %collective-permute-start = (f32[128,512]{1,0:T(8,128)S(1)}, f32[128,512]{1,0:T(8,128)}, u32[]{:S(2)}, u32[]{:S(2)}) collective-permute-start(f32[128,512]{1,0:T(8,128)S(1)} %get-tuple-element.132.refs_0_), channel_id=1, source_target_pairs={{0,2},{1,3},{2,4},{3,5},{4,6},{5,7},{8,10},{9,11},{10,12},{11,13},... | collective-permute-start | bytes 786440 | tf_op jit(solution)/shard_map/ppermute | solution.py:326
  16.5 3.5 %collective-permute-start.9 = (f32[128,512]{1,0:T(8,128)S(1)}, f32[128,512]{1,0:T(8,128)}, u32[]{:S(2)}, u32[]{:S(2)}) collective-permute-start(f32[128,512]{1,0:T(8,128)S(1)} %get-tuple-element.80.refs_1_), channel_id=1, source_target_pairs={{0,2},{1,3},{2,4},{3,5},{4,6},{5,7},{8,10},{9,11},{10,12},{11,13},... | collective-permute-start | bytes 786440 | tf_op jit(solution)/shard_map/ppermute | solution.py:326
  22.4 2.6 %copy-done = f32[2048,640]{1,0:T(8,128)S(1)} copy-done((f32[2048,640]{1,0:T(8,128)S(1)}, f32[2048,640]{1,0:T(8,128)}, u32[]{:S(2)}) %copy-start) | copy-done | bytes 5242904
  25.0 3.5 %shard_map.56.held_ref = f32[512,640]{1,0:T(8,128)S(1)} custom-call(s32[8,512]{1,0:T(8,128)S(1)} %get-tuple-element.63.table_ref, f32[2048,640]{1,0:T(8,128)S(1)} %copy-done), custom_call_target="tpu_custom_call" | custom-call | tf_op jit(solution)/shard_map/pallas_call | solution.py:434
  30.5 2.2 %collective-permute-start.6 = (f32[128,512]{1,0:T(8,128)S(1)}, f32[128,512]{1,0:T(8,128)S(1)}, u32[]{:S(2)}, u32[]{:S(2)}) collective-permute-start(f32[128,512]{1,0:T(8,128)S(1)} %select_select_fusion.5), channel_id=1, source_target_pairs={{0,2},{1,3},{2,4},{3,5},{4,6},{5,7},{8,10},{9,11},{10,12},{11,13},... | collective-permute-start | bytes 786440 | tf_op jit(solution)/shard_map/ppermute | solution.py:326
  34.4 4.4 %collective-permute-start.11 = (f32[128,512]{1,0:T(8,128)S(1)}, f32[128,512]{1,0:T(8,128)S(1)}, u32[]{:S(2)}, u32[]{:S(2)}) collective-permute-start(f32[128,512]{1,0:T(8,128)S(1)} %select_select_fusion.3), channel_id=1, source_target_pairs={{0,2},{1,3},{2,4},{3,5},{4,6},{5,7},{8,10},{9,11},{10,12},{11,13},... | collective-permute-start | bytes 786440 | tf_op jit(solution)/shard_map/ppermute | solution.py:326
  39.5 3.3 %collective-permute-done.6.refs_10_ = f32[128,512]{1,0:T(8,128)S(1)} collective-permute-done((f32[128,512]{1,0:T(8,128)S(1)}, f32[128,512]{1,0:T(8,128)S(1)}, u32[]{:S(2)}, u32[]{:S(2)}) %collective-permute-start.6) | collective-permute-done | bytes 262176 | tf_op jit(solution)/shard_map/ppermute | solution.py:326
  43.5 2.1 %collective-permute-start.8 = (f32[128,512]{1,0:T(8,128)S(1)}, f32[128,512]{1,0:T(8,128)S(1)}, u32[]{:S(2)}, u32[]{:S(2)}) collective-permute-start(f32[128,512]{1,0:T(8,128)S(1)} %select_select_fusion.4), channel_id=1, source_target_pairs={{0,2},{1,3},{2,4},{3,5},{4,6},{5,7},{8,10},{9,11},{10,12},{11,13},... | collective-permute-start | bytes 786440 | tf_op jit(solution)/shard_map/ppermute | solution.py:326
  45.6 2.8 %collective-permute-done.11.refs_11_ = f32[128,512]{1,0:T(8,128)S(1)} collective-permute-done((f32[128,512]{1,0:T(8,128)S(1)}, f32[128,512]{1,0:T(8,128)S(1)}, u32[]{:S(2)}, u32[]{:S(2)}) %collective-permute-start.11) | collective-permute-done | bytes 262176 | tf_op jit(solution)/shard_map/ppermute | solution.py:326
  54.9 4.2 %collective-permute-done.14.refs_13_.refs_9_ = f32[128,512]{1,0:T(8,128)S(1)} collective-permute-done((f32[128,512]{1,0:T(8,128)S(1)}, f32[128,512]{1,0:T(8,128)S(1)}, u32[]{:S(2)}, u32[]{:S(2)}) %collective-permute-start.14) | collective-permute-done | bytes 262176 | tf_op jit(solution)/shard_map/ppermute | solution.py:326
  59.2 1.9 collective-permute-start.16
  61.2 3.4 %collective-permute-start.15 = (f32[128,512]{1,0:T(8,128)S(1)}, f32[128,512]{1,0:T(8,128)S(1)}, u32[]{:S(2)}, u32[]{:S(2)}) collective-permute-start(f32[128,512]{1,0:T(8,128)S(1)} %select_select_fusion.1), channel_id=1, source_target_pairs={{0,2},{1,3},{2,4},{3,5},{4,6},{5,7},{8,10},{9,11},{10,12},{11,13},... | collective-permute-start | bytes 786440 | tf_op jit(solution)/shard_map/ppermute | solution.py:326
  64.6 5.8 %collective-permute-done.16.refs_15_.refs_11_ = f32[128,512]{1,0:T(8,128)S(1)} collective-permute-done((f32[128,512]{1,0:T(8,128)S(1)}, f32[128,512]{1,0:T(8,128)S(1)}, u32[]{:S(2)}, u32[]{:S(2)}) %collective-permute-start.16) | collective-permute-done | bytes 262176 | tf_op jit(solution)/shard_map/ppermute | solution.py:326
  70.4 3.7 %collective-permute-done.15.refs_14_.refs_10_ = f32[128,512]{1,0:T(8,128)S(1)} collective-permute-done((f32[128,512]{1,0:T(8,128)S(1)}, f32[128,512]{1,0:T(8,128)S(1)}, u32[]{:S(2)}, u32[]{:S(2)}) %collective-permute-start.15) | collective-permute-done | bytes 262176 | tf_op jit(solution)/shard_map/ppermute | solution.py:326
  74.8 2.2 %collective-permute-start.17 = (f32[128,512]{1,0:T(8,128)S(1)}, f32[128,512]{1,0:T(8,128)S(1)}, u32[]{:S(2)}, u32[]{:S(2)}) collective-permute-start(f32[128,512]{1,0:T(8,128)S(1)} %broadcast_select_fusion.6), channel_id=1, source_target_pairs={{0,2},{1,3},{2,4},{3,5},{4,6},{5,7},{8,10},{9,11},{10,12},{11,13},... | collective-permute-start | bytes 786440 | tf_op jit(solution)/shard_map/ppermute | solution.py:326
  77.8 3.1 %collective-permute-start.19 = (f32[128,512]{1,0:T(8,128)}, f32[128,512]{1,0:T(8,128)S(1)}, u32[]{:S(2)}, u32[]{:S(2)}) collective-permute-start(f32[128,512]{1,0:T(8,128)} %broadcast_select_fusion.5), channel_id=1, source_target_pairs={{0,2},{1,3},{2,4},{3,5},{4,6},{5,7},{8,10},{9,11},{10,12},{11,13},... | collective-permute-start | bytes 786440 | tf_op jit(solution)/shard_map/ppermute | solution.py:326
  80.8 4.7 %collective-permute-done.17.refs_16_.refs_12_ = f32[128,512]{1,0:T(8,128)S(1)} collective-permute-done((f32[128,512]{1,0:T(8,128)S(1)}, f32[128,512]{1,0:T(8,128)S(1)}, u32[]{:S(2)}, u32[]{:S(2)}) %collective-permute-start.17) | collective-permute-done | bytes 262176 | tf_op jit(solution)/shard_map/ppermute | solution.py:326
  87.2 2.2 %collective-permute-start.21 = (f32[128,512]{1,0:T(8,128)}, f32[128,512]{1,0:T(8,128)}, u32[]{:S(2)}, u32[]{:S(2)}) collective-permute-start(f32[128,512]{1,0:T(8,128)} %broadcast_select_fusion.4), channel_id=1, source_target_pairs={{0,2},{1,3},{2,4},{3,5},{4,6},{5,7},{8,10},{9,11},{10,12},{11,13},... | collective-permute-start | bytes 786440 | tf_op jit(solution)/shard_map/ppermute | solution.py:326
  97.6 2.3 %shard_map.58 = f32[512,512]{1,0:T(8,128)} custom-call(s32[8]{0:T(128)S(1)} %dynamic-slice_bitcast_fusion.choice_ref, f32[128,512]{1,0:T(8,128)S(1)} %copy-done.13, f32[128,512]{1,0:T(8,128)S(1)} %copy-done.11, f32[128,512]{1,0:T(8,128)S(1)} %get-tuple-element.73.refs_2_, f32[128,512]{1,0:T(8,128)S(1)} %get-tuple-element.79.refs_3_, ...), custom_call_target="tpu_custom_call" | custom-call | tf_op jit(solution)/shard_map/pallas_call | solution.py:379
  100.1 2.6 %collective-permute-start.22 = (f32[128,512]{1,0:T(8,128)S(1)}, f32[128,512]{1,0:T(8,128)S(1)}, u32[]{:S(2)}, u32[]{:S(2)}) collective-permute-start(f32[128,512]{1,0:T(8,128)S(1)} %broadcast_select_fusion.3), channel_id=1, source_target_pairs={{0,2},{1,3},{2,4},{3,5},{4,6},{5,7},{8,10},{9,11},{10,12},{11,13},... | collective-permute-start | bytes 786440 | tf_op jit(solution)/shard_map/ppermute | solution.py:326
  102.7 7.0 %collective-permute-done.22.refs_15_ = f32[128,512]{1,0:T(8,128)S(1)} collective-permute-done((f32[128,512]{1,0:T(8,128)S(1)}, f32[128,512]{1,0:T(8,128)S(1)}, u32[]{:S(2)}, u32[]{:S(2)}) %collective-permute-start.22) | collective-permute-done | bytes 262176 | tf_op jit(solution)/shard_map/ppermute | solution.py:326
  109.7 2.1 %collective-permute-start.24 = (f32[128,512]{1,0:T(8,128)S(1)}, f32[128,512]{1,0:T(8,128)S(1)}, u32[]{:S(2)}, u32[]{:S(2)}) collective-permute-start(f32[128,512]{1,0:T(8,128)S(1)} %broadcast_select_fusion.1), channel_id=1, source_target_pairs={{0,2},{1,3},{2,4},{3,5},{4,6},{5,7},{8,10},{9,11},{10,12},{11,13},... | collective-permute-start | bytes 786440 | tf_op jit(solution)/shard_map/ppermute | solution.py:326
  112.8 3.5 %collective-permute-start.23 = (f32[128,512]{1,0:T(8,128)S(1)}, f32[128,512]{1,0:T(8,128)S(1)}, u32[]{:S(2)}, u32[]{:S(2)}) collective-permute-start(f32[128,512]{1,0:T(8,128)S(1)} %broadcast_select_fusion.2), channel_id=1, source_target_pairs={{0,2},{1,3},{2,4},{3,5},{4,6},{5,7},{8,10},{9,11},{10,12},{11,13},... | collective-permute-start | bytes 786440 | tf_op jit(solution)/shard_map/ppermute | solution.py:326
  118.0 3.1 %collective-permute-done.23.refs_16_ = f32[128,512]{1,0:T(8,128)S(1)} collective-permute-done((f32[128,512]{1,0:T(8,128)S(1)}, f32[128,512]{1,0:T(8,128)S(1)}, u32[]{:S(2)}, u32[]{:S(2)}) %collective-permute-start.23) | collective-permute-done | bytes 262176 | tf_op jit(solution)/shard_map/ppermute | solution.py:326
  121.1 2.2 %shard_map.59 = f32[512,512]{1,0:T(8,128)} custom-call(s32[8]{0:T(128)S(1)} %dynamic-slice_bitcast_fusion.choice_ref, f32[128,512]{1,0:T(8,128)S(1)} %get-tuple-element.65.refs_0_, f32[128,512]{1,0:T(8,128)S(1)} %get-tuple-element.66.refs_1_, f32[128,512]{1,0:T(8,128)S(1)} %get-tuple-element.67.refs_2_, f32[128,512]{1,0:T(8,128)S(1)} %get-tuple-element.68.refs_3_, ...), custom_call_target="tpu_custom_call" | custom-call | tf_op jit(solution)/shard_map/pallas_call | solution.py:379
  123.3 9.4 %all-gather.3.cloned.1.call-done.refs_0_ = f32[1024,512]{1,0:T(8,128)} async-done(((f32[512,512]{1,0:T(8,128)}), f32[1024,512]{1,0:T(8,128)}) %all-gather.3.cloned.1.call-update) | async-done | bytes 2097168 | tf_op jit(solution)/shard_map/all_gather | solution.py:386
  136.8 16.1 %collective-permute-done.26.refs_3_ = f32[256,512]{1,0:T(8,128)} collective-permute-done((f32[256,512]{1,0:T(8,128)S(1)}, f32[256,512]{1,0:T(8,128)}, u32[]{:S(2)}, u32[]{:S(2)}) %collective-permute-start.26) | collective-permute-done | bytes 524320 | tf_op jit(solution)/shard_map/ppermute | solution.py:417
  156.0 6.1 %shard_map.60 = (f32[512,640]{1,0:T(8,128)S(1)}, f32[512,640]{1,0:T(8,128)S(1)}, f32[512,640]{1,0:T(8,128)S(1)}) custom-call(s32[2]{0:T(128)S(1)} %pad_add_fusion.where_ref, s32[512,128]{1,0:T(8,128)S(1)} %copy-done.32, f32[512,640]{1,0:T(8,128)S(1)} %copy-done.35, f32[256,640]{1,0:T(8,128)S(1)} %copy-done.39, f32[256,640]{1,0:T(8,128)S(1)} %copy-done.41, ...), custom_call_target="tpu_custom_call" | custom-call | flops 2013265920 | tf_op jit(solution)/shard_map/pallas_call | solution.py:468
  165.4 2.9 %all-gather.5.cloned.1.call-done.refs_1_ = f32[1024,512]{1,0:T(8,128)} async-done(((f32[512,512]{1,0:T(8,128)}), f32[1024,512]{1,0:T(8,128)}) %all-gather.5.cloned.1.call-update) | async-done | bytes 2097168 | tf_op jit(solution)/shard_map/all_gather | solution.py:386
  168.3 2.5 %copy-done.1 = f32[2048,640]{1,0:T(8,128)S(1)} copy-done((f32[2048,640]{1,0:T(8,128)S(1)}, f32[2048,640]{1,0:T(8,128)}, u32[]{:S(2)}) %copy-start.1) | copy-done | bytes 5242904
  176.3 10.6 %shard_map.61 = f32[2048,640]{1,0:T(8,128)} custom-call(s32[2]{0:T(128)S(1)} %pad_add_fusion.where_ref, s32[8,512]{1,0:T(8,128)S(1)} %get-tuple-element.63.table_ref, f32[512,640]{1,0:T(8,128)S(1)} %copy-done.9, f32[512,640]{1,0:T(8,128)S(1)} %copy-done.5, f32[512,640]{1,0:T(8,128)S(1)} %copy-done.7, f32[2048,640]{1,0:T(8,128)S(1)} %copy-done.1, ...), custom_call_target="tpu_custom_call" | custom-call | flops 4026531840 | bytes 14680064 | tf_op jit(solution)/shard_map/pallas_call | solution.py:474
  (148 shorter events, 46.6 us)
Async XLA Ops:
  6.5 126.2 %all-gather.3.cloned.1.call-start = ((), (), s32[]{:S(2)}) async-start(), calls=%async_computation | async-start | bytes 3145728 | tf_op jit(solution)/shard_map/all_gather | solution.py:386
  10.2 12.2 %collective-permute-start.1 = (f32[128,512]{1,0:T(8,128)S(1)}, f32[128,512]{1,0:T(8,128)S(1)}, u32[]{:S(2)}, u32[]{:S(2)}) collective-permute-start(f32[128,512]{1,0:T(8,128)S(1)} %get-tuple-element.131), channel_id=1, source_target_pairs={{0,1},{8,9},{16,17},{24,25}} | collective-permute-start | bytes 786440 | tf_op jit(solution)/shard_map/ppermute | solution.py:328
  10.9 11.5 %collective-permute-start = (f32[128,512]{1,0:T(8,128)S(1)}, f32[128,512]{1,0:T(8,128)}, u32[]{:S(2)}, u32[]{:S(2)}) collective-permute-start(f32[128,512]{1,0:T(8,128)S(1)} %get-tuple-element.132.refs_0_), channel_id=1, source_target_pairs={{0,2},{1,3},{2,4},{3,5},{4,6},{5,7},{8,10},{9,11},{10,12},{11,13},... | collective-permute-start | bytes 786440 | tf_op jit(solution)/shard_map/ppermute | solution.py:326
  15.1 13.4 %collective-permute-start.10 = (f32[128,512]{1,0:T(8,128)}, f32[128,512]{1,0:T(8,128)}, u32[]{:S(2)}, u32[]{:S(2)}) collective-permute-start(f32[128,512]{1,0:T(8,128)} %get-tuple-element.81), channel_id=1, source_target_pairs={{0,1},{8,9},{16,17},{24,25}} | collective-permute-start | bytes 786440 | tf_op jit(solution)/shard_map/ppermute | solution.py:328
  16.5 12.1 %collective-permute-start.9 = (f32[128,512]{1,0:T(8,128)S(1)}, f32[128,512]{1,0:T(8,128)}, u32[]{:S(2)}, u32[]{:S(2)}) collective-permute-start(f32[128,512]{1,0:T(8,128)S(1)} %get-tuple-element.80.refs_1_), channel_id=1, source_target_pairs={{0,2},{1,3},{2,4},{3,5},{4,6},{5,7},{8,10},{9,11},{10,12},{11,13},... | collective-permute-start | bytes 786440 | tf_op jit(solution)/shard_map/ppermute | solution.py:326
  28.6 19.8 %collective-permute-start.13 = (f32[512,640]{1,0:T(8,128)S(1)}, f32[512,640]{1,0:T(8,128)}, u32[]{:S(2)}, u32[]{:S(2)}) collective-permute-start(f32[512,640]{1,0:T(8,128)S(1)} %shard_map.56.held_ref), channel_id=1, source_target_pairs={{0,8},{8,0},{16,24},{24,16},{1,9},{9,1},{17,25},{25,17},{2,10},{10... | collective-permute-start | bytes 3932168 | tf_op jit(solution)/shard_map/ppermute | solution.py:443
  28.6 10.1 %collective-permute-start.7 = (f32[128,512]{1,0:T(8,128)}, f32[128,512]{1,0:T(8,128)S(1)}, u32[]{:S(2)}, u32[]{:S(2)}) collective-permute-start(f32[128,512]{1,0:T(8,128)} %get-tuple-element.76), channel_id=1, source_target_pairs={{0,1},{8,9},{16,17},{24,25}} | collective-permute-start | bytes 786440 | tf_op jit(solution)/shard_map/ppermute | solution.py:328
  30.5 12.3 %collective-permute-start.6 = (f32[128,512]{1,0:T(8,128)S(1)}, f32[128,512]{1,0:T(8,128)S(1)}, u32[]{:S(2)}, u32[]{:S(2)}) collective-permute-start(f32[128,512]{1,0:T(8,128)S(1)} %select_select_fusion.5), channel_id=1, source_target_pairs={{0,2},{1,3},{2,4},{3,5},{4,6},{5,7},{8,10},{9,11},{10,12},{11,13},... | collective-permute-start | bytes 786440 | tf_op jit(solution)/shard_map/ppermute | solution.py:326
  32.7 10.9 %collective-permute-start.12 = (f32[128,512]{1,0:T(8,128)}, f32[128,512]{1,0:T(8,128)S(1)}, u32[]{:S(2)}, u32[]{:S(2)}) collective-permute-start(f32[128,512]{1,0:T(8,128)} %get-tuple-element.84), channel_id=1, source_target_pairs={{0,1},{8,9},{16,17},{24,25}} | collective-permute-start | bytes 786440 | tf_op jit(solution)/shard_map/ppermute | solution.py:328
  34.4 14.0 %collective-permute-start.11 = (f32[128,512]{1,0:T(8,128)S(1)}, f32[128,512]{1,0:T(8,128)S(1)}, u32[]{:S(2)}, u32[]{:S(2)}) collective-permute-start(f32[128,512]{1,0:T(8,128)S(1)} %select_select_fusion.3), channel_id=1, source_target_pairs={{0,2},{1,3},{2,4},{3,5},{4,6},{5,7},{8,10},{9,11},{10,12},{11,13},... | collective-permute-start | bytes 786440 | tf_op jit(solution)/shard_map/ppermute | solution.py:326
  38.8 14.4 %collective-permute-start.2 = (f32[128,512]{1,0:T(8,128)S(1)}, f32[128,512]{1,0:T(8,128)S(1)}, u32[]{:S(2)}, u32[]{:S(2)}) collective-permute-start(f32[128,512]{1,0:T(8,128)S(1)} %copy-done.45), channel_id=1, source_target_pairs={{0,1},{8,9},{16,17},{24,25}} | collective-permute-start | bytes 786440 | tf_op jit(solution)/shard_map/ppermute | solution.py:328
  42.7 12.2 %collective-permute-start.3 = (f32[128,512]{1,0:T(8,128)S(1)}, f32[128,512]{1,0:T(8,128)S(1)}, u32[]{:S(2)}, u32[]{:S(2)}) collective-permute-start(f32[128,512]{1,0:T(8,128)S(1)} %copy-done.44), channel_id=1, source_target_pairs={{0,1},{8,9},{16,17},{24,25}} | collective-permute-start | bytes 786440 | tf_op jit(solution)/shard_map/ppermute | solution.py:328
  43.5 10.7 %collective-permute-start.8 = (f32[128,512]{1,0:T(8,128)S(1)}, f32[128,512]{1,0:T(8,128)S(1)}, u32[]{:S(2)}, u32[]{:S(2)}) collective-permute-start(f32[128,512]{1,0:T(8,128)S(1)} %select_select_fusion.4), channel_id=1, source_target_pairs={{0,2},{1,3},{2,4},{3,5},{4,6},{5,7},{8,10},{9,11},{10,12},{11,13},... | collective-permute-start | bytes 786440 | tf_op jit(solution)/shard_map/ppermute | solution.py:326
  49.0 10.1 %collective-permute-start.14 = (f32[128,512]{1,0:T(8,128)S(1)}, f32[128,512]{1,0:T(8,128)S(1)}, u32[]{:S(2)}, u32[]{:S(2)}) collective-permute-start(f32[128,512]{1,0:T(8,128)S(1)} %select_select_fusion.2), channel_id=1, source_target_pairs={{0,2},{1,3},{2,4},{3,5},{4,6},{5,7},{8,10},{9,11},{10,12},{11,13},... | collective-permute-start | bytes 786440 | tf_op jit(solution)/shard_map/ppermute | solution.py:326
  52.5 34.6 %copy-start.34 = (f32[512,640]{1,0:T(8,128)}, f32[512,640]{1,0:T(8,128)S(1)}, u32[]{:S(2)}) copy-start(f32[512,640]{1,0:T(8,128)S(1)} %get-tuple-element.110.held_ref) | copy-start | bytes 3932164
  52.6 17.8 %collective-permute-start.18 = (f32[256,640]{1,0:T(8,128)S(1)}, f32[256,640]{1,0:T(8,128)S(1)}, u32[]{:S(2)}, u32[]{:S(2)}) collective-permute-start(f32[256,640]{1,0:T(8,128)S(1)} %get-tuple-element.95), channel_id=1, source_target_pairs={{0,16},{8,24},{16,0},{24,8},{1,17},{9,25},{17,1},{25,9},{2,18},{10... | collective-permute-start | bytes 1966088 | tf_op jit(solution)/shard_map/ppermute | solution.py:447
  53.2 34.0 %copy-start.16 = (f32[128,512]{1,0:T(8,128)}, f32[128,512]{1,0:T(8,128)S(1)}, u32[]{:S(2)}) copy-start(f32[128,512]{1,0:T(8,128)S(1)} %collective-permute-done.2.refs_4_) | copy-start | bytes 786436
  53.2 17.2 %collective-permute-start.4 = (f32[128,512]{1,0:T(8,128)S(1)}, f32[128,512]{1,0:T(8,128)S(1)}, u32[]{:S(2)}, u32[]{:S(2)}) collective-permute-start(f32[128,512]{1,0:T(8,128)S(1)} %copy-done.42), channel_id=1, source_target_pairs={{0,1},{8,9},{16,17},{24,25}} | collective-permute-start | bytes 786440 | tf_op jit(solution)/shard_map/ppermute | solution.py:328
  54.2 10.4 %collective-permute-start.5 = (f32[128,512]{1,0:T(8,128)S(1)}, f32[128,512]{1,0:T(8,128)S(1)}, u32[]{:S(2)}, u32[]{:S(2)}) collective-permute-start(f32[128,512]{1,0:T(8,128)S(1)} %copy-done.43), channel_id=1, source_target_pairs={{0,1},{8,9},{16,17},{24,25}} | collective-permute-start | bytes 786440 | tf_op jit(solution)/shard_map/ppermute | solution.py:328
  59.2 11.1 %collective-permute-start.16 = (f32[128,512]{1,0:T(8,128)S(1)}, f32[128,512]{1,0:T(8,128)S(1)}, u32[]{:S(2)}, u32[]{:S(2)}) collective-permute-start(f32[128,512]{1,0:T(8,128)S(1)} %select_select_fusion), channel_id=1, source_target_pairs={{0,2},{1,3},{2,4},{3,5},{4,6},{5,7},{8,10},{9,11},{10,12},{11,13},... | collective-permute-start | bytes 786440 | tf_op jit(solution)/shard_map/ppermute | solution.py:326
  61.2 12.9 %collective-permute-start.15 = (f32[128,512]{1,0:T(8,128)S(1)}, f32[128,512]{1,0:T(8,128)S(1)}, u32[]{:S(2)}, u32[]{:S(2)}) collective-permute-start(f32[128,512]{1,0:T(8,128)S(1)} %select_select_fusion.1), channel_id=1, source_target_pairs={{0,2},{1,3},{2,4},{3,5},{4,6},{5,7},{8,10},{9,11},{10,12},{11,13},... | collective-permute-start | bytes 786440 | tf_op jit(solution)/shard_map/ppermute | solution.py:326
  70.4 15.2 %collective-permute-start.20 = (f32[256,640]{1,0:T(8,128)S(1)}, f32[256,640]{1,0:T(8,128)S(1)}, u32[]{:S(2)}, u32[]{:S(2)}) collective-permute-start(f32[256,640]{1,0:T(8,128)S(1)} %collective-permute-done.18.one_ref), channel_id=1, source_target_pairs={{0,8},{8,0},{16,24},{24,16},{1,9},{9,1},{17,25},{25,17},{2,10},{10... | collective-permute-start | bytes 1966088 | tf_op jit(solution)/shard_map/ppermute | solution.py:449
  74.8 10.8 %collective-permute-start.17 = (f32[128,512]{1,0:T(8,128)S(1)}, f32[128,512]{1,0:T(8,128)S(1)}, u32[]{:S(2)}, u32[]{:S(2)}) collective-permute-start(f32[128,512]{1,0:T(8,128)S(1)} %broadcast_select_fusion.6), channel_id=1, source_target_pairs={{0,2},{1,3},{2,4},{3,5},{4,6},{5,7},{8,10},{9,11},{10,12},{11,13},... | collective-permute-start | bytes 786440 | tf_op jit(solution)/shard_map/ppermute | solution.py:326
  77.8 13.2 %collective-permute-start.19 = (f32[128,512]{1,0:T(8,128)}, f32[128,512]{1,0:T(8,128)S(1)}, u32[]{:S(2)}, u32[]{:S(2)}) collective-permute-start(f32[128,512]{1,0:T(8,128)} %broadcast_select_fusion.5), channel_id=1, source_target_pairs={{0,2},{1,3},{2,4},{3,5},{4,6},{5,7},{8,10},{9,11},{10,12},{11,13},... | collective-permute-start | bytes 786440 | tf_op jit(solution)/shard_map/ppermute | solution.py:326
  87.2 12.8 %collective-permute-start.21 = (f32[128,512]{1,0:T(8,128)}, f32[128,512]{1,0:T(8,128)}, u32[]{:S(2)}, u32[]{:S(2)}) collective-permute-start(f32[128,512]{1,0:T(8,128)} %broadcast_select_fusion.4), channel_id=1, source_target_pairs={{0,2},{1,3},{2,4},{3,5},{4,6},{5,7},{8,10},{9,11},{10,12},{11,13},... | collective-permute-start | bytes 786440 | tf_op jit(solution)/shard_map/ppermute | solution.py:326
  100.0 68.3 %all-gather.5.cloned.1.call-start = ((), (), s32[]{:S(2)}) async-start(), calls=%async_computation.1 | async-start | bytes 3145728 | tf_op jit(solution)/shard_map/all_gather | solution.py:386
  100.1 9.6 %collective-permute-start.22 = (f32[128,512]{1,0:T(8,128)S(1)}, f32[128,512]{1,0:T(8,128)S(1)}, u32[]{:S(2)}, u32[]{:S(2)}) collective-permute-start(f32[128,512]{1,0:T(8,128)S(1)} %broadcast_select_fusion.3), channel_id=1, source_target_pairs={{0,2},{1,3},{2,4},{3,5},{4,6},{5,7},{8,10},{9,11},{10,12},{11,13},... | collective-permute-start | bytes 786440 | tf_op jit(solution)/shard_map/ppermute | solution.py:326
  109.7 8.3 %collective-permute-start.24 = (f32[128,512]{1,0:T(8,128)S(1)}, f32[128,512]{1,0:T(8,128)S(1)}, u32[]{:S(2)}, u32[]{:S(2)}) collective-permute-start(f32[128,512]{1,0:T(8,128)S(1)} %broadcast_select_fusion.1), channel_id=1, source_target_pairs={{0,2},{1,3},{2,4},{3,5},{4,6},{5,7},{8,10},{9,11},{10,12},{11,13},... | collective-permute-start | bytes 786440 | tf_op jit(solution)/shard_map/ppermute | solution.py:326
  112.8 8.3 %collective-permute-start.23 = (f32[128,512]{1,0:T(8,128)S(1)}, f32[128,512]{1,0:T(8,128)S(1)}, u32[]{:S(2)}, u32[]{:S(2)}) collective-permute-start(f32[128,512]{1,0:T(8,128)S(1)} %broadcast_select_fusion.2), channel_id=1, source_target_pairs={{0,2},{1,3},{2,4},{3,5},{4,6},{5,7},{8,10},{9,11},{10,12},{11,13},... | collective-permute-start | bytes 786440 | tf_op jit(solution)/shard_map/ppermute | solution.py:326
  134.1 0.8 collective-permute-start.25
  135.2 17.7 %collective-permute-start.26 = (f32[256,512]{1,0:T(8,128)S(1)}, f32[256,512]{1,0:T(8,128)}, u32[]{:S(2)}, u32[]{:S(2)}) collective-permute-start(f32[256,512]{1,0:T(8,128)S(1)} %slice_select_fusion), channel_id=1, source_target_pairs={{0,16},{8,24},{1,17},{9,25},{2,18},{10,26},{3,19},{11,27},{4,20},{... | collective-permute-start | bytes 1572872 | tf_op jit(solution)/shard_map/ppermute | solution.py:417
  152.9 15.4 %collective-permute-start.27 = (f32[256,512]{1,0:T(8,128)}, f32[256,512]{1,0:T(8,128)}, u32[]{:S(2)}, u32[]{:S(2)}) collective-permute-start(f32[256,512]{1,0:T(8,128)} %collective-permute-done.26.refs_3_), channel_id=1, source_target_pairs={{16,24},{24,16},{17,25},{25,17},{18,26},{26,18},{19,27},{27,19},{2... | collective-permute-start | bytes 1572872 | tf_op jit(solution)/shard_map/ppermute | solution.py:418
  (44 other events, 387.9 us)
Sparse Core Ops, SparseCore 0:
  100.1 32.5 all-gather.2
  134.9 33.2 all-gather.4

commit v9 on v3

--- a/solution.py
+++ b/solution.py
@@ -288,7 +288,7 @@
         copy.wait()
 
 
-LAG = 2
+LAG = 1
 
 
 def steps(n_cols, parts):
@@ -404,12 +404,12 @@
             d = 1 << log
             far = [(p, p + d) for p in range(d)]
             if log == 0:
-                at += 2
+                at += 1
                 whole = yield give(at, lax.ppermute(old_top, "prow", far))
                 tops.append(whole)
             else:
                 half = jnp.where(odd, old_top[nb // 2 :], old_top[: nb // 2])
-                at += 3
+                at += 1
                 one = yield give(at, lax.ppermute(half, "prow", far))
                 two = lax.ppermute(one, "prow", [(p, p ^ 1) for p in range(d, 2 * d)])
                 tops += [one, two]
@@ -422,13 +422,13 @@
     half_slot = jax.ShapeDtypeStruct((nb // 2, cols), f32)
 
     def exchange_rider():
-        table, owner = yield give(2, call(
+        table, owner = yield give(1, call(
             functools.partial(index_kernel, row_dev=row_dev),
             (jax.ShapeDtypeStruct((8, nb), jnp.int32), jax.ShapeDtypeStruct((nb, LANES), jnp.int32)),
             [SMEM, VMEM], (VMEM, VMEM),
         )(here, pivots.reshape(1, nb)))
-        held = yield give(3, call(gather_kernel, slot, [SMEM, VMEM], VMEM)(table, matrix))
-        at = 5
+        held = yield give(2, call(gather_kernel, slot, [SMEM, VMEM], VMEM)(table, matrix))
+        at = 3
         displaced = held
         log = 0
         half = None
@@ -440,8 +440,8 @@
                 arrived = [whole]
             else:
                 near = [(p, p ^ 1) for p in range(n_rows)]
-                one = yield give(at + 4, lax.ppermute(half, "prow", far))
-                at += 5
+                one = yield give(at + 2, lax.ppermute(half, "prow", far))
+                at += 3
                 two = yield give(at, lax.ppermute(one, "prow", near))
                 arrived = [one, two]
                 whole = both_halves(one, two)
@@ -489,7 +489,7 @@
 def solution(mesh):
     n_rows, n_cols = mesh.shape["prow"], mesh.shape["pcol"]
     return jax.shard_map(
-        functools.partial(local, n_rows=n_rows, n_cols=n_cols, parts=8),
+        functools.partial(local, n_rows=n_rows, n_cols=n_cols, parts=4),
         mesh=mesh,
         in_specs=(P("prow", "pcol"), P(), P(), P()),
         out_specs=P("prow", "pcol"),

time: 168 us -> 196 us (1.17)
  waiting for transfers between devices: 27.3 us -> 84.3 us
  starting transfers between devices: 90.4 us -> 54 us
  local copies, waits for them, and re-layouts: 13.8 us -> 18.5 us
  other arithmetic: 7.25 us -> 10 us
    ppermute x16 -> x8, waiting for transfers between devices: 16.3 us -> 45.7 us  [spread(): cross.append(lax.ppermute(aside, 'pcol', across))]
    ppermute x16 -> x8, starting transfers between devices: 44.3 us -> 23.8 us  [spread(): cross.append(lax.ppermute(aside, 'pcol', across))]
    ppermute x1, waiting for transfers between devices: 0.01 us -> 19.8 us  [old_top_rider(): one = (yield give(at, lax.ppermute(half, 'prow', far)))]
    ppermute x14 -> x7, starting transfers between devices: 41.3 us -> 24.4 us  [spread(): chain.append(lax.ppermute(ahead, 'pcol', along))]
    ppermute x14 -> x7, waiting for transfers between devices: 11 us -> 18.8 us  [spread(): chain.append(lax.ppermute(ahead, 'pcol', along))]
    unnamed x120 -> x76, local copies, waits for them, and re-layouts: 9.3 us -> 14 us
    select_n x10 -> x7, other arithmetic: 3.1 us -> 6.71 us  [spread(): aside = jnp.where(col == 0, aside, came)]
    select_n x1 -> x0, other arithmetic: 2.18 us -> none  [spread(): ahead = jnp.where(col == 0, ahead, jnp.where(col == 1, fed, came))]
  transfers between devices with their start and end apart: 36 -> 21, of which waited for: 13 -> 16; matrix products, arithmetic and copies ran while one was open for 4% -> 5% of each run, Pallas kernels for 9% -> 8%
where the time goes in v9:
time: 196 us; the launch traced here: 194 us
  waiting for transfers between devices  84.3 us (43%)
  starting transfers between devices  54 us (28%)
  Pallas kernels  26.3 us (13%)
  local copies, waits for them, and re-layouts  18.5 us (9%)
  other arithmetic  10 us (5%)
    ppermute x8, waiting for transfers between devices, spread(): cross.append(lax.ppermute(aside, 'pcol', across))  45.7 us
    ppermute x7, starting transfers between devices, spread(): chain.append(lax.ppermute(ahead, 'pcol', along))  24.4 us
    ppermute x8, starting transfers between devices, spread(): cross.append(lax.ppermute(aside, 'pcol', across))  23.8 us
    ppermute x1, waiting for transfers between devices, old_top_rider(): one = (yield give(at, lax.ppermute(half, 'prow', far)))  19.8 us
    ppermute x7, waiting for transfers between devices, spread(): chain.append(lax.ppermute(ahead, 'pcol', along))  18.8 us
    unnamed x76, local copies, waits for them, and re-layouts  14 us
    pallas_call x1, Pallas kernels, local(): call(functools.partial(final_kernel, n_bufs=len(bufs), n_tops=len(tops),...  10.6 us
    select_n x7, other arithmetic, spread(): aside = jnp.where(col == 0, aside, came)  6.71 us
  transfers between devices with their start and end apart: 21, of which 16 were waited for; matrix products, arithmetic and copies ran while one was open for 5% of the time, Pallas kernels for 8%

profile of v9, /device:TPU:10, one launch (start us, length us, event | category | flops | bytes accessed | tf_op | source)
XLA Modules:
  0.0 193.8 jit_solution(5573421576019326824)
XLA Ops:
  0.0 3.7 %fusion = (f32[256,512]{1,0:T(8,128)}, f32[256,512]{1,0:T(8,128)}, f32[256,512]{1,0:T(8,128)}, f32[256,512]{1,0:T(8,128)}, f32[256,512]{1,0:T(8,128)S(1)}, /*ind...) fusion(f32[2048,640]{1,0:T(8,128)} %matrix_ref.5), kind=kLoop, calls=%fused_computation.20 | loop fusion | bytes 8388608 | tf_op jit(solution)/shard_map/slice | solution.py:362
  3.8 3.4 %collective-permute-start.1 = (f32[256,512]{1,0:T(8,128)}, f32[256,512]{1,0:T(8,128)S(1)}, u32[]{:S(2)}, u32[]{:S(2)}) collective-permute-start(f32[256,512]{1,0:T(8,128)} %get-tuple-element.101), channel_id=1, source_target_pairs={{0,1},{2,3},{3,2},{4,5},{5,4},{6,7},{7,6},{8,9},{10,11},{11,10},{1... | collective-permute-start | bytes 1572872 | tf_op jit(solution)/shard_map/ppermute | solution.py:328
  7.2 3.5 %collective-permute-start = (f32[256,512]{1,0:T(8,128)S(1)}, f32[256,512]{1,0:T(8,128)S(1)}, u32[]{:S(2)}, u32[]{:S(2)}) collective-permute-start(f32[256,512]{1,0:T(8,128)S(1)} %get-tuple-element.102), channel_id=1, source_target_pairs={{0,2},{1,3},{2,4},{3,5},{4,6},{5,7},{8,10},{9,11},{10,12},{11,13},... | collective-permute-start | bytes 1572872 | tf_op jit(solution)/shard_map/ppermute | solution.py:327
  12.4 7.1 %collective-permute-done.1.refs_4_.refs_7_ = f32[256,512]{1,0:T(8,128)S(1)} collective-permute-done((f32[256,512]{1,0:T(8,128)}, f32[256,512]{1,0:T(8,128)S(1)}, u32[]{:S(2)}, u32[]{:S(2)}) %collective-permute-start.1) | collective-permute-done | bytes 524320 | tf_op jit(solution)/shard_map/ppermute | solution.py:328
  19.5 2.9 %collective-permute-done.refs_0_ = f32[256,512]{1,0:T(8,128)S(1)} collective-permute-done((f32[256,512]{1,0:T(8,128)S(1)}, f32[256,512]{1,0:T(8,128)S(1)}, u32[]{:S(2)}, u32[]{:S(2)}) %collective-permute-start) | collective-permute-done | bytes 524320 | tf_op jit(solution)/shard_map/ppermute | solution.py:327
  25.7 3.5 %collective-permute-start.2 = (f32[256,512]{1,0:T(8,128)S(1)}, f32[256,512]{1,0:T(8,128)S(1)}, u32[]{:S(2)}, u32[]{:S(2)}) collective-permute-start(f32[256,512]{1,0:T(8,128)S(1)} %get-tuple-element.116), channel_id=1, source_target_pairs={{0,2},{1,3},{2,4},{3,5},{4,6},{5,7},{8,10},{9,11},{10,12},{11,13},... | collective-permute-start | bytes 1572872 | tf_op jit(solution)/shard_map/ppermute | solution.py:327
  29.2 2.5 %copy-done = f32[2048,640]{1,0:T(8,128)S(1)} copy-done((f32[2048,640]{1,0:T(8,128)S(1)}, f32[2048,640]{1,0:T(8,128)}, u32[]{:S(2)}) %copy-start) | copy-done | bytes 5242904
  31.6 3.5 %shard_map.56.held_ref = f32[512,640]{1,0:T(8,128)S(1)} custom-call(s32[8,512]{1,0:T(8,128)S(1)} %get-tuple-element.52.table_ref, f32[2048,640]{1,0:T(8,128)S(1)} %copy-done), custom_call_target="tpu_custom_call" | custom-call | tf_op jit(solution)/shard_map/pallas_call | solution.py:430
  40.6 3.4 %collective-permute-start.5 = (f32[256,512]{1,0:T(8,128)S(1)}, f32[256,512]{1,0:T(8,128)S(1)}, u32[]{:S(2)}, u32[]{:S(2)}) collective-permute-start(f32[256,512]{1,0:T(8,128)S(1)} %get-tuple-element.113), channel_id=1, source_target_pairs={{0,1},{2,3},{3,2},{4,5},{5,4},{6,7},{7,6},{8,9},{10,11},{11,10},{1... | collective-permute-start | bytes 1572872 | tf_op jit(solution)/shard_map/ppermute | solution.py:328
  44.0 3.5 %collective-permute-start.4 = (f32[256,512]{1,0:T(8,128)S(1)}, f32[256,512]{1,0:T(8,128)S(1)}, u32[]{:S(2)}, u32[]{:S(2)}) collective-permute-start(f32[256,512]{1,0:T(8,128)S(1)} %get-tuple-element.114), channel_id=1, source_target_pairs={{0,2},{1,3},{2,4},{3,5},{4,6},{5,7},{8,10},{9,11},{10,12},{11,13},... | collective-permute-start | bytes 1572872 | tf_op jit(solution)/shard_map/ppermute | solution.py:327
  47.5 8.7 %collective-permute-done.5.refs_6_.refs_9_ = f32[256,512]{1,0:T(8,128)S(1)} collective-permute-done((f32[256,512]{1,0:T(8,128)S(1)}, f32[256,512]{1,0:T(8,128)S(1)}, u32[]{:S(2)}, u32[]{:S(2)}) %collective-permute-start.5) | collective-permute-done | bytes 524320 | tf_op jit(solution)/shard_map/ppermute | solution.py:328
  56.2 3.2 %collective-permute-done.4.refs_2_ = f32[256,512]{1,0:T(8,128)S(1)} collective-permute-done((f32[256,512]{1,0:T(8,128)S(1)}, f32[256,512]{1,0:T(8,128)S(1)}, u32[]{:S(2)}, u32[]{:S(2)}) %collective-permute-start.4) | collective-permute-done | bytes 524320 | tf_op jit(solution)/shard_map/ppermute | solution.py:327
  62.6 3.5 %collective-permute-start.7 = (f32[256,512]{1,0:T(8,128)S(1)}, f32[256,512]{1,0:T(8,128)S(1)}, u32[]{:S(2)}, u32[]{:S(2)}) collective-permute-start(f32[256,512]{1,0:T(8,128)S(1)} %get-tuple-element.112), channel_id=1, source_target_pairs={{0,2},{1,3},{2,4},{3,5},{4,6},{5,7},{8,10},{9,11},{10,12},{11,13},... | collective-permute-start | bytes 1572872 | tf_op jit(solution)/shard_map/ppermute | solution.py:327
  68.3 6.4 %collective-permute-done.8.refs_7_.refs_10_ = f32[256,512]{1,0:T(8,128)S(1)} collective-permute-done((f32[256,512]{1,0:T(8,128)S(1)}, f32[256,512]{1,0:T(8,128)S(1)}, u32[]{:S(2)}, u32[]{:S(2)}) %collective-permute-start.8) | collective-permute-done | bytes 524320 | tf_op jit(solution)/shard_map/ppermute | solution.py:328
  76.8 2.4 %broadcast_select_fusion.6 = (f32[256,512]{1,0:T(8,128)}, f32[256,512]{1,0:T(8,128)}) fusion(f32[256,512]{1,0:T(8,128)S(1)} %collective-permute-done.7.refs_3_, pred[]{:T(512)S(6)} %eq.12, f32[2048,640]{1,0:T(8,128)} %matrix_ref.5, f32[256,512]{1,0:T(8,128)S(1)} %copy-done.28, f32[256,512]{1,0:T(8,128)S(1)} %collective-permute-done.8.refs_7_.refs_10_, ...), kind=kLoop, calls=%fused_computation.14 | loop fusion | flops 393216 | bytes 3145730 | tf_op jit(solution)/shard_map/jit(_where)/select_n | solution.py:325
  79.3 3.4 %collective-permute-start.10 = (f32[256,512]{1,0:T(8,128)}, f32[256,512]{1,0:T(8,128)}, u32[]{:S(2)}, u32[]{:S(2)}) collective-permute-start(f32[256,512]{1,0:T(8,128)} %get-tuple-element.109), channel_id=1, source_target_pairs={{0,1},{2,3},{3,2},{4,5},{5,4},{6,7},{7,6},{8,9},{10,11},{11,10},{1... | collective-permute-start | bytes 1572872 | tf_op jit(solution)/shard_map/ppermute | solution.py:328
  82.7 3.5 %collective-permute-start.9 = (f32[256,512]{1,0:T(8,128)}, f32[256,512]{1,0:T(8,128)}, u32[]{:S(2)}, u32[]{:S(2)}) collective-permute-start(f32[256,512]{1,0:T(8,128)} %get-tuple-element.110), channel_id=1, source_target_pairs={{0,2},{1,3},{2,4},{3,5},{4,6},{5,7},{8,10},{9,11},{10,12},{11,13},... | collective-permute-start | bytes 1572872 | tf_op jit(solution)/shard_map/ppermute | solution.py:327
  86.9 6.1 %collective-permute-done.10.refs_8_.refs_11_ = f32[256,512]{1,0:T(8,128)} collective-permute-done((f32[256,512]{1,0:T(8,128)}, f32[256,512]{1,0:T(8,128)}, u32[]{:S(2)}, u32[]{:S(2)}) %collective-permute-start.10) | collective-permute-done | bytes 524320 | tf_op jit(solution)/shard_map/ppermute | solution.py:328
  93.0 3.2 %collective-permute-done.9.refs_4_ = f32[256,512]{1,0:T(8,128)} collective-permute-done((f32[256,512]{1,0:T(8,128)}, f32[256,512]{1,0:T(8,128)}, u32[]{:S(2)}, u32[]{:S(2)}) %collective-permute-start.9) | collective-permute-done | bytes 524320 | tf_op jit(solution)/shard_map/ppermute | solution.py:327
  96.1 2.5 %copy-done.1 = f32[2048,640]{1,0:T(8,128)S(1)} copy-done((f32[2048,640]{1,0:T(8,128)S(1)}, f32[2048,640]{1,0:T(8,128)}, u32[]{:S(2)}) %copy-start.1) | copy-done | bytes 5242904
  110.5 2.4 %collective-permute-start.13 = (f32[256,512]{1,0:T(8,128)}, f32[256,512]{1,0:T(8,128)}, u32[]{:S(2)}, u32[]{:S(2)}) collective-permute-start(f32[256,512]{1,0:T(8,128)} %get-tuple-element.107), channel_id=1, source_target_pairs={{0,1},{2,3},{3,2},{4,5},{5,4},{6,7},{7,6},{8,9},{10,11},{11,10},{1... | collective-permute-start | bytes 1572872 | tf_op jit(solution)/shard_map/ppermute | solution.py:328
  112.9 3.5 %collective-permute-start.12 = (f32[256,512]{1,0:T(8,128)}, f32[256,512]{1,0:T(8,128)}, u32[]{:S(2)}, u32[]{:S(2)}) collective-permute-start(f32[256,512]{1,0:T(8,128)} %get-tuple-element.108), channel_id=1, source_target_pairs={{0,2},{1,3},{2,4},{3,5},{4,6},{5,7},{8,10},{9,11},{10,12},{11,13},... | collective-permute-start | bytes 1572872 | tf_op jit(solution)/shard_map/ppermute | solution.py:327
  116.4 10.6 %collective-permute-done.13.refs_12_ = f32[256,512]{1,0:T(8,128)} collective-permute-done((f32[256,512]{1,0:T(8,128)}, f32[256,512]{1,0:T(8,128)}, u32[]{:S(2)}, u32[]{:S(2)}) %collective-permute-start.13) | collective-permute-done | bytes 524320 | tf_op jit(solution)/shard_map/ppermute | solution.py:328
  130.4 3.4 %collective-permute-start.17 = (f32[256,512]{1,0:T(8,128)S(1)}, f32[256,512]{1,0:T(8,128)S(1)}, u32[]{:S(2)}, u32[]{:S(2)}) collective-permute-start(f32[256,512]{1,0:T(8,128)S(1)} %get-tuple-element.105), channel_id=1, source_target_pairs={{0,1},{2,3},{3,2},{4,5},{5,4},{6,7},{7,6},{8,9},{10,11},{11,10},{1... | collective-permute-start | bytes 1572872 | tf_op jit(solution)/shard_map/ppermute | solution.py:328
  133.9 3.5 %collective-permute-start.16 = (f32[256,512]{1,0:T(8,128)S(1)}, f32[256,512]{1,0:T(8,128)S(1)}, u32[]{:S(2)}, u32[]{:S(2)}) collective-permute-start(f32[256,512]{1,0:T(8,128)S(1)} %get-tuple-element.106), channel_id=1, source_target_pairs={{0,2},{1,3},{2,4},{3,5},{4,6},{5,7},{8,10},{9,11},{10,12},{11,13},... | collective-permute-start | bytes 1572872 | tf_op jit(solution)/shard_map/ppermute | solution.py:327
  140.4 2.4 %shard_map.59 = (f32[512,640]{1,0:T(8,128)S(1)}, f32[256,640]{1,0:T(8,128)}) custom-call(s32[2]{0:T(128)S(1)} %pad_add_fusion.where_ref, s32[512,128]{1,0:T(8,128)S(1)} %get-tuple-element.68.owner_ref, f32[512,640]{1,0:T(8,128)S(1)} %copy-done.24, f32[256,640]{1,0:T(8,128)} %collective-permute-done.11.refs_0_, f32[256,640]{1,0:T(8,128)} %collective-permute-done.15.refs_1_), custom_call_target="tpu_custom_call" | custom-call | tf_op jit(solution)/shard_map/pallas_call | solution.py:448
  145.6 3.2 %collective-permute-done.16.refs_6_ = f32[256,512]{1,0:T(8,128)S(1)} collective-permute-done((f32[256,512]{1,0:T(8,128)S(1)}, f32[256,512]{1,0:T(8,128)S(1)}, u32[]{:S(2)}, u32[]{:S(2)}) %collective-permute-start.16) | collective-permute-done | bytes 524320 | tf_op jit(solution)/shard_map/ppermute | solution.py:327
  148.7 19.8 %collective-permute-done.18.refs_16_ = f32[256,512]{1,0:T(8,128)S(1)} collective-permute-done((f32[256,512]{1,0:T(8,128)S(1)}, f32[256,512]{1,0:T(8,128)S(1)}, u32[]{:S(2)}, u32[]{:S(2)}) %collective-permute-start.18) | collective-permute-done | bytes 524320 | tf_op jit(solution)/shard_map/ppermute | solution.py:413
  168.7 2.9 %collective-permute-start.19 = (f32[256,512]{1,0:T(8,128)S(1)}, f32[256,512]{1,0:T(8,128)S(1)}, u32[]{:S(2)}, u32[]{:S(2)}) collective-permute-start(f32[256,512]{1,0:T(8,128)S(1)} %broadcast_select_fusion.3), channel_id=1, source_target_pairs={{0,1},{2,3},{3,2},{4,5},{5,4},{6,7},{7,6},{8,9},{10,11},{11,10},{1... | collective-permute-start | bytes 1572872 | tf_op jit(solution)/shard_map/ppermute | solution.py:328
  173.7 5.9 %shard_map.60 = (f32[512,640]{1,0:T(8,128)S(1)}, f32[512,640]{1,0:T(8,128)S(1)}) custom-call(s32[2]{0:T(128)S(1)} %pad_add_fusion.where_ref, f32[512,640]{1,0:T(8,128)S(1)} %get-tuple-element.90.top_in_ref, f32[512,512]{1,0:T(8,128)S(1)} %copy-done.26, f32[512,512]{1,0:T(8,128)S(1)} %copy-done.27), custom_call_target="tpu_custom_call" | custom-call | flops 4026531840 | tf_op jit(solution)/shard_map/pallas_call | solution.py:455
  179.6 3.4 %collective-permute-done.19.refs_14_ = f32[256,512]{1,0:T(8,128)S(1)} collective-permute-done((f32[256,512]{1,0:T(8,128)S(1)}, f32[256,512]{1,0:T(8,128)S(1)}, u32[]{:S(2)}, u32[]{:S(2)}) %collective-permute-start.19) | collective-permute-done | bytes 524320 | tf_op jit(solution)/shard_map/ppermute | solution.py:328
  183.1 10.6 %shard_map.61 = f32[2048,640]{1,0:T(8,128)} custom-call(s32[2]{0:T(128)S(1)} %pad_add_fusion.where_ref, s32[8,512]{1,0:T(8,128)S(1)} %get-tuple-element.52.table_ref, s32[8]{0:T(128)S(1)} %dynamic-slice_bitcast_fusion.choice_ref, f32[512,640]{1,0:T(8,128)S(1)} %maximum_select_fusion.displaced_ref, f32[512,640]{1,0:T(8,128)S(1)} %get-tuple-element.91.weights_ref, ...), custom_call_target="tpu_custom_call" | custom-call | flops 4026531840 | bytes 14680064 | tf_op jit(solution)/shard_map/pallas_call | solution.py:467
  (108 shorter events, 41.7 us)
Async XLA Ops:
  3.7 18.9 %copy-start.32 = (f32[256,512]{1,0:T(8,128)}, f32[256,512]{1,0:T(8,128)S(1)}, u32[]{:S(2)}) copy-start(f32[256,512]{1,0:T(8,128)S(1)} %get-tuple-element.55) | copy-start | bytes 1572868
  3.8 15.8 %collective-permute-start.1 = (f32[256,512]{1,0:T(8,128)}, f32[256,512]{1,0:T(8,128)S(1)}, u32[]{:S(2)}, u32[]{:S(2)}) collective-permute-start(f32[256,512]{1,0:T(8,128)} %get-tuple-element.101), channel_id=1, source_target_pairs={{0,1},{2,3},{3,2},{4,5},{5,4},{6,7},{7,6},{8,9},{10,11},{11,10},{1... | collective-permute-start | bytes 1572872 | tf_op jit(solution)/shard_map/ppermute | solution.py:328
  7.2 15.3 %collective-permute-start = (f32[256,512]{1,0:T(8,128)S(1)}, f32[256,512]{1,0:T(8,128)S(1)}, u32[]{:S(2)}, u32[]{:S(2)}) collective-permute-start(f32[256,512]{1,0:T(8,128)S(1)} %get-tuple-element.102), channel_id=1, source_target_pairs={{0,2},{1,3},{2,4},{3,5},{4,6},{5,7},{8,10},{9,11},{10,12},{11,13},... | collective-permute-start | bytes 1572872 | tf_op jit(solution)/shard_map/ppermute | solution.py:327
  23.3 14.4 %collective-permute-start.3 = (f32[256,512]{1,0:T(8,128)S(1)}, f32[256,512]{1,0:T(8,128)S(1)}, u32[]{:S(2)}, u32[]{:S(2)}) collective-permute-start(f32[256,512]{1,0:T(8,128)S(1)} %get-tuple-element.115), channel_id=1, source_target_pairs={{0,1},{2,3},{3,2},{4,5},{5,4},{6,7},{7,6},{8,9},{10,11},{11,10},{1... | collective-permute-start | bytes 1572872 | tf_op jit(solution)/shard_map/ppermute | solution.py:328
  25.7 14.1 %collective-permute-start.2 = (f32[256,512]{1,0:T(8,128)S(1)}, f32[256,512]{1,0:T(8,128)S(1)}, u32[]{:S(2)}, u32[]{:S(2)}) collective-permute-start(f32[256,512]{1,0:T(8,128)S(1)} %get-tuple-element.116), channel_id=1, source_target_pairs={{0,2},{1,3},{2,4},{3,5},{4,6},{5,7},{8,10},{9,11},{10,12},{11,13},... | collective-permute-start | bytes 1572872 | tf_op jit(solution)/shard_map/ppermute | solution.py:327
  35.2 24.2 %copy-start.28 = (f32[256,512]{1,0:T(8,128)S(1)}, f32[256,512]{1,0:T(8,128)}, u32[]{:S(2)}) copy-start(f32[256,512]{1,0:T(8,128)} %get-tuple-element.53) | copy-start | bytes 1572868
  35.2 24.2 %copy-start.34 = (f32[256,512]{1,0:T(8,128)S(1)}, f32[256,512]{1,0:T(8,128)}, u32[]{:S(2)}) copy-start(f32[256,512]{1,0:T(8,128)} %get-tuple-element.65) | copy-start | bytes 1572868
  39.8 19.6 %collective-permute-start.6 = (f32[512,640]{1,0:T(8,128)S(1)}, f32[512,640]{1,0:T(8,128)S(1)}, u32[]{:S(2)}, u32[]{:S(2)}) collective-permute-start(f32[512,640]{1,0:T(8,128)S(1)} %shard_map.56.held_ref), channel_id=1, source_target_pairs={{0,8},{8,0},{16,24},{24,16},{1,9},{9,1},{17,25},{25,17},{2,10},{10... | collective-permute-start | bytes 3932168 | tf_op jit(solution)/shard_map/ppermute | solution.py:439
  40.6 15.7 %collective-permute-start.5 = (f32[256,512]{1,0:T(8,128)S(1)}, f32[256,512]{1,0:T(8,128)S(1)}, u32[]{:S(2)}, u32[]{:S(2)}) collective-permute-start(f32[256,512]{1,0:T(8,128)S(1)} %get-tuple-element.113), channel_id=1, source_target_pairs={{0,1},{2,3},{3,2},{4,5},{5,4},{6,7},{7,6},{8,9},{10,11},{11,10},{1... | collective-permute-start | bytes 1572872 | tf_op jit(solution)/shard_map/ppermute | solution.py:328
  44.0 15.4 %collective-permute-start.4 = (f32[256,512]{1,0:T(8,128)S(1)}, f32[256,512]{1,0:T(8,128)S(1)}, u32[]{:S(2)}, u32[]{:S(2)}) collective-permute-start(f32[256,512]{1,0:T(8,128)S(1)} %get-tuple-element.114), channel_id=1, source_target_pairs={{0,2},{1,3},{2,4},{3,5},{4,6},{5,7},{8,10},{9,11},{10,12},{11,13},... | collective-permute-start | bytes 1572872 | tf_op jit(solution)/shard_map/ppermute | solution.py:327
  60.2 14.5 %collective-permute-start.8 = (f32[256,512]{1,0:T(8,128)S(1)}, f32[256,512]{1,0:T(8,128)S(1)}, u32[]{:S(2)}, u32[]{:S(2)}) collective-permute-start(f32[256,512]{1,0:T(8,128)S(1)} %get-tuple-element.111), channel_id=1, source_target_pairs={{0,1},{2,3},{3,2},{4,5},{5,4},{6,7},{7,6},{8,9},{10,11},{11,10},{1... | collective-permute-start | bytes 1572872 | tf_op jit(solution)/shard_map/ppermute | solution.py:328
  62.6 14.2 %collective-permute-start.7 = (f32[256,512]{1,0:T(8,128)S(1)}, f32[256,512]{1,0:T(8,128)S(1)}, u32[]{:S(2)}, u32[]{:S(2)}) collective-permute-start(f32[256,512]{1,0:T(8,128)S(1)} %get-tuple-element.112), channel_id=1, source_target_pairs={{0,2},{1,3},{2,4},{3,5},{4,6},{5,7},{8,10},{9,11},{10,12},{11,13},... | collective-permute-start | bytes 1572872 | tf_op jit(solution)/shard_map/ppermute | solution.py:327
  67.7 19.1 %collective-permute-start.11 = (f32[256,640]{1,0:T(8,128)}, f32[256,640]{1,0:T(8,128)}, u32[]{:S(2)}, u32[]{:S(2)}) collective-permute-start(f32[256,640]{1,0:T(8,128)} %get-tuple-element.70), channel_id=1, source_target_pairs={{0,16},{8,24},{16,0},{24,8},{1,17},{9,25},{17,1},{25,9},{2,18},{10... | collective-permute-start | bytes 1966088 | tf_op jit(solution)/shard_map/ppermute | solution.py:443
  79.3 13.7 %collective-permute-start.10 = (f32[256,512]{1,0:T(8,128)}, f32[256,512]{1,0:T(8,128)}, u32[]{:S(2)}, u32[]{:S(2)}) collective-permute-start(f32[256,512]{1,0:T(8,128)} %get-tuple-element.109), channel_id=1, source_target_pairs={{0,1},{2,3},{3,2},{4,5},{5,4},{6,7},{7,6},{8,9},{10,11},{11,10},{1... | collective-permute-start | bytes 1572872 | tf_op jit(solution)/shard_map/ppermute | solution.py:328
  82.7 13.4 %collective-permute-start.9 = (f32[256,512]{1,0:T(8,128)}, f32[256,512]{1,0:T(8,128)}, u32[]{:S(2)}, u32[]{:S(2)}) collective-permute-start(f32[256,512]{1,0:T(8,128)} %get-tuple-element.110), channel_id=1, source_target_pairs={{0,2},{1,3},{2,4},{3,5},{4,6},{5,7},{8,10},{9,11},{10,12},{11,13},... | collective-permute-start | bytes 1572872 | tf_op jit(solution)/shard_map/ppermute | solution.py:327
  106.5 22.7 %collective-permute-start.14 = (f32[512,512]{1,0:T(8,128)}, f32[512,512]{1,0:T(8,128)}, u32[]{:S(2)}, u32[]{:S(2)}) collective-permute-start(f32[512,512]{1,0:T(8,128)} %shard_map.58), channel_id=1, source_target_pairs={{0,8},{1,9},{2,10},{3,11},{4,12},{5,13},{6,14},{7,15}} | collective-permute-start | bytes 3145736 | tf_op jit(solution)/shard_map/ppermute | solution.py:408
  108.2 21.0 %collective-permute-start.15 = (f32[256,640]{1,0:T(8,128)}, f32[256,640]{1,0:T(8,128)}, u32[]{:S(2)}, u32[]{:S(2)}) collective-permute-start(f32[256,640]{1,0:T(8,128)} %collective-permute-done.11.refs_0_), channel_id=1, source_target_pairs={{0,8},{8,0},{16,24},{24,16},{1,9},{9,1},{17,25},{25,17},{2,10},{10... | collective-permute-start | bytes 1966088 | tf_op jit(solution)/shard_map/ppermute | solution.py:445
  110.5 16.5 %collective-permute-start.13 = (f32[256,512]{1,0:T(8,128)}, f32[256,512]{1,0:T(8,128)}, u32[]{:S(2)}, u32[]{:S(2)}) collective-permute-start(f32[256,512]{1,0:T(8,128)} %get-tuple-element.107), channel_id=1, source_target_pairs={{0,1},{2,3},{3,2},{4,5},{5,4},{6,7},{7,6},{8,9},{10,11},{11,10},{1... | collective-permute-start | bytes 1572872 | tf_op jit(solution)/shard_map/ppermute | solution.py:328
  112.9 16.3 %collective-permute-start.12 = (f32[256,512]{1,0:T(8,128)}, f32[256,512]{1,0:T(8,128)}, u32[]{:S(2)}, u32[]{:S(2)}) collective-permute-start(f32[256,512]{1,0:T(8,128)} %get-tuple-element.108), channel_id=1, source_target_pairs={{0,2},{1,3},{2,4},{3,5},{4,6},{5,7},{8,10},{9,11},{10,12},{11,13},... | collective-permute-start | bytes 1572872 | tf_op jit(solution)/shard_map/ppermute | solution.py:327
  130.4 15.1 %collective-permute-start.17 = (f32[256,512]{1,0:T(8,128)S(1)}, f32[256,512]{1,0:T(8,128)S(1)}, u32[]{:S(2)}, u32[]{:S(2)}) collective-permute-start(f32[256,512]{1,0:T(8,128)S(1)} %get-tuple-element.105), channel_id=1, source_target_pairs={{0,1},{2,3},{3,2},{4,5},{5,4},{6,7},{7,6},{8,9},{10,11},{11,10},{1... | collective-permute-start | bytes 1572872 | tf_op jit(solution)/shard_map/ppermute | solution.py:328
  133.9 14.8 %collective-permute-start.16 = (f32[256,512]{1,0:T(8,128)S(1)}, f32[256,512]{1,0:T(8,128)S(1)}, u32[]{:S(2)}, u32[]{:S(2)}) collective-permute-start(f32[256,512]{1,0:T(8,128)S(1)} %get-tuple-element.106), channel_id=1, source_target_pairs={{0,2},{1,3},{2,4},{3,5},{4,6},{5,7},{8,10},{9,11},{10,12},{11,13},... | collective-permute-start | bytes 1572872 | tf_op jit(solution)/shard_map/ppermute | solution.py:327
  138.9 29.6 %collective-permute-start.18 = (f32[256,512]{1,0:T(8,128)S(1)}, f32[256,512]{1,0:T(8,128)S(1)}, u32[]{:S(2)}, u32[]{:S(2)}) collective-permute-start(f32[256,512]{1,0:T(8,128)S(1)} %slice_select_fusion), channel_id=1, source_target_pairs={{0,16},{8,24},{1,17},{9,25},{2,18},{10,26},{3,19},{11,27},{4,20},{... | collective-permute-start | bytes 1572872 | tf_op jit(solution)/shard_map/ppermute | solution.py:413
  144.2 24.3 %copy-start.30 = (f32[256,512]{1,0:T(8,128)S(1)}, f32[256,512]{1,0:T(8,128)}, u32[]{:S(2)}) copy-start(f32[256,512]{1,0:T(8,128)} %get-tuple-element.53) | copy-start | bytes 1572868
  144.2 29.5 %copy-start.27 = (f32[512,512]{1,0:T(8,128)S(1)}, f32[512,512]{1,0:T(8,128)}, u32[]{:S(2)}) copy-start(f32[512,512]{1,0:T(8,128)} %upper_ref.1) | copy-start | bytes 3145732
  144.5 29.2 %copy-start.26 = (f32[512,512]{1,0:T(8,128)S(1)}, f32[512,512]{1,0:T(8,128)}, u32[]{:S(2)}) copy-start(f32[512,512]{1,0:T(8,128)} %lower_ref.1) | copy-start | bytes 3145732
  168.5 14.5 %slice-start = ((s8[5242880]{0:T(1024)(128)(4,1)}), s8[4194304]{0:T(1024)(128)(4,1)S(1)}, s32[]{:S(2)}) async-start(s8[5242880]{0:T(1024)(128)(4,1)} %bitcast.5), calls=%async_computation | async-start | bytes 8388608
  168.6 14.4 %slice-start.1 = ((s8[5242880]{0:T(1024)(128)(4,1)}), s8[1048576]{0:T(1024)(128)(4,1)S(1)}, s32[]{:S(2)}) async-start(s8[5242880]{0:T(1024)(128)(4,1)} %bitcast.5), calls=%async_computation.1 | async-start | bytes 2097152
  168.6 14.4 %copy-start.4 = (f32[256,512]{1,0:T(8,128)S(1)}, f32[256,512]{1,0:T(8,128)}, u32[]{:S(2)}) copy-start(f32[256,512]{1,0:T(8,128)} %copy-done.2) | copy-start | bytes 1572868
  168.6 14.4 %copy-start.7 = (f32[256,512]{1,0:T(8,128)S(1)}, f32[256,512]{1,0:T(8,128)}, u32[]{:S(2)}) copy-start(f32[256,512]{1,0:T(8,128)} %copy-done.5) | copy-start | bytes 1572868
  168.6 14.4 %copy-start.10 = (f32[256,512]{1,0:T(8,128)S(1)}, f32[256,512]{1,0:T(8,128)}, u32[]{:S(2)}) copy-start(f32[256,512]{1,0:T(8,128)} %copy-done.8) | copy-start | bytes 1572868
  168.7 14.3 %collective-permute-start.19 = (f32[256,512]{1,0:T(8,128)S(1)}, f32[256,512]{1,0:T(8,128)S(1)}, u32[]{:S(2)}, u32[]{:S(2)}) collective-permute-start(f32[256,512]{1,0:T(8,128)S(1)} %broadcast_select_fusion.3), channel_id=1, source_target_pairs={{0,1},{2,3},{3,2},{4,5},{5,4},{6,7},{7,6},{8,9},{10,11},{11,10},{1... | collective-permute-start | bytes 1572872 | tf_op jit(solution)/shard_map/ppermute | solution.py:328
  171.6 11.4 %collective-permute-start.20 = (f32[256,512]{1,0:T(8,128)S(1)}, f32[256,512]{1,0:T(8,128)S(1)}, u32[]{:S(2)}, u32[]{:S(2)}) collective-permute-start(f32[256,512]{1,0:T(8,128)S(1)} %collective-permute-done.18.refs_16_), channel_id=1, source_target_pairs={{16,24},{24,16},{17,25},{25,17},{18,26},{26,18},{19,27},{27,19},{2... | collective-permute-start | bytes 1572872 | tf_op jit(solution)/shard_map/ppermute | solution.py:414
  (27 other events, 129.7 us)

commit v10 on v3

--- a/solution.py
+++ b/solution.py
@@ -7,7 +7,6 @@
 from jax.experimental.pallas import tpu as pltpu
 from jax.sharding import PartitionSpec as P
 
-HIGHEST = lax.Precision.HIGHEST
 VMEM = pl.BlockSpec(memory_space=pltpu.VMEM)
 SMEM = pl.BlockSpec(memory_space=pltpu.SMEM)
 ANY = pl.BlockSpec(memory_space=pl.ANY)
@@ -100,58 +99,42 @@
             out_ref[pl.ds(j, 1), :] = matrix_ref[pl.ds(table_ref[PICK, j], 1), :]
 
 
-def merge_kernel(where_ref, owner_ref, held_ref, *refs, log, halves):
-    arrived, (merged_ref, half_ref) = refs[: 2 if halves else 1], refs[-2:]
-    me = where_ref[0]
-    mine, theirs = me >> log, (me >> log) ^ 1
-    odd = me & 1
-    nb, cols = held_ref.shape
-    half = nb // 2
-
-    def merge(rows, piece):
-        group = owner_ref[rows, :] >> log
-        take = (group == theirs) | ((theirs == 0) & (group != mine))
-        for q in range(cols // LANES):
-            lane = slice(q * LANES, (q + 1) * LANES)
-            merged_ref[rows, lane] = jnp.where(take, piece[:, lane], held_ref[rows, lane])
-
-    low, high = slice(0, half), slice(half, nb)
-    if halves:
-        @pl.when(odd == 0)
-        def _():
-            merge(low, arrived[0])
-            merge(high, arrived[1])
-
-        @pl.when(odd == 1)
-        def _():
-            merge(low, arrived[1])
-            merge(high, arrived[0])
-    else:
-        merge(slice(0, nb), arrived[0])
-
-    @pl.when(odd == 0)
-    def _():
-        half_ref[...] = merged_ref[low, :]
-
-    @pl.when(odd == 1)
-    def _():
-        half_ref[...] = merged_ref[high, :]
-
-
-def factor_kernel(where_ref, top_in_ref, lower_ref, upper_ref, weights_ref, top_ref):
-    nb, cols = top_in_ref.shape
-    u = jnp.dot(
-        lower_ref[...], top_in_ref[...], precision=HIGHEST,
-        preferred_element_type=jnp.float32,
-    )
+def merge(where_ref, owner_ref, held_ref, came_ref, merged_ref, log):
+    mine, theirs = where_ref[0] >> log, (where_ref[0] >> log) ^ 1
+    group = owner_ref[...] >> log
+    take = (group == theirs) | ((theirs == 0) & (group != mine))
+    for q in range(held_ref.shape[1] // LANES):
+        lane = slice(q * LANES, (q + 1) * LANES)
+        merged_ref[:, lane] = jnp.where(take, came_ref[:, lane], held_ref[:, lane])
+
+
+def merge_kernel(where_ref, owner_ref, held_ref, came_ref, merged_ref, *, log):
+    merge(where_ref, owner_ref, held_ref, came_ref, merged_ref, log)
+
+
+def split(x):
+    hi = x.astype(jnp.bfloat16)
+    return hi, (x - hi.astype(jnp.float32)).astype(jnp.bfloat16)
+
+
+def product(a, b):
+    dot = functools.partial(jnp.dot, preferred_element_type=jnp.float32)
+    return dot(a[1], b[0]) + dot(a[0], b[1]) + dot(a[0], b[0])
+
+
+def factor_kernel(
+    where_ref, owner_ref, held_ref, came_ref, lower_ref, upper_ref, weights_ref, top_ref,
+    new_top, *, log,
+):
+    nb = held_ref.shape[0]
+    merge(where_ref, owner_ref, held_ref, came_ref, new_top, log)
+    u = product(split(lower_ref[...]), split(new_top[...]))
     top_ref[...] = u
-    weights_ref[...] = jnp.dot(
-        upper_ref[...], u, precision=HIGHEST, preferred_element_type=jnp.float32
-    )
+    weights_ref[...] = product(split(upper_ref[...]), split(u))
 
     @pl.when(where_ref[1] == 0)
     def _():
-        top_ref[:, :nb] = top_in_ref[:, :nb]
+        top_ref[:, :nb] = new_top[:, :nb]
         weights_ref[:, :nb] = -upper_ref[...]
 
 
@@ -164,42 +147,33 @@
                     pltpu.make_async_copy(bufs[b], place(i, h), sem).start()
 
 
-def old_top_kernel(where_ref, choice_ref, matrix_ref, *refs, used, n_cols, parts, pairs):
-    bufs, top_ref, sem = dict(zip(used, refs)), refs[-2], refs[-1]
-    nb = top_ref.shape[0]
-    chunk = nb // (2 * pairs)
-    from_matrix = pltpu.make_async_copy(
-        matrix_ref.at[pl.ds(0, nb), pl.ds(0, nb)], top_ref, sem
-    )
-
-    @pl.when(where_ref[0] == 0)
-    def _():
+def old_top_kernel(
+    where_ref, choice_ref, *refs, used, n_cols, parts, pairs
+):
+    own, bufs, top_ref = refs[: 2 * pairs], dict(zip(used, refs[2 * pairs :])), refs[-1]
+    chunk = own[0].shape[0]
+    for k in range(2 * pairs):
+        span = slice(k * chunk, (k + 1) * chunk)
+
         @pl.when(where_ref[1] == 0)
         def _():
-            from_matrix.start()
-
-        @pl.when(where_ref[1] > 0)
-        def _():
-            fetch(
-                choice_ref, bufs,
-                lambda i, h: top_ref.at[pl.ds((2 * i + h) * chunk, chunk), :],
-                sem, n_cols, parts, pairs,
-            )
-
-        from_matrix.wait()
+            top_ref[span, :] = own[k][...]
+
+        for b in sorted({arrival(p, k // 2, k % 2, n_cols, parts) for p in range(1, n_cols)}):
+            @pl.when((where_ref[1] > 0) & (choice_ref[k] == b))
+            def _():
+                top_ref[span, :] = bufs[b][...]
 
 
 def final_kernel(
-    where_ref, table_ref, choice_ref, displaced_ref, weights_ref, top_ref, matrix_ref,
+    where_ref, table_ref, choice_ref, weights_ref, top_ref, matrix_ref,
     *refs, n_bufs, n_tops, n_cols, parts, block,
 ):
-    bufs, tops, out_ref = refs[:n_bufs], refs[n_bufs : n_bufs + n_tops], refs[n_bufs + n_tops]
-    mat, pan, low, w_hi, w_lo, result, in_sem, low_sem, mat_sem, out_sem = refs[
-        n_bufs + n_tops + 1 :
-    ]
+    bufs, refs = refs[:n_bufs], refs[n_bufs:]
+    tops, slots, refs = refs[:n_tops], refs[n_tops : 2 * n_tops], refs[2 * n_tops :]
+    out_ref, mat, pan, low, displaced, w_hi, w_lo, result, in_sem, low_sem, mat_sem, out_sem = refs
     rows, cols = matrix_ref.shape
     nb = weights_ref.shape[0]
-    half = nb // 2
     chunk = rows // (2 * parts)
     row = where_ref[0]
     first_row, first_col = row == 0, where_ref[1] == 0
@@ -219,17 +193,14 @@
             in_sem, n_cols, parts, parts,
         )
 
-    @pl.when(row == 1)
-    def _():
-        pltpu.make_async_copy(tops[0], low, low_sem).start()
-
-    for log in range(1, (n_tops + 1) // 2):
-        for odd in range(2):
-            @pl.when(((row >> log) == 1) & ((row & 1) == odd))
-            def _():
-                for part, ref in enumerate(tops[2 * log - 1 : 2 * log + 1]):
-                    at = half * (part ^ odd)
-                    pltpu.make_async_copy(ref, low.at[pl.ds(at, half), :], low_sem).start()
+    for log in range(n_tops):
+        @pl.when((row & ((2 << log) - 1)) == (1 << log))
+        def _():
+            pltpu.make_async_copy(tops[log], low, low_sem).start()
+
+        @pl.when((row >> log) == 1)
+        def _():
+            pltpu.make_async_copy(slots[log], displaced, low_sem).start()
 
     w = weights_ref[...]
     w_hi[...] = w.astype(jnp.bfloat16)
@@ -255,7 +226,8 @@
     @pl.when(jnp.logical_not(first_row))
     def _():
         pltpu.make_async_copy(tops[0], low, low_sem).wait()
-        swap(displaced_ref, low)
+        pltpu.make_async_copy(slots[0], displaced, low_sem).wait()
+        swap(displaced, low)
 
     @pl.when(first_col)
     def _():
@@ -355,7 +327,6 @@
     f32 = jnp.float32
     row, col = lax.axis_index("prow"), lax.axis_index("pcol")
     here = jnp.stack([row, col]).astype(jnp.int32)
-    odd = row % 2 == 1
 
     chunk = row_dev // (2 * parts)
     flat = [
@@ -379,9 +350,6 @@
     n_chain = steps(n_cols, parts)[0]
     last = max(b - n_chain if b >= n_chain else b for b in used)
 
-    def both_halves(one, two):
-        return jnp.concatenate([jnp.where(odd, two, one), jnp.where(odd, one, two)], axis=0)
-
     def old_top_rider():
         at = last + LAG
 
@@ -395,31 +363,21 @@
                 old_top_kernel, used=used, n_cols=n_cols, parts=parts, pairs=pairs
             ),
             jax.ShapeDtypeStruct((nb, nb), f32),
-            [SMEM, SMEM, ANY] + [ANY] * len(used), ANY, [pltpu.SemaphoreType.DMA],
-            vmem=4 << 20,
-        )(here, choice, matrix, *arrived)
+            [SMEM, SMEM] + [VMEM] * (2 * pairs + len(used)), VMEM,
+        )(here, choice, *flat[: 2 * pairs], *arrived)
         tops = []
-        log = 0
-        while (1 << log) < n_rows:
-            d = 1 << log
-            far = [(p, p + d) for p in range(d)]
-            if log == 0:
+        d = n_rows // 2
+        while d:
+            came = lax.ppermute(old_top, "prow", [(p, p + d) for p in range(0, n_rows, 2 * d)])
+            if d > 1:
                 at += 2
-                whole = yield give(at, lax.ppermute(old_top, "prow", far))
-                tops.append(whole)
-            else:
-                half = jnp.where(odd, old_top[nb // 2 :], old_top[: nb // 2])
-                at += 3
-                one = yield give(at, lax.ppermute(half, "prow", far))
-                two = lax.ppermute(one, "prow", [(p, p ^ 1) for p in range(d, 2 * d)])
-                tops += [one, two]
-                whole = both_halves(one, two)
-            old_top = jnp.where((row >> log) == 1, whole, old_top)
-            log += 1
+                came = yield give(at, came)
+                old_top = jnp.where(row % (2 * d) == d, came, old_top)
+            tops.insert(0, came)
+            d //= 2
         yield give(DONE, tops)
 
     slot = jax.ShapeDtypeStruct((nb, cols), f32)
-    half_slot = jax.ShapeDtypeStruct((nb // 2, cols), f32)
 
     def exchange_rider():
         table, owner = yield give(2, call(
@@ -429,36 +387,26 @@
         )(here, pivots.reshape(1, nb)))
         held = yield give(3, call(gather_kernel, slot, [SMEM, VMEM], VMEM)(table, matrix))
         at = 5
-        displaced = held
-        log = 0
-        half = None
-        while (1 << log) < n_rows:
+        slots = []
+        for log in range(n_rows.bit_length() - 1):
             d = 1 << log
-            far = [(p, p ^ d) for p in range(n_rows)]
-            if log == 0:
-                whole = yield give(at, lax.ppermute(held, "prow", far))
-                arrived = [whole]
-            else:
-                near = [(p, p ^ 1) for p in range(n_rows)]
-                one = yield give(at + 4, lax.ppermute(half, "prow", far))
+            came = lax.ppermute(held, "prow", [(p, p ^ d) for p in range(n_rows)])
+            came = yield give(at, came)
+            slots.append(came)
+            if 2 * d < n_rows:
+                held = call(
+                    functools.partial(merge_kernel, log=log), slot, [SMEM] + [VMEM] * 3, VMEM
+                )(here, owner, held, came)
+                held = yield give(at + 1, held)
                 at += 5
-                two = yield give(at, lax.ppermute(one, "prow", near))
-                arrived = [one, two]
-                whole = both_halves(one, two)
-            held, half = call(
-                functools.partial(merge_kernel, log=log, halves=log > 0),
-                (slot, half_slot), [SMEM] + [VMEM] * (2 + len(arrived)), (VMEM, VMEM),
-            )(here, owner, held, *arrived)
-            displaced = jnp.where((row >> log) == 1, whole, displaced)
-            log += 1
-        held, displaced = yield give(at + 1, (held, displaced))
         weights, top = yield give(at + 2, call(
-            factor_kernel, (slot, slot), [SMEM, VMEM, VMEM, VMEM], (VMEM, VMEM),
-            flops=4 * nb * nb * cols * 6,
-        )(here, held, lower_inverse, upper_inverse))
-        yield give(DONE, (table, displaced, weights, top))
-
-    chain, cross, (tops, (table, displaced, weights, top)) = spread(
+            functools.partial(factor_kernel, log=log), (slot,) * 2,
+            [SMEM] + [VMEM] * 5, (VMEM,) * 2, [pltpu.VMEM((nb, cols), f32)],
+            flops=4 * nb * nb * cols * 3,
+        )(here, owner, held, came, lower_inverse, upper_inverse))
+        yield give(DONE, (table, slots, weights, top))
+
+    chain, cross, (tops, (table, slots, weights, top)) = spread(
         [(flat[2 * i], flat[2 * i + 1]) for i in range(parts)], col, n_cols,
         [old_top_rider(), exchange_rider()],
     )
@@ -470,12 +418,13 @@
             block=256,
         ),
         jax.ShapeDtypeStruct(matrix.shape, f32),
-        [SMEM, SMEM, SMEM, VMEM, VMEM, VMEM, ANY] + [ANY] * (len(bufs) + len(tops)),
+        [SMEM, SMEM, SMEM, VMEM, VMEM, ANY] + [ANY] * (len(bufs) + 2 * len(tops)),
         ANY,
         [
             pltpu.VMEM((row_dev, cols), f32),
             pltpu.VMEM((row_dev, nb), f32),
             pltpu.VMEM((nb, nb), f32),
+            pltpu.VMEM((nb, cols), f32),
             pltpu.VMEM((nb, cols), jnp.bfloat16),
             pltpu.VMEM((nb, cols), jnp.bfloat16),
             pltpu.VMEM((row_dev, cols), f32),
@@ -483,7 +432,7 @@
         vmem=30 << 20,
         flops=2 * row_dev * nb * cols * 3,
         moved=4 * row_dev * (2 * cols + nb),
-    )(here, table, choice, displaced, weights, top, matrix, *bufs, *tops)
+    )(here, table, choice, weights, top, matrix, *bufs, *tops, *slots)
 
 
 def solution(mesh):

time: 168 us -> 177 us (1.054)
  local copies, waits for them, and re-layouts: 13.8 us -> 19.5 us
  starting transfers between devices: 90.4 us -> 93.1 us
  waiting for transfers between devices: 27.3 us -> 25.2 us
  Pallas kernels: 25.5 us -> 27.5 us
    unnamed x120 -> x138, local copies, waits for them, and re-layouts: 9.3 us -> 15 us
    select_n x10 -> x12, other arithmetic: 3.1 us -> 7.51 us  [spread(): aside = jnp.where(col == 0, aside, came)]
    select_n x5 -> x1, other arithmetic: 4.08 us -> 0.26 us  [old_top_rider(): old_top = jnp.where(row % (2 * d) == d, came, old_top)]
    ppermute x16, starting transfers between devices: 44.3 us -> 47.5 us  [spread(): cross.append(lax.ppermute(aside, 'pcol', across))]
    ppermute x16, waiting for transfers between devices: 16.3 us -> 14.1 us  [spread(): cross.append(lax.ppermute(aside, 'pcol', across))]
    pallas_call x1, Pallas kernels: 0.57 us -> 2.4 us  [old_top_rider(): call(functools.partial(old_top_kernel, used=used, n_cols=n_cols, parts=pa...]
    ppermute x6 -> x4, starting transfers between devices: 4.79 us -> 3.57 us  [the longest x2 2.9 us: old_top_rider(): lax.ppermute(old_top, 'prow', [(p, p + d) for p in range(0, n_rows, 2 * d)])]
    pallas_call x3 -> x2, Pallas kernels: 8.95 us -> 8.2 us  [the longest x1 6.39 us: exchange_rider(): call(functools.partial(factor_kernel, log=log), (slot,) * 2, [SMEM] + [VM...]
  transfers between devices with their start and end apart: 36 -> 34, of which waited for: 13 -> 14; matrix products, arithmetic and copies ran while one was open for 4% -> 4% of each run, Pallas kernels for 9% -> 9%
where the time goes in v10:
time: 177 us; the launch traced here: 174 us
  starting transfers between devices  93.1 us (53%)
  Pallas kernels  27.5 us (16%)
  waiting for transfers between devices  25.2 us (14%)
  local copies, waits for them, and re-layouts  19.5 us (11%)
  other arithmetic  7.84 us (4%)
    ppermute x16, starting transfers between devices, spread(): cross.append(lax.ppermute(aside, 'pcol', across))  47.5 us
    ppermute x14, starting transfers between devices, spread(): chain.append(lax.ppermute(ahead, 'pcol', along))  42 us
    unnamed x138, local copies, waits for them, and re-layouts  15 us
    ppermute x16, waiting for transfers between devices, spread(): cross.append(lax.ppermute(aside, 'pcol', across))  14.1 us
    pallas_call x1, Pallas kernels, local(): call(functools.partial(final_kernel, n_bufs=len(bufs), n_tops=len(tops),...  11.7 us
    ppermute x14, waiting for transfers between devices, spread(): chain.append(lax.ppermute(ahead, 'pcol', along))  10.4 us
    select_n x12, other arithmetic, spread(): aside = jnp.where(col == 0, aside, came)  7.51 us
    pallas_call x1, Pallas kernels, exchange_rider(): call(functools.partial(factor_kernel, log=log), (slot,) * 2, [SMEM] + [VM...  6.39 us
  transfers between devices with their start and end apart: 34, of which 14 were waited for; matrix products, arithmetic and copies ran while one was open for 4% of the time, Pallas kernels for 9%

profile of v10, /device:TPU:10, one launch (start us, length us, event | category | flops | bytes accessed | tf_op | source)
XLA Modules:
  0.0 174.4 jit_solution(11494189055123507727)
XLA Ops:
  0.0 3.8 %fusion = (f32[128,512]{1,0:T(8,128)}, f32[128,512]{1,0:T(8,128)}, f32[128,512]{1,0:T(8,128)}, f32[128,512]{1,0:T(8,128)}, f32[128,512]{1,0:T(8,128)}, /*index=5...) fusion(f32[2048,640]{1,0:T(8,128)} %matrix_ref.3), kind=kLoop, calls=%fused_computation.29 | loop fusion | bytes 8388608 | tf_op jit(solution)/shard_map/slice | solution.py:333
  3.9 3.4 %collective-permute-start.1 = (f32[128,512]{1,0:T(8,128)S(1)}, f32[128,512]{1,0:T(8,128)S(1)}, u32[]{:S(2)}, u32[]{:S(2)}) collective-permute-start(f32[128,512]{1,0:T(8,128)S(1)} %get-tuple-element.161.refs_0_), channel_id=1, source_target_pairs={{0,1},{2,3},{3,2},{4,5},{5,4},{6,7},{7,6},{8,9},{10,11},{11,10},{1... | collective-permute-start | bytes 786440 | tf_op jit(solution)/shard_map/ppermute | solution.py:300
  7.3 3.5 %collective-permute-start = (f32[128,512]{1,0:T(8,128)S(1)}, f32[128,512]{1,0:T(8,128)S(1)}, u32[]{:S(2)}, u32[]{:S(2)}) collective-permute-start(f32[128,512]{1,0:T(8,128)S(1)} %get-tuple-element.162.refs_1_), channel_id=1, source_target_pairs={{0,2},{1,3},{2,4},{3,5},{4,6},{5,7},{8,10},{9,11},{10,12},{11,13},... | collective-permute-start | bytes 786440 | tf_op jit(solution)/shard_map/ppermute | solution.py:299
  13.2 3.5 %collective-permute-start.6 = (f32[128,512]{1,0:T(8,128)S(1)}, f32[128,512]{1,0:T(8,128)}, u32[]{:S(2)}, u32[]{:S(2)}) collective-permute-start(f32[128,512]{1,0:T(8,128)S(1)} %get-tuple-element.90.refs_3_), channel_id=1, source_target_pairs={{0,2},{1,3},{2,4},{3,5},{4,6},{5,7},{8,10},{9,11},{10,12},{11,13},... | collective-permute-start | bytes 786440 | tf_op jit(solution)/shard_map/ppermute | solution.py:299
  18.5 2.6 %copy-done = f32[2048,640]{1,0:T(8,128)S(1)} copy-done((f32[2048,640]{1,0:T(8,128)S(1)}, f32[2048,640]{1,0:T(8,128)}, u32[]{:S(2)}) %copy-start) | copy-done | bytes 5242904
  21.1 3.5 %shard_map.56.held_ref = f32[512,640]{1,0:T(8,128)S(1)} custom-call(s32[8,512]{1,0:T(8,128)S(1)} %get-tuple-element.78.table_ref, f32[2048,640]{1,0:T(8,128)S(1)} %copy-done), custom_call_target="tpu_custom_call" | custom-call | tf_op jit(solution)/shard_map/pallas_call | solution.py:388
  25.0 3.6 %collective-permute-start.3 = (f32[128,512]{1,0:T(8,128)S(1)}, f32[128,512]{1,0:T(8,128)S(1)}, u32[]{:S(2)}, u32[]{:S(2)}) collective-permute-start(f32[128,512]{1,0:T(8,128)S(1)} %get-tuple-element.185), channel_id=1, source_target_pairs={{0,1},{2,3},{3,2},{4,5},{5,4},{6,7},{7,6},{8,9},{10,11},{11,10},{1... | collective-permute-start | bytes 786440 | tf_op jit(solution)/shard_map/ppermute | solution.py:300
  31.7 2.9 %collective-permute-start.9 = (f32[128,512]{1,0:T(8,128)S(1)}, f32[128,512]{1,0:T(8,128)S(1)}, u32[]{:S(2)}, u32[]{:S(2)}) collective-permute-start(f32[128,512]{1,0:T(8,128)S(1)} %get-tuple-element.181), channel_id=1, source_target_pairs={{0,1},{2,3},{3,2},{4,5},{5,4},{6,7},{7,6},{8,9},{10,11},{11,10},{1... | collective-permute-start | bytes 786440 | tf_op jit(solution)/shard_map/ppermute | solution.py:300
  34.6 4.4 %collective-permute-start.8 = (f32[128,512]{1,0:T(8,128)S(1)}, f32[128,512]{1,0:T(8,128)S(1)}, u32[]{:S(2)}, u32[]{:S(2)}) collective-permute-start(f32[128,512]{1,0:T(8,128)S(1)} %get-tuple-element.182), channel_id=1, source_target_pairs={{0,2},{1,3},{2,4},{3,5},{4,6},{5,7},{8,10},{9,11},{10,12},{11,13},... | collective-permute-start | bytes 786440 | tf_op jit(solution)/shard_map/ppermute | solution.py:299
  41.5 3.2 %collective-permute-start.4 = (f32[128,512]{1,0:T(8,128)S(1)}, f32[128,512]{1,0:T(8,128)S(1)}, u32[]{:S(2)}, u32[]{:S(2)}) collective-permute-start(f32[128,512]{1,0:T(8,128)S(1)} %get-tuple-element.184), channel_id=1, source_target_pairs={{0,2},{1,3},{2,4},{3,5},{4,6},{5,7},{8,10},{9,11},{10,12},{11,13},... | collective-permute-start | bytes 786440 | tf_op jit(solution)/shard_map/ppermute | solution.py:299
  51.0 3.5 %collective-permute-start.19 = (f32[128,512]{1,0:T(8,128)S(1)}, f32[128,512]{1,0:T(8,128)S(1)}, u32[]{:S(2)}, u32[]{:S(2)}) collective-permute-start(f32[128,512]{1,0:T(8,128)S(1)} %get-tuple-element.177), channel_id=1, source_target_pairs={{0,1},{2,3},{3,2},{4,5},{5,4},{6,7},{7,6},{8,9},{10,11},{11,10},{1... | collective-permute-start | bytes 786440 | tf_op jit(solution)/shard_map/ppermute | solution.py:300
  54.5 2.4 %collective-permute-start.18 = (f32[128,512]{1,0:T(8,128)S(1)}, f32[128,512]{1,0:T(8,128)S(1)}, u32[]{:S(2)}, u32[]{:S(2)}) collective-permute-start(f32[128,512]{1,0:T(8,128)S(1)} %get-tuple-element.178), channel_id=1, source_target_pairs={{0,2},{1,3},{2,4},{3,5},{4,6},{5,7},{8,10},{9,11},{10,12},{11,13},... | collective-permute-start | bytes 786440 | tf_op jit(solution)/shard_map/ppermute | solution.py:299
  57.1 3.6 %collective-permute-start.12 = (f32[128,512]{1,0:T(8,128)S(1)}, f32[128,512]{1,0:T(8,128)S(1)}, u32[]{:S(2)}, u32[]{:S(2)}) collective-permute-start(f32[128,512]{1,0:T(8,128)S(1)} %get-tuple-element.179), channel_id=1, source_target_pairs={{0,1},{2,3},{3,2},{4,5},{5,4},{6,7},{7,6},{8,9},{10,11},{11,10},{1... | collective-permute-start | bytes 786440 | tf_op jit(solution)/shard_map/ppermute | solution.py:300
  60.6 3.3 %collective-permute-start.11 = (f32[128,512]{1,0:T(8,128)S(1)}, f32[128,512]{1,0:T(8,128)S(1)}, u32[]{:S(2)}, u32[]{:S(2)}) collective-permute-start(f32[128,512]{1,0:T(8,128)S(1)} %get-tuple-element.180), channel_id=1, source_target_pairs={{0,2},{1,3},{2,4},{3,5},{4,6},{5,7},{8,10},{9,11},{10,12},{11,13},... | collective-permute-start | bytes 786440 | tf_op jit(solution)/shard_map/ppermute | solution.py:299
  64.9 2.6 %collective-permute-start.21 = (f32[128,512]{1,0:T(8,128)S(1)}, f32[128,512]{1,0:T(8,128)S(1)}, u32[]{:S(2)}, u32[]{:S(2)}) collective-permute-start(f32[128,512]{1,0:T(8,128)S(1)} %get-tuple-element.175), channel_id=1, source_target_pairs={{0,1},{2,3},{3,2},{4,5},{5,4},{6,7},{7,6},{8,9},{10,11},{11,10},{1... | collective-permute-start | bytes 786440 | tf_op jit(solution)/shard_map/ppermute | solution.py:300
  67.5 2.7 %collective-permute-start.20 = (f32[128,512]{1,0:T(8,128)S(1)}, f32[128,512]{1,0:T(8,128)S(1)}, u32[]{:S(2)}, u32[]{:S(2)}) collective-permute-start(f32[128,512]{1,0:T(8,128)S(1)} %get-tuple-element.176), channel_id=1, source_target_pairs={{0,2},{1,3},{2,4},{3,5},{4,6},{5,7},{8,10},{9,11},{10,12},{11,13},... | collective-permute-start | bytes 786440 | tf_op jit(solution)/shard_map/ppermute | solution.py:299
  71.9 2.6 %collective-permute-start.14 = (f32[128,512]{1,0:T(8,128)}, f32[128,512]{1,0:T(8,128)}, u32[]{:S(2)}, u32[]{:S(2)}) collective-permute-start(f32[128,512]{1,0:T(8,128)} %broadcast_select_fusion.10), channel_id=1, source_target_pairs={{0,1},{2,3},{3,2},{4,5},{5,4},{6,7},{7,6},{8,9},{10,11},{11,10},{1... | collective-permute-start | bytes 786440 | tf_op jit(solution)/shard_map/ppermute | solution.py:300
  76.7 3.3 %collective-permute-start.23 = (f32[128,512]{1,0:T(8,128)}, f32[128,512]{1,0:T(8,128)S(1)}, u32[]{:S(2)}, u32[]{:S(2)}) collective-permute-start(f32[128,512]{1,0:T(8,128)} %get-tuple-element.173), channel_id=1, source_target_pairs={{0,1},{2,3},{3,2},{4,5},{5,4},{6,7},{7,6},{8,9},{10,11},{11,10},{1... | collective-permute-start | bytes 786440 | tf_op jit(solution)/shard_map/ppermute | solution.py:300
  80.0 2.8 %collective-permute-start.22 = (f32[128,512]{1,0:T(8,128)}, f32[128,512]{1,0:T(8,128)}, u32[]{:S(2)}, u32[]{:S(2)}) collective-permute-start(f32[128,512]{1,0:T(8,128)} %get-tuple-element.174), channel_id=1, source_target_pairs={{0,2},{1,3},{2,4},{3,5},{4,6},{5,7},{8,10},{9,11},{10,12},{11,13},... | collective-permute-start | bytes 786440 | tf_op jit(solution)/shard_map/ppermute | solution.py:299
  85.9 2.8 %collective-permute-done.22.refs_9_ = f32[128,512]{1,0:T(8,128)} collective-permute-done((f32[128,512]{1,0:T(8,128)}, f32[128,512]{1,0:T(8,128)}, u32[]{:S(2)}, u32[]{:S(2)}) %collective-permute-start.22) | collective-permute-done | bytes 262176 | tf_op jit(solution)/shard_map/ppermute | solution.py:299
  105.7 2.8 %collective-permute-start.13 = (f32[128,512]{1,0:T(8,128)}, f32[128,512]{1,0:T(8,128)}, u32[]{:S(2)}, u32[]{:S(2)}) collective-permute-start(f32[128,512]{1,0:T(8,128)} %get-tuple-element.172), channel_id=1, source_target_pairs={{0,2},{1,3},{2,4},{3,5},{4,6},{5,7},{8,10},{9,11},{10,12},{11,13},... | collective-permute-start | bytes 786440 | tf_op jit(solution)/shard_map/ppermute | solution.py:299
  110.9 4.1 %collective-permute-start.24 = (f32[128,512]{1,0:T(8,128)}, f32[128,512]{1,0:T(8,128)}, u32[]{:S(2)}, u32[]{:S(2)}) collective-permute-start(f32[128,512]{1,0:T(8,128)} %get-tuple-element.171), channel_id=1, source_target_pairs={{0,2},{1,3},{2,4},{3,5},{4,6},{5,7},{8,10},{9,11},{10,12},{11,13},... | collective-permute-start | bytes 786440 | tf_op jit(solution)/shard_map/ppermute | solution.py:299
  121.5 3.3 %collective-permute-start.30 = (f32[128,512]{1,0:T(8,128)S(1)}, f32[128,512]{1,0:T(8,128)S(1)}, u32[]{:S(2)}, u32[]{:S(2)}) collective-permute-start(f32[128,512]{1,0:T(8,128)S(1)} %get-tuple-element.166), channel_id=1, source_target_pairs={{0,1},{2,3},{3,2},{4,5},{5,4},{6,7},{7,6},{8,9},{10,11},{11,10},{1... | collective-permute-start | bytes 786440 | tf_op jit(solution)/shard_map/ppermute | solution.py:300
  127.2 2.7 %collective-permute-start.16 = (f32[128,512]{1,0:T(8,128)S(1)}, f32[128,512]{1,0:T(8,128)S(1)}, u32[]{:S(2)}, u32[]{:S(2)}) collective-permute-start(f32[128,512]{1,0:T(8,128)S(1)} %get-tuple-element.168), channel_id=1, source_target_pairs={{0,2},{1,3},{2,4},{3,5},{4,6},{5,7},{8,10},{9,11},{10,12},{11,13},... | collective-permute-start | bytes 786440 | tf_op jit(solution)/shard_map/ppermute | solution.py:299
  130.0 2.9 %collective-permute-start.17 = (f32[128,512]{1,0:T(8,128)S(1)}, f32[128,512]{1,0:T(8,128)S(1)}, u32[]{:S(2)}, u32[]{:S(2)}) collective-permute-start(f32[128,512]{1,0:T(8,128)S(1)} %get-tuple-element.169), channel_id=1, source_target_pairs={{0,1},{2,3},{3,2},{4,5},{5,4},{6,7},{7,6},{8,9},{10,11},{11,10},{1... | collective-permute-start | bytes 786440 | tf_op jit(solution)/shard_map/ppermute | solution.py:300
  134.9 6.4 %shard_map.58 = (f32[512,640]{1,0:T(8,128)S(1)}, f32[512,640]{1,0:T(8,128)S(1)}) custom-call(s32[2]{0:T(128)S(1)} %pad_add_fusion.where_ref, s32[512,128]{1,0:T(8,128)S(1)} %copy-done.48, f32[512,640]{1,0:T(8,128)} %shard_map.57.held_ref, f32[512,640]{1,0:T(8,128)} %collective-permute-done.15.came_ref.refs_33_, f32[512,512]{1,0:T(8,128)S(1)} %copy-done.50, ...), custom_call_target="tpu_custom_call" | custom-call | flops 2013265920 | tf_op jit(solution)/shard_map/pallas_call | solution.py:402
  143.6 3.1 %collective-permute-start.29 = (f32[128,512]{1,0:T(8,128)S(1)}, f32[128,512]{1,0:T(8,128)S(1)}, u32[]{:S(2)}, u32[]{:S(2)}) collective-permute-start(f32[128,512]{1,0:T(8,128)S(1)} %get-tuple-element.165), channel_id=1, source_target_pairs={{0,1},{2,3},{3,2},{4,5},{5,4},{6,7},{7,6},{8,9},{10,11},{11,10},{1... | collective-permute-start | bytes 786440 | tf_op jit(solution)/shard_map/ppermute | solution.py:300
  146.8 2.7 %collective-permute-start.32 = (f32[128,512]{1,0:T(8,128)S(1)}, f32[128,512]{1,0:T(8,128)S(1)}, u32[]{:S(2)}, u32[]{:S(2)}) collective-permute-start(f32[128,512]{1,0:T(8,128)S(1)} %get-tuple-element.163), channel_id=1, source_target_pairs={{0,1},{2,3},{3,2},{4,5},{5,4},{6,7},{7,6},{8,9},{10,11},{11,10},{1... | collective-permute-start | bytes 786440 | tf_op jit(solution)/shard_map/ppermute | solution.py:300
  150.0 4.1 %collective-permute-done.29.refs_26_ = f32[128,512]{1,0:T(8,128)S(1)} collective-permute-done((f32[128,512]{1,0:T(8,128)S(1)}, f32[128,512]{1,0:T(8,128)S(1)}, u32[]{:S(2)}, u32[]{:S(2)}) %collective-permute-start.29) | collective-permute-done | bytes 262176 | tf_op jit(solution)/shard_map/ppermute | solution.py:300
  154.1 2.9 %collective-permute-start.31 = (f32[128,512]{1,0:T(8,128)S(1)}, f32[128,512]{1,0:T(8,128)S(1)}, u32[]{:S(2)}, u32[]{:S(2)}) collective-permute-start(f32[128,512]{1,0:T(8,128)S(1)} %broadcast_select_fusion.2), channel_id=1, source_target_pairs={{0,1},{2,3},{3,2},{4,5},{5,4},{6,7},{7,6},{8,9},{10,11},{11,10},{1... | collective-permute-start | bytes 786440 | tf_op jit(solution)/shard_map/ppermute | solution.py:300
  157.1 5.3 %collective-permute-done.31.refs_28_ = f32[128,512]{1,0:T(8,128)S(1)} collective-permute-done((f32[128,512]{1,0:T(8,128)S(1)}, f32[128,512]{1,0:T(8,128)S(1)}, u32[]{:S(2)}, u32[]{:S(2)}) %collective-permute-start.31) | collective-permute-done | bytes 262176 | tf_op jit(solution)/shard_map/ppermute | solution.py:300
  162.5 11.7 %shard_map.60 = f32[2048,640]{1,0:T(8,128)} custom-call(s32[2]{0:T(128)S(1)} %pad_add_fusion.where_ref, s32[8,512]{1,0:T(8,128)S(1)} %get-tuple-element.78.table_ref, s32[16]{0:T(128)S(1)} %dynamic-slice_bitcast_fusion.choice_ref, f32[512,640]{1,0:T(8,128)S(1)} %get-tuple-element.109.weights_ref, f32[512,640]{1,0:T(8,128)S(1)} %get-tuple-element.110.top_ref, ...), custom_call_target="tpu_custom_call" | custom-call | flops 4026531840 | bytes 14680064 | tf_op jit(solution)/shard_map/pallas_call | solution.py:415
  (197 shorter events, 56.8 us)
Async XLA Ops:
  3.9 14.6 %collective-permute-start.1 = (f32[128,512]{1,0:T(8,128)S(1)}, f32[128,512]{1,0:T(8,128)S(1)}, u32[]{:S(2)}, u32[]{:S(2)}) collective-permute-start(f32[128,512]{1,0:T(8,128)S(1)} %get-tuple-element.161.refs_0_), channel_id=1, source_target_pairs={{0,1},{2,3},{3,2},{4,5},{5,4},{6,7},{7,6},{8,9},{10,11},{11,10},{1... | collective-permute-start | bytes 786440 | tf_op jit(solution)/shard_map/ppermute | solution.py:300
  7.3 11.2 %collective-permute-start = (f32[128,512]{1,0:T(8,128)S(1)}, f32[128,512]{1,0:T(8,128)S(1)}, u32[]{:S(2)}, u32[]{:S(2)}) collective-permute-start(f32[128,512]{1,0:T(8,128)S(1)} %get-tuple-element.162.refs_1_), channel_id=1, source_target_pairs={{0,2},{1,3},{2,4},{3,5},{4,6},{5,7},{8,10},{9,11},{10,12},{11,13},... | collective-permute-start | bytes 786440 | tf_op jit(solution)/shard_map/ppermute | solution.py:299
  10.8 13.9 %collective-permute-start.7 = (f32[128,512]{1,0:T(8,128)S(1)}, f32[128,512]{1,0:T(8,128)S(1)}, u32[]{:S(2)}, u32[]{:S(2)}) collective-permute-start(f32[128,512]{1,0:T(8,128)S(1)} %get-tuple-element.91.refs_2_), channel_id=1, source_target_pairs={{0,1},{2,3},{3,2},{4,5},{5,4},{6,7},{7,6},{8,9},{10,11},{11,10},{1... | collective-permute-start | bytes 786440 | tf_op jit(solution)/shard_map/ppermute | solution.py:300
  13.2 11.5 %collective-permute-start.6 = (f32[128,512]{1,0:T(8,128)S(1)}, f32[128,512]{1,0:T(8,128)}, u32[]{:S(2)}, u32[]{:S(2)}) collective-permute-start(f32[128,512]{1,0:T(8,128)S(1)} %get-tuple-element.90.refs_3_), channel_id=1, source_target_pairs={{0,2},{1,3},{2,4},{3,5},{4,6},{5,7},{8,10},{9,11},{10,12},{11,13},... | collective-permute-start | bytes 786440 | tf_op jit(solution)/shard_map/ppermute | solution.py:299
  24.7 20.6 %collective-permute-start.10 = (f32[512,640]{1,0:T(8,128)S(1)}, f32[512,640]{1,0:T(8,128)S(1)}, u32[]{:S(2)}, u32[]{:S(2)}) collective-permute-start(f32[512,640]{1,0:T(8,128)S(1)} %shard_map.56.held_ref), channel_id=1, source_target_pairs={{0,8},{8,0},{16,24},{24,16},{1,9},{9,1},{17,25},{25,17},{2,10},{10... | collective-permute-start | bytes 3932168 | tf_op jit(solution)/shard_map/ppermute | solution.py:393
  25.0 14.1 %collective-permute-start.3 = (f32[128,512]{1,0:T(8,128)S(1)}, f32[128,512]{1,0:T(8,128)S(1)}, u32[]{:S(2)}, u32[]{:S(2)}) collective-permute-start(f32[128,512]{1,0:T(8,128)S(1)} %get-tuple-element.185), channel_id=1, source_target_pairs={{0,1},{2,3},{3,2},{4,5},{5,4},{6,7},{7,6},{8,9},{10,11},{11,10},{1... | collective-permute-start | bytes 786440 | tf_op jit(solution)/shard_map/ppermute | solution.py:300
  28.6 10.6 %collective-permute-start.2 = (f32[128,512]{1,0:T(8,128)S(1)}, f32[128,512]{1,0:T(8,128)S(1)}, u32[]{:S(2)}, u32[]{:S(2)}) collective-permute-start(f32[128,512]{1,0:T(8,128)S(1)} %get-tuple-element.186), channel_id=1, source_target_pairs={{0,2},{1,3},{2,4},{3,5},{4,6},{5,7},{8,10},{9,11},{10,12},{11,13},... | collective-permute-start | bytes 786440 | tf_op jit(solution)/shard_map/ppermute | solution.py:299
  31.7 13.1 %collective-permute-start.9 = (f32[128,512]{1,0:T(8,128)S(1)}, f32[128,512]{1,0:T(8,128)S(1)}, u32[]{:S(2)}, u32[]{:S(2)}) collective-permute-start(f32[128,512]{1,0:T(8,128)S(1)} %get-tuple-element.181), channel_id=1, source_target_pairs={{0,1},{2,3},{3,2},{4,5},{5,4},{6,7},{7,6},{8,9},{10,11},{11,10},{1... | collective-permute-start | bytes 786440 | tf_op jit(solution)/shard_map/ppermute | solution.py:300
  34.6 10.7 %collective-permute-start.8 = (f32[128,512]{1,0:T(8,128)S(1)}, f32[128,512]{1,0:T(8,128)S(1)}, u32[]{:S(2)}, u32[]{:S(2)}) collective-permute-start(f32[128,512]{1,0:T(8,128)S(1)} %get-tuple-element.182), channel_id=1, source_target_pairs={{0,2},{1,3},{2,4},{3,5},{4,6},{5,7},{8,10},{9,11},{10,12},{11,13},... | collective-permute-start | bytes 786440 | tf_op jit(solution)/shard_map/ppermute | solution.py:299
  39.2 9.4 %collective-permute-start.5 = (f32[128,512]{1,0:T(8,128)S(1)}, f32[128,512]{1,0:T(8,128)S(1)}, u32[]{:S(2)}, u32[]{:S(2)}) collective-permute-start(f32[128,512]{1,0:T(8,128)S(1)} %get-tuple-element.183), channel_id=1, source_target_pairs={{0,1},{2,3},{3,2},{4,5},{5,4},{6,7},{7,6},{8,9},{10,11},{11,10},{1... | collective-permute-start | bytes 786440 | tf_op jit(solution)/shard_map/ppermute | solution.py:300
  41.5 9.3 %collective-permute-start.4 = (f32[128,512]{1,0:T(8,128)S(1)}, f32[128,512]{1,0:T(8,128)S(1)}, u32[]{:S(2)}, u32[]{:S(2)}) collective-permute-start(f32[128,512]{1,0:T(8,128)S(1)} %get-tuple-element.184), channel_id=1, source_target_pairs={{0,2},{1,3},{2,4},{3,5},{4,6},{5,7},{8,10},{9,11},{10,12},{11,13},... | collective-permute-start | bytes 786440 | tf_op jit(solution)/shard_map/ppermute | solution.py:299
  51.0 13.0 %collective-permute-start.19 = (f32[128,512]{1,0:T(8,128)S(1)}, f32[128,512]{1,0:T(8,128)S(1)}, u32[]{:S(2)}, u32[]{:S(2)}) collective-permute-start(f32[128,512]{1,0:T(8,128)S(1)} %get-tuple-element.177), channel_id=1, source_target_pairs={{0,1},{2,3},{3,2},{4,5},{5,4},{6,7},{7,6},{8,9},{10,11},{11,10},{1... | collective-permute-start | bytes 786440 | tf_op jit(solution)/shard_map/ppermute | solution.py:300
  54.5 9.5 %collective-permute-start.18 = (f32[128,512]{1,0:T(8,128)S(1)}, f32[128,512]{1,0:T(8,128)S(1)}, u32[]{:S(2)}, u32[]{:S(2)}) collective-permute-start(f32[128,512]{1,0:T(8,128)S(1)} %get-tuple-element.178), channel_id=1, source_target_pairs={{0,2},{1,3},{2,4},{3,5},{4,6},{5,7},{8,10},{9,11},{10,12},{11,13},... | collective-permute-start | bytes 786440 | tf_op jit(solution)/shard_map/ppermute | solution.py:299
  57.1 13.1 %collective-permute-start.12 = (f32[128,512]{1,0:T(8,128)S(1)}, f32[128,512]{1,0:T(8,128)S(1)}, u32[]{:S(2)}, u32[]{:S(2)}) collective-permute-start(f32[128,512]{1,0:T(8,128)S(1)} %get-tuple-element.179), channel_id=1, source_target_pairs={{0,1},{2,3},{3,2},{4,5},{5,4},{6,7},{7,6},{8,9},{10,11},{11,10},{1... | collective-permute-start | bytes 786440 | tf_op jit(solution)/shard_map/ppermute | solution.py:300
  60.6 9.6 %collective-permute-start.11 = (f32[128,512]{1,0:T(8,128)S(1)}, f32[128,512]{1,0:T(8,128)S(1)}, u32[]{:S(2)}, u32[]{:S(2)}) collective-permute-start(f32[128,512]{1,0:T(8,128)S(1)} %get-tuple-element.180), channel_id=1, source_target_pairs={{0,2},{1,3},{2,4},{3,5},{4,6},{5,7},{8,10},{9,11},{10,12},{11,13},... | collective-permute-start | bytes 786440 | tf_op jit(solution)/shard_map/ppermute | solution.py:299
  64.9 9.6 %collective-permute-start.21 = (f32[128,512]{1,0:T(8,128)S(1)}, f32[128,512]{1,0:T(8,128)S(1)}, u32[]{:S(2)}, u32[]{:S(2)}) collective-permute-start(f32[128,512]{1,0:T(8,128)S(1)} %get-tuple-element.175), channel_id=1, source_target_pairs={{0,1},{2,3},{3,2},{4,5},{5,4},{6,7},{7,6},{8,9},{10,11},{11,10},{1... | collective-permute-start | bytes 786440 | tf_op jit(solution)/shard_map/ppermute | solution.py:300
  71.9 12.3 %collective-permute-start.14 = (f32[128,512]{1,0:T(8,128)}, f32[128,512]{1,0:T(8,128)}, u32[]{:S(2)}, u32[]{:S(2)}) collective-permute-start(f32[128,512]{1,0:T(8,128)} %broadcast_select_fusion.10), channel_id=1, source_target_pairs={{0,1},{2,3},{3,2},{4,5},{5,4},{6,7},{7,6},{8,9},{10,11},{11,10},{1... | collective-permute-start | bytes 786440 | tf_op jit(solution)/shard_map/ppermute | solution.py:300
  76.7 9.2 %collective-permute-start.23 = (f32[128,512]{1,0:T(8,128)}, f32[128,512]{1,0:T(8,128)S(1)}, u32[]{:S(2)}, u32[]{:S(2)}) collective-permute-start(f32[128,512]{1,0:T(8,128)} %get-tuple-element.173), channel_id=1, source_target_pairs={{0,1},{2,3},{3,2},{4,5},{5,4},{6,7},{7,6},{8,9},{10,11},{11,10},{1... | collective-permute-start | bytes 786440 | tf_op jit(solution)/shard_map/ppermute | solution.py:300
  80.0 8.6 %collective-permute-start.22 = (f32[128,512]{1,0:T(8,128)}, f32[128,512]{1,0:T(8,128)}, u32[]{:S(2)}, u32[]{:S(2)}) collective-permute-start(f32[128,512]{1,0:T(8,128)} %get-tuple-element.174), channel_id=1, source_target_pairs={{0,2},{1,3},{2,4},{3,5},{4,6},{5,7},{8,10},{9,11},{10,12},{11,13},... | collective-permute-start | bytes 786440 | tf_op jit(solution)/shard_map/ppermute | solution.py:299
  82.9 32.8 %collective-permute-start.15 = (f32[512,640]{1,0:T(8,128)}, f32[512,640]{1,0:T(8,128)}, u32[]{:S(2)}, u32[]{:S(2)}) collective-permute-start(f32[512,640]{1,0:T(8,128)} %shard_map.57.held_ref), channel_id=1, source_target_pairs={{0,16},{8,24},{16,0},{24,8},{1,17},{9,25},{17,1},{25,9},{2,18},{10... | collective-permute-start | bytes 3932168 | tf_op jit(solution)/shard_map/ppermute | solution.py:393
  102.5 17.8 %collective-permute-start.27 = (f32[512,512]{1,0:T(8,128)}, f32[512,512]{1,0:T(8,128)S(1)}, u32[]{:S(2)}, u32[]{:S(2)}) collective-permute-start(f32[512,512]{1,0:T(8,128)} %shard_map.59), channel_id=1, source_target_pairs={{0,16},{1,17},{2,18},{3,19},{4,20},{5,21},{6,22},{7,23}} | collective-permute-start | bytes 3145736 | tf_op jit(solution)/shard_map/ppermute | solution.py:371
  105.7 9.9 %collective-permute-start.13 = (f32[128,512]{1,0:T(8,128)}, f32[128,512]{1,0:T(8,128)}, u32[]{:S(2)}, u32[]{:S(2)}) collective-permute-start(f32[128,512]{1,0:T(8,128)} %get-tuple-element.172), channel_id=1, source_target_pairs={{0,2},{1,3},{2,4},{3,5},{4,6},{5,7},{8,10},{9,11},{10,12},{11,13},... | collective-permute-start | bytes 786440 | tf_op jit(solution)/shard_map/ppermute | solution.py:299
  108.6 8.6 %collective-permute-start.26 = (f32[128,512]{1,0:T(8,128)}, f32[128,512]{1,0:T(8,128)}, u32[]{:S(2)}, u32[]{:S(2)}) collective-permute-start(f32[128,512]{1,0:T(8,128)} %get-tuple-element.170), channel_id=1, source_target_pairs={{0,1},{2,3},{3,2},{4,5},{5,4},{6,7},{7,6},{8,9},{10,11},{11,10},{1... | collective-permute-start | bytes 786440 | tf_op jit(solution)/shard_map/ppermute | solution.py:300
  110.9 8.6 %collective-permute-start.24 = (f32[128,512]{1,0:T(8,128)}, f32[128,512]{1,0:T(8,128)}, u32[]{:S(2)}, u32[]{:S(2)}) collective-permute-start(f32[128,512]{1,0:T(8,128)} %get-tuple-element.171), channel_id=1, source_target_pairs={{0,2},{1,3},{2,4},{3,5},{4,6},{5,7},{8,10},{9,11},{10,12},{11,13},... | collective-permute-start | bytes 786440 | tf_op jit(solution)/shard_map/ppermute | solution.py:299
  121.5 19.7 %collective-permute-start.30 = (f32[128,512]{1,0:T(8,128)S(1)}, f32[128,512]{1,0:T(8,128)S(1)}, u32[]{:S(2)}, u32[]{:S(2)}) collective-permute-start(f32[128,512]{1,0:T(8,128)S(1)} %get-tuple-element.166), channel_id=1, source_target_pairs={{0,1},{2,3},{3,2},{4,5},{5,4},{6,7},{7,6},{8,9},{10,11},{11,10},{1... | collective-permute-start | bytes 786440 | tf_op jit(solution)/shard_map/ppermute | solution.py:300
  124.9 16.4 %collective-permute-start.28 = (f32[128,512]{1,0:T(8,128)S(1)}, f32[128,512]{1,0:T(8,128)S(1)}, u32[]{:S(2)}, u32[]{:S(2)}) collective-permute-start(f32[128,512]{1,0:T(8,128)S(1)} %get-tuple-element.167), channel_id=1, source_target_pairs={{0,2},{1,3},{2,4},{3,5},{4,6},{5,7},{8,10},{9,11},{10,12},{11,13},... | collective-permute-start | bytes 786440 | tf_op jit(solution)/shard_map/ppermute | solution.py:299
  127.2 14.1 %collective-permute-start.16 = (f32[128,512]{1,0:T(8,128)S(1)}, f32[128,512]{1,0:T(8,128)S(1)}, u32[]{:S(2)}, u32[]{:S(2)}) collective-permute-start(f32[128,512]{1,0:T(8,128)S(1)} %get-tuple-element.168), channel_id=1, source_target_pairs={{0,2},{1,3},{2,4},{3,5},{4,6},{5,7},{8,10},{9,11},{10,12},{11,13},... | collective-permute-start | bytes 786440 | tf_op jit(solution)/shard_map/ppermute | solution.py:299
  130.0 11.3 %collective-permute-start.17 = (f32[128,512]{1,0:T(8,128)S(1)}, f32[128,512]{1,0:T(8,128)S(1)}, u32[]{:S(2)}, u32[]{:S(2)}) collective-permute-start(f32[128,512]{1,0:T(8,128)S(1)} %get-tuple-element.169), channel_id=1, source_target_pairs={{0,1},{2,3},{3,2},{4,5},{5,4},{6,7},{7,6},{8,9},{10,11},{11,10},{1... | collective-permute-start | bytes 786440 | tf_op jit(solution)/shard_map/ppermute | solution.py:300
  133.2 29.2 %collective-permute-start.33 = (f32[512,512]{1,0:T(8,128)S(1)}, f32[512,512]{1,0:T(8,128)S(1)}, u32[]{:S(2)}, u32[]{:S(2)}) collective-permute-start(f32[512,512]{1,0:T(8,128)S(1)} %broadcast_select_fusion), channel_id=1, source_target_pairs={{0,8},{16,24},{1,9},{17,25},{2,10},{18,26},{3,11},{19,27},{4,12},{... | collective-permute-start | bytes 3145736 | tf_op jit(solution)/shard_map/ppermute | solution.py:371
  141.6 8.4 %collective-permute-start.25 = (f32[128,512]{1,0:T(8,128)S(1)}, f32[128,512]{1,0:T(8,128)S(1)}, u32[]{:S(2)}, u32[]{:S(2)}) collective-permute-start(f32[128,512]{1,0:T(8,128)S(1)} %get-tuple-element.164), channel_id=1, source_target_pairs={{0,2},{1,3},{2,4},{3,5},{4,6},{5,7},{8,10},{9,11},{10,12},{11,13},... | collective-permute-start | bytes 786440 | tf_op jit(solution)/shard_map/ppermute | solution.py:299
  143.6 10.5 %collective-permute-start.29 = (f32[128,512]{1,0:T(8,128)S(1)}, f32[128,512]{1,0:T(8,128)S(1)}, u32[]{:S(2)}, u32[]{:S(2)}) collective-permute-start(f32[128,512]{1,0:T(8,128)S(1)} %get-tuple-element.165), channel_id=1, source_target_pairs={{0,1},{2,3},{3,2},{4,5},{5,4},{6,7},{7,6},{8,9},{10,11},{11,10},{1... | collective-permute-start | bytes 786440 | tf_op jit(solution)/shard_map/ppermute | solution.py:300
  146.8 10.3 %collective-permute-start.32 = (f32[128,512]{1,0:T(8,128)S(1)}, f32[128,512]{1,0:T(8,128)S(1)}, u32[]{:S(2)}, u32[]{:S(2)}) collective-permute-start(f32[128,512]{1,0:T(8,128)S(1)} %get-tuple-element.163), channel_id=1, source_target_pairs={{0,1},{2,3},{3,2},{4,5},{5,4},{6,7},{7,6},{8,9},{10,11},{11,10},{1... | collective-permute-start | bytes 786440 | tf_op jit(solution)/shard_map/ppermute | solution.py:300
  (71 other events, 828.4 us)

commit v11 on v10

--- a/solution.py
+++ b/solution.py
@@ -14,7 +14,7 @@
 PICK, FROM, ROW, COUNT, TOP = 0, 1, 2, 3, 4
 
 
-def call(kernel, out, ins, outs, scratch=(), vmem=16 << 20, flops=0, moved=0):
+def call(kernel, out, ins, outs, scratch=(), vmem=10 << 20, flops=0, moved=0):
     return pl.pallas_call(
         kernel,
         out_shape=out,
@@ -147,22 +147,29 @@
                     pltpu.make_async_copy(bufs[b], place(i, h), sem).start()
 
 
-def old_top_kernel(
-    where_ref, choice_ref, *refs, used, n_cols, parts, pairs
-):
-    own, bufs, top_ref = refs[: 2 * pairs], dict(zip(used, refs[2 * pairs :])), refs[-1]
-    chunk = own[0].shape[0]
-    for k in range(2 * pairs):
-        span = slice(k * chunk, (k + 1) * chunk)
-
+def old_top_kernel(where_ref, choice_ref, matrix_ref, *refs, used, n_cols, parts, pairs):
+    bufs, top_ref, sem = dict(zip(used, refs)), refs[-2], refs[-1]
+    nb = top_ref.shape[0]
+    chunk = nb // (2 * pairs)
+    from_matrix = pltpu.make_async_copy(
+        matrix_ref.at[pl.ds(0, nb), pl.ds(0, nb)], top_ref, sem
+    )
+
+    @pl.when(where_ref[0] == 0)
+    def _():
         @pl.when(where_ref[1] == 0)
         def _():
-            top_ref[span, :] = own[k][...]
-
-        for b in sorted({arrival(p, k // 2, k % 2, n_cols, parts) for p in range(1, n_cols)}):
-            @pl.when((where_ref[1] > 0) & (choice_ref[k] == b))
-            def _():
-                top_ref[span, :] = bufs[b][...]
+            from_matrix.start()
+
+        @pl.when(where_ref[1] > 0)
+        def _():
+            fetch(
+                choice_ref, bufs,
+                lambda i, h: top_ref.at[pl.ds((2 * i + h) * chunk, chunk), :],
+                sem, n_cols, parts, pairs,
+            )
+
+        from_matrix.wait()
 
 
 def final_kernel(
@@ -363,8 +370,9 @@
                 old_top_kernel, used=used, n_cols=n_cols, parts=parts, pairs=pairs
             ),
             jax.ShapeDtypeStruct((nb, nb), f32),
-            [SMEM, SMEM] + [VMEM] * (2 * pairs + len(used)), VMEM,
-        )(here, choice, *flat[: 2 * pairs], *arrived)
+            [SMEM, SMEM, ANY] + [ANY] * len(used), ANY, [pltpu.SemaphoreType.DMA],
+            vmem=4 << 20,
+        )(here, choice, matrix, *arrived)
         tops = []
         d = n_rows // 2
         while d:
@@ -402,7 +410,7 @@
         weights, top = yield give(at + 2, call(
             functools.partial(factor_kernel, log=log), (slot,) * 2,
             [SMEM] + [VMEM] * 5, (VMEM,) * 2, [pltpu.VMEM((nb, cols), f32)],
-            flops=4 * nb * nb * cols * 3,
+            vmem=16 << 20, flops=4 * nb * nb * cols * 3,
         )(here, owner, held, came, lower_inverse, upper_inverse))
         yield give(DONE, (table, slots, weights, top))
 

time: 177 us -> 181 us (1.023)
  the two profiles are of different devices: /device:TPU:10 before, /device:TPU:0 now
where the time goes in v11:
time: 181 us; the launch traced here: 179 us
  starting transfers between devices  106 us (59%)
  Pallas kernels  23.6 us (13%)
  local copies, waits for them, and re-layouts  18.8 us (10%)
  waiting for transfers between devices  18.7 us (10%)
  other arithmetic  10.6 us (6%)
    ppermute x14, starting transfers between devices, spread(): chain.append(lax.ppermute(ahead, 'pcol', along))  56.3 us
    ppermute x16, starting transfers between devices, spread(): cross.append(lax.ppermute(aside, 'pcol', across))  44.4 us
    unnamed x126, local copies, waits for them, and re-layouts  14.3 us
    ppermute x14, waiting for transfers between devices, spread(): chain.append(lax.ppermute(ahead, 'pcol', along))  12.9 us
    select_n x12, other arithmetic, spread(): aside = jnp.where(col == 0, aside, came)  8.85 us
    pallas_call x1, Pallas kernels, local(): call(functools.partial(final_kernel, n_bufs=len(bufs), n_tops=len(tops),...  8.56 us
    pallas_call x1, Pallas kernels, exchange_rider(): call(functools.partial(factor_kernel, log=log), (slot,) * 2, [SMEM] + [VM...  6.5 us
    ppermute x16, waiting for transfers between devices, spread(): cross.append(lax.ppermute(aside, 'pcol', across))  5.82 us
  transfers between devices with their start and end apart: 34, of which 8 were waited for; matrix products, arithmetic and copies ran while one was open for 5% of the time, Pallas kernels for 8%

profile of v11, /device:TPU:0, one launch (start us, length us, event | category | flops | bytes accessed | tf_op | source)
XLA Modules:
  0.0 179.1 jit_solution(14533133167364717557)
XLA Ops:
  0.0 3.8 %fusion = (f32[128,512]{1,0:T(8,128)}, f32[128,512]{1,0:T(8,128)}, f32[128,512]{1,0:T(8,128)}, f32[128,512]{1,0:T(8,128)}, f32[128,512]{1,0:T(8,128)}, /*index=5...) fusion(f32[2048,640]{1,0:T(8,128)} %matrix_ref.5), kind=kLoop, calls=%fused_computation.29 | loop fusion | bytes 8388608 | tf_op jit(solution)/shard_map/slice | solution.py:340
  3.8 4.9 %collective-permute-start.1 = (f32[128,512]{1,0:T(8,128)S(1)}, f32[128,512]{1,0:T(8,128)S(1)}, u32[]{:S(2)}, u32[]{:S(2)}) collective-permute-start(f32[128,512]{1,0:T(8,128)S(1)} %get-tuple-element.161), channel_id=1, source_target_pairs={{0,1},{2,3},{3,2},{4,5},{5,4},{6,7},{7,6},{8,9},{10,11},{11,10},{1... | collective-permute-start | bytes 786440 | tf_op jit(solution)/shard_map/ppermute | solution.py:307
  8.7 3.5 %collective-permute-start = (f32[128,512]{1,0:T(8,128)S(1)}, f32[128,512]{1,0:T(8,128)S(1)}, u32[]{:S(2)}, u32[]{:S(2)}) collective-permute-start(f32[128,512]{1,0:T(8,128)S(1)} %get-tuple-element.162), channel_id=1, source_target_pairs={{0,2},{1,3},{2,4},{3,5},{4,6},{5,7},{8,10},{9,11},{10,12},{11,13},... | collective-permute-start | bytes 786440 | tf_op jit(solution)/shard_map/ppermute | solution.py:306
  12.2 2.4 %collective-permute-start.7 = (f32[128,512]{1,0:T(8,128)S(1)}, f32[128,512]{1,0:T(8,128)S(1)}, u32[]{:S(2)}, u32[]{:S(2)}) collective-permute-start(f32[128,512]{1,0:T(8,128)S(1)} %get-tuple-element.91), channel_id=1, source_target_pairs={{0,1},{2,3},{3,2},{4,5},{5,4},{6,7},{7,6},{8,9},{10,11},{11,10},{1... | collective-permute-start | bytes 786440 | tf_op jit(solution)/shard_map/ppermute | solution.py:307
  14.7 4.2 %collective-permute-start.6 = (f32[128,512]{1,0:T(8,128)S(1)}, f32[128,512]{1,0:T(8,128)}, u32[]{:S(2)}, u32[]{:S(2)}) collective-permute-start(f32[128,512]{1,0:T(8,128)S(1)} %get-tuple-element.90), channel_id=1, source_target_pairs={{0,2},{1,3},{2,4},{3,5},{4,6},{5,7},{8,10},{9,11},{10,12},{11,13},... | collective-permute-start | bytes 786440 | tf_op jit(solution)/shard_map/ppermute | solution.py:306
  21.3 2.6 %copy-done = f32[2048,640]{1,0:T(8,128)S(1)} copy-done((f32[2048,640]{1,0:T(8,128)S(1)}, f32[2048,640]{1,0:T(8,128)}, u32[]{:S(2)}) %copy-start) | copy-done | bytes 5242904
  23.8 3.5 %shard_map.56.held_ref = f32[512,640]{1,0:T(8,128)S(1)} custom-call(s32[8,512]{1,0:T(8,128)S(1)} %get-tuple-element.78.table_ref, f32[2048,640]{1,0:T(8,128)S(1)} %copy-done), custom_call_target="tpu_custom_call" | custom-call | tf_op jit(solution)/shard_map/pallas_call | solution.py:396
  28.7 2.5 %collective-permute-start.3 = (f32[128,512]{1,0:T(8,128)S(1)}, f32[128,512]{1,0:T(8,128)S(1)}, u32[]{:S(2)}, u32[]{:S(2)}) collective-permute-start(f32[128,512]{1,0:T(8,128)S(1)} %get-tuple-element.185), channel_id=1, source_target_pairs={{0,1},{2,3},{3,2},{4,5},{5,4},{6,7},{7,6},{8,9},{10,11},{11,10},{1... | collective-permute-start | bytes 786440 | tf_op jit(solution)/shard_map/ppermute | solution.py:307
  31.2 2.9 %collective-permute-start.2 = (f32[128,512]{1,0:T(8,128)S(1)}, f32[128,512]{1,0:T(8,128)S(1)}, u32[]{:S(2)}, u32[]{:S(2)}) collective-permute-start(f32[128,512]{1,0:T(8,128)S(1)} %get-tuple-element.186), channel_id=1, source_target_pairs={{0,2},{1,3},{2,4},{3,5},{4,6},{5,7},{8,10},{9,11},{10,12},{11,13},... | collective-permute-start | bytes 786440 | tf_op jit(solution)/shard_map/ppermute | solution.py:306
  40.6 2.6 %collective-permute-start.5 = (f32[128,512]{1,0:T(8,128)S(1)}, f32[128,512]{1,0:T(8,128)S(1)}, u32[]{:S(2)}, u32[]{:S(2)}) collective-permute-start(f32[128,512]{1,0:T(8,128)S(1)} %get-tuple-element.183), channel_id=1, source_target_pairs={{0,1},{2,3},{3,2},{4,5},{5,4},{6,7},{7,6},{8,9},{10,11},{11,10},{1... | collective-permute-start | bytes 786440 | tf_op jit(solution)/shard_map/ppermute | solution.py:307
  43.2 3.9 %collective-permute-start.4 = (f32[128,512]{1,0:T(8,128)S(1)}, f32[128,512]{1,0:T(8,128)S(1)}, u32[]{:S(2)}, u32[]{:S(2)}) collective-permute-start(f32[128,512]{1,0:T(8,128)S(1)} %get-tuple-element.184), channel_id=1, source_target_pairs={{0,2},{1,3},{2,4},{3,5},{4,6},{5,7},{8,10},{9,11},{10,12},{11,13},... | collective-permute-start | bytes 786440 | tf_op jit(solution)/shard_map/ppermute | solution.py:306
  49.1 2.9 %collective-permute-done.4.refs_4_ = f32[128,512]{1,0:T(8,128)S(1)} collective-permute-done((f32[128,512]{1,0:T(8,128)S(1)}, f32[128,512]{1,0:T(8,128)S(1)}, u32[]{:S(2)}, u32[]{:S(2)}) %collective-permute-start.4) | collective-permute-done | bytes 262176 | tf_op jit(solution)/shard_map/ppermute | solution.py:306
  52.0 3.4 %collective-permute-start.19 = (f32[128,512]{1,0:T(8,128)S(1)}, f32[128,512]{1,0:T(8,128)S(1)}, u32[]{:S(2)}, u32[]{:S(2)}) collective-permute-start(f32[128,512]{1,0:T(8,128)S(1)} %get-tuple-element.177), channel_id=1, source_target_pairs={{0,1},{2,3},{3,2},{4,5},{5,4},{6,7},{7,6},{8,9},{10,11},{11,10},{1... | collective-permute-start | bytes 786440 | tf_op jit(solution)/shard_map/ppermute | solution.py:307
  55.5 4.4 %collective-permute-start.18 = (f32[128,512]{1,0:T(8,128)S(1)}, f32[128,512]{1,0:T(8,128)S(1)}, u32[]{:S(2)}, u32[]{:S(2)}) collective-permute-start(f32[128,512]{1,0:T(8,128)S(1)} %get-tuple-element.178), channel_id=1, source_target_pairs={{0,2},{1,3},{2,4},{3,5},{4,6},{5,7},{8,10},{9,11},{10,12},{11,13},... | collective-permute-start | bytes 786440 | tf_op jit(solution)/shard_map/ppermute | solution.py:306
  60.0 2.6 %collective-permute-start.12 = (f32[128,512]{1,0:T(8,128)S(1)}, f32[128,512]{1,0:T(8,128)S(1)}, u32[]{:S(2)}, u32[]{:S(2)}) collective-permute-start(f32[128,512]{1,0:T(8,128)S(1)} %get-tuple-element.179), channel_id=1, source_target_pairs={{0,1},{2,3},{3,2},{4,5},{5,4},{6,7},{7,6},{8,9},{10,11},{11,10},{1... | collective-permute-start | bytes 786440 | tf_op jit(solution)/shard_map/ppermute | solution.py:307
  62.6 2.9 %collective-permute-start.11 = (f32[128,512]{1,0:T(8,128)S(1)}, f32[128,512]{1,0:T(8,128)S(1)}, u32[]{:S(2)}, u32[]{:S(2)}) collective-permute-start(f32[128,512]{1,0:T(8,128)S(1)} %get-tuple-element.180), channel_id=1, source_target_pairs={{0,2},{1,3},{2,4},{3,5},{4,6},{5,7},{8,10},{9,11},{10,12},{11,13},... | collective-permute-start | bytes 786440 | tf_op jit(solution)/shard_map/ppermute | solution.py:306
  66.4 3.1 %collective-permute-start.21 = (f32[128,512]{1,0:T(8,128)S(1)}, f32[128,512]{1,0:T(8,128)S(1)}, u32[]{:S(2)}, u32[]{:S(2)}) collective-permute-start(f32[128,512]{1,0:T(8,128)S(1)} %get-tuple-element.175), channel_id=1, source_target_pairs={{0,1},{2,3},{3,2},{4,5},{5,4},{6,7},{7,6},{8,9},{10,11},{11,10},{1... | collective-permute-start | bytes 786440 | tf_op jit(solution)/shard_map/ppermute | solution.py:307
  69.6 2.8 %collective-permute-start.20 = (f32[128,512]{1,0:T(8,128)S(1)}, f32[128,512]{1,0:T(8,128)S(1)}, u32[]{:S(2)}, u32[]{:S(2)}) collective-permute-start(f32[128,512]{1,0:T(8,128)S(1)} %get-tuple-element.176), channel_id=1, source_target_pairs={{0,2},{1,3},{2,4},{3,5},{4,6},{5,7},{8,10},{9,11},{10,12},{11,13},... | collective-permute-start | bytes 786440 | tf_op jit(solution)/shard_map/ppermute | solution.py:306
  74.1 4.0 %collective-permute-start.14 = (f32[128,512]{1,0:T(8,128)}, f32[128,512]{1,0:T(8,128)}, u32[]{:S(2)}, u32[]{:S(2)}) collective-permute-start(f32[128,512]{1,0:T(8,128)} %broadcast_select_fusion.10), channel_id=1, source_target_pairs={{0,1},{2,3},{3,2},{4,5},{5,4},{6,7},{7,6},{8,9},{10,11},{11,10},{1... | collective-permute-start | bytes 786440 | tf_op jit(solution)/shard_map/ppermute | solution.py:307
  80.5 5.1 %collective-permute-start.22 = (f32[128,512]{1,0:T(8,128)}, f32[128,512]{1,0:T(8,128)}, u32[]{:S(2)}, u32[]{:S(2)}) collective-permute-start(f32[128,512]{1,0:T(8,128)} %get-tuple-element.174), channel_id=1, source_target_pairs={{0,2},{1,3},{2,4},{3,5},{4,6},{5,7},{8,10},{9,11},{10,12},{11,13},... | collective-permute-start | bytes 786440 | tf_op jit(solution)/shard_map/ppermute | solution.py:306
  89.1 2.5 %copy-done.1 = f32[2048,640]{1,0:T(8,128)S(1)} copy-done((f32[2048,640]{1,0:T(8,128)S(1)}, f32[2048,640]{1,0:T(8,128)}, u32[]{:S(2)}) %copy-start.1) | copy-done | bytes 5242904
  100.7 2.5 %collective-permute-start.27 = (f32[512,512]{1,0:T(8,128)}, f32[512,512]{1,0:T(8,128)S(1)}, u32[]{:S(2)}, u32[]{:S(2)}) collective-permute-start(f32[512,512]{1,0:T(8,128)} %shard_map.59), channel_id=1, source_target_pairs={{0,16},{1,17},{2,18},{3,19},{4,20},{5,21},{6,22},{7,23}} | collective-permute-start | bytes 3145736 | tf_op jit(solution)/shard_map/ppermute | solution.py:379
  105.2 12.1 %collective-permute-start.13 = (f32[128,512]{1,0:T(8,128)}, f32[128,512]{1,0:T(8,128)}, u32[]{:S(2)}, u32[]{:S(2)}) collective-permute-start(f32[128,512]{1,0:T(8,128)} %get-tuple-element.172), channel_id=1, source_target_pairs={{0,2},{1,3},{2,4},{3,5},{4,6},{5,7},{8,10},{9,11},{10,12},{11,13},... | collective-permute-start | bytes 786440 | tf_op jit(solution)/shard_map/ppermute | solution.py:306
  122.9 5.6 %collective-permute-done.24.refs_11_ = f32[128,512]{1,0:T(8,128)} collective-permute-done((f32[128,512]{1,0:T(8,128)}, f32[128,512]{1,0:T(8,128)}, u32[]{:S(2)}, u32[]{:S(2)}) %collective-permute-start.24) | collective-permute-done | bytes 262176 | tf_op jit(solution)/shard_map/ppermute | solution.py:306
  131.4 4.8 %collective-permute-start.28 = (f32[128,512]{1,0:T(8,128)S(1)}, f32[128,512]{1,0:T(8,128)S(1)}, u32[]{:S(2)}, u32[]{:S(2)}) collective-permute-start(f32[128,512]{1,0:T(8,128)S(1)} %get-tuple-element.167), channel_id=1, source_target_pairs={{0,2},{1,3},{2,4},{3,5},{4,6},{5,7},{8,10},{9,11},{10,12},{11,13},... | collective-permute-start | bytes 786440 | tf_op jit(solution)/shard_map/ppermute | solution.py:306
  136.2 2.5 %collective-permute-start.16 = (f32[128,512]{1,0:T(8,128)S(1)}, f32[128,512]{1,0:T(8,128)S(1)}, u32[]{:S(2)}, u32[]{:S(2)}) collective-permute-start(f32[128,512]{1,0:T(8,128)S(1)} %get-tuple-element.168), channel_id=1, source_target_pairs={{0,2},{1,3},{2,4},{3,5},{4,6},{5,7},{8,10},{9,11},{10,12},{11,13},... | collective-permute-start | bytes 786440 | tf_op jit(solution)/shard_map/ppermute | solution.py:306
  138.8 4.1 %collective-permute-start.17 = (f32[128,512]{1,0:T(8,128)S(1)}, f32[128,512]{1,0:T(8,128)S(1)}, u32[]{:S(2)}, u32[]{:S(2)}) collective-permute-start(f32[128,512]{1,0:T(8,128)S(1)} %get-tuple-element.169), channel_id=1, source_target_pairs={{0,1},{2,3},{3,2},{4,5},{5,4},{6,7},{7,6},{8,9},{10,11},{11,10},{1... | collective-permute-start | bytes 786440 | tf_op jit(solution)/shard_map/ppermute | solution.py:307
  146.1 6.5 %shard_map.58 = (f32[512,640]{1,0:T(8,128)S(1)}, f32[512,640]{1,0:T(8,128)S(1)}) custom-call(s32[2]{0:T(128)S(1)} %pad_add_fusion.where_ref, s32[512,128]{1,0:T(8,128)S(1)} %copy-done.40, f32[512,640]{1,0:T(8,128)} %shard_map.57.held_ref, f32[512,640]{1,0:T(8,128)} %collective-permute-done.15.came_ref.refs_33_, f32[512,512]{1,0:T(8,128)S(1)} %copy-done.42, ...), custom_call_target="tpu_custom_call" | custom-call | flops 2013265920 | tf_op jit(solution)/shard_map/pallas_call | solution.py:410
  152.9 3.3 %collective-permute-start.25 = (f32[128,512]{1,0:T(8,128)S(1)}, f32[128,512]{1,0:T(8,128)S(1)}, u32[]{:S(2)}, u32[]{:S(2)}) collective-permute-start(f32[128,512]{1,0:T(8,128)S(1)} %get-tuple-element.164), channel_id=1, source_target_pairs={{0,2},{1,3},{2,4},{3,5},{4,6},{5,7},{8,10},{9,11},{10,12},{11,13},... | collective-permute-start | bytes 786440 | tf_op jit(solution)/shard_map/ppermute | solution.py:306
  162.0 4.4 %collective-permute-start.31 = (f32[128,512]{1,0:T(8,128)S(1)}, f32[128,512]{1,0:T(8,128)S(1)}, u32[]{:S(2)}, u32[]{:S(2)}) collective-permute-start(f32[128,512]{1,0:T(8,128)S(1)} %broadcast_select_fusion.2), channel_id=1, source_target_pairs={{0,1},{2,3},{3,2},{4,5},{5,4},{6,7},{7,6},{8,9},{10,11},{11,10},{1... | collective-permute-start | bytes 786440 | tf_op jit(solution)/shard_map/ppermute | solution.py:307
  166.4 3.8 %collective-permute-done.31.refs_28_ = f32[128,512]{1,0:T(8,128)S(1)} collective-permute-done((f32[128,512]{1,0:T(8,128)S(1)}, f32[128,512]{1,0:T(8,128)S(1)}, u32[]{:S(2)}, u32[]{:S(2)}) %collective-permute-start.31) | collective-permute-done | bytes 262176 | tf_op jit(solution)/shard_map/ppermute | solution.py:307
  170.4 8.6 %shard_map.60 = f32[2048,640]{1,0:T(8,128)} custom-call(s32[2]{0:T(128)S(1)} %pad_add_fusion.where_ref, s32[8,512]{1,0:T(8,128)S(1)} %get-tuple-element.78.table_ref, s32[16]{0:T(128)S(1)} %dynamic-slice_bitcast_fusion.choice_ref, f32[512,640]{1,0:T(8,128)S(1)} %get-tuple-element.109.weights_ref, f32[512,640]{1,0:T(8,128)S(1)} %get-tuple-element.110.top_ref, ...), custom_call_target="tpu_custom_call" | custom-call | flops 4026531840 | bytes 14680064 | tf_op jit(solution)/shard_map/pallas_call | solution.py:423
  (185 shorter events, 49.2 us)
Async XLA Ops:
  3.8 17.4 %collective-permute-start.1 = (f32[128,512]{1,0:T(8,128)S(1)}, f32[128,512]{1,0:T(8,128)S(1)}, u32[]{:S(2)}, u32[]{:S(2)}) collective-permute-start(f32[128,512]{1,0:T(8,128)S(1)} %get-tuple-element.161), channel_id=1, source_target_pairs={{0,1},{2,3},{3,2},{4,5},{5,4},{6,7},{7,6},{8,9},{10,11},{11,10},{1... | collective-permute-start | bytes 786440 | tf_op jit(solution)/shard_map/ppermute | solution.py:307
  8.7 12.5 %collective-permute-start = (f32[128,512]{1,0:T(8,128)S(1)}, f32[128,512]{1,0:T(8,128)S(1)}, u32[]{:S(2)}, u32[]{:S(2)}) collective-permute-start(f32[128,512]{1,0:T(8,128)S(1)} %get-tuple-element.162), channel_id=1, source_target_pairs={{0,2},{1,3},{2,4},{3,5},{4,6},{5,7},{8,10},{9,11},{10,12},{11,13},... | collective-permute-start | bytes 786440 | tf_op jit(solution)/shard_map/ppermute | solution.py:306
  12.2 15.1 %collective-permute-start.7 = (f32[128,512]{1,0:T(8,128)S(1)}, f32[128,512]{1,0:T(8,128)S(1)}, u32[]{:S(2)}, u32[]{:S(2)}) collective-permute-start(f32[128,512]{1,0:T(8,128)S(1)} %get-tuple-element.91), channel_id=1, source_target_pairs={{0,1},{2,3},{3,2},{4,5},{5,4},{6,7},{7,6},{8,9},{10,11},{11,10},{1... | collective-permute-start | bytes 786440 | tf_op jit(solution)/shard_map/ppermute | solution.py:307
  14.7 12.7 %collective-permute-start.6 = (f32[128,512]{1,0:T(8,128)S(1)}, f32[128,512]{1,0:T(8,128)}, u32[]{:S(2)}, u32[]{:S(2)}) collective-permute-start(f32[128,512]{1,0:T(8,128)S(1)} %get-tuple-element.90), channel_id=1, source_target_pairs={{0,2},{1,3},{2,4},{3,5},{4,6},{5,7},{8,10},{9,11},{10,12},{11,13},... | collective-permute-start | bytes 786440 | tf_op jit(solution)/shard_map/ppermute | solution.py:306
  27.4 19.8 %collective-permute-start.10 = (f32[512,640]{1,0:T(8,128)S(1)}, f32[512,640]{1,0:T(8,128)S(1)}, u32[]{:S(2)}, u32[]{:S(2)}) collective-permute-start(f32[512,640]{1,0:T(8,128)S(1)} %shard_map.56.held_ref), channel_id=1, source_target_pairs={{0,8},{8,0},{16,24},{24,16},{1,9},{9,1},{17,25},{25,17},{2,10},{10... | collective-permute-start | bytes 3932168 | tf_op jit(solution)/shard_map/ppermute | solution.py:401
  28.7 10.9 %collective-permute-start.3 = (f32[128,512]{1,0:T(8,128)S(1)}, f32[128,512]{1,0:T(8,128)S(1)}, u32[]{:S(2)}, u32[]{:S(2)}) collective-permute-start(f32[128,512]{1,0:T(8,128)S(1)} %get-tuple-element.185), channel_id=1, source_target_pairs={{0,1},{2,3},{3,2},{4,5},{5,4},{6,7},{7,6},{8,9},{10,11},{11,10},{1... | collective-permute-start | bytes 786440 | tf_op jit(solution)/shard_map/ppermute | solution.py:307
  31.2 9.2 %collective-permute-start.2 = (f32[128,512]{1,0:T(8,128)S(1)}, f32[128,512]{1,0:T(8,128)S(1)}, u32[]{:S(2)}, u32[]{:S(2)}) collective-permute-start(f32[128,512]{1,0:T(8,128)S(1)} %get-tuple-element.186), channel_id=1, source_target_pairs={{0,2},{1,3},{2,4},{3,5},{4,6},{5,7},{8,10},{9,11},{10,12},{11,13},... | collective-permute-start | bytes 786440 | tf_op jit(solution)/shard_map/ppermute | solution.py:306
  35.2 11.9 %collective-permute-start.9 = (f32[128,512]{1,0:T(8,128)S(1)}, f32[128,512]{1,0:T(8,128)S(1)}, u32[]{:S(2)}, u32[]{:S(2)}) collective-permute-start(f32[128,512]{1,0:T(8,128)S(1)} %get-tuple-element.181), channel_id=1, source_target_pairs={{0,1},{2,3},{3,2},{4,5},{5,4},{6,7},{7,6},{8,9},{10,11},{11,10},{1... | collective-permute-start | bytes 786440 | tf_op jit(solution)/shard_map/ppermute | solution.py:307
  37.7 9.5 %collective-permute-start.8 = (f32[128,512]{1,0:T(8,128)S(1)}, f32[128,512]{1,0:T(8,128)S(1)}, u32[]{:S(2)}, u32[]{:S(2)}) collective-permute-start(f32[128,512]{1,0:T(8,128)S(1)} %get-tuple-element.182), channel_id=1, source_target_pairs={{0,2},{1,3},{2,4},{3,5},{4,6},{5,7},{8,10},{9,11},{10,12},{11,13},... | collective-permute-start | bytes 786440 | tf_op jit(solution)/shard_map/ppermute | solution.py:306
  40.6 8.5 %collective-permute-start.5 = (f32[128,512]{1,0:T(8,128)S(1)}, f32[128,512]{1,0:T(8,128)S(1)}, u32[]{:S(2)}, u32[]{:S(2)}) collective-permute-start(f32[128,512]{1,0:T(8,128)S(1)} %get-tuple-element.183), channel_id=1, source_target_pairs={{0,1},{2,3},{3,2},{4,5},{5,4},{6,7},{7,6},{8,9},{10,11},{11,10},{1... | collective-permute-start | bytes 786440 | tf_op jit(solution)/shard_map/ppermute | solution.py:307
  43.2 8.7 %collective-permute-start.4 = (f32[128,512]{1,0:T(8,128)S(1)}, f32[128,512]{1,0:T(8,128)S(1)}, u32[]{:S(2)}, u32[]{:S(2)}) collective-permute-start(f32[128,512]{1,0:T(8,128)S(1)} %get-tuple-element.184), channel_id=1, source_target_pairs={{0,2},{1,3},{2,4},{3,5},{4,6},{5,7},{8,10},{9,11},{10,12},{11,13},... | collective-permute-start | bytes 786440 | tf_op jit(solution)/shard_map/ppermute | solution.py:306
  52.0 13.5 %collective-permute-start.19 = (f32[128,512]{1,0:T(8,128)S(1)}, f32[128,512]{1,0:T(8,128)S(1)}, u32[]{:S(2)}, u32[]{:S(2)}) collective-permute-start(f32[128,512]{1,0:T(8,128)S(1)} %get-tuple-element.177), channel_id=1, source_target_pairs={{0,1},{2,3},{3,2},{4,5},{5,4},{6,7},{7,6},{8,9},{10,11},{11,10},{1... | collective-permute-start | bytes 786440 | tf_op jit(solution)/shard_map/ppermute | solution.py:307
  55.5 10.1 %collective-permute-start.18 = (f32[128,512]{1,0:T(8,128)S(1)}, f32[128,512]{1,0:T(8,128)S(1)}, u32[]{:S(2)}, u32[]{:S(2)}) collective-permute-start(f32[128,512]{1,0:T(8,128)S(1)} %get-tuple-element.178), channel_id=1, source_target_pairs={{0,2},{1,3},{2,4},{3,5},{4,6},{5,7},{8,10},{9,11},{10,12},{11,13},... | collective-permute-start | bytes 786440 | tf_op jit(solution)/shard_map/ppermute | solution.py:306
  60.0 12.3 %collective-permute-start.12 = (f32[128,512]{1,0:T(8,128)S(1)}, f32[128,512]{1,0:T(8,128)S(1)}, u32[]{:S(2)}, u32[]{:S(2)}) collective-permute-start(f32[128,512]{1,0:T(8,128)S(1)} %get-tuple-element.179), channel_id=1, source_target_pairs={{0,1},{2,3},{3,2},{4,5},{5,4},{6,7},{7,6},{8,9},{10,11},{11,10},{1... | collective-permute-start | bytes 786440 | tf_op jit(solution)/shard_map/ppermute | solution.py:307
  62.6 9.8 %collective-permute-start.11 = (f32[128,512]{1,0:T(8,128)S(1)}, f32[128,512]{1,0:T(8,128)S(1)}, u32[]{:S(2)}, u32[]{:S(2)}) collective-permute-start(f32[128,512]{1,0:T(8,128)S(1)} %get-tuple-element.180), channel_id=1, source_target_pairs={{0,2},{1,3},{2,4},{3,5},{4,6},{5,7},{8,10},{9,11},{10,12},{11,13},... | collective-permute-start | bytes 786440 | tf_op jit(solution)/shard_map/ppermute | solution.py:306
  66.4 11.7 %collective-permute-start.21 = (f32[128,512]{1,0:T(8,128)S(1)}, f32[128,512]{1,0:T(8,128)S(1)}, u32[]{:S(2)}, u32[]{:S(2)}) collective-permute-start(f32[128,512]{1,0:T(8,128)S(1)} %get-tuple-element.175), channel_id=1, source_target_pairs={{0,1},{2,3},{3,2},{4,5},{5,4},{6,7},{7,6},{8,9},{10,11},{11,10},{1... | collective-permute-start | bytes 786440 | tf_op jit(solution)/shard_map/ppermute | solution.py:307
  69.6 8.6 %collective-permute-start.20 = (f32[128,512]{1,0:T(8,128)S(1)}, f32[128,512]{1,0:T(8,128)S(1)}, u32[]{:S(2)}, u32[]{:S(2)}) collective-permute-start(f32[128,512]{1,0:T(8,128)S(1)} %get-tuple-element.176), channel_id=1, source_target_pairs={{0,2},{1,3},{2,4},{3,5},{4,6},{5,7},{8,10},{9,11},{10,12},{11,13},... | collective-permute-start | bytes 786440 | tf_op jit(solution)/shard_map/ppermute | solution.py:306
  74.1 13.7 %collective-permute-start.14 = (f32[128,512]{1,0:T(8,128)}, f32[128,512]{1,0:T(8,128)}, u32[]{:S(2)}, u32[]{:S(2)}) collective-permute-start(f32[128,512]{1,0:T(8,128)} %broadcast_select_fusion.10), channel_id=1, source_target_pairs={{0,1},{2,3},{3,2},{4,5},{5,4},{6,7},{7,6},{8,9},{10,11},{11,10},{1... | collective-permute-start | bytes 786440 | tf_op jit(solution)/shard_map/ppermute | solution.py:307
  79.2 8.6 %collective-permute-start.23 = (f32[128,512]{1,0:T(8,128)}, f32[128,512]{1,0:T(8,128)S(1)}, u32[]{:S(2)}, u32[]{:S(2)}) collective-permute-start(f32[128,512]{1,0:T(8,128)} %get-tuple-element.173), channel_id=1, source_target_pairs={{0,1},{2,3},{3,2},{4,5},{5,4},{6,7},{7,6},{8,9},{10,11},{11,10},{1... | collective-permute-start | bytes 786440 | tf_op jit(solution)/shard_map/ppermute | solution.py:307
  80.5 8.6 %collective-permute-start.22 = (f32[128,512]{1,0:T(8,128)}, f32[128,512]{1,0:T(8,128)}, u32[]{:S(2)}, u32[]{:S(2)}) collective-permute-start(f32[128,512]{1,0:T(8,128)} %get-tuple-element.174), channel_id=1, source_target_pairs={{0,2},{1,3},{2,4},{3,5},{4,6},{5,7},{8,10},{9,11},{10,12},{11,13},... | collective-permute-start | bytes 786440 | tf_op jit(solution)/shard_map/ppermute | solution.py:306
  85.6 37.4 %collective-permute-start.15 = (f32[512,640]{1,0:T(8,128)}, f32[512,640]{1,0:T(8,128)}, u32[]{:S(2)}, u32[]{:S(2)}) collective-permute-start(f32[512,640]{1,0:T(8,128)} %shard_map.57.held_ref), channel_id=1, source_target_pairs={{0,16},{8,24},{16,0},{24,8},{1,17},{9,25},{17,1},{25,9},{2,18},{10... | collective-permute-start | bytes 3932168 | tf_op jit(solution)/shard_map/ppermute | solution.py:401
  100.7 27.8 %collective-permute-start.27 = (f32[512,512]{1,0:T(8,128)}, f32[512,512]{1,0:T(8,128)S(1)}, u32[]{:S(2)}, u32[]{:S(2)}) collective-permute-start(f32[512,512]{1,0:T(8,128)} %shard_map.59), channel_id=1, source_target_pairs={{0,16},{1,17},{2,18},{3,19},{4,20},{5,21},{6,22},{7,23}} | collective-permute-start | bytes 3145736 | tf_op jit(solution)/shard_map/ppermute | solution.py:379
  105.2 17.8 %collective-permute-start.13 = (f32[128,512]{1,0:T(8,128)}, f32[128,512]{1,0:T(8,128)}, u32[]{:S(2)}, u32[]{:S(2)}) collective-permute-start(f32[128,512]{1,0:T(8,128)} %get-tuple-element.172), channel_id=1, source_target_pairs={{0,2},{1,3},{2,4},{3,5},{4,6},{5,7},{8,10},{9,11},{10,12},{11,13},... | collective-permute-start | bytes 786440 | tf_op jit(solution)/shard_map/ppermute | solution.py:306
  119.3 9.3 %collective-permute-start.24 = (f32[128,512]{1,0:T(8,128)}, f32[128,512]{1,0:T(8,128)}, u32[]{:S(2)}, u32[]{:S(2)}) collective-permute-start(f32[128,512]{1,0:T(8,128)} %get-tuple-element.171), channel_id=1, source_target_pairs={{0,2},{1,3},{2,4},{3,5},{4,6},{5,7},{8,10},{9,11},{10,12},{11,13},... | collective-permute-start | bytes 786440 | tf_op jit(solution)/shard_map/ppermute | solution.py:306
  130.0 22.5 %collective-permute-start.30 = (f32[128,512]{1,0:T(8,128)S(1)}, f32[128,512]{1,0:T(8,128)S(1)}, u32[]{:S(2)}, u32[]{:S(2)}) collective-permute-start(f32[128,512]{1,0:T(8,128)S(1)} %get-tuple-element.166), channel_id=1, source_target_pairs={{0,1},{2,3},{3,2},{4,5},{5,4},{6,7},{7,6},{8,9},{10,11},{11,10},{1... | collective-permute-start | bytes 786440 | tf_op jit(solution)/shard_map/ppermute | solution.py:307
  131.4 21.2 %collective-permute-start.28 = (f32[128,512]{1,0:T(8,128)S(1)}, f32[128,512]{1,0:T(8,128)S(1)}, u32[]{:S(2)}, u32[]{:S(2)}) collective-permute-start(f32[128,512]{1,0:T(8,128)S(1)} %get-tuple-element.167), channel_id=1, source_target_pairs={{0,2},{1,3},{2,4},{3,5},{4,6},{5,7},{8,10},{9,11},{10,12},{11,13},... | collective-permute-start | bytes 786440 | tf_op jit(solution)/shard_map/ppermute | solution.py:306
  136.2 16.4 %collective-permute-start.16 = (f32[128,512]{1,0:T(8,128)S(1)}, f32[128,512]{1,0:T(8,128)S(1)}, u32[]{:S(2)}, u32[]{:S(2)}) collective-permute-start(f32[128,512]{1,0:T(8,128)S(1)} %get-tuple-element.168), channel_id=1, source_target_pairs={{0,2},{1,3},{2,4},{3,5},{4,6},{5,7},{8,10},{9,11},{10,12},{11,13},... | collective-permute-start | bytes 786440 | tf_op jit(solution)/shard_map/ppermute | solution.py:306
  138.8 13.8 %collective-permute-start.17 = (f32[128,512]{1,0:T(8,128)S(1)}, f32[128,512]{1,0:T(8,128)S(1)}, u32[]{:S(2)}, u32[]{:S(2)}) collective-permute-start(f32[128,512]{1,0:T(8,128)S(1)} %get-tuple-element.169), channel_id=1, source_target_pairs={{0,1},{2,3},{3,2},{4,5},{5,4},{6,7},{7,6},{8,9},{10,11},{11,10},{1... | collective-permute-start | bytes 786440 | tf_op jit(solution)/shard_map/ppermute | solution.py:307
  144.5 25.7 %collective-permute-start.33 = (f32[512,512]{1,0:T(8,128)S(1)}, f32[512,512]{1,0:T(8,128)S(1)}, u32[]{:S(2)}, u32[]{:S(2)}) collective-permute-start(f32[512,512]{1,0:T(8,128)S(1)} %broadcast_select_fusion), channel_id=1, source_target_pairs={{0,8},{16,24},{1,9},{17,25},{2,10},{18,26},{3,11},{19,27},{4,12},{... | collective-permute-start | bytes 3145736 | tf_op jit(solution)/shard_map/ppermute | solution.py:379
  152.9 7.1 %collective-permute-start.25 = (f32[128,512]{1,0:T(8,128)S(1)}, f32[128,512]{1,0:T(8,128)S(1)}, u32[]{:S(2)}, u32[]{:S(2)}) collective-permute-start(f32[128,512]{1,0:T(8,128)S(1)} %get-tuple-element.164), channel_id=1, source_target_pairs={{0,2},{1,3},{2,4},{3,5},{4,6},{5,7},{8,10},{9,11},{10,12},{11,13},... | collective-permute-start | bytes 786440 | tf_op jit(solution)/shard_map/ppermute | solution.py:306
  158.1 8.3 %collective-permute-start.32 = (f32[128,512]{1,0:T(8,128)S(1)}, f32[128,512]{1,0:T(8,128)S(1)}, u32[]{:S(2)}, u32[]{:S(2)}) collective-permute-start(f32[128,512]{1,0:T(8,128)S(1)} %get-tuple-element.163), channel_id=1, source_target_pairs={{0,1},{2,3},{3,2},{4,5},{5,4},{6,7},{7,6},{8,9},{10,11},{11,10},{1... | collective-permute-start | bytes 786440 | tf_op jit(solution)/shard_map/ppermute | solution.py:307
  162.0 8.3 %collective-permute-start.31 = (f32[128,512]{1,0:T(8,128)S(1)}, f32[128,512]{1,0:T(8,128)S(1)}, u32[]{:S(2)}, u32[]{:S(2)}) collective-permute-start(f32[128,512]{1,0:T(8,128)S(1)} %broadcast_select_fusion.2), channel_id=1, source_target_pairs={{0,1},{2,3},{3,2},{4,5},{5,4},{6,7},{7,6},{8,9},{10,11},{11,10},{1... | collective-permute-start | bytes 786440 | tf_op jit(solution)/shard_map/ppermute | solution.py:307
  (65 other events, 715.3 us)

commit v12 on v3

--- a/solution.py
+++ b/solution.py
@@ -7,7 +7,6 @@
 from jax.experimental.pallas import tpu as pltpu
 from jax.sharding import PartitionSpec as P
 
-HIGHEST = lax.Precision.HIGHEST
 VMEM = pl.BlockSpec(memory_space=pltpu.VMEM)
 SMEM = pl.BlockSpec(memory_space=pltpu.SMEM)
 ANY = pl.BlockSpec(memory_space=pl.ANY)
@@ -138,20 +137,53 @@
         half_ref[...] = merged_ref[high, :]
 
 
-def factor_kernel(where_ref, top_in_ref, lower_ref, upper_ref, weights_ref, top_ref):
-    nb, cols = top_in_ref.shape
-    u = jnp.dot(
-        lower_ref[...], top_in_ref[...], precision=HIGHEST,
-        preferred_element_type=jnp.float32,
-    )
+def split(x):
+    hi = x.astype(jnp.bfloat16)
+    return hi, (x - hi.astype(jnp.float32)).astype(jnp.bfloat16)
+
+
+def product(a, b):
+    dot = functools.partial(jnp.dot, preferred_element_type=jnp.float32)
+    return dot(a[1], b[0]) + dot(a[0], b[1]) + dot(a[0], b[0])
+
+
+def factor_kernel(
+    where_ref, owner_ref, held_ref, one_ref, two_ref, before_ref, lower_ref, upper_ref,
+    weights_ref, top_ref, displaced_ref, new_top, *, log,
+):
+    me = where_ref[0]
+    mine, theirs = me >> log, (me >> log) ^ 1
+    nb, cols = held_ref.shape
+    half = nb // 2
+
+    def merge(rows, piece):
+        group = owner_ref[rows, :] >> log
+        take = (group == theirs) | ((theirs == 0) & (group != mine))
+        for q in range(cols // LANES):
+            lane = slice(q * LANES, (q + 1) * LANES)
+            new_top[rows, lane] = jnp.where(take, piece[:, lane], held_ref[rows, lane])
+
+        @pl.when(mine == 1)
+        def _():
+            displaced_ref[rows, :] = piece[...]
+
+    @pl.when(mine != 1)
+    def _():
+        displaced_ref[...] = before_ref[...]
+
+    for odd, (first, second) in enumerate([(one_ref, two_ref), (two_ref, one_ref)]):
+        @pl.when((me & 1) == odd)
+        def _():
+            merge(slice(0, half), first)
+            merge(slice(half, nb), second)
+
+    u = product(split(lower_ref[...]), split(new_top[...]))
     top_ref[...] = u
-    weights_ref[...] = jnp.dot(
-        upper_ref[...], u, precision=HIGHEST, preferred_element_type=jnp.float32
-    )
+    weights_ref[...] = product(split(upper_ref[...]), split(u))
 
     @pl.when(where_ref[1] == 0)
     def _():
-        top_ref[:, :nb] = top_in_ref[:, :nb]
+        top_ref[:, :nb] = new_top[:, :nb]
         weights_ref[:, :nb] = -upper_ref[...]
 
 
@@ -199,7 +231,6 @@
     ]
     rows, cols = matrix_ref.shape
     nb = weights_ref.shape[0]
-    half = nb // 2
     chunk = rows // (2 * parts)
     row = where_ref[0]
     first_row, first_col = row == 0, where_ref[1] == 0
@@ -219,17 +250,10 @@
             in_sem, n_cols, parts, parts,
         )
 
-    @pl.when(row == 1)
-    def _():
-        pltpu.make_async_copy(tops[0], low, low_sem).start()
-
-    for log in range(1, (n_tops + 1) // 2):
-        for odd in range(2):
-            @pl.when(((row >> log) == 1) & ((row & 1) == odd))
-            def _():
-                for part, ref in enumerate(tops[2 * log - 1 : 2 * log + 1]):
-                    at = half * (part ^ odd)
-                    pltpu.make_async_copy(ref, low.at[pl.ds(at, half), :], low_sem).start()
+    for log in range(n_tops):
+        @pl.when((row & ((2 << log) - 1)) == (1 << log))
+        def _():
+            pltpu.make_async_copy(tops[log], low, low_sem).start()
 
     w = weights_ref[...]
     w_hi[...] = w.astype(jnp.bfloat16)
@@ -399,23 +423,15 @@
             vmem=4 << 20,
         )(here, choice, matrix, *arrived)
         tops = []
-        log = 0
-        while (1 << log) < n_rows:
-            d = 1 << log
-            far = [(p, p + d) for p in range(d)]
-            if log == 0:
+        d = n_rows // 2
+        while d:
+            came = lax.ppermute(old_top, "prow", [(p, p + d) for p in range(0, n_rows, 2 * d)])
+            if d > 1:
                 at += 2
-                whole = yield give(at, lax.ppermute(old_top, "prow", far))
-                tops.append(whole)
-            else:
-                half = jnp.where(odd, old_top[nb // 2 :], old_top[: nb // 2])
-                at += 3
-                one = yield give(at, lax.ppermute(half, "prow", far))
-                two = lax.ppermute(one, "prow", [(p, p ^ 1) for p in range(d, 2 * d)])
-                tops += [one, two]
-                whole = both_halves(one, two)
-            old_top = jnp.where((row >> log) == 1, whole, old_top)
-            log += 1
+                came = yield give(at, came)
+                old_top = jnp.where(row % (2 * d) == d, came, old_top)
+            tops.insert(0, came)
+            d //= 2
         yield give(DONE, tops)
 
     slot = jax.ShapeDtypeStruct((nb, cols), f32)
@@ -444,18 +460,20 @@
                 at += 5
                 two = yield give(at, lax.ppermute(one, "prow", near))
                 arrived = [one, two]
-                whole = both_halves(one, two)
+                whole = None if 2 << log == n_rows else both_halves(one, two)
+            if 2 << log == n_rows:
+                break
             held, half = call(
                 functools.partial(merge_kernel, log=log, halves=log > 0),
                 (slot, half_slot), [SMEM] + [VMEM] * (2 + len(arrived)), (VMEM, VMEM),
             )(here, owner, held, *arrived)
-            displaced = jnp.where((row >> log) == 1, whole, displaced)
+            displaced = jnp.where((row >> log) == 1, whole, displaced) if log else whole
             log += 1
-        held, displaced = yield give(at + 1, (held, displaced))
-        weights, top = yield give(at + 2, call(
-            factor_kernel, (slot, slot), [SMEM, VMEM, VMEM, VMEM], (VMEM, VMEM),
-            flops=4 * nb * nb * cols * 6,
-        )(here, held, lower_inverse, upper_inverse))
+        weights, top, displaced = yield give(at + 2, call(
+            functools.partial(factor_kernel, log=log), (slot,) * 3,
+            [SMEM] + [VMEM] * 7, (VMEM,) * 3, [pltpu.VMEM((nb, cols), f32)],
+            flops=4 * nb * nb * cols * 3,
+        )(here, owner, held, *arrived, displaced, lower_inverse, upper_inverse))
         yield give(DONE, (table, displaced, weights, top))
 
     chain, cross, (tops, (table, displaced, weights, top)) = spread(

time: 168 us -> 184 us (1.095)
  waiting for transfers between devices: 27.3 us -> 42.5 us
  local copies, waits for them, and re-layouts: 13.8 us -> 19.6 us
  starting transfers between devices: 90.4 us -> 87.6 us
    ppermute x14, waiting for transfers between devices: 11 us -> 19 us  [spread(): chain.append(lax.ppermute(ahead, 'pcol', along))]
    ppermute x16, waiting for transfers between devices: 16.3 us -> 23.5 us  [spread(): cross.append(lax.ppermute(aside, 'pcol', across))]
    unnamed x120 -> x124, local copies, waits for them, and re-layouts: 9.3 us -> 15.1 us
    select_n x5 -> x1, other arithmetic: 4.08 us -> 0.21 us  [old_top_rider(): old_top = jnp.where(row % (2 * d) == d, came, old_top)]
    ppermute x14, starting transfers between devices: 41.3 us -> 37.9 us  [spread(): chain.append(lax.ppermute(ahead, 'pcol', along))]
    select_n x10 -> x12, other arithmetic: 3.1 us -> 5.95 us  [spread(): aside = jnp.where(col == 0, aside, came)]
    ppermute x16, starting transfers between devices: 44.3 us -> 46.3 us  [spread(): cross.append(lax.ppermute(aside, 'pcol', across))]
    ppermute x3 -> x2, starting transfers between devices: 4.12 us -> 2.65 us  [old_top_rider(): lax.ppermute(old_top, 'prow', [(p, p + d) for p in range(0, n_rows, 2 * d)])]
  transfers between devices with their start and end apart: 36 -> 35, of which waited for: 13 -> 17; matrix products, arithmetic and copies ran while one was open for 4% -> 3% of each run, Pallas kernels for 9% -> 7%
where the time goes in v12:
time: 184 us; the launch traced here: 183 us
  starting transfers between devices  87.6 us (48%)
  waiting for transfers between devices  42.5 us (23%)
  Pallas kernels  25.4 us (14%)
  local copies, waits for them, and re-layouts  19.6 us (11%)
  other arithmetic  6.24 us (3%)
    ppermute x16, starting transfers between devices, spread(): cross.append(lax.ppermute(aside, 'pcol', across))  46.3 us
    ppermute x14, starting transfers between devices, spread(): chain.append(lax.ppermute(ahead, 'pcol', along))  37.9 us
    ppermute x16, waiting for transfers between devices, spread(): cross.append(lax.ppermute(aside, 'pcol', across))  23.5 us
    ppermute x14, waiting for transfers between devices, spread(): chain.append(lax.ppermute(ahead, 'pcol', along))  19 us
    unnamed x124, local copies, waits for them, and re-layouts  15.1 us
    pallas_call x1, Pallas kernels, local(): call(functools.partial(final_kernel, n_bufs=len(bufs), n_tops=len(tops),...  11.3 us
    pallas_call x1, Pallas kernels, exchange_rider(): call(functools.partial(factor_kernel, log=log), (slot,) * 3, [SMEM] + [VM...  6.75 us
    select_n x12, other arithmetic, spread(): aside = jnp.where(col == 0, aside, came)  5.95 us
  transfers between devices with their start and end apart: 35, of which 17 were waited for; matrix products, arithmetic and copies ran while one was open for 3% of the time, Pallas kernels for 7%

profile of v12, /device:TPU:10, one launch (start us, length us, event | category | flops | bytes accessed | tf_op | source)
XLA Modules:
  0.0 182.7 jit_solution(7467695078573630687)
XLA Ops:
  0.0 3.8 %fusion = (f32[128,512]{1,0:T(8,128)}, f32[128,512]{1,0:T(8,128)}, f32[128,512]{1,0:T(8,128)}, f32[128,512]{1,0:T(8,128)}, f32[128,512]{1,0:T(8,128)}, /*index=5...) fusion(f32[2048,640]{1,0:T(8,128)} %matrix_ref.5), kind=kLoop, calls=%fused_computation.29 | loop fusion | bytes 8388608 | tf_op jit(solution)/shard_map/slice | solution.py:386
  3.9 3.4 %collective-permute-start.1 = (f32[128,512]{1,0:T(8,128)S(1)}, f32[128,512]{1,0:T(8,128)S(1)}, u32[]{:S(2)}, u32[]{:S(2)}) collective-permute-start(f32[128,512]{1,0:T(8,128)S(1)} %get-tuple-element.169), channel_id=1, source_target_pairs={{0,1},{2,3},{3,2},{4,5},{5,4},{6,7},{7,6},{8,9},{10,11},{11,10},{1... | collective-permute-start | bytes 786440 | tf_op jit(solution)/shard_map/ppermute | solution.py:352
  7.3 3.5 %collective-permute-start = (f32[128,512]{1,0:T(8,128)S(1)}, f32[128,512]{1,0:T(8,128)S(1)}, u32[]{:S(2)}, u32[]{:S(2)}) collective-permute-start(f32[128,512]{1,0:T(8,128)S(1)} %get-tuple-element.170), channel_id=1, source_target_pairs={{0,2},{1,3},{2,4},{3,5},{4,6},{5,7},{8,10},{9,11},{10,12},{11,13},... | collective-permute-start | bytes 786440 | tf_op jit(solution)/shard_map/ppermute | solution.py:351
  13.2 3.5 %collective-permute-start.10 = (f32[128,512]{1,0:T(8,128)}, f32[128,512]{1,0:T(8,128)S(1)}, u32[]{:S(2)}, u32[]{:S(2)}) collective-permute-start(f32[128,512]{1,0:T(8,128)} %get-tuple-element.100), channel_id=1, source_target_pairs={{0,2},{1,3},{2,4},{3,5},{4,6},{5,7},{8,10},{9,11},{10,12},{11,13},... | collective-permute-start | bytes 786440 | tf_op jit(solution)/shard_map/ppermute | solution.py:351
  18.5 2.6 %copy-done = f32[2048,640]{1,0:T(8,128)S(1)} copy-done((f32[2048,640]{1,0:T(8,128)S(1)}, f32[2048,640]{1,0:T(8,128)}, u32[]{:S(2)}) %copy-start) | copy-done | bytes 5242904
  21.0 3.5 %shard_map.56.held_ref = f32[512,640]{1,0:T(8,128)S(1)} custom-call(s32[8,512]{1,0:T(8,128)S(1)} %get-tuple-element.82.table_ref, f32[2048,640]{1,0:T(8,128)S(1)} %copy-done), custom_call_target="tpu_custom_call" | custom-call | tf_op jit(solution)/shard_map/pallas_call | solution.py:446
  24.8 3.6 %collective-permute-start.3 = (f32[128,512]{1,0:T(8,128)S(1)}, f32[128,512]{1,0:T(8,128)S(1)}, u32[]{:S(2)}, u32[]{:S(2)}) collective-permute-start(f32[128,512]{1,0:T(8,128)S(1)} %get-tuple-element.193), channel_id=1, source_target_pairs={{0,1},{2,3},{3,2},{4,5},{5,4},{6,7},{7,6},{8,9},{10,11},{11,10},{1... | collective-permute-start | bytes 786440 | tf_op jit(solution)/shard_map/ppermute | solution.py:352
  30.6 4.8 %collective-permute-done.3.refs_10_.refs_16_ = f32[128,512]{1,0:T(8,128)S(1)} collective-permute-done((f32[128,512]{1,0:T(8,128)S(1)}, f32[128,512]{1,0:T(8,128)S(1)}, u32[]{:S(2)}, u32[]{:S(2)}) %collective-permute-start.3) | collective-permute-done | bytes 262176 | tf_op jit(solution)/shard_map/ppermute | solution.py:352
  35.4 3.3 %collective-permute-done.2.refs_2_ = f32[128,512]{1,0:T(8,128)S(1)} collective-permute-done((f32[128,512]{1,0:T(8,128)S(1)}, f32[128,512]{1,0:T(8,128)S(1)}, u32[]{:S(2)}, u32[]{:S(2)}) %collective-permute-start.2) | collective-permute-done | bytes 262176 | tf_op jit(solution)/shard_map/ppermute | solution.py:351
  43.5 3.4 %collective-permute-start.13 = (f32[128,512]{1,0:T(8,128)S(1)}, f32[128,512]{1,0:T(8,128)S(1)}, u32[]{:S(2)}, u32[]{:S(2)}) collective-permute-start(f32[128,512]{1,0:T(8,128)S(1)} %get-tuple-element.187), channel_id=1, source_target_pairs={{0,1},{2,3},{3,2},{4,5},{5,4},{6,7},{7,6},{8,9},{10,11},{11,10},{1... | collective-permute-start | bytes 786440 | tf_op jit(solution)/shard_map/ppermute | solution.py:352
  46.9 3.2 %collective-permute-start.12 = (f32[128,512]{1,0:T(8,128)S(1)}, f32[128,512]{1,0:T(8,128)S(1)}, u32[]{:S(2)}, u32[]{:S(2)}) collective-permute-start(f32[128,512]{1,0:T(8,128)S(1)} %get-tuple-element.188), channel_id=1, source_target_pairs={{0,2},{1,3},{2,4},{3,5},{4,6},{5,7},{8,10},{9,11},{10,12},{11,13},... | collective-permute-start | bytes 786440 | tf_op jit(solution)/shard_map/ppermute | solution.py:351
  50.4 3.3 %collective-permute-done.13.refs_11_.refs_17_ = f32[128,512]{1,0:T(8,128)S(1)} collective-permute-done((f32[128,512]{1,0:T(8,128)S(1)}, f32[128,512]{1,0:T(8,128)S(1)}, u32[]{:S(2)}, u32[]{:S(2)}) %collective-permute-start.13) | collective-permute-done | bytes 262176 | tf_op jit(solution)/shard_map/ppermute | solution.py:352
  57.3 3.4 %collective-permute-start.16 = (f32[128,512]{1,0:T(8,128)S(1)}, f32[128,512]{1,0:T(8,128)S(1)}, u32[]{:S(2)}, u32[]{:S(2)}) collective-permute-start(f32[128,512]{1,0:T(8,128)S(1)} %get-tuple-element.185), channel_id=1, source_target_pairs={{0,1},{2,3},{3,2},{4,5},{5,4},{6,7},{7,6},{8,9},{10,11},{11,10},{1... | collective-permute-start | bytes 786440 | tf_op jit(solution)/shard_map/ppermute | solution.py:352
  60.7 3.0 %collective-permute-start.15 = (f32[128,512]{1,0:T(8,128)S(1)}, f32[128,512]{1,0:T(8,128)S(1)}, u32[]{:S(2)}, u32[]{:S(2)}) collective-permute-start(f32[128,512]{1,0:T(8,128)S(1)} %get-tuple-element.186), channel_id=1, source_target_pairs={{0,2},{1,3},{2,4},{3,5},{4,6},{5,7},{8,10},{9,11},{10,12},{11,13},... | collective-permute-start | bytes 786440 | tf_op jit(solution)/shard_map/ppermute | solution.py:351
  66.1 2.5 %collective-permute-start.7 = (f32[128,512]{1,0:T(8,128)S(1)}, f32[128,512]{1,0:T(8,128)S(1)}, u32[]{:S(2)}, u32[]{:S(2)}) collective-permute-start(f32[128,512]{1,0:T(8,128)S(1)} %get-tuple-element.189), channel_id=1, source_target_pairs={{0,1},{2,3},{3,2},{4,5},{5,4},{6,7},{7,6},{8,9},{10,11},{11,10},{1... | collective-permute-start | bytes 786440 | tf_op jit(solution)/shard_map/ppermute | solution.py:352
  68.6 3.6 %collective-permute-start.6 = (f32[128,512]{1,0:T(8,128)S(1)}, f32[128,512]{1,0:T(8,128)S(1)}, u32[]{:S(2)}, u32[]{:S(2)}) collective-permute-start(f32[128,512]{1,0:T(8,128)S(1)} %get-tuple-element.190), channel_id=1, source_target_pairs={{0,2},{1,3},{2,4},{3,5},{4,6},{5,7},{8,10},{9,11},{10,12},{11,13},... | collective-permute-start | bytes 786440 | tf_op jit(solution)/shard_map/ppermute | solution.py:351
  84.2 3.3 %collective-permute-start.24 = (f32[128,512]{1,0:T(8,128)}, f32[128,512]{1,0:T(8,128)S(1)}, u32[]{:S(2)}, u32[]{:S(2)}) collective-permute-start(f32[128,512]{1,0:T(8,128)} %get-tuple-element.181), channel_id=1, source_target_pairs={{0,1},{2,3},{3,2},{4,5},{5,4},{6,7},{7,6},{8,9},{10,11},{11,10},{1... | collective-permute-start | bytes 786440 | tf_op jit(solution)/shard_map/ppermute | solution.py:352
  87.5 3.0 %collective-permute-start.23 = (f32[128,512]{1,0:T(8,128)}, f32[128,512]{1,0:T(8,128)}, u32[]{:S(2)}, u32[]{:S(2)}) collective-permute-start(f32[128,512]{1,0:T(8,128)} %get-tuple-element.182), channel_id=1, source_target_pairs={{0,2},{1,3},{2,4},{3,5},{4,6},{5,7},{8,10},{9,11},{10,12},{11,13},... | collective-permute-start | bytes 786440 | tf_op jit(solution)/shard_map/ppermute | solution.py:351
  93.0 3.0 %collective-permute-done.23.refs_9_ = f32[128,512]{1,0:T(8,128)} collective-permute-done((f32[128,512]{1,0:T(8,128)}, f32[128,512]{1,0:T(8,128)}, u32[]{:S(2)}, u32[]{:S(2)}) %collective-permute-start.23) | collective-permute-done | bytes 262176 | tf_op jit(solution)/shard_map/ppermute | solution.py:351
  111.1 3.0 %collective-permute-start.8 = (f32[128,512]{1,0:T(8,128)}, f32[128,512]{1,0:T(8,128)}, u32[]{:S(2)}, u32[]{:S(2)}) collective-permute-start(f32[128,512]{1,0:T(8,128)} %get-tuple-element.180), channel_id=1, source_target_pairs={{0,2},{1,3},{2,4},{3,5},{4,6},{5,7},{8,10},{9,11},{10,12},{11,13},... | collective-permute-start | bytes 786440 | tf_op jit(solution)/shard_map/ppermute | solution.py:351
  118.4 3.9 %collective-permute-done.8.refs_8_ = f32[128,512]{1,0:T(8,128)} collective-permute-done((f32[128,512]{1,0:T(8,128)}, f32[128,512]{1,0:T(8,128)}, u32[]{:S(2)}, u32[]{:S(2)}) %collective-permute-start.8) | collective-permute-done | bytes 262176 | tf_op jit(solution)/shard_map/ppermute | solution.py:351
  124.6 2.9 %collective-permute-done.25.refs_11_ = f32[128,512]{1,0:T(8,128)} collective-permute-done((f32[128,512]{1,0:T(8,128)}, f32[128,512]{1,0:T(8,128)}, u32[]{:S(2)}, u32[]{:S(2)}) %collective-permute-start.25) | collective-permute-done | bytes 262176 | tf_op jit(solution)/shard_map/ppermute | solution.py:351
  129.0 2.6 %collective-permute-start.31 = (f32[128,512]{1,0:T(8,128)S(1)}, f32[128,512]{1,0:T(8,128)S(1)}, u32[]{:S(2)}, u32[]{:S(2)}) collective-permute-start(f32[128,512]{1,0:T(8,128)S(1)} %get-tuple-element.174), channel_id=1, source_target_pairs={{0,1},{2,3},{3,2},{4,5},{5,4},{6,7},{7,6},{8,9},{10,11},{11,10},{1... | collective-permute-start | bytes 786440 | tf_op jit(solution)/shard_map/ppermute | solution.py:352
  131.6 2.8 %collective-permute-start.29 = (f32[128,512]{1,0:T(8,128)S(1)}, f32[128,512]{1,0:T(8,128)S(1)}, u32[]{:S(2)}, u32[]{:S(2)}) collective-permute-start(f32[128,512]{1,0:T(8,128)S(1)} %get-tuple-element.175), channel_id=1, source_target_pairs={{0,2},{1,3},{2,4},{3,5},{4,6},{5,7},{8,10},{9,11},{10,12},{11,13},... | collective-permute-start | bytes 786440 | tf_op jit(solution)/shard_map/ppermute | solution.py:351
  136.7 3.5 %collective-permute-start.22 = (f32[128,512]{1,0:T(8,128)S(1)}, f32[128,512]{1,0:T(8,128)S(1)}, u32[]{:S(2)}, u32[]{:S(2)}) collective-permute-start(f32[128,512]{1,0:T(8,128)S(1)} %get-tuple-element.177), channel_id=1, source_target_pairs={{0,1},{2,3},{3,2},{4,5},{5,4},{6,7},{7,6},{8,9},{10,11},{11,10},{1... | collective-permute-start | bytes 786440 | tf_op jit(solution)/shard_map/ppermute | solution.py:352
  141.9 6.8 %shard_map.58 = (f32[512,640]{1,0:T(8,128)S(1)}, f32[512,640]{1,0:T(8,128)S(1)}, f32[512,640]{1,0:T(8,128)S(1)}) custom-call(s32[2]{0:T(128)S(1)} %pad_add_fusion.where_ref, s32[512,128]{1,0:T(8,128)S(1)} %copy-done.39, f32[512,640]{1,0:T(8,128)S(1)} %copy-done.42, f32[256,640]{1,0:T(8,128)} %collective-permute-done.19.one_ref, ...), custom_call_target="tpu_custom_call" | custom-call | flops 2013265920 | tf_op jit(solution)/shard_map/pallas_call | solution.py:472
  153.4 3.4 %collective-permute-start.33 = (f32[128,512]{1,0:T(8,128)S(1)}, f32[128,512]{1,0:T(8,128)S(1)}, u32[]{:S(2)}, u32[]{:S(2)}) collective-permute-start(f32[128,512]{1,0:T(8,128)S(1)} %get-tuple-element.171), channel_id=1, source_target_pairs={{0,1},{2,3},{3,2},{4,5},{5,4},{6,7},{7,6},{8,9},{10,11},{11,10},{1... | collective-permute-start | bytes 786440 | tf_op jit(solution)/shard_map/ppermute | solution.py:352
  157.9 4.2 %collective-permute-done.30.refs_26_ = f32[128,512]{1,0:T(8,128)S(1)} collective-permute-done((f32[128,512]{1,0:T(8,128)S(1)}, f32[128,512]{1,0:T(8,128)S(1)}, u32[]{:S(2)}, u32[]{:S(2)}) %collective-permute-start.30) | collective-permute-done | bytes 262176 | tf_op jit(solution)/shard_map/ppermute | solution.py:352
  162.2 2.6 %collective-permute-start.32 = (f32[128,512]{1,0:T(8,128)S(1)}, f32[128,512]{1,0:T(8,128)S(1)}, u32[]{:S(2)}, u32[]{:S(2)}) collective-permute-start(f32[128,512]{1,0:T(8,128)S(1)} %broadcast_select_fusion.2), channel_id=1, source_target_pairs={{0,1},{2,3},{3,2},{4,5},{5,4},{6,7},{7,6},{8,9},{10,11},{11,10},{1... | collective-permute-start | bytes 786440 | tf_op jit(solution)/shard_map/ppermute | solution.py:352
  164.8 2.9 %collective-permute-done.33.refs_29_ = f32[128,512]{1,0:T(8,128)S(1)} collective-permute-done((f32[128,512]{1,0:T(8,128)S(1)}, f32[128,512]{1,0:T(8,128)S(1)}, u32[]{:S(2)}, u32[]{:S(2)}) %collective-permute-start.33) | collective-permute-done | bytes 262176 | tf_op jit(solution)/shard_map/ppermute | solution.py:352
  167.7 3.3 %collective-permute-done.32.refs_28_ = f32[128,512]{1,0:T(8,128)S(1)} collective-permute-done((f32[128,512]{1,0:T(8,128)S(1)}, f32[128,512]{1,0:T(8,128)S(1)}, u32[]{:S(2)}, u32[]{:S(2)}) %collective-permute-start.32) | collective-permute-done | bytes 262176 | tf_op jit(solution)/shard_map/ppermute | solution.py:352
  171.2 11.3 %shard_map.60 = f32[2048,640]{1,0:T(8,128)} custom-call(s32[2]{0:T(128)S(1)} %pad_add_fusion.where_ref, s32[8,512]{1,0:T(8,128)S(1)} %get-tuple-element.82.table_ref, s32[16]{0:T(128)S(1)} %dynamic-slice_bitcast_fusion.choice_ref, f32[512,640]{1,0:T(8,128)S(1)} %get-tuple-element.123.displaced_ref, f32[512,640]{1,0:T(8,128)S(1)} %get-tuple-element.124.weights_ref, ...), custom_call_target="tpu_custom_call" | custom-call | flops 4026531840 | bytes 14680064 | tf_op jit(solution)/shard_map/pallas_call | solution.py:485
  (185 shorter events, 64.3 us)
Async XLA Ops:
  3.9 14.6 %collective-permute-start.1 = (f32[128,512]{1,0:T(8,128)S(1)}, f32[128,512]{1,0:T(8,128)S(1)}, u32[]{:S(2)}, u32[]{:S(2)}) collective-permute-start(f32[128,512]{1,0:T(8,128)S(1)} %get-tuple-element.169), channel_id=1, source_target_pairs={{0,1},{2,3},{3,2},{4,5},{5,4},{6,7},{7,6},{8,9},{10,11},{11,10},{1... | collective-permute-start | bytes 786440 | tf_op jit(solution)/shard_map/ppermute | solution.py:352
  7.3 11.2 %collective-permute-start = (f32[128,512]{1,0:T(8,128)S(1)}, f32[128,512]{1,0:T(8,128)S(1)}, u32[]{:S(2)}, u32[]{:S(2)}) collective-permute-start(f32[128,512]{1,0:T(8,128)S(1)} %get-tuple-element.170), channel_id=1, source_target_pairs={{0,2},{1,3},{2,4},{3,5},{4,6},{5,7},{8,10},{9,11},{10,12},{11,13},... | collective-permute-start | bytes 786440 | tf_op jit(solution)/shard_map/ppermute | solution.py:351
  10.8 13.8 %collective-permute-start.11 = (f32[128,512]{1,0:T(8,128)}, f32[128,512]{1,0:T(8,128)S(1)}, u32[]{:S(2)}, u32[]{:S(2)}) collective-permute-start(f32[128,512]{1,0:T(8,128)} %get-tuple-element.101), channel_id=1, source_target_pairs={{0,1},{2,3},{3,2},{4,5},{5,4},{6,7},{7,6},{8,9},{10,11},{11,10},{1... | collective-permute-start | bytes 786440 | tf_op jit(solution)/shard_map/ppermute | solution.py:352
  13.2 11.4 %collective-permute-start.10 = (f32[128,512]{1,0:T(8,128)}, f32[128,512]{1,0:T(8,128)S(1)}, u32[]{:S(2)}, u32[]{:S(2)}) collective-permute-start(f32[128,512]{1,0:T(8,128)} %get-tuple-element.100), channel_id=1, source_target_pairs={{0,2},{1,3},{2,4},{3,5},{4,6},{5,7},{8,10},{9,11},{10,12},{11,13},... | collective-permute-start | bytes 786440 | tf_op jit(solution)/shard_map/ppermute | solution.py:351
  24.6 31.3 %collective-permute-start.14 = (f32[512,640]{1,0:T(8,128)S(1)}, f32[512,640]{1,0:T(8,128)}, u32[]{:S(2)}, u32[]{:S(2)}) collective-permute-start(f32[512,640]{1,0:T(8,128)S(1)} %shard_map.56.held_ref), channel_id=1, source_target_pairs={{0,8},{8,0},{16,24},{24,16},{1,9},{9,1},{17,25},{25,17},{2,10},{10... | collective-permute-start | bytes 3932168 | tf_op jit(solution)/shard_map/ppermute | solution.py:455
  24.8 10.6 %collective-permute-start.3 = (f32[128,512]{1,0:T(8,128)S(1)}, f32[128,512]{1,0:T(8,128)S(1)}, u32[]{:S(2)}, u32[]{:S(2)}) collective-permute-start(f32[128,512]{1,0:T(8,128)S(1)} %get-tuple-element.193), channel_id=1, source_target_pairs={{0,1},{2,3},{3,2},{4,5},{5,4},{6,7},{7,6},{8,9},{10,11},{11,10},{1... | collective-permute-start | bytes 786440 | tf_op jit(solution)/shard_map/ppermute | solution.py:352
  28.4 10.3 %collective-permute-start.2 = (f32[128,512]{1,0:T(8,128)S(1)}, f32[128,512]{1,0:T(8,128)S(1)}, u32[]{:S(2)}, u32[]{:S(2)}) collective-permute-start(f32[128,512]{1,0:T(8,128)S(1)} %get-tuple-element.194), channel_id=1, source_target_pairs={{0,2},{1,3},{2,4},{3,5},{4,6},{5,7},{8,10},{9,11},{10,12},{11,13},... | collective-permute-start | bytes 786440 | tf_op jit(solution)/shard_map/ppermute | solution.py:351
  38.8 11.3 %collective-permute-start.5 = (f32[128,512]{1,0:T(8,128)S(1)}, f32[128,512]{1,0:T(8,128)S(1)}, u32[]{:S(2)}, u32[]{:S(2)}) collective-permute-start(f32[128,512]{1,0:T(8,128)S(1)} %get-tuple-element.191), channel_id=1, source_target_pairs={{0,1},{2,3},{3,2},{4,5},{5,4},{6,7},{7,6},{8,9},{10,11},{11,10},{1... | collective-permute-start | bytes 786440 | tf_op jit(solution)/shard_map/ppermute | solution.py:352
  41.2 9.2 %collective-permute-start.4 = (f32[128,512]{1,0:T(8,128)S(1)}, f32[128,512]{1,0:T(8,128)S(1)}, u32[]{:S(2)}, u32[]{:S(2)}) collective-permute-start(f32[128,512]{1,0:T(8,128)S(1)} %get-tuple-element.192), channel_id=1, source_target_pairs={{0,2},{1,3},{2,4},{3,5},{4,6},{5,7},{8,10},{9,11},{10,12},{11,13},... | collective-permute-start | bytes 786440 | tf_op jit(solution)/shard_map/ppermute | solution.py:351
  43.5 10.2 %collective-permute-start.13 = (f32[128,512]{1,0:T(8,128)S(1)}, f32[128,512]{1,0:T(8,128)S(1)}, u32[]{:S(2)}, u32[]{:S(2)}) collective-permute-start(f32[128,512]{1,0:T(8,128)S(1)} %get-tuple-element.187), channel_id=1, source_target_pairs={{0,1},{2,3},{3,2},{4,5},{5,4},{6,7},{7,6},{8,9},{10,11},{11,10},{1... | collective-permute-start | bytes 786440 | tf_op jit(solution)/shard_map/ppermute | solution.py:352
  46.9 9.0 %collective-permute-start.12 = (f32[128,512]{1,0:T(8,128)S(1)}, f32[128,512]{1,0:T(8,128)S(1)}, u32[]{:S(2)}, u32[]{:S(2)}) collective-permute-start(f32[128,512]{1,0:T(8,128)S(1)} %get-tuple-element.188), channel_id=1, source_target_pairs={{0,2},{1,3},{2,4},{3,5},{4,6},{5,7},{8,10},{9,11},{10,12},{11,13},... | collective-permute-start | bytes 786440 | tf_op jit(solution)/shard_map/ppermute | solution.py:351
  57.3 15.0 %collective-permute-start.16 = (f32[128,512]{1,0:T(8,128)S(1)}, f32[128,512]{1,0:T(8,128)S(1)}, u32[]{:S(2)}, u32[]{:S(2)}) collective-permute-start(f32[128,512]{1,0:T(8,128)S(1)} %get-tuple-element.185), channel_id=1, source_target_pairs={{0,1},{2,3},{3,2},{4,5},{5,4},{6,7},{7,6},{8,9},{10,11},{11,10},{1... | collective-permute-start | bytes 786440 | tf_op jit(solution)/shard_map/ppermute | solution.py:352
  60.7 11.6 %collective-permute-start.15 = (f32[128,512]{1,0:T(8,128)S(1)}, f32[128,512]{1,0:T(8,128)S(1)}, u32[]{:S(2)}, u32[]{:S(2)}) collective-permute-start(f32[128,512]{1,0:T(8,128)S(1)} %get-tuple-element.186), channel_id=1, source_target_pairs={{0,2},{1,3},{2,4},{3,5},{4,6},{5,7},{8,10},{9,11},{10,12},{11,13},... | collective-permute-start | bytes 786440 | tf_op jit(solution)/shard_map/ppermute | solution.py:351
  65.4 17.9 %collective-permute-start.19 = (f32[256,640]{1,0:T(8,128)S(1)}, f32[256,640]{1,0:T(8,128)}, u32[]{:S(2)}, u32[]{:S(2)}) collective-permute-start(f32[256,640]{1,0:T(8,128)S(1)} %get-tuple-element.114), channel_id=1, source_target_pairs={{0,16},{8,24},{16,0},{24,8},{1,17},{9,25},{17,1},{25,9},{2,18},{10... | collective-permute-start | bytes 1966088 | tf_op jit(solution)/shard_map/ppermute | solution.py:459
  66.1 10.8 %collective-permute-start.7 = (f32[128,512]{1,0:T(8,128)S(1)}, f32[128,512]{1,0:T(8,128)S(1)}, u32[]{:S(2)}, u32[]{:S(2)}) collective-permute-start(f32[128,512]{1,0:T(8,128)S(1)} %get-tuple-element.189), channel_id=1, source_target_pairs={{0,1},{2,3},{3,2},{4,5},{5,4},{6,7},{7,6},{8,9},{10,11},{11,10},{1... | collective-permute-start | bytes 786440 | tf_op jit(solution)/shard_map/ppermute | solution.py:352
  68.6 9.5 %collective-permute-start.6 = (f32[128,512]{1,0:T(8,128)S(1)}, f32[128,512]{1,0:T(8,128)S(1)}, u32[]{:S(2)}, u32[]{:S(2)}) collective-permute-start(f32[128,512]{1,0:T(8,128)S(1)} %get-tuple-element.190), channel_id=1, source_target_pairs={{0,2},{1,3},{2,4},{3,5},{4,6},{5,7},{8,10},{9,11},{10,12},{11,13},... | collective-permute-start | bytes 786440 | tf_op jit(solution)/shard_map/ppermute | solution.py:351
  72.5 9.6 %collective-permute-start.18 = (f32[128,512]{1,0:T(8,128)S(1)}, f32[128,512]{1,0:T(8,128)S(1)}, u32[]{:S(2)}, u32[]{:S(2)}) collective-permute-start(f32[128,512]{1,0:T(8,128)S(1)} %get-tuple-element.183), channel_id=1, source_target_pairs={{0,1},{2,3},{3,2},{4,5},{5,4},{6,7},{7,6},{8,9},{10,11},{11,10},{1... | collective-permute-start | bytes 786440 | tf_op jit(solution)/shard_map/ppermute | solution.py:352
  79.2 12.0 %collective-permute-start.9 = (f32[128,512]{1,0:T(8,128)S(1)}, f32[128,512]{1,0:T(8,128)S(1)}, u32[]{:S(2)}, u32[]{:S(2)}) collective-permute-start(f32[128,512]{1,0:T(8,128)S(1)} %broadcast_select_fusion.11), channel_id=1, source_target_pairs={{0,1},{2,3},{3,2},{4,5},{5,4},{6,7},{7,6},{8,9},{10,11},{11,10},{1... | collective-permute-start | bytes 786440 | tf_op jit(solution)/shard_map/ppermute | solution.py:352
  107.7 19.9 %collective-permute-start.28 = (f32[512,512]{1,0:T(8,128)S(1)}, f32[512,512]{1,0:T(8,128)S(1)}, u32[]{:S(2)}, u32[]{:S(2)}) collective-permute-start(f32[512,512]{1,0:T(8,128)S(1)} %shard_map.59), channel_id=1, source_target_pairs={{0,16},{1,17},{2,18},{3,19},{4,20},{5,21},{6,22},{7,23}} | collective-permute-start | bytes 3145736 | tf_op jit(solution)/shard_map/ppermute | solution.py:428
  109.0 13.4 %collective-permute-start.20 = (f32[256,640]{1,0:T(8,128)}, f32[256,640]{1,0:T(8,128)}, u32[]{:S(2)}, u32[]{:S(2)}) collective-permute-start(f32[256,640]{1,0:T(8,128)} %collective-permute-done.19.one_ref), channel_id=1, source_target_pairs={{0,8},{8,0},{16,24},{24,16},{1,9},{9,1},{17,25},{25,17},{2,10},{10... | collective-permute-start | bytes 1966088 | tf_op jit(solution)/shard_map/ppermute | solution.py:461
  111.1 11.3 %collective-permute-start.8 = (f32[128,512]{1,0:T(8,128)}, f32[128,512]{1,0:T(8,128)}, u32[]{:S(2)}, u32[]{:S(2)}) collective-permute-start(f32[128,512]{1,0:T(8,128)} %get-tuple-element.180), channel_id=1, source_target_pairs={{0,2},{1,3},{2,4},{3,5},{4,6},{5,7},{8,10},{9,11},{10,12},{11,13},... | collective-permute-start | bytes 786440 | tf_op jit(solution)/shard_map/ppermute | solution.py:351
  114.0 10.6 %collective-permute-start.27 = (f32[128,512]{1,0:T(8,128)}, f32[128,512]{1,0:T(8,128)}, u32[]{:S(2)}, u32[]{:S(2)}) collective-permute-start(f32[128,512]{1,0:T(8,128)} %get-tuple-element.178), channel_id=1, source_target_pairs={{0,1},{2,3},{3,2},{4,5},{5,4},{6,7},{7,6},{8,9},{10,11},{11,10},{1... | collective-permute-start | bytes 786440 | tf_op jit(solution)/shard_map/ppermute | solution.py:352
  116.5 11.1 %collective-permute-start.25 = (f32[128,512]{1,0:T(8,128)}, f32[128,512]{1,0:T(8,128)}, u32[]{:S(2)}, u32[]{:S(2)}) collective-permute-start(f32[128,512]{1,0:T(8,128)} %get-tuple-element.179), channel_id=1, source_target_pairs={{0,2},{1,3},{2,4},{3,5},{4,6},{5,7},{8,10},{9,11},{10,12},{11,13},... | collective-permute-start | bytes 786440 | tf_op jit(solution)/shard_map/ppermute | solution.py:351
  129.0 19.7 %collective-permute-start.31 = (f32[128,512]{1,0:T(8,128)S(1)}, f32[128,512]{1,0:T(8,128)S(1)}, u32[]{:S(2)}, u32[]{:S(2)}) collective-permute-start(f32[128,512]{1,0:T(8,128)S(1)} %get-tuple-element.174), channel_id=1, source_target_pairs={{0,1},{2,3},{3,2},{4,5},{5,4},{6,7},{7,6},{8,9},{10,11},{11,10},{1... | collective-permute-start | bytes 786440 | tf_op jit(solution)/shard_map/ppermute | solution.py:352
  131.6 17.0 %collective-permute-start.29 = (f32[128,512]{1,0:T(8,128)S(1)}, f32[128,512]{1,0:T(8,128)S(1)}, u32[]{:S(2)}, u32[]{:S(2)}) collective-permute-start(f32[128,512]{1,0:T(8,128)S(1)} %get-tuple-element.175), channel_id=1, source_target_pairs={{0,2},{1,3},{2,4},{3,5},{4,6},{5,7},{8,10},{9,11},{10,12},{11,13},... | collective-permute-start | bytes 786440 | tf_op jit(solution)/shard_map/ppermute | solution.py:351
  134.4 14.2 %collective-permute-start.21 = (f32[128,512]{1,0:T(8,128)S(1)}, f32[128,512]{1,0:T(8,128)S(1)}, u32[]{:S(2)}, u32[]{:S(2)}) collective-permute-start(f32[128,512]{1,0:T(8,128)S(1)} %get-tuple-element.176), channel_id=1, source_target_pairs={{0,2},{1,3},{2,4},{3,5},{4,6},{5,7},{8,10},{9,11},{10,12},{11,13},... | collective-permute-start | bytes 786440 | tf_op jit(solution)/shard_map/ppermute | solution.py:351
  136.7 12.0 %collective-permute-start.22 = (f32[128,512]{1,0:T(8,128)S(1)}, f32[128,512]{1,0:T(8,128)S(1)}, u32[]{:S(2)}, u32[]{:S(2)}) collective-permute-start(f32[128,512]{1,0:T(8,128)S(1)} %get-tuple-element.177), channel_id=1, source_target_pairs={{0,1},{2,3},{3,2},{4,5},{5,4},{6,7},{7,6},{8,9},{10,11},{11,10},{1... | collective-permute-start | bytes 786440 | tf_op jit(solution)/shard_map/ppermute | solution.py:352
  140.4 30.7 %collective-permute-start.34 = (f32[512,512]{1,0:T(8,128)S(1)}, f32[512,512]{1,0:T(8,128)S(1)}, u32[]{:S(2)}, u32[]{:S(2)}) collective-permute-start(f32[512,512]{1,0:T(8,128)S(1)} %broadcast_select_fusion), channel_id=1, source_target_pairs={{0,8},{16,24},{1,9},{17,25},{2,10},{18,26},{3,11},{19,27},{4,12},{... | collective-permute-start | bytes 3145736 | tf_op jit(solution)/shard_map/ppermute | solution.py:428
  148.9 9.0 %collective-permute-start.26 = (f32[128,512]{1,0:T(8,128)S(1)}, f32[128,512]{1,0:T(8,128)S(1)}, u32[]{:S(2)}, u32[]{:S(2)}) collective-permute-start(f32[128,512]{1,0:T(8,128)S(1)} %get-tuple-element.172), channel_id=1, source_target_pairs={{0,2},{1,3},{2,4},{3,5},{4,6},{5,7},{8,10},{9,11},{10,12},{11,13},... | collective-permute-start | bytes 786440 | tf_op jit(solution)/shard_map/ppermute | solution.py:351
  151.0 11.1 %collective-permute-start.30 = (f32[128,512]{1,0:T(8,128)S(1)}, f32[128,512]{1,0:T(8,128)S(1)}, u32[]{:S(2)}, u32[]{:S(2)}) collective-permute-start(f32[128,512]{1,0:T(8,128)S(1)} %get-tuple-element.173), channel_id=1, source_target_pairs={{0,1},{2,3},{3,2},{4,5},{5,4},{6,7},{7,6},{8,9},{10,11},{11,10},{1... | collective-permute-start | bytes 786440 | tf_op jit(solution)/shard_map/ppermute | solution.py:352
  153.4 14.3 %collective-permute-start.33 = (f32[128,512]{1,0:T(8,128)S(1)}, f32[128,512]{1,0:T(8,128)S(1)}, u32[]{:S(2)}, u32[]{:S(2)}) collective-permute-start(f32[128,512]{1,0:T(8,128)S(1)} %get-tuple-element.171), channel_id=1, source_target_pairs={{0,1},{2,3},{3,2},{4,5},{5,4},{6,7},{7,6},{8,9},{10,11},{11,10},{1... | collective-permute-start | bytes 786440 | tf_op jit(solution)/shard_map/ppermute | solution.py:352
  162.2 8.9 %collective-permute-start.32 = (f32[128,512]{1,0:T(8,128)S(1)}, f32[128,512]{1,0:T(8,128)S(1)}, u32[]{:S(2)}, u32[]{:S(2)}) collective-permute-start(f32[128,512]{1,0:T(8,128)S(1)} %broadcast_select_fusion.2), channel_id=1, source_target_pairs={{0,1},{2,3},{3,2},{4,5},{5,4},{6,7},{7,6},{8,9},{10,11},{11,10},{1... | collective-permute-start | bytes 786440 | tf_op jit(solution)/shard_map/ppermute | solution.py:352
  (65 other events, 1023.3 us)

commit v13 on v3

--- a/solution.py
+++ b/solution.py
@@ -199,7 +199,6 @@
     ]
     rows, cols = matrix_ref.shape
     nb = weights_ref.shape[0]
-    half = nb // 2
     chunk = rows // (2 * parts)
     row = where_ref[0]
     first_row, first_col = row == 0, where_ref[1] == 0
@@ -219,17 +218,10 @@
             in_sem, n_cols, parts, parts,
         )
 
-    @pl.when(row == 1)
-    def _():
-        pltpu.make_async_copy(tops[0], low, low_sem).start()
-
-    for log in range(1, (n_tops + 1) // 2):
-        for odd in range(2):
-            @pl.when(((row >> log) == 1) & ((row & 1) == odd))
-            def _():
-                for part, ref in enumerate(tops[2 * log - 1 : 2 * log + 1]):
-                    at = half * (part ^ odd)
-                    pltpu.make_async_copy(ref, low.at[pl.ds(at, half), :], low_sem).start()
+    for log in range(n_tops):
+        @pl.when((row & ((2 << log) - 1)) == (1 << log))
+        def _():
+            pltpu.make_async_copy(tops[log], low, low_sem).start()
 
     w = weights_ref[...]
     w_hi[...] = w.astype(jnp.bfloat16)
@@ -399,23 +391,15 @@
             vmem=4 << 20,
         )(here, choice, matrix, *arrived)
         tops = []
-        log = 0
-        while (1 << log) < n_rows:
-            d = 1 << log
-            far = [(p, p + d) for p in range(d)]
-            if log == 0:
-                at += 2
-                whole = yield give(at, lax.ppermute(old_top, "prow", far))
-                tops.append(whole)
-            else:
-                half = jnp.where(odd, old_top[nb // 2 :], old_top[: nb // 2])
+        d = n_rows // 2
+        while d:
+            came = lax.ppermute(old_top, "prow", [(p, p + d) for p in range(0, n_rows, 2 * d)])
+            if d > 1:
                 at += 3
-                one = yield give(at, lax.ppermute(half, "prow", far))
-                two = lax.ppermute(one, "prow", [(p, p ^ 1) for p in range(d, 2 * d)])
-                tops += [one, two]
-                whole = both_halves(one, two)
-            old_top = jnp.where((row >> log) == 1, whole, old_top)
-            log += 1
+                came = yield give(at, came)
+                old_top = jnp.where(row % (2 * d) == d, came, old_top)
+            tops.insert(0, came)
+            d //= 2
         yield give(DONE, tops)
 
     slot = jax.ShapeDtypeStruct((nb, cols), f32)

time: 168 us -> 193 us (1.15)
  the two profiles are of different devices: /device:TPU:10 before, /device:TPU:0 now
where the time goes in v13:
time: 193 us; the launch traced here: 191 us
  starting transfers between devices  97.7 us (51%)
  local copies, waits for them, and re-layouts  36.9 us (19%)
  Pallas kernels  23.4 us (12%)
  waiting for transfers between devices  19.1 us (10%)
  other arithmetic  12.2 us (6%)
    ppermute x16, starting transfers between devices, spread(): cross.append(lax.ppermute(aside, 'pcol', across))  50.9 us
    ppermute x14, starting transfers between devices, spread(): chain.append(lax.ppermute(ahead, 'pcol', along))  40.3 us
    unnamed x180, local copies, waits for them, and re-layouts  32.4 us
    ppermute x16, waiting for transfers between devices, spread(): cross.append(lax.ppermute(aside, 'pcol', across))  13 us
    pallas_call x1, Pallas kernels, local(): call(functools.partial(final_kernel, n_bufs=len(bufs), n_tops=len(tops),...  8.65 us
    select_n x10, other arithmetic, spread(): aside = jnp.where(col == 0, aside, came)  6.89 us
    ppermute x14, waiting for transfers between devices, spread(): chain.append(lax.ppermute(ahead, 'pcol', along))  6.09 us
    pallas_call x1, Pallas kernels, exchange_rider(): call(factor_kernel, (slot, slot), [SMEM, VMEM, VMEM, VMEM], (VMEM, VMEM),...  5.93 us
  transfers between devices with their start and end apart: 35, of which 9 were waited for; matrix products, arithmetic and copies ran while one was open for 6% of the time, Pallas kernels for 8%

profile of v13, /device:TPU:0, one launch (start us, length us, event | category | flops | bytes accessed | tf_op | source)
XLA Modules:
  0.0 190.7 jit_solution(3144322809815391255)
XLA Ops:
  0.0 3.8 %fusion = (f32[128,512]{1,0:T(8,128)}, f32[128,512]{1,0:T(8,128)}, f32[128,512]{1,0:T(8,128)}, f32[128,512]{1,0:T(8,128)}, f32[128,512]{1,0:T(8,128)}, /*index=5...) fusion(f32[2048,640]{1,0:T(8,128)} %matrix_ref.5), kind=kLoop, calls=%fused_computation.32 | loop fusion | bytes 8388608 | tf_op jit(solution)/shard_map/slice | solution.py:354
  3.8 4.9 %collective-permute-start.1 = (f32[128,512]{1,0:T(8,128)S(1)}, f32[128,512]{1,0:T(8,128)S(1)}, u32[]{:S(2)}, u32[]{:S(2)}) collective-permute-start(f32[128,512]{1,0:T(8,128)S(1)} %get-tuple-element.171), channel_id=1, source_target_pairs={{0,1},{2,3},{3,2},{4,5},{5,4},{6,7},{7,6},{8,9},{10,11},{11,10},{1... | collective-permute-start | bytes 786440 | tf_op jit(solution)/shard_map/ppermute | solution.py:320
  8.7 3.5 %collective-permute-start = (f32[128,512]{1,0:T(8,128)S(1)}, f32[128,512]{1,0:T(8,128)S(1)}, u32[]{:S(2)}, u32[]{:S(2)}) collective-permute-start(f32[128,512]{1,0:T(8,128)S(1)} %get-tuple-element.172), channel_id=1, source_target_pairs={{0,2},{1,3},{2,4},{3,5},{4,6},{5,7},{8,10},{9,11},{10,12},{11,13},... | collective-permute-start | bytes 786440 | tf_op jit(solution)/shard_map/ppermute | solution.py:319
  14.6 4.2 %collective-permute-start.2 = (f32[128,512]{1,0:T(8,128)S(1)}, f32[128,512]{1,0:T(8,128)}, u32[]{:S(2)}, u32[]{:S(2)}) collective-permute-start(f32[128,512]{1,0:T(8,128)S(1)} %get-tuple-element.87), channel_id=1, source_target_pairs={{0,2},{1,3},{2,4},{3,5},{4,6},{5,7},{8,10},{9,11},{10,12},{11,13},... | collective-permute-start | bytes 786440 | tf_op jit(solution)/shard_map/ppermute | solution.py:319
  21.3 2.6 %copy-done = f32[2048,640]{1,0:T(8,128)S(1)} copy-done((f32[2048,640]{1,0:T(8,128)S(1)}, f32[2048,640]{1,0:T(8,128)}, u32[]{:S(2)}) %copy-start) | copy-done | bytes 5242904
  23.9 3.5 %shard_map.56.held_ref = f32[512,640]{1,0:T(8,128)S(1)} custom-call(s32[8,512]{1,0:T(8,128)S(1)} %get-tuple-element.83.table_ref, f32[2048,640]{1,0:T(8,128)S(1)} %copy-done), custom_call_target="tpu_custom_call" | custom-call | tf_op jit(solution)/shard_map/pallas_call | solution.py:414
  28.8 2.5 %collective-permute-start.15 = (f32[128,512]{1,0:T(8,128)S(1)}, f32[128,512]{1,0:T(8,128)S(1)}, u32[]{:S(2)}, u32[]{:S(2)}) collective-permute-start(f32[128,512]{1,0:T(8,128)S(1)} %get-tuple-element.192), channel_id=1, source_target_pairs={{0,1},{2,3},{3,2},{4,5},{5,4},{6,7},{7,6},{8,9},{10,11},{11,10},{1... | collective-permute-start | bytes 786440 | tf_op jit(solution)/shard_map/ppermute | solution.py:320
  31.3 2.9 %collective-permute-start.14 = (f32[128,512]{1,0:T(8,128)S(1)}, f32[128,512]{1,0:T(8,128)S(1)}, u32[]{:S(2)}, u32[]{:S(2)}) collective-permute-start(f32[128,512]{1,0:T(8,128)S(1)} %get-tuple-element.193), channel_id=1, source_target_pairs={{0,2},{1,3},{2,4},{3,5},{4,6},{5,7},{8,10},{9,11},{10,12},{11,13},... | collective-permute-start | bytes 786440 | tf_op jit(solution)/shard_map/ppermute | solution.py:319
  40.4 3.0 %collective-permute-start.17 = (f32[128,512]{1,0:T(8,128)S(1)}, f32[128,512]{1,0:T(8,128)S(1)}, u32[]{:S(2)}, u32[]{:S(2)}) collective-permute-start(f32[128,512]{1,0:T(8,128)S(1)} %get-tuple-element.190), channel_id=1, source_target_pairs={{0,1},{2,3},{3,2},{4,5},{5,4},{6,7},{7,6},{8,9},{10,11},{11,10},{1... | collective-permute-start | bytes 786440 | tf_op jit(solution)/shard_map/ppermute | solution.py:320
  43.4 3.6 %collective-permute-start.16 = (f32[128,512]{1,0:T(8,128)S(1)}, f32[128,512]{1,0:T(8,128)S(1)}, u32[]{:S(2)}, u32[]{:S(2)}) collective-permute-start(f32[128,512]{1,0:T(8,128)S(1)} %get-tuple-element.191), channel_id=1, source_target_pairs={{0,2},{1,3},{2,4},{3,5},{4,6},{5,7},{8,10},{9,11},{10,12},{11,13},... | collective-permute-start | bytes 786440 | tf_op jit(solution)/shard_map/ppermute | solution.py:319
  47.8 3.7 %collective-permute-start.8 = (f32[128,512]{1,0:T(8,128)S(1)}, f32[128,512]{1,0:T(8,128)S(1)}, u32[]{:S(2)}, u32[]{:S(2)}) collective-permute-start(f32[128,512]{1,0:T(8,128)S(1)} %get-tuple-element.196), channel_id=1, source_target_pairs={{0,1},{2,3},{3,2},{4,5},{5,4},{6,7},{7,6},{8,9},{10,11},{11,10},{1... | collective-permute-start | bytes 786440 | tf_op jit(solution)/shard_map/ppermute | solution.py:320
  51.5 2.6 %collective-permute-start.7 = (f32[128,512]{1,0:T(8,128)S(1)}, f32[128,512]{1,0:T(8,128)S(1)}, u32[]{:S(2)}, u32[]{:S(2)}) collective-permute-start(f32[128,512]{1,0:T(8,128)S(1)} %get-tuple-element.197), channel_id=1, source_target_pairs={{0,2},{1,3},{2,4},{3,5},{4,6},{5,7},{8,10},{9,11},{10,12},{11,13},... | collective-permute-start | bytes 786440 | tf_op jit(solution)/shard_map/ppermute | solution.py:319
  58.6 3.1 %collective-permute-start.10 = (f32[128,512]{1,0:T(8,128)S(1)}, f32[128,512]{1,0:T(8,128)S(1)}, u32[]{:S(2)}, u32[]{:S(2)}) collective-permute-start(f32[128,512]{1,0:T(8,128)S(1)} %get-tuple-element.194), channel_id=1, source_target_pairs={{0,1},{2,3},{3,2},{4,5},{5,4},{6,7},{7,6},{8,9},{10,11},{11,10},{1... | collective-permute-start | bytes 786440 | tf_op jit(solution)/shard_map/ppermute | solution.py:320
  61.7 4.4 %collective-permute-start.9 = (f32[128,512]{1,0:T(8,128)S(1)}, f32[128,512]{1,0:T(8,128)S(1)}, u32[]{:S(2)}, u32[]{:S(2)}) collective-permute-start(f32[128,512]{1,0:T(8,128)S(1)} %get-tuple-element.195), channel_id=1, source_target_pairs={{0,2},{1,3},{2,4},{3,5},{4,6},{5,7},{8,10},{9,11},{10,12},{11,13},... | collective-permute-start | bytes 786440 | tf_op jit(solution)/shard_map/ppermute | solution.py:319
  66.3 2.8 %collective-permute-start.19 = (f32[128,512]{1,0:T(8,128)S(1)}, f32[128,512]{1,0:T(8,128)S(1)}, u32[]{:S(2)}, u32[]{:S(2)}) collective-permute-start(f32[128,512]{1,0:T(8,128)S(1)} %get-tuple-element.188), channel_id=1, source_target_pairs={{0,1},{2,3},{3,2},{4,5},{5,4},{6,7},{7,6},{8,9},{10,11},{11,10},{1... | collective-permute-start | bytes 786440 | tf_op jit(solution)/shard_map/ppermute | solution.py:320
  69.1 2.8 %collective-permute-start.18 = (f32[128,512]{1,0:T(8,128)S(1)}, f32[128,512]{1,0:T(8,128)S(1)}, u32[]{:S(2)}, u32[]{:S(2)}) collective-permute-start(f32[128,512]{1,0:T(8,128)S(1)} %get-tuple-element.189), channel_id=1, source_target_pairs={{0,2},{1,3},{2,4},{3,5},{4,6},{5,7},{8,10},{9,11},{10,12},{11,13},... | collective-permute-start | bytes 786440 | tf_op jit(solution)/shard_map/ppermute | solution.py:319
  72.9 2.8 %collective-permute-done.18.refs_6_ = f32[128,512]{1,0:T(8,128)S(1)} collective-permute-done((f32[128,512]{1,0:T(8,128)S(1)}, f32[128,512]{1,0:T(8,128)S(1)}, u32[]{:S(2)}, u32[]{:S(2)}) %collective-permute-start.18) | collective-permute-done | bytes 262176 | tf_op jit(solution)/shard_map/ppermute | solution.py:319
  77.8 5.1 %collective-permute-start.21 = (f32[128,512]{1,0:T(8,128)}, f32[128,512]{1,0:T(8,128)}, u32[]{:S(2)}, u32[]{:S(2)}) collective-permute-start(f32[128,512]{1,0:T(8,128)} %get-tuple-element.184), channel_id=1, source_target_pairs={{0,2},{1,3},{2,4},{3,5},{4,6},{5,7},{8,10},{9,11},{10,12},{11,13},... | collective-permute-start | bytes 786440 | tf_op jit(solution)/shard_map/ppermute | solution.py:319
  83.0 4.4 %collective-permute-start.20 = (f32[128,512]{1,0:T(8,128)}, f32[128,512]{1,0:T(8,128)}, u32[]{:S(2)}, u32[]{:S(2)}) collective-permute-start(f32[128,512]{1,0:T(8,128)} %get-tuple-element.185), channel_id=1, source_target_pairs={{0,1},{2,3},{3,2},{4,5},{5,4},{6,7},{7,6},{8,9},{10,11},{11,10},{1... | collective-permute-start | bytes 786440 | tf_op jit(solution)/shard_map/ppermute | solution.py:320
  88.6 2.8 %collective-permute-start.13 = (f32[128,512]{1,0:T(8,128)}, f32[128,512]{1,0:T(8,128)S(1)}, u32[]{:S(2)}, u32[]{:S(2)}) collective-permute-start(f32[128,512]{1,0:T(8,128)} %get-tuple-element.187), channel_id=1, source_target_pairs={{0,1},{2,3},{3,2},{4,5},{5,4},{6,7},{7,6},{8,9},{10,11},{11,10},{1... | collective-permute-start | bytes 786440 | tf_op jit(solution)/shard_map/ppermute | solution.py:320
  103.3 5.1 %collective-permute-start.27 = (f32[128,512]{1,0:T(8,128)}, f32[128,512]{1,0:T(8,128)}, u32[]{:S(2)}, u32[]{:S(2)}) collective-permute-start(f32[128,512]{1,0:T(8,128)} %get-tuple-element.182), channel_id=1, source_target_pairs={{0,1},{2,3},{3,2},{4,5},{5,4},{6,7},{7,6},{8,9},{10,11},{11,10},{1... | collective-permute-start | bytes 786440 | tf_op jit(solution)/shard_map/ppermute | solution.py:320
  111.2 2.5 %copy-done.1 = f32[2048,640]{1,0:T(8,128)S(1)} copy-done((f32[2048,640]{1,0:T(8,128)S(1)}, f32[2048,640]{1,0:T(8,128)}, u32[]{:S(2)}) %copy-start.1) | copy-done | bytes 5242904
  123.0 3.4 %collective-permute-start.31 = (f32[512,512]{1,0:T(8,128)S(1)}, f32[512,512]{1,0:T(8,128)S(1)}, u32[]{:S(2)}, u32[]{:S(2)}) collective-permute-start(f32[512,512]{1,0:T(8,128)S(1)} %shard_map.60), channel_id=1, source_target_pairs={{0,16},{1,17},{2,18},{3,19},{4,20},{5,21},{6,22},{7,23}} | collective-permute-start | bytes 3145736 | tf_op jit(solution)/shard_map/ppermute | solution.py:396
  132.5 4.2 %collective-permute-start.24 = (f32[128,512]{1,0:T(8,128)S(1)}, f32[128,512]{1,0:T(8,128)S(1)}, u32[]{:S(2)}, u32[]{:S(2)}) collective-permute-start(f32[128,512]{1,0:T(8,128)S(1)} %get-tuple-element.181), channel_id=1, source_target_pairs={{0,1},{2,3},{3,2},{4,5},{5,4},{6,7},{7,6},{8,9},{10,11},{11,10},{1... | collective-permute-start | bytes 786440 | tf_op jit(solution)/shard_map/ppermute | solution.py:320
  136.7 5.9 %shard_map.59 = (f32[512,640]{1,0:T(8,128)S(1)}, f32[512,640]{1,0:T(8,128)S(1)}) custom-call(s32[2]{0:T(128)S(1)} %copy-done.66, f32[512,640]{1,0:T(8,128)S(1)} %copy-done.69, f32[512,512]{1,0:T(8,128)S(1)} %copy-done.70, f32[512,512]{1,0:T(8,128)S(1)} %copy-done.71), custom_call_target="tpu_custom_call" | custom-call | flops 4026531840 | tf_op jit(solution)/shard_map/pallas_call | solution.py:439
  146.7 2.5 %collective-permute-start.26 = (f32[128,512]{1,0:T(8,128)}, f32[128,512]{1,0:T(8,128)}, u32[]{:S(2)}, u32[]{:S(2)}) collective-permute-start(f32[128,512]{1,0:T(8,128)} %get-tuple-element.176), channel_id=1, source_target_pairs={{0,2},{1,3},{2,4},{3,5},{4,6},{5,7},{8,10},{9,11},{10,12},{11,13},... | collective-permute-start | bytes 786440 | tf_op jit(solution)/shard_map/ppermute | solution.py:319
  149.2 2.6 %collective-permute-start.29 = (f32[128,512]{1,0:T(8,128)}, f32[128,512]{1,0:T(8,128)}, u32[]{:S(2)}, u32[]{:S(2)}) collective-permute-start(f32[128,512]{1,0:T(8,128)} %get-tuple-element.177), channel_id=1, source_target_pairs={{0,1},{2,3},{3,2},{4,5},{5,4},{6,7},{7,6},{8,9},{10,11},{11,10},{1... | collective-permute-start | bytes 786440 | tf_op jit(solution)/shard_map/ppermute | solution.py:320
  152.7 5.4 %collective-permute-done.29.refs_26_ = f32[128,512]{1,0:T(8,128)} collective-permute-done((f32[128,512]{1,0:T(8,128)}, f32[128,512]{1,0:T(8,128)}, u32[]{:S(2)}, u32[]{:S(2)}) %collective-permute-start.29) | collective-permute-done | bytes 262176 | tf_op jit(solution)/shard_map/ppermute | solution.py:320
  159.7 4.4 %collective-permute-start.33 = (f32[128,512]{1,0:T(8,128)}, f32[128,512]{1,0:T(8,128)S(1)}, u32[]{:S(2)}, u32[]{:S(2)}) collective-permute-start(f32[128,512]{1,0:T(8,128)} %get-tuple-element.175), channel_id=1, source_target_pairs={{0,1},{2,3},{3,2},{4,5},{5,4},{6,7},{7,6},{8,9},{10,11},{11,10},{1... | collective-permute-start | bytes 786440 | tf_op jit(solution)/shard_map/ppermute | solution.py:320
  168.3 2.7 %collective-permute-done.32.refs_28_ = f32[128,512]{1,0:T(8,128)S(1)} collective-permute-done((f32[128,512]{1,0:T(8,128)S(1)}, f32[128,512]{1,0:T(8,128)S(1)}, u32[]{:S(2)}, u32[]{:S(2)}) %collective-permute-start.32) | collective-permute-done | bytes 262176 | tf_op jit(solution)/shard_map/ppermute | solution.py:320
  171.1 2.5 %copy-done.2 = f32[2048,640]{1,0:T(8,128)S(1)} copy-done((f32[2048,640]{1,0:T(8,128)S(1)}, f32[2048,640]{1,0:T(8,128)}, u32[]{:S(2)}) %copy-start.2) | copy-done | bytes 5242904
  181.9 8.6 %shard_map.61 = f32[2048,640]{1,0:T(8,128)} custom-call(s32[2]{0:T(128)S(1)} %copy-done.66, s32[8,512]{1,0:T(8,128)S(1)} %get-tuple-element.83.table_ref, s32[16]{0:T(128)S(1)} %dynamic-slice_bitcast_fusion.choice_ref, f32[512,640]{1,0:T(8,128)S(1)} %copy-done.3, f32[512,640]{1,0:T(8,128)S(1)} %copy-done.48, f32[512,640]{1,0:T(8,128)S(1)} %copy-done.50, ...), custom_call_target="tpu_custom_call" | custom-call | flops 4026531840 | bytes 14680064 | tf_op jit(solution)/shard_map/pallas_call | solution.py:451
  (242 shorter events, 70.6 us)
Async XLA Ops:
  3.8 17.5 %collective-permute-start.1 = (f32[128,512]{1,0:T(8,128)S(1)}, f32[128,512]{1,0:T(8,128)S(1)}, u32[]{:S(2)}, u32[]{:S(2)}) collective-permute-start(f32[128,512]{1,0:T(8,128)S(1)} %get-tuple-element.171), channel_id=1, source_target_pairs={{0,1},{2,3},{3,2},{4,5},{5,4},{6,7},{7,6},{8,9},{10,11},{11,10},{1... | collective-permute-start | bytes 786440 | tf_op jit(solution)/shard_map/ppermute | solution.py:320
  8.7 12.6 %collective-permute-start = (f32[128,512]{1,0:T(8,128)S(1)}, f32[128,512]{1,0:T(8,128)S(1)}, u32[]{:S(2)}, u32[]{:S(2)}) collective-permute-start(f32[128,512]{1,0:T(8,128)S(1)} %get-tuple-element.172), channel_id=1, source_target_pairs={{0,2},{1,3},{2,4},{3,5},{4,6},{5,7},{8,10},{9,11},{10,12},{11,13},... | collective-permute-start | bytes 786440 | tf_op jit(solution)/shard_map/ppermute | solution.py:319
  12.2 15.2 %collective-permute-start.3 = (f32[128,512]{1,0:T(8,128)S(1)}, f32[128,512]{1,0:T(8,128)S(1)}, u32[]{:S(2)}, u32[]{:S(2)}) collective-permute-start(f32[128,512]{1,0:T(8,128)S(1)} %get-tuple-element.88), channel_id=1, source_target_pairs={{0,1},{2,3},{3,2},{4,5},{5,4},{6,7},{7,6},{8,9},{10,11},{11,10},{1... | collective-permute-start | bytes 786440 | tf_op jit(solution)/shard_map/ppermute | solution.py:320
  14.6 12.8 %collective-permute-start.2 = (f32[128,512]{1,0:T(8,128)S(1)}, f32[128,512]{1,0:T(8,128)}, u32[]{:S(2)}, u32[]{:S(2)}) collective-permute-start(f32[128,512]{1,0:T(8,128)S(1)} %get-tuple-element.87), channel_id=1, source_target_pairs={{0,2},{1,3},{2,4},{3,5},{4,6},{5,7},{8,10},{9,11},{10,12},{11,13},... | collective-permute-start | bytes 786440 | tf_op jit(solution)/shard_map/ppermute | solution.py:319
  27.4 19.6 %collective-permute-start.6 = (f32[512,640]{1,0:T(8,128)S(1)}, f32[512,640]{1,0:T(8,128)S(1)}, u32[]{:S(2)}, u32[]{:S(2)}) collective-permute-start(f32[512,640]{1,0:T(8,128)S(1)} %shard_map.56.held_ref), channel_id=1, source_target_pairs={{0,8},{8,0},{16,24},{24,16},{1,9},{9,1},{17,25},{25,17},{2,10},{10... | collective-permute-start | bytes 3932168 | tf_op jit(solution)/shard_map/ppermute | solution.py:423
  28.8 11.0 %collective-permute-start.15 = (f32[128,512]{1,0:T(8,128)S(1)}, f32[128,512]{1,0:T(8,128)S(1)}, u32[]{:S(2)}, u32[]{:S(2)}) collective-permute-start(f32[128,512]{1,0:T(8,128)S(1)} %get-tuple-element.192), channel_id=1, source_target_pairs={{0,1},{2,3},{3,2},{4,5},{5,4},{6,7},{7,6},{8,9},{10,11},{11,10},{1... | collective-permute-start | bytes 786440 | tf_op jit(solution)/shard_map/ppermute | solution.py:320
  31.3 9.0 %collective-permute-start.14 = (f32[128,512]{1,0:T(8,128)S(1)}, f32[128,512]{1,0:T(8,128)S(1)}, u32[]{:S(2)}, u32[]{:S(2)}) collective-permute-start(f32[128,512]{1,0:T(8,128)S(1)} %get-tuple-element.193), channel_id=1, source_target_pairs={{0,2},{1,3},{2,4},{3,5},{4,6},{5,7},{8,10},{9,11},{10,12},{11,13},... | collective-permute-start | bytes 786440 | tf_op jit(solution)/shard_map/ppermute | solution.py:319
  35.3 11.7 %collective-permute-start.5 = (f32[128,512]{1,0:T(8,128)S(1)}, f32[128,512]{1,0:T(8,128)S(1)}, u32[]{:S(2)}, u32[]{:S(2)}) collective-permute-start(f32[128,512]{1,0:T(8,128)S(1)} %get-tuple-element.198), channel_id=1, source_target_pairs={{0,1},{2,3},{3,2},{4,5},{5,4},{6,7},{7,6},{8,9},{10,11},{11,10},{1... | collective-permute-start | bytes 786440 | tf_op jit(solution)/shard_map/ppermute | solution.py:320
  37.7 9.3 %collective-permute-start.4 = (f32[128,512]{1,0:T(8,128)S(1)}, f32[128,512]{1,0:T(8,128)S(1)}, u32[]{:S(2)}, u32[]{:S(2)}) collective-permute-start(f32[128,512]{1,0:T(8,128)S(1)} %get-tuple-element.199), channel_id=1, source_target_pairs={{0,2},{1,3},{2,4},{3,5},{4,6},{5,7},{8,10},{9,11},{10,12},{11,13},... | collective-permute-start | bytes 786440 | tf_op jit(solution)/shard_map/ppermute | solution.py:319
  40.4 13.6 %collective-permute-start.17 = (f32[128,512]{1,0:T(8,128)S(1)}, f32[128,512]{1,0:T(8,128)S(1)}, u32[]{:S(2)}, u32[]{:S(2)}) collective-permute-start(f32[128,512]{1,0:T(8,128)S(1)} %get-tuple-element.190), channel_id=1, source_target_pairs={{0,1},{2,3},{3,2},{4,5},{5,4},{6,7},{7,6},{8,9},{10,11},{11,10},{1... | collective-permute-start | bytes 786440 | tf_op jit(solution)/shard_map/ppermute | solution.py:320
  43.4 10.7 %collective-permute-start.16 = (f32[128,512]{1,0:T(8,128)S(1)}, f32[128,512]{1,0:T(8,128)S(1)}, u32[]{:S(2)}, u32[]{:S(2)}) collective-permute-start(f32[128,512]{1,0:T(8,128)S(1)} %get-tuple-element.191), channel_id=1, source_target_pairs={{0,2},{1,3},{2,4},{3,5},{4,6},{5,7},{8,10},{9,11},{10,12},{11,13},... | collective-permute-start | bytes 786440 | tf_op jit(solution)/shard_map/ppermute | solution.py:319
  47.8 8.7 %collective-permute-start.8 = (f32[128,512]{1,0:T(8,128)S(1)}, f32[128,512]{1,0:T(8,128)S(1)}, u32[]{:S(2)}, u32[]{:S(2)}) collective-permute-start(f32[128,512]{1,0:T(8,128)S(1)} %get-tuple-element.196), channel_id=1, source_target_pairs={{0,1},{2,3},{3,2},{4,5},{5,4},{6,7},{7,6},{8,9},{10,11},{11,10},{1... | collective-permute-start | bytes 786440 | tf_op jit(solution)/shard_map/ppermute | solution.py:320
  51.5 7.0 %collective-permute-start.7 = (f32[128,512]{1,0:T(8,128)S(1)}, f32[128,512]{1,0:T(8,128)S(1)}, u32[]{:S(2)}, u32[]{:S(2)}) collective-permute-start(f32[128,512]{1,0:T(8,128)S(1)} %get-tuple-element.197), channel_id=1, source_target_pairs={{0,2},{1,3},{2,4},{3,5},{4,6},{5,7},{8,10},{9,11},{10,12},{11,13},... | collective-permute-start | bytes 786440 | tf_op jit(solution)/shard_map/ppermute | solution.py:319
  55.0 16.9 %collective-permute-start.11 = (f32[256,640]{1,0:T(8,128)S(1)}, f32[256,640]{1,0:T(8,128)S(1)}, u32[]{:S(2)}, u32[]{:S(2)}) collective-permute-start(f32[256,640]{1,0:T(8,128)S(1)} %get-tuple-element.101), channel_id=1, source_target_pairs={{0,16},{8,24},{16,0},{24,8},{1,17},{9,25},{17,1},{25,9},{2,18},{10... | collective-permute-start | bytes 1966088 | tf_op jit(solution)/shard_map/ppermute | solution.py:427
  58.6 13.2 %collective-permute-start.10 = (f32[128,512]{1,0:T(8,128)S(1)}, f32[128,512]{1,0:T(8,128)S(1)}, u32[]{:S(2)}, u32[]{:S(2)}) collective-permute-start(f32[128,512]{1,0:T(8,128)S(1)} %get-tuple-element.194), channel_id=1, source_target_pairs={{0,1},{2,3},{3,2},{4,5},{5,4},{6,7},{7,6},{8,9},{10,11},{11,10},{1... | collective-permute-start | bytes 786440 | tf_op jit(solution)/shard_map/ppermute | solution.py:320
  61.7 10.2 %collective-permute-start.9 = (f32[128,512]{1,0:T(8,128)S(1)}, f32[128,512]{1,0:T(8,128)S(1)}, u32[]{:S(2)}, u32[]{:S(2)}) collective-permute-start(f32[128,512]{1,0:T(8,128)S(1)} %get-tuple-element.195), channel_id=1, source_target_pairs={{0,2},{1,3},{2,4},{3,5},{4,6},{5,7},{8,10},{9,11},{10,12},{11,13},... | collective-permute-start | bytes 786440 | tf_op jit(solution)/shard_map/ppermute | solution.py:319
  66.3 6.7 %collective-permute-start.19 = (f32[128,512]{1,0:T(8,128)S(1)}, f32[128,512]{1,0:T(8,128)S(1)}, u32[]{:S(2)}, u32[]{:S(2)}) collective-permute-start(f32[128,512]{1,0:T(8,128)S(1)} %get-tuple-element.188), channel_id=1, source_target_pairs={{0,1},{2,3},{3,2},{4,5},{5,4},{6,7},{7,6},{8,9},{10,11},{11,10},{1... | collective-permute-start | bytes 786440 | tf_op jit(solution)/shard_map/ppermute | solution.py:320
  71.9 21.7 %collective-permute-start.22 = (f32[256,640]{1,0:T(8,128)S(1)}, f32[256,640]{1,0:T(8,128)}, u32[]{:S(2)}, u32[]{:S(2)}) collective-permute-start(f32[256,640]{1,0:T(8,128)S(1)} %collective-permute-done.11.refs_0_), channel_id=1, source_target_pairs={{0,8},{8,0},{16,24},{24,16},{1,9},{9,1},{17,25},{25,17},{2,10},{10... | collective-permute-start | bytes 1966088 | tf_op jit(solution)/shard_map/ppermute | solution.py:429
  77.8 13.6 %collective-permute-start.21 = (f32[128,512]{1,0:T(8,128)}, f32[128,512]{1,0:T(8,128)}, u32[]{:S(2)}, u32[]{:S(2)}) collective-permute-start(f32[128,512]{1,0:T(8,128)} %get-tuple-element.184), channel_id=1, source_target_pairs={{0,2},{1,3},{2,4},{3,5},{4,6},{5,7},{8,10},{9,11},{10,12},{11,13},... | collective-permute-start | bytes 786440 | tf_op jit(solution)/shard_map/ppermute | solution.py:319
  83.0 10.6 %collective-permute-start.20 = (f32[128,512]{1,0:T(8,128)}, f32[128,512]{1,0:T(8,128)}, u32[]{:S(2)}, u32[]{:S(2)}) collective-permute-start(f32[128,512]{1,0:T(8,128)} %get-tuple-element.185), channel_id=1, source_target_pairs={{0,1},{2,3},{3,2},{4,5},{5,4},{6,7},{7,6},{8,9},{10,11},{11,10},{1... | collective-permute-start | bytes 786440 | tf_op jit(solution)/shard_map/ppermute | solution.py:320
  87.3 14.3 %collective-permute-start.12 = (f32[128,512]{1,0:T(8,128)}, f32[128,512]{1,0:T(8,128)S(1)}, u32[]{:S(2)}, u32[]{:S(2)}) collective-permute-start(f32[128,512]{1,0:T(8,128)} %get-tuple-element.186), channel_id=1, source_target_pairs={{0,2},{1,3},{2,4},{3,5},{4,6},{5,7},{8,10},{9,11},{10,12},{11,13},... | collective-permute-start | bytes 786440 | tf_op jit(solution)/shard_map/ppermute | solution.py:319
  88.6 13.0 %collective-permute-start.13 = (f32[128,512]{1,0:T(8,128)}, f32[128,512]{1,0:T(8,128)S(1)}, u32[]{:S(2)}, u32[]{:S(2)}) collective-permute-start(f32[128,512]{1,0:T(8,128)} %get-tuple-element.187), channel_id=1, source_target_pairs={{0,1},{2,3},{3,2},{4,5},{5,4},{6,7},{7,6},{8,9},{10,11},{11,10},{1... | collective-permute-start | bytes 786440 | tf_op jit(solution)/shard_map/ppermute | solution.py:320
  103.3 23.1 %collective-permute-start.27 = (f32[128,512]{1,0:T(8,128)}, f32[128,512]{1,0:T(8,128)}, u32[]{:S(2)}, u32[]{:S(2)}) collective-permute-start(f32[128,512]{1,0:T(8,128)} %get-tuple-element.182), channel_id=1, source_target_pairs={{0,1},{2,3},{3,2},{4,5},{5,4},{6,7},{7,6},{8,9},{10,11},{11,10},{1... | collective-permute-start | bytes 786440 | tf_op jit(solution)/shard_map/ppermute | solution.py:320
  108.4 18.0 %collective-permute-start.25 = (f32[128,512]{1,0:T(8,128)}, f32[128,512]{1,0:T(8,128)}, u32[]{:S(2)}, u32[]{:S(2)}) collective-permute-start(f32[128,512]{1,0:T(8,128)} %get-tuple-element.183), channel_id=1, source_target_pairs={{0,2},{1,3},{2,4},{3,5},{4,6},{5,7},{8,10},{9,11},{10,12},{11,13},... | collective-permute-start | bytes 786440 | tf_op jit(solution)/shard_map/ppermute | solution.py:319
  123.0 35.2 %collective-permute-start.31 = (f32[512,512]{1,0:T(8,128)S(1)}, f32[512,512]{1,0:T(8,128)S(1)}, u32[]{:S(2)}, u32[]{:S(2)}) collective-permute-start(f32[512,512]{1,0:T(8,128)S(1)} %shard_map.60), channel_id=1, source_target_pairs={{0,16},{1,17},{2,18},{3,19},{4,20},{5,21},{6,22},{7,23}} | collective-permute-start | bytes 3145736 | tf_op jit(solution)/shard_map/ppermute | solution.py:396
  127.7 17.1 %collective-permute-start.30 = (f32[128,512]{1,0:T(8,128)S(1)}, f32[128,512]{1,0:T(8,128)S(1)}, u32[]{:S(2)}, u32[]{:S(2)}) collective-permute-start(f32[128,512]{1,0:T(8,128)S(1)} %get-tuple-element.178), channel_id=1, source_target_pairs={{0,1},{2,3},{3,2},{4,5},{5,4},{6,7},{7,6},{8,9},{10,11},{11,10},{1... | collective-permute-start | bytes 786440 | tf_op jit(solution)/shard_map/ppermute | solution.py:320
  129.0 15.8 %collective-permute-start.28 = (f32[128,512]{1,0:T(8,128)S(1)}, f32[128,512]{1,0:T(8,128)S(1)}, u32[]{:S(2)}, u32[]{:S(2)}) collective-permute-start(f32[128,512]{1,0:T(8,128)S(1)} %get-tuple-element.179), channel_id=1, source_target_pairs={{0,2},{1,3},{2,4},{3,5},{4,6},{5,7},{8,10},{9,11},{10,12},{11,13},... | collective-permute-start | bytes 786440 | tf_op jit(solution)/shard_map/ppermute | solution.py:319
  130.5 14.3 %collective-permute-start.23 = (f32[128,512]{1,0:T(8,128)S(1)}, f32[128,512]{1,0:T(8,128)S(1)}, u32[]{:S(2)}, u32[]{:S(2)}) collective-permute-start(f32[128,512]{1,0:T(8,128)S(1)} %get-tuple-element.180), channel_id=1, source_target_pairs={{0,2},{1,3},{2,4},{3,5},{4,6},{5,7},{8,10},{9,11},{10,12},{11,13},... | collective-permute-start | bytes 786440 | tf_op jit(solution)/shard_map/ppermute | solution.py:319
  132.5 12.4 %collective-permute-start.24 = (f32[128,512]{1,0:T(8,128)S(1)}, f32[128,512]{1,0:T(8,128)S(1)}, u32[]{:S(2)}, u32[]{:S(2)}) collective-permute-start(f32[128,512]{1,0:T(8,128)S(1)} %get-tuple-element.181), channel_id=1, source_target_pairs={{0,1},{2,3},{3,2},{4,5},{5,4},{6,7},{7,6},{8,9},{10,11},{11,10},{1... | collective-permute-start | bytes 786440 | tf_op jit(solution)/shard_map/ppermute | solution.py:320
  149.2 8.9 %collective-permute-start.29 = (f32[128,512]{1,0:T(8,128)}, f32[128,512]{1,0:T(8,128)}, u32[]{:S(2)}, u32[]{:S(2)}) collective-permute-start(f32[128,512]{1,0:T(8,128)} %get-tuple-element.177), channel_id=1, source_target_pairs={{0,1},{2,3},{3,2},{4,5},{5,4},{6,7},{7,6},{8,9},{10,11},{11,10},{1... | collective-permute-start | bytes 786440 | tf_op jit(solution)/shard_map/ppermute | solution.py:320
  158.3 12.7 %collective-permute-start.34 = (f32[512,512]{1,0:T(8,128)S(1)}, f32[512,512]{1,0:T(8,128)S(1)}, u32[]{:S(2)}, u32[]{:S(2)}) collective-permute-start(f32[512,512]{1,0:T(8,128)S(1)} %broadcast_select_fusion), channel_id=1, source_target_pairs={{0,8},{16,24},{1,9},{17,25},{2,10},{18,26},{3,11},{19,27},{4,12},{... | collective-permute-start | bytes 3145736 | tf_op jit(solution)/shard_map/ppermute | solution.py:396
  159.7 8.6 %collective-permute-start.33 = (f32[128,512]{1,0:T(8,128)}, f32[128,512]{1,0:T(8,128)S(1)}, u32[]{:S(2)}, u32[]{:S(2)}) collective-permute-start(f32[128,512]{1,0:T(8,128)} %get-tuple-element.175), channel_id=1, source_target_pairs={{0,1},{2,3},{3,2},{4,5},{5,4},{6,7},{7,6},{8,9},{10,11},{11,10},{1... | collective-permute-start | bytes 786440 | tf_op jit(solution)/shard_map/ppermute | solution.py:320
  (93 other events, 737.4 us)

commit v14 on v3

--- a/solution.py
+++ b/solution.py
@@ -7,7 +7,6 @@
 from jax.experimental.pallas import tpu as pltpu
 from jax.sharding import PartitionSpec as P
 
-HIGHEST = lax.Precision.HIGHEST
 VMEM = pl.BlockSpec(memory_space=pltpu.VMEM)
 SMEM = pl.BlockSpec(memory_space=pltpu.SMEM)
 ANY = pl.BlockSpec(memory_space=pl.ANY)
@@ -138,16 +137,21 @@
         half_ref[...] = merged_ref[high, :]
 
 
+def split(x):
+    hi = x.astype(jnp.bfloat16)
+    return hi, (x - hi.astype(jnp.float32)).astype(jnp.bfloat16)
+
+
+def product(a, b):
+    dot = functools.partial(jnp.dot, preferred_element_type=jnp.float32)
+    return dot(a[1], b[0]) + dot(a[0], b[1]) + dot(a[0], b[0])
+
+
 def factor_kernel(where_ref, top_in_ref, lower_ref, upper_ref, weights_ref, top_ref):
-    nb, cols = top_in_ref.shape
-    u = jnp.dot(
-        lower_ref[...], top_in_ref[...], precision=HIGHEST,
-        preferred_element_type=jnp.float32,
-    )
+    nb = top_in_ref.shape[0]
+    u = product(split(lower_ref[...]), split(top_in_ref[...]))
     top_ref[...] = u
-    weights_ref[...] = jnp.dot(
-        upper_ref[...], u, precision=HIGHEST, preferred_element_type=jnp.float32
-    )
+    weights_ref[...] = product(split(upper_ref[...]), split(u))
 
     @pl.when(where_ref[1] == 0)
     def _():
@@ -240,13 +244,16 @@
     count = table_ref[COUNT, 0]
 
     def swap(from_mat, from_pan):
-        def body(k, _):
-            to = table_ref[ROW, k]
-            mat[pl.ds(to, 1), :] = from_mat[pl.ds(table_ref[FROM, k], 1), :]
-            pan[pl.ds(to, 1), :] = from_pan[pl.ds(table_ref[TOP, k], 1), :]
+        def body(turn, _):
+            at = [jnp.minimum(4 * turn + k, count - 1) for k in range(4)]
+            mats = [from_mat[pl.ds(table_ref[FROM, k], 1), :] for k in at]
+            pans = [from_pan[pl.ds(table_ref[TOP, k], 1), :] for k in at]
+            for k, row_mat, row_pan in zip(at, mats, pans):
+                mat[pl.ds(table_ref[ROW, k], 1), :] = row_mat
+                pan[pl.ds(table_ref[ROW, k], 1), :] = row_pan
             return 0
 
-        lax.fori_loop(0, count, body, 0)
+        lax.fori_loop(0, (count + 3) // 4, body, 0)
 
     @pl.when(first_row)
     def _():

time: 168 us -> 166 us (0.988)
  transfers between devices with their start and end apart: 36 -> 36, of which waited for: 13 -> 14; matrix products, arithmetic and copies ran while one was open for 4% -> 4% of each run, Pallas kernels for 9% -> 8%
where the time goes in v14:
time: 166 us; the launch traced here: 164 us
  starting transfers between devices  90.1 us (54%)
  waiting for transfers between devices  27.7 us (17%)
  Pallas kernels  24.3 us (15%)
  local copies, waits for them, and re-layouts  13.8 us (8%)
  other arithmetic  7.25 us (4%)
    ppermute x16, starting transfers between devices, spread(): cross.append(lax.ppermute(aside, 'pcol', across))  44.2 us
    ppermute x14, starting transfers between devices, spread(): chain.append(lax.ppermute(ahead, 'pcol', along))  41.3 us
    ppermute x16, waiting for transfers between devices, spread(): cross.append(lax.ppermute(aside, 'pcol', across))  16.1 us
    ppermute x14, waiting for transfers between devices, spread(): chain.append(lax.ppermute(ahead, 'pcol', along))  11 us
    pallas_call x1, Pallas kernels, local(): call(functools.partial(final_kernel, n_bufs=len(bufs), n_tops=len(tops),...  10.4 us
    unnamed x120, local copies, waits for them, and re-layouts  9.3 us
    pallas_call x1, Pallas kernels, exchange_rider(): call(factor_kernel, (slot, slot), [SMEM, VMEM, VMEM, VMEM], (VMEM, VMEM),...  5.09 us
    slice x1, local copies, waits for them, and re-layouts, local(): lax.slice(matrix, (k * chunk, 0), ((k + 1) * chunk, nb))  3.84 us
  transfers between devices with their start and end apart: 36, of which 14 were waited for; matrix products, arithmetic and copies ran while one was open for 4% of the time, Pallas kernels for 8%

profile of v14, /device:TPU:10, one launch (start us, length us, event | category | flops | bytes accessed | tf_op | source)
XLA Modules:
  0.0 164.4 jit_solution(17624966627446016296)
XLA Ops:
  0.0 3.8 %fusion = (f32[128,512]{1,0:T(8,128)}, f32[128,512]{1,0:T(8,128)}, f32[128,512]{1,0:T(8,128)}, f32[128,512]{1,0:T(8,128)}, f32[128,512]{1,0:T(8,128)}, /*index=5...) fusion(f32[2048,640]{1,0:T(8,128)} %matrix_ref.5), kind=kLoop, calls=%fused_computation.33 | loop fusion | bytes 8388608 | tf_op jit(solution)/shard_map/slice | solution.py:369
  3.9 3.4 %collective-permute-start.1 = (f32[128,512]{1,0:T(8,128)S(1)}, f32[128,512]{1,0:T(8,128)S(1)}, u32[]{:S(2)}, u32[]{:S(2)}) collective-permute-start(f32[128,512]{1,0:T(8,128)S(1)} %get-tuple-element.171), channel_id=1, source_target_pairs={{0,1},{2,3},{3,2},{4,5},{5,4},{6,7},{7,6},{8,9},{10,11},{11,10},{1... | collective-permute-start | bytes 786440 | tf_op jit(solution)/shard_map/ppermute | solution.py:335
  7.3 3.5 %collective-permute-start = (f32[128,512]{1,0:T(8,128)S(1)}, f32[128,512]{1,0:T(8,128)S(1)}, u32[]{:S(2)}, u32[]{:S(2)}) collective-permute-start(f32[128,512]{1,0:T(8,128)S(1)} %get-tuple-element.172), channel_id=1, source_target_pairs={{0,2},{1,3},{2,4},{3,5},{4,6},{5,7},{8,10},{9,11},{10,12},{11,13},... | collective-permute-start | bytes 786440 | tf_op jit(solution)/shard_map/ppermute | solution.py:334
  10.8 2.4 %collective-permute-start.3 = (f32[128,512]{1,0:T(8,128)S(1)}, f32[128,512]{1,0:T(8,128)S(1)}, u32[]{:S(2)}, u32[]{:S(2)}) collective-permute-start(f32[128,512]{1,0:T(8,128)S(1)} %get-tuple-element.88), channel_id=1, source_target_pairs={{0,1},{2,3},{3,2},{4,5},{5,4},{6,7},{7,6},{8,9},{10,11},{11,10},{1... | collective-permute-start | bytes 786440 | tf_op jit(solution)/shard_map/ppermute | solution.py:335
  13.2 3.5 %collective-permute-start.2 = (f32[128,512]{1,0:T(8,128)S(1)}, f32[128,512]{1,0:T(8,128)}, u32[]{:S(2)}, u32[]{:S(2)}) collective-permute-start(f32[128,512]{1,0:T(8,128)S(1)} %get-tuple-element.87), channel_id=1, source_target_pairs={{0,2},{1,3},{2,4},{3,5},{4,6},{5,7},{8,10},{9,11},{10,12},{11,13},... | collective-permute-start | bytes 786440 | tf_op jit(solution)/shard_map/ppermute | solution.py:334
  19.1 2.6 %copy-done = f32[2048,640]{1,0:T(8,128)S(1)} copy-done((f32[2048,640]{1,0:T(8,128)S(1)}, f32[2048,640]{1,0:T(8,128)}, u32[]{:S(2)}) %copy-start) | copy-done | bytes 5242904
  21.7 3.5 %shard_map.56.held_ref = f32[512,640]{1,0:T(8,128)S(1)} custom-call(s32[8,512]{1,0:T(8,128)S(1)} %get-tuple-element.83.table_ref, f32[2048,640]{1,0:T(8,128)S(1)} %copy-done), custom_call_target="tpu_custom_call" | custom-call | tf_op jit(solution)/shard_map/pallas_call | solution.py:437
  25.6 3.6 %collective-permute-start.15 = (f32[128,512]{1,0:T(8,128)S(1)}, f32[128,512]{1,0:T(8,128)S(1)}, u32[]{:S(2)}, u32[]{:S(2)}) collective-permute-start(f32[128,512]{1,0:T(8,128)S(1)} %get-tuple-element.192), channel_id=1, source_target_pairs={{0,1},{2,3},{3,2},{4,5},{5,4},{6,7},{7,6},{8,9},{10,11},{11,10},{1... | collective-permute-start | bytes 786440 | tf_op jit(solution)/shard_map/ppermute | solution.py:335
  32.3 2.4 %collective-permute-start.5 = (f32[128,512]{1,0:T(8,128)S(1)}, f32[128,512]{1,0:T(8,128)S(1)}, u32[]{:S(2)}, u32[]{:S(2)}) collective-permute-start(f32[128,512]{1,0:T(8,128)S(1)} %get-tuple-element.198), channel_id=1, source_target_pairs={{0,1},{2,3},{3,2},{4,5},{5,4},{6,7},{7,6},{8,9},{10,11},{11,10},{1... | collective-permute-start | bytes 786440 | tf_op jit(solution)/shard_map/ppermute | solution.py:335
  34.7 4.5 %collective-permute-start.4 = (f32[128,512]{1,0:T(8,128)S(1)}, f32[128,512]{1,0:T(8,128)S(1)}, u32[]{:S(2)}, u32[]{:S(2)}) collective-permute-start(f32[128,512]{1,0:T(8,128)S(1)} %get-tuple-element.199), channel_id=1, source_target_pairs={{0,2},{1,3},{2,4},{3,5},{4,6},{5,7},{8,10},{9,11},{10,12},{11,13},... | collective-permute-start | bytes 786440 | tf_op jit(solution)/shard_map/ppermute | solution.py:334
  42.1 2.3 %collective-permute-start.16 = (f32[128,512]{1,0:T(8,128)S(1)}, f32[128,512]{1,0:T(8,128)S(1)}, u32[]{:S(2)}, u32[]{:S(2)}) collective-permute-start(f32[128,512]{1,0:T(8,128)S(1)} %get-tuple-element.191), channel_id=1, source_target_pairs={{0,2},{1,3},{2,4},{3,5},{4,6},{5,7},{8,10},{9,11},{10,12},{11,13},... | collective-permute-start | bytes 786440 | tf_op jit(solution)/shard_map/ppermute | solution.py:334
  45.9 3.1 %collective-permute-start.8 = (f32[128,512]{1,0:T(8,128)S(1)}, f32[128,512]{1,0:T(8,128)S(1)}, u32[]{:S(2)}, u32[]{:S(2)}) collective-permute-start(f32[128,512]{1,0:T(8,128)S(1)} %get-tuple-element.196), channel_id=1, source_target_pairs={{0,1},{2,3},{3,2},{4,5},{5,4},{6,7},{7,6},{8,9},{10,11},{11,10},{1... | collective-permute-start | bytes 786440 | tf_op jit(solution)/shard_map/ppermute | solution.py:335
  49.0 3.3 %collective-permute-start.7 = (f32[128,512]{1,0:T(8,128)S(1)}, f32[128,512]{1,0:T(8,128)S(1)}, u32[]{:S(2)}, u32[]{:S(2)}) collective-permute-start(f32[128,512]{1,0:T(8,128)S(1)} %get-tuple-element.197), channel_id=1, source_target_pairs={{0,2},{1,3},{2,4},{3,5},{4,6},{5,7},{8,10},{9,11},{10,12},{11,13},... | collective-permute-start | bytes 786440 | tf_op jit(solution)/shard_map/ppermute | solution.py:334
  55.3 2.7 %collective-permute-done.7.refs_5_ = f32[128,512]{1,0:T(8,128)S(1)} collective-permute-done((f32[128,512]{1,0:T(8,128)S(1)}, f32[128,512]{1,0:T(8,128)S(1)}, u32[]{:S(2)}, u32[]{:S(2)}) %collective-permute-start.7) | collective-permute-done | bytes 262176 | tf_op jit(solution)/shard_map/ppermute | solution.py:334
  58.1 3.0 %collective-permute-start.10 = (f32[128,512]{1,0:T(8,128)S(1)}, f32[128,512]{1,0:T(8,128)S(1)}, u32[]{:S(2)}, u32[]{:S(2)}) collective-permute-start(f32[128,512]{1,0:T(8,128)S(1)} %get-tuple-element.194), channel_id=1, source_target_pairs={{0,1},{2,3},{3,2},{4,5},{5,4},{6,7},{7,6},{8,9},{10,11},{11,10},{1... | collective-permute-start | bytes 786440 | tf_op jit(solution)/shard_map/ppermute | solution.py:335
  61.2 3.5 %collective-permute-start.9 = (f32[128,512]{1,0:T(8,128)S(1)}, f32[128,512]{1,0:T(8,128)S(1)}, u32[]{:S(2)}, u32[]{:S(2)}) collective-permute-start(f32[128,512]{1,0:T(8,128)S(1)} %get-tuple-element.195), channel_id=1, source_target_pairs={{0,2},{1,3},{2,4},{3,5},{4,6},{5,7},{8,10},{9,11},{10,12},{11,13},... | collective-permute-start | bytes 786440 | tf_op jit(solution)/shard_map/ppermute | solution.py:334
  67.0 3.3 %collective-permute-start.18 = (f32[128,512]{1,0:T(8,128)S(1)}, f32[128,512]{1,0:T(8,128)S(1)}, u32[]{:S(2)}, u32[]{:S(2)}) collective-permute-start(f32[128,512]{1,0:T(8,128)S(1)} %get-tuple-element.189), channel_id=1, source_target_pairs={{0,2},{1,3},{2,4},{3,5},{4,6},{5,7},{8,10},{9,11},{10,12},{11,13},... | collective-permute-start | bytes 786440 | tf_op jit(solution)/shard_map/ppermute | solution.py:334
  70.7 2.4 %collective-permute-done.19.refs_14_.refs_20_ = f32[128,512]{1,0:T(8,128)S(1)} collective-permute-done((f32[128,512]{1,0:T(8,128)S(1)}, f32[128,512]{1,0:T(8,128)S(1)}, u32[]{:S(2)}, u32[]{:S(2)}) %collective-permute-start.19) | collective-permute-done | bytes 262176 | tf_op jit(solution)/shard_map/ppermute | solution.py:335
  77.4 3.3 %collective-permute-start.21 = (f32[128,512]{1,0:T(8,128)}, f32[128,512]{1,0:T(8,128)}, u32[]{:S(2)}, u32[]{:S(2)}) collective-permute-start(f32[128,512]{1,0:T(8,128)} %get-tuple-element.184), channel_id=1, source_target_pairs={{0,2},{1,3},{2,4},{3,5},{4,6},{5,7},{8,10},{9,11},{10,12},{11,13},... | collective-permute-start | bytes 786440 | tf_op jit(solution)/shard_map/ppermute | solution.py:334
  80.8 2.5 %collective-permute-start.20 = (f32[128,512]{1,0:T(8,128)}, f32[128,512]{1,0:T(8,128)}, u32[]{:S(2)}, u32[]{:S(2)}) collective-permute-start(f32[128,512]{1,0:T(8,128)} %get-tuple-element.185), channel_id=1, source_target_pairs={{0,1},{2,3},{3,2},{4,5},{5,4},{6,7},{7,6},{8,9},{10,11},{11,10},{1... | collective-permute-start | bytes 786440 | tf_op jit(solution)/shard_map/ppermute | solution.py:335
  84.0 2.9 %collective-permute-start.12 = (f32[128,512]{1,0:T(8,128)}, f32[128,512]{1,0:T(8,128)S(1)}, u32[]{:S(2)}, u32[]{:S(2)}) collective-permute-start(f32[128,512]{1,0:T(8,128)} %get-tuple-element.186), channel_id=1, source_target_pairs={{0,2},{1,3},{2,4},{3,5},{4,6},{5,7},{8,10},{9,11},{10,12},{11,13},... | collective-permute-start | bytes 786440 | tf_op jit(solution)/shard_map/ppermute | solution.py:334
  86.9 2.5 %collective-permute-start.13 = (f32[128,512]{1,0:T(8,128)}, f32[128,512]{1,0:T(8,128)S(1)}, u32[]{:S(2)}, u32[]{:S(2)}) collective-permute-start(f32[128,512]{1,0:T(8,128)} %get-tuple-element.187), channel_id=1, source_target_pairs={{0,1},{2,3},{3,2},{4,5},{5,4},{6,7},{7,6},{8,9},{10,11},{11,10},{1... | collective-permute-start | bytes 786440 | tf_op jit(solution)/shard_map/ppermute | solution.py:335
  92.4 2.3 %shard_map.58 = (f32[512,640]{1,0:T(8,128)S(1)}, f32[256,640]{1,0:T(8,128)}) custom-call(s32[2]{0:T(128)S(1)} %copy-done.35, s32[512,128]{1,0:T(8,128)S(1)} %copy-done.33, f32[512,640]{1,0:T(8,128)S(1)} %copy-done.30, f32[256,640]{1,0:T(8,128)S(1)} %collective-permute-done.11.refs_0_, f32[256,640]{1,0:T(8,128)} %collective-permute-done.22.refs_1_), custom_call_target="tpu_custom_call" | custom-call | tf_op jit(solution)/shard_map/pallas_call | solution.py:455
  99.5 3.3 %collective-permute-start.27 = (f32[128,512]{1,0:T(8,128)S(1)}, f32[128,512]{1,0:T(8,128)S(1)}, u32[]{:S(2)}, u32[]{:S(2)}) collective-permute-start(f32[128,512]{1,0:T(8,128)S(1)} %get-tuple-element.182), channel_id=1, source_target_pairs={{0,1},{2,3},{3,2},{4,5},{5,4},{6,7},{7,6},{8,9},{10,11},{11,10},{1... | collective-permute-start | bytes 786440 | tf_op jit(solution)/shard_map/ppermute | solution.py:335
  102.8 3.2 %collective-permute-start.25 = (f32[128,512]{1,0:T(8,128)S(1)}, f32[128,512]{1,0:T(8,128)S(1)}, u32[]{:S(2)}, u32[]{:S(2)}) collective-permute-start(f32[128,512]{1,0:T(8,128)S(1)} %get-tuple-element.183), channel_id=1, source_target_pairs={{0,2},{1,3},{2,4},{3,5},{4,6},{5,7},{8,10},{9,11},{10,12},{11,13},... | collective-permute-start | bytes 786440 | tf_op jit(solution)/shard_map/ppermute | solution.py:334
  107.7 4.4 %collective-permute-done.25.refs_11_ = f32[128,512]{1,0:T(8,128)S(1)} collective-permute-done((f32[128,512]{1,0:T(8,128)S(1)}, f32[128,512]{1,0:T(8,128)S(1)}, u32[]{:S(2)}, u32[]{:S(2)}) %collective-permute-start.25) | collective-permute-done | bytes 262176 | tf_op jit(solution)/shard_map/ppermute | solution.py:334
  120.6 4.1 %collective-permute-start.24 = (f32[128,512]{1,0:T(8,128)S(1)}, f32[128,512]{1,0:T(8,128)S(1)}, u32[]{:S(2)}, u32[]{:S(2)}) collective-permute-start(f32[128,512]{1,0:T(8,128)S(1)} %get-tuple-element.181), channel_id=1, source_target_pairs={{0,1},{2,3},{3,2},{4,5},{5,4},{6,7},{7,6},{8,9},{10,11},{11,10},{1... | collective-permute-start | bytes 786440 | tf_op jit(solution)/shard_map/ppermute | solution.py:335
  126.0 5.1 %shard_map.59 = (f32[512,640]{1,0:T(8,128)S(1)}, f32[512,640]{1,0:T(8,128)S(1)}) custom-call(s32[2]{0:T(128)S(1)} %copy-done.36, f32[512,640]{1,0:T(8,128)S(1)} %get-tuple-element.125.top_in_ref, f32[512,512]{1,0:T(8,128)S(1)} %copy-done.38, f32[512,512]{1,0:T(8,128)S(1)} %copy-done.39), custom_call_target="tpu_custom_call" | custom-call | flops 4026531840 | tf_op jit(solution)/shard_map/pallas_call | solution.py:462
  137.7 3.5 %collective-permute-start.33 = (f32[128,512]{1,0:T(8,128)S(1)}, f32[128,512]{1,0:T(8,128)S(1)}, u32[]{:S(2)}, u32[]{:S(2)}) collective-permute-start(f32[128,512]{1,0:T(8,128)S(1)} %get-tuple-element.175), channel_id=1, source_target_pairs={{0,1},{2,3},{3,2},{4,5},{5,4},{6,7},{7,6},{8,9},{10,11},{11,10},{1... | collective-permute-start | bytes 786440 | tf_op jit(solution)/shard_map/ppermute | solution.py:335
  143.8 4.9 %collective-permute-done.33.refs_29_ = f32[128,512]{1,0:T(8,128)S(1)} collective-permute-done((f32[128,512]{1,0:T(8,128)S(1)}, f32[128,512]{1,0:T(8,128)S(1)}, u32[]{:S(2)}, u32[]{:S(2)}) %collective-permute-start.33) | collective-permute-done | bytes 262176 | tf_op jit(solution)/shard_map/ppermute | solution.py:335
  148.7 5.2 %collective-permute-done.32.refs_28_ = f32[128,512]{1,0:T(8,128)S(1)} collective-permute-done((f32[128,512]{1,0:T(8,128)S(1)}, f32[128,512]{1,0:T(8,128)S(1)}, u32[]{:S(2)}, u32[]{:S(2)}) %collective-permute-start.32) | collective-permute-done | bytes 262176 | tf_op jit(solution)/shard_map/ppermute | solution.py:335
  153.9 10.4 %shard_map.61 = f32[2048,640]{1,0:T(8,128)} custom-call(s32[2]{0:T(128)S(1)} %copy-done.36, s32[8,512]{1,0:T(8,128)S(1)} %get-tuple-element.83.table_ref, s32[16]{0:T(128)S(1)} %dynamic-slice_bitcast_fusion.choice_ref, f32[512,640]{1,0:T(8,128)S(1)} %maximum_select_fusion.displaced_ref, f32[512,640]{1,0:T(8,128)S(1)} %get-tuple-element.128.weights_ref, ...), custom_call_target="tpu_custom_call" | custom-call | flops 4026531840 | bytes 14680064 | tf_op jit(solution)/shard_map/pallas_call | solution.py:474
  (186 shorter events, 48.8 us)
Async XLA Ops:
  3.9 15.3 %collective-permute-start.1 = (f32[128,512]{1,0:T(8,128)S(1)}, f32[128,512]{1,0:T(8,128)S(1)}, u32[]{:S(2)}, u32[]{:S(2)}) collective-permute-start(f32[128,512]{1,0:T(8,128)S(1)} %get-tuple-element.171), channel_id=1, source_target_pairs={{0,1},{2,3},{3,2},{4,5},{5,4},{6,7},{7,6},{8,9},{10,11},{11,10},{1... | collective-permute-start | bytes 786440 | tf_op jit(solution)/shard_map/ppermute | solution.py:335
  7.3 11.8 %collective-permute-start = (f32[128,512]{1,0:T(8,128)S(1)}, f32[128,512]{1,0:T(8,128)S(1)}, u32[]{:S(2)}, u32[]{:S(2)}) collective-permute-start(f32[128,512]{1,0:T(8,128)S(1)} %get-tuple-element.172), channel_id=1, source_target_pairs={{0,2},{1,3},{2,4},{3,5},{4,6},{5,7},{8,10},{9,11},{10,12},{11,13},... | collective-permute-start | bytes 786440 | tf_op jit(solution)/shard_map/ppermute | solution.py:334
  10.8 14.5 %collective-permute-start.3 = (f32[128,512]{1,0:T(8,128)S(1)}, f32[128,512]{1,0:T(8,128)S(1)}, u32[]{:S(2)}, u32[]{:S(2)}) collective-permute-start(f32[128,512]{1,0:T(8,128)S(1)} %get-tuple-element.88), channel_id=1, source_target_pairs={{0,1},{2,3},{3,2},{4,5},{5,4},{6,7},{7,6},{8,9},{10,11},{11,10},{1... | collective-permute-start | bytes 786440 | tf_op jit(solution)/shard_map/ppermute | solution.py:335
  13.2 12.1 %collective-permute-start.2 = (f32[128,512]{1,0:T(8,128)S(1)}, f32[128,512]{1,0:T(8,128)}, u32[]{:S(2)}, u32[]{:S(2)}) collective-permute-start(f32[128,512]{1,0:T(8,128)S(1)} %get-tuple-element.87), channel_id=1, source_target_pairs={{0,2},{1,3},{2,4},{3,5},{4,6},{5,7},{8,10},{9,11},{10,12},{11,13},... | collective-permute-start | bytes 786440 | tf_op jit(solution)/shard_map/ppermute | solution.py:334
  25.3 19.9 %collective-permute-start.6 = (f32[512,640]{1,0:T(8,128)S(1)}, f32[512,640]{1,0:T(8,128)S(1)}, u32[]{:S(2)}, u32[]{:S(2)}) collective-permute-start(f32[512,640]{1,0:T(8,128)S(1)} %shard_map.56.held_ref), channel_id=1, source_target_pairs={{0,8},{8,0},{16,24},{24,16},{1,9},{9,1},{17,25},{25,17},{2,10},{10... | collective-permute-start | bytes 3932168 | tf_op jit(solution)/shard_map/ppermute | solution.py:446
  25.6 13.6 %collective-permute-start.15 = (f32[128,512]{1,0:T(8,128)S(1)}, f32[128,512]{1,0:T(8,128)S(1)}, u32[]{:S(2)}, u32[]{:S(2)}) collective-permute-start(f32[128,512]{1,0:T(8,128)S(1)} %get-tuple-element.192), channel_id=1, source_target_pairs={{0,1},{2,3},{3,2},{4,5},{5,4},{6,7},{7,6},{8,9},{10,11},{11,10},{1... | collective-permute-start | bytes 786440 | tf_op jit(solution)/shard_map/ppermute | solution.py:335
  29.1 10.7 %collective-permute-start.14 = (f32[128,512]{1,0:T(8,128)S(1)}, f32[128,512]{1,0:T(8,128)S(1)}, u32[]{:S(2)}, u32[]{:S(2)}) collective-permute-start(f32[128,512]{1,0:T(8,128)S(1)} %get-tuple-element.193), channel_id=1, source_target_pairs={{0,2},{1,3},{2,4},{3,5},{4,6},{5,7},{8,10},{9,11},{10,12},{11,13},... | collective-permute-start | bytes 786440 | tf_op jit(solution)/shard_map/ppermute | solution.py:334
  32.3 12.1 %collective-permute-start.5 = (f32[128,512]{1,0:T(8,128)S(1)}, f32[128,512]{1,0:T(8,128)S(1)}, u32[]{:S(2)}, u32[]{:S(2)}) collective-permute-start(f32[128,512]{1,0:T(8,128)S(1)} %get-tuple-element.198), channel_id=1, source_target_pairs={{0,1},{2,3},{3,2},{4,5},{5,4},{6,7},{7,6},{8,9},{10,11},{11,10},{1... | collective-permute-start | bytes 786440 | tf_op jit(solution)/shard_map/ppermute | solution.py:335
  34.7 10.5 %collective-permute-start.4 = (f32[128,512]{1,0:T(8,128)S(1)}, f32[128,512]{1,0:T(8,128)S(1)}, u32[]{:S(2)}, u32[]{:S(2)}) collective-permute-start(f32[128,512]{1,0:T(8,128)S(1)} %get-tuple-element.199), channel_id=1, source_target_pairs={{0,2},{1,3},{2,4},{3,5},{4,6},{5,7},{8,10},{9,11},{10,12},{11,13},... | collective-permute-start | bytes 786440 | tf_op jit(solution)/shard_map/ppermute | solution.py:334
  39.9 12.4 %collective-permute-start.17 = (f32[128,512]{1,0:T(8,128)S(1)}, f32[128,512]{1,0:T(8,128)S(1)}, u32[]{:S(2)}, u32[]{:S(2)}) collective-permute-start(f32[128,512]{1,0:T(8,128)S(1)} %get-tuple-element.190), channel_id=1, source_target_pairs={{0,1},{2,3},{3,2},{4,5},{5,4},{6,7},{7,6},{8,9},{10,11},{11,10},{1... | collective-permute-start | bytes 786440 | tf_op jit(solution)/shard_map/ppermute | solution.py:335
  42.1 10.3 %collective-permute-start.16 = (f32[128,512]{1,0:T(8,128)S(1)}, f32[128,512]{1,0:T(8,128)S(1)}, u32[]{:S(2)}, u32[]{:S(2)}) collective-permute-start(f32[128,512]{1,0:T(8,128)S(1)} %get-tuple-element.191), channel_id=1, source_target_pairs={{0,2},{1,3},{2,4},{3,5},{4,6},{5,7},{8,10},{9,11},{10,12},{11,13},... | collective-permute-start | bytes 786440 | tf_op jit(solution)/shard_map/ppermute | solution.py:334
  45.9 9.4 %collective-permute-start.8 = (f32[128,512]{1,0:T(8,128)S(1)}, f32[128,512]{1,0:T(8,128)S(1)}, u32[]{:S(2)}, u32[]{:S(2)}) collective-permute-start(f32[128,512]{1,0:T(8,128)S(1)} %get-tuple-element.196), channel_id=1, source_target_pairs={{0,1},{2,3},{3,2},{4,5},{5,4},{6,7},{7,6},{8,9},{10,11},{11,10},{1... | collective-permute-start | bytes 786440 | tf_op jit(solution)/shard_map/ppermute | solution.py:335
  49.0 9.0 %collective-permute-start.7 = (f32[128,512]{1,0:T(8,128)S(1)}, f32[128,512]{1,0:T(8,128)S(1)}, u32[]{:S(2)}, u32[]{:S(2)}) collective-permute-start(f32[128,512]{1,0:T(8,128)S(1)} %get-tuple-element.197), channel_id=1, source_target_pairs={{0,2},{1,3},{2,4},{3,5},{4,6},{5,7},{8,10},{9,11},{10,12},{11,13},... | collective-permute-start | bytes 786440 | tf_op jit(solution)/shard_map/ppermute | solution.py:334
  53.3 17.5 %collective-permute-start.11 = (f32[256,640]{1,0:T(8,128)S(1)}, f32[256,640]{1,0:T(8,128)S(1)}, u32[]{:S(2)}, u32[]{:S(2)}) collective-permute-start(f32[256,640]{1,0:T(8,128)S(1)} %get-tuple-element.101), channel_id=1, source_target_pairs={{0,16},{8,24},{16,0},{24,8},{1,17},{9,25},{17,1},{25,9},{2,18},{10... | collective-permute-start | bytes 1966088 | tf_op jit(solution)/shard_map/ppermute | solution.py:450
  58.1 12.2 %collective-permute-start.10 = (f32[128,512]{1,0:T(8,128)S(1)}, f32[128,512]{1,0:T(8,128)S(1)}, u32[]{:S(2)}, u32[]{:S(2)}) collective-permute-start(f32[128,512]{1,0:T(8,128)S(1)} %get-tuple-element.194), channel_id=1, source_target_pairs={{0,1},{2,3},{3,2},{4,5},{5,4},{6,7},{7,6},{8,9},{10,11},{11,10},{1... | collective-permute-start | bytes 786440 | tf_op jit(solution)/shard_map/ppermute | solution.py:335
  61.2 9.6 %collective-permute-start.9 = (f32[128,512]{1,0:T(8,128)S(1)}, f32[128,512]{1,0:T(8,128)S(1)}, u32[]{:S(2)}, u32[]{:S(2)}) collective-permute-start(f32[128,512]{1,0:T(8,128)S(1)} %get-tuple-element.195), channel_id=1, source_target_pairs={{0,2},{1,3},{2,4},{3,5},{4,6},{5,7},{8,10},{9,11},{10,12},{11,13},... | collective-permute-start | bytes 786440 | tf_op jit(solution)/shard_map/ppermute | solution.py:334
  70.7 18.8 %collective-permute-start.22 = (f32[256,640]{1,0:T(8,128)S(1)}, f32[256,640]{1,0:T(8,128)}, u32[]{:S(2)}, u32[]{:S(2)}) collective-permute-start(f32[256,640]{1,0:T(8,128)S(1)} %collective-permute-done.11.refs_0_), channel_id=1, source_target_pairs={{0,8},{8,0},{16,24},{24,16},{1,9},{9,1},{17,25},{25,17},{2,10},{10... | collective-permute-start | bytes 1966088 | tf_op jit(solution)/shard_map/ppermute | solution.py:452
  77.4 12.0 %collective-permute-start.21 = (f32[128,512]{1,0:T(8,128)}, f32[128,512]{1,0:T(8,128)}, u32[]{:S(2)}, u32[]{:S(2)}) collective-permute-start(f32[128,512]{1,0:T(8,128)} %get-tuple-element.184), channel_id=1, source_target_pairs={{0,2},{1,3},{2,4},{3,5},{4,6},{5,7},{8,10},{9,11},{10,12},{11,13},... | collective-permute-start | bytes 786440 | tf_op jit(solution)/shard_map/ppermute | solution.py:334
  80.8 8.7 %collective-permute-start.20 = (f32[128,512]{1,0:T(8,128)}, f32[128,512]{1,0:T(8,128)}, u32[]{:S(2)}, u32[]{:S(2)}) collective-permute-start(f32[128,512]{1,0:T(8,128)} %get-tuple-element.185), channel_id=1, source_target_pairs={{0,1},{2,3},{3,2},{4,5},{5,4},{6,7},{7,6},{8,9},{10,11},{11,10},{1... | collective-permute-start | bytes 786440 | tf_op jit(solution)/shard_map/ppermute | solution.py:335
  84.0 12.5 %collective-permute-start.12 = (f32[128,512]{1,0:T(8,128)}, f32[128,512]{1,0:T(8,128)S(1)}, u32[]{:S(2)}, u32[]{:S(2)}) collective-permute-start(f32[128,512]{1,0:T(8,128)} %get-tuple-element.186), channel_id=1, source_target_pairs={{0,2},{1,3},{2,4},{3,5},{4,6},{5,7},{8,10},{9,11},{10,12},{11,13},... | collective-permute-start | bytes 786440 | tf_op jit(solution)/shard_map/ppermute | solution.py:334
  86.9 9.6 %collective-permute-start.13 = (f32[128,512]{1,0:T(8,128)}, f32[128,512]{1,0:T(8,128)S(1)}, u32[]{:S(2)}, u32[]{:S(2)}) collective-permute-start(f32[128,512]{1,0:T(8,128)} %get-tuple-element.187), channel_id=1, source_target_pairs={{0,1},{2,3},{3,2},{4,5},{5,4},{6,7},{7,6},{8,9},{10,11},{11,10},{1... | collective-permute-start | bytes 786440 | tf_op jit(solution)/shard_map/ppermute | solution.py:335
  98.6 13.5 %collective-permute-start.28 = (f32[512,512]{1,0:T(8,128)S(1)}, f32[512,512]{1,0:T(8,128)S(1)}, u32[]{:S(2)}, u32[]{:S(2)}) collective-permute-start(f32[512,512]{1,0:T(8,128)S(1)} %shard_map.60), channel_id=1, source_target_pairs={{0,8},{1,9},{2,10},{3,11},{4,12},{5,13},{6,14},{7,15}} | collective-permute-start | bytes 3145736 | tf_op jit(solution)/shard_map/ppermute | solution.py:415
  102.8 9.4 %collective-permute-start.25 = (f32[128,512]{1,0:T(8,128)S(1)}, f32[128,512]{1,0:T(8,128)S(1)}, u32[]{:S(2)}, u32[]{:S(2)}) collective-permute-start(f32[128,512]{1,0:T(8,128)S(1)} %get-tuple-element.183), channel_id=1, source_target_pairs={{0,2},{1,3},{2,4},{3,5},{4,6},{5,7},{8,10},{9,11},{10,12},{11,13},... | collective-permute-start | bytes 786440 | tf_op jit(solution)/shard_map/ppermute | solution.py:334
  114.7 16.4 %collective-permute-start.31 = (f32[128,512]{1,0:T(8,128)S(1)}, f32[128,512]{1,0:T(8,128)S(1)}, u32[]{:S(2)}, u32[]{:S(2)}) collective-permute-start(f32[128,512]{1,0:T(8,128)S(1)} %get-tuple-element.178), channel_id=1, source_target_pairs={{0,1},{2,3},{3,2},{4,5},{5,4},{6,7},{7,6},{8,9},{10,11},{11,10},{1... | collective-permute-start | bytes 786440 | tf_op jit(solution)/shard_map/ppermute | solution.py:335
  116.6 14.5 %collective-permute-start.29 = (f32[128,512]{1,0:T(8,128)S(1)}, f32[128,512]{1,0:T(8,128)S(1)}, u32[]{:S(2)}, u32[]{:S(2)}) collective-permute-start(f32[128,512]{1,0:T(8,128)S(1)} %get-tuple-element.179), channel_id=1, source_target_pairs={{0,2},{1,3},{2,4},{3,5},{4,6},{5,7},{8,10},{9,11},{10,12},{11,13},... | collective-permute-start | bytes 786440 | tf_op jit(solution)/shard_map/ppermute | solution.py:334
  118.7 12.5 %collective-permute-start.23 = (f32[128,512]{1,0:T(8,128)S(1)}, f32[128,512]{1,0:T(8,128)S(1)}, u32[]{:S(2)}, u32[]{:S(2)}) collective-permute-start(f32[128,512]{1,0:T(8,128)S(1)} %get-tuple-element.180), channel_id=1, source_target_pairs={{0,2},{1,3},{2,4},{3,5},{4,6},{5,7},{8,10},{9,11},{10,12},{11,13},... | collective-permute-start | bytes 786440 | tf_op jit(solution)/shard_map/ppermute | solution.py:334
  120.6 10.5 %collective-permute-start.24 = (f32[128,512]{1,0:T(8,128)S(1)}, f32[128,512]{1,0:T(8,128)S(1)}, u32[]{:S(2)}, u32[]{:S(2)}) collective-permute-start(f32[128,512]{1,0:T(8,128)S(1)} %get-tuple-element.181), channel_id=1, source_target_pairs={{0,1},{2,3},{3,2},{4,5},{5,4},{6,7},{7,6},{8,9},{10,11},{11,10},{1... | collective-permute-start | bytes 786440 | tf_op jit(solution)/shard_map/ppermute | solution.py:335
  124.7 11.1 %collective-permute-start.34 = (f32[256,512]{1,0:T(8,128)S(1)}, f32[256,512]{1,0:T(8,128)S(1)}, u32[]{:S(2)}, u32[]{:S(2)}) collective-permute-start(f32[256,512]{1,0:T(8,128)S(1)} %slice_select_fusion), channel_id=1, source_target_pairs={{0,16},{8,24},{1,17},{9,25},{2,18},{10,26},{3,19},{11,27},{4,20},{... | collective-permute-start | bytes 1572872 | tf_op jit(solution)/shard_map/ppermute | solution.py:420
  131.3 9.9 %collective-permute-start.26 = (f32[128,512]{1,0:T(8,128)S(1)}, f32[128,512]{1,0:T(8,128)S(1)}, u32[]{:S(2)}, u32[]{:S(2)}) collective-permute-start(f32[128,512]{1,0:T(8,128)S(1)} %get-tuple-element.176), channel_id=1, source_target_pairs={{0,2},{1,3},{2,4},{3,5},{4,6},{5,7},{8,10},{9,11},{10,12},{11,13},... | collective-permute-start | bytes 786440 | tf_op jit(solution)/shard_map/ppermute | solution.py:334
  135.7 18.1 %collective-permute-start.35 = (f32[256,512]{1,0:T(8,128)S(1)}, f32[256,512]{1,0:T(8,128)S(1)}, u32[]{:S(2)}, u32[]{:S(2)}) collective-permute-start(f32[256,512]{1,0:T(8,128)S(1)} %collective-permute-done.34.refs_31_), channel_id=1, source_target_pairs={{16,24},{24,16},{17,25},{25,17},{18,26},{26,18},{19,27},{27,19},{2... | collective-permute-start | bytes 1572872 | tf_op jit(solution)/shard_map/ppermute | solution.py:421
  137.7 11.0 %collective-permute-start.33 = (f32[128,512]{1,0:T(8,128)S(1)}, f32[128,512]{1,0:T(8,128)S(1)}, u32[]{:S(2)}, u32[]{:S(2)}) collective-permute-start(f32[128,512]{1,0:T(8,128)S(1)} %get-tuple-element.175), channel_id=1, source_target_pairs={{0,1},{2,3},{3,2},{4,5},{5,4},{6,7},{7,6},{8,9},{10,11},{11,10},{1... | collective-permute-start | bytes 786440 | tf_op jit(solution)/shard_map/ppermute | solution.py:335
  141.5 12.4 %collective-permute-start.32 = (f32[128,512]{1,0:T(8,128)S(1)}, f32[128,512]{1,0:T(8,128)S(1)}, u32[]{:S(2)}, u32[]{:S(2)}) collective-permute-start(f32[128,512]{1,0:T(8,128)S(1)} %broadcast_select_fusion.4), channel_id=1, source_target_pairs={{0,1},{2,3},{3,2},{4,5},{5,4},{6,7},{7,6},{8,9},{10,11},{11,10},{1... | collective-permute-start | bytes 786440 | tf_op jit(solution)/shard_map/ppermute | solution.py:335
  (64 other events, 451.8 us)

commit v15 on v14

--- a/solution.py
+++ b/solution.py
@@ -11,7 +11,7 @@
 SMEM = pl.BlockSpec(memory_space=pltpu.SMEM)
 ANY = pl.BlockSpec(memory_space=pl.ANY)
 LANES = 128
-PICK, FROM, ROW, COUNT, TOP = 0, 1, 2, 3, 4
+PICK, FROM, ROW, COUNT, TOP, EARLY = 0, 1, 2, 3, 4, 5
 
 
 def call(kernel, out, ins, outs, scratch=(), vmem=16 << 20, flops=0, moved=0):
@@ -82,6 +82,9 @@
     table_ref[PICK : PICK + 1, :] = pick
     table_ref[FROM : FROM + 1, :] = listed_from.astype(jnp.int32)
     table_ref[ROW : ROW + 1, :] = listed_row.astype(jnp.int32)
+    near = jnp.where(pivots_ref[...] - start < row_dev // 2, moved_row, 0.0)
+    early = jnp.sum(near, axis=1, keepdims=True)
+    table_ref[EARLY : EARLY + 1, :] = jnp.broadcast_to(early.astype(jnp.int32), (1, nb))
     table_ref[TOP : TOP + 1, :] = listed_top.astype(jnp.int32)
     table_ref[COUNT : COUNT + 1, :] = jnp.broadcast_to(
         count.astype(jnp.int32), (1, nb)
@@ -94,9 +97,9 @@
 
     @pl.loop(0, nb, step=8)
     def _(base):
-        for k in range(8):
-            j = base + k
-            out_ref[pl.ds(j, 1), :] = matrix_ref[pl.ds(table_ref[PICK, j], 1), :]
+        rows = [matrix_ref[pl.ds(table_ref[PICK, base + k], 1), :] for k in range(8)]
+        for k, row in enumerate(rows):
+            out_ref[pl.ds(base + k, 1), :] = row
 
 
 def merge_kernel(where_ref, owner_ref, held_ref, *refs, log, halves):
@@ -165,7 +168,7 @@
             for b in sorted({arrival(p, i, h, n_cols, parts) for p in range(1, n_cols)}):
                 @pl.when(choice_ref[2 * i + h] == b)
                 def _():
-                    pltpu.make_async_copy(bufs[b], place(i, h), sem).start()
+                    pltpu.make_async_copy(bufs[b], place(i, h), sem(i)).start()
 
 
 def old_top_kernel(where_ref, choice_ref, matrix_ref, *refs, used, n_cols, parts, pairs):
@@ -187,7 +190,7 @@
             fetch(
                 choice_ref, bufs,
                 lambda i, h: top_ref.at[pl.ds((2 * i + h) * chunk, chunk), :],
-                sem, n_cols, parts, pairs,
+                lambda i: sem, n_cols, parts, pairs,
             )
 
         from_matrix.wait()
@@ -208,19 +211,28 @@
     row = where_ref[0]
     first_row, first_col = row == 0, where_ref[1] == 0
 
-    load = pltpu.make_async_copy(matrix_ref, mat, mat_sem)
-    load.start()
-    whole_panel = pltpu.make_async_copy(matrix_ref.at[:, pl.ds(0, nb)], pan, in_sem)
+    middle = rows // 2
+    sides = [pl.ds(0, middle), pl.ds(middle, middle)]
+    loads = [
+        pltpu.make_async_copy(matrix_ref.at[side, :], mat.at[side, :], mat_sem.at[k])
+        for k, side in enumerate(sides)
+    ]
+    panels = [
+        pltpu.make_async_copy(matrix_ref.at[side, pl.ds(0, nb)], pan.at[side, :], in_sem.at[k])
+        for k, side in enumerate(sides)
+    ]
+    loads[0].start()
 
     @pl.when(first_col)
     def _():
-        whole_panel.start()
+        for panel in panels:
+            panel.start()
 
     @pl.when(jnp.logical_not(first_col))
     def _():
         fetch(
             choice_ref, bufs, lambda i, h: pan.at[pl.ds((2 * i + h) * chunk, chunk), :],
-            in_sem, n_cols, parts, parts,
+            lambda i: in_sem.at[2 * i // parts], n_cols, parts, parts,
         )
 
     @pl.when(row == 1)
@@ -235,17 +247,18 @@
                     at = half * (part ^ odd)
                     pltpu.make_async_copy(ref, low.at[pl.ds(at, half), :], low_sem).start()
 
+    loads[1].start()
     w = weights_ref[...]
     w_hi[...] = w.astype(jnp.bfloat16)
     w_lo[...] = (w - w_hi[...].astype(jnp.float32)).astype(jnp.bfloat16)
 
-    whole_panel.wait()
-    load.wait()
-    count = table_ref[COUNT, 0]
-
-    def swap(from_mat, from_pan):
+    @pl.when(jnp.logical_not(first_row))
+    def _():
+        pltpu.make_async_copy(tops[0], low, low_sem).wait()
+
+    def swap(from_mat, from_pan, begin, end):
         def body(turn, _):
-            at = [jnp.minimum(4 * turn + k, count - 1) for k in range(4)]
+            at = [jnp.minimum(begin + 4 * turn + k, end - 1) for k in range(4)]
             mats = [from_mat[pl.ds(table_ref[FROM, k], 1), :] for k in at]
             pans = [from_pan[pl.ds(table_ref[TOP, k], 1), :] for k in at]
             for k, row_mat, row_pan in zip(at, mats, pans):
@@ -253,24 +266,29 @@
                 pan[pl.ds(table_ref[ROW, k], 1), :] = row_pan
             return 0
 
-        lax.fori_loop(0, (count + 3) // 4, body, 0)
-
-    @pl.when(first_row)
-    def _():
-        swap(mat, pan)
-
-    @pl.when(jnp.logical_not(first_row))
-    def _():
-        pltpu.make_async_copy(tops[0], low, low_sem).wait()
-        swap(displaced_ref, low)
-
-    @pl.when(first_col)
-    def _():
-        mat[:, :nb] = jnp.zeros((rows, nb), jnp.float32)
+        lax.fori_loop(0, (end - begin + 3) // 4, body, 0)
 
     copies = []
     for b in range(rows // block):
         span = pl.ds(b * block, block)
+        if b * block % middle == 0:
+            k = b * block // middle
+            panels[k].wait()
+            loads[k].wait()
+            begin = table_ref[EARLY, 0] if k else 0
+            end = table_ref[COUNT if k else EARLY, 0]
+
+            @pl.when(first_row)
+            def _():
+                swap(mat, pan, begin, end)
+
+            @pl.when(jnp.logical_not(first_row))
+            def _():
+                swap(displaced_ref, low, begin, end)
+
+            @pl.when(first_col)
+            def _():
+                mat[sides[k], :nb] = jnp.zeros((middle, nb), jnp.float32)
 
         def update():
             p = pan[span, :]
@@ -486,7 +504,11 @@
             pltpu.VMEM((nb, cols), jnp.bfloat16),
             pltpu.VMEM((nb, cols), jnp.bfloat16),
             pltpu.VMEM((row_dev, cols), f32),
-        ] + [pltpu.SemaphoreType.DMA] * 4,
+            pltpu.SemaphoreType.DMA((2,)),
+            pltpu.SemaphoreType.DMA,
+            pltpu.SemaphoreType.DMA((2,)),
+            pltpu.SemaphoreType.DMA,
+        ],
         vmem=30 << 20,
         flops=2 * row_dev * nb * cols * 3,
         moved=4 * row_dev * (2 * cols + nb),

time: 166 us -> 166 us (level)
  no operation moved by 1% of the time
where the time goes in v15:
time: 166 us; the launch traced here: 165 us
  starting transfers between devices  90.1 us (54%)
  waiting for transfers between devices  27.7 us (17%)
  Pallas kernels  24.6 us (15%)
  local copies, waits for them, and re-layouts  13.8 us (8%)
  other arithmetic  7.25 us (4%)
    ppermute x16, starting transfers between devices, spread(): cross.append(lax.ppermute(aside, 'pcol', across))  44.2 us
    ppermute x14, starting transfers between devices, spread(): chain.append(lax.ppermute(ahead, 'pcol', along))  41.3 us
    ppermute x16, waiting for transfers between devices, spread(): cross.append(lax.ppermute(aside, 'pcol', across))  16.1 us
    ppermute x14, waiting for transfers between devices, spread(): chain.append(lax.ppermute(ahead, 'pcol', along))  11 us
    pallas_call x1, Pallas kernels, local(): call(functools.partial(final_kernel, n_bufs=len(bufs), n_tops=len(tops),...  10.8 us
    unnamed x120, local copies, waits for them, and re-layouts  9.3 us
    pallas_call x1, Pallas kernels, exchange_rider(): call(factor_kernel, (slot, slot), [SMEM, VMEM, VMEM, VMEM], (VMEM, VMEM),...  5.09 us
    slice x1, local copies, waits for them, and re-layouts, local(): lax.slice(matrix, (k * chunk, 0), ((k + 1) * chunk, nb))  3.84 us
  transfers between devices with their start and end apart: 36, of which 14 were waited for; matrix products, arithmetic and copies ran while one was open for 4% of the time, Pallas kernels for 8%

profile of v15, /device:TPU:10, one launch (start us, length us, event | category | flops | bytes accessed | tf_op | source)
XLA Modules:
  0.0 164.8 jit_solution(14128099988456203747)
XLA Ops:
  0.0 3.8 %fusion = (f32[128,512]{1,0:T(8,128)}, f32[128,512]{1,0:T(8,128)}, f32[128,512]{1,0:T(8,128)}, f32[128,512]{1,0:T(8,128)}, f32[128,512]{1,0:T(8,128)}, /*index=5...) fusion(f32[2048,640]{1,0:T(8,128)} %matrix_ref.5), kind=kLoop, calls=%fused_computation.33 | loop fusion | bytes 8388608 | tf_op jit(solution)/shard_map/slice | solution.py:387
  3.9 3.4 %collective-permute-start.1 = (f32[128,512]{1,0:T(8,128)S(1)}, f32[128,512]{1,0:T(8,128)S(1)}, u32[]{:S(2)}, u32[]{:S(2)}) collective-permute-start(f32[128,512]{1,0:T(8,128)S(1)} %get-tuple-element.171), channel_id=1, source_target_pairs={{0,1},{2,3},{3,2},{4,5},{5,4},{6,7},{7,6},{8,9},{10,11},{11,10},{1... | collective-permute-start | bytes 786440 | tf_op jit(solution)/shard_map/ppermute | solution.py:353
  7.3 3.5 %collective-permute-start = (f32[128,512]{1,0:T(8,128)S(1)}, f32[128,512]{1,0:T(8,128)S(1)}, u32[]{:S(2)}, u32[]{:S(2)}) collective-permute-start(f32[128,512]{1,0:T(8,128)S(1)} %get-tuple-element.172), channel_id=1, source_target_pairs={{0,2},{1,3},{2,4},{3,5},{4,6},{5,7},{8,10},{9,11},{10,12},{11,13},... | collective-permute-start | bytes 786440 | tf_op jit(solution)/shard_map/ppermute | solution.py:352
  10.8 2.4 %collective-permute-start.3 = (f32[128,512]{1,0:T(8,128)S(1)}, f32[128,512]{1,0:T(8,128)S(1)}, u32[]{:S(2)}, u32[]{:S(2)}) collective-permute-start(f32[128,512]{1,0:T(8,128)S(1)} %get-tuple-element.88), channel_id=1, source_target_pairs={{0,1},{2,3},{3,2},{4,5},{5,4},{6,7},{7,6},{8,9},{10,11},{11,10},{1... | collective-permute-start | bytes 786440 | tf_op jit(solution)/shard_map/ppermute | solution.py:353
  13.2 3.5 %collective-permute-start.2 = (f32[128,512]{1,0:T(8,128)S(1)}, f32[128,512]{1,0:T(8,128)}, u32[]{:S(2)}, u32[]{:S(2)}) collective-permute-start(f32[128,512]{1,0:T(8,128)S(1)} %get-tuple-element.87), channel_id=1, source_target_pairs={{0,2},{1,3},{2,4},{3,5},{4,6},{5,7},{8,10},{9,11},{10,12},{11,13},... | collective-permute-start | bytes 786440 | tf_op jit(solution)/shard_map/ppermute | solution.py:352
  19.1 2.6 %copy-done = f32[2048,640]{1,0:T(8,128)S(1)} copy-done((f32[2048,640]{1,0:T(8,128)S(1)}, f32[2048,640]{1,0:T(8,128)}, u32[]{:S(2)}) %copy-start) | copy-done | bytes 5242904
  21.7 3.5 %shard_map.56.held_ref = f32[512,640]{1,0:T(8,128)S(1)} custom-call(s32[8,512]{1,0:T(8,128)S(1)} %get-tuple-element.83.table_ref, f32[2048,640]{1,0:T(8,128)S(1)} %copy-done), custom_call_target="tpu_custom_call" | custom-call | tf_op jit(solution)/shard_map/pallas_call | solution.py:455
  25.5 3.6 %collective-permute-start.15 = (f32[128,512]{1,0:T(8,128)S(1)}, f32[128,512]{1,0:T(8,128)S(1)}, u32[]{:S(2)}, u32[]{:S(2)}) collective-permute-start(f32[128,512]{1,0:T(8,128)S(1)} %get-tuple-element.192), channel_id=1, source_target_pairs={{0,1},{2,3},{3,2},{4,5},{5,4},{6,7},{7,6},{8,9},{10,11},{11,10},{1... | collective-permute-start | bytes 786440 | tf_op jit(solution)/shard_map/ppermute | solution.py:353
  32.3 2.4 %collective-permute-start.5 = (f32[128,512]{1,0:T(8,128)S(1)}, f32[128,512]{1,0:T(8,128)S(1)}, u32[]{:S(2)}, u32[]{:S(2)}) collective-permute-start(f32[128,512]{1,0:T(8,128)S(1)} %get-tuple-element.198), channel_id=1, source_target_pairs={{0,1},{2,3},{3,2},{4,5},{5,4},{6,7},{7,6},{8,9},{10,11},{11,10},{1... | collective-permute-start | bytes 786440 | tf_op jit(solution)/shard_map/ppermute | solution.py:353
  34.7 4.5 %collective-permute-start.4 = (f32[128,512]{1,0:T(8,128)S(1)}, f32[128,512]{1,0:T(8,128)S(1)}, u32[]{:S(2)}, u32[]{:S(2)}) collective-permute-start(f32[128,512]{1,0:T(8,128)S(1)} %get-tuple-element.199), channel_id=1, source_target_pairs={{0,2},{1,3},{2,4},{3,5},{4,6},{5,7},{8,10},{9,11},{10,12},{11,13},... | collective-permute-start | bytes 786440 | tf_op jit(solution)/shard_map/ppermute | solution.py:352
  42.1 2.3 %collective-permute-start.16 = (f32[128,512]{1,0:T(8,128)S(1)}, f32[128,512]{1,0:T(8,128)S(1)}, u32[]{:S(2)}, u32[]{:S(2)}) collective-permute-start(f32[128,512]{1,0:T(8,128)S(1)} %get-tuple-element.191), channel_id=1, source_target_pairs={{0,2},{1,3},{2,4},{3,5},{4,6},{5,7},{8,10},{9,11},{10,12},{11,13},... | collective-permute-start | bytes 786440 | tf_op jit(solution)/shard_map/ppermute | solution.py:352
  45.9 3.1 %collective-permute-start.8 = (f32[128,512]{1,0:T(8,128)S(1)}, f32[128,512]{1,0:T(8,128)S(1)}, u32[]{:S(2)}, u32[]{:S(2)}) collective-permute-start(f32[128,512]{1,0:T(8,128)S(1)} %get-tuple-element.196), channel_id=1, source_target_pairs={{0,1},{2,3},{3,2},{4,5},{5,4},{6,7},{7,6},{8,9},{10,11},{11,10},{1... | collective-permute-start | bytes 786440 | tf_op jit(solution)/shard_map/ppermute | solution.py:353
  49.0 3.3 %collective-permute-start.7 = (f32[128,512]{1,0:T(8,128)S(1)}, f32[128,512]{1,0:T(8,128)S(1)}, u32[]{:S(2)}, u32[]{:S(2)}) collective-permute-start(f32[128,512]{1,0:T(8,128)S(1)} %get-tuple-element.197), channel_id=1, source_target_pairs={{0,2},{1,3},{2,4},{3,5},{4,6},{5,7},{8,10},{9,11},{10,12},{11,13},... | collective-permute-start | bytes 786440 | tf_op jit(solution)/shard_map/ppermute | solution.py:352
  55.3 2.7 %collective-permute-done.7.refs_5_ = f32[128,512]{1,0:T(8,128)S(1)} collective-permute-done((f32[128,512]{1,0:T(8,128)S(1)}, f32[128,512]{1,0:T(8,128)S(1)}, u32[]{:S(2)}, u32[]{:S(2)}) %collective-permute-start.7) | collective-permute-done | bytes 262176 | tf_op jit(solution)/shard_map/ppermute | solution.py:352
  58.1 3.0 %collective-permute-start.10 = (f32[128,512]{1,0:T(8,128)S(1)}, f32[128,512]{1,0:T(8,128)S(1)}, u32[]{:S(2)}, u32[]{:S(2)}) collective-permute-start(f32[128,512]{1,0:T(8,128)S(1)} %get-tuple-element.194), channel_id=1, source_target_pairs={{0,1},{2,3},{3,2},{4,5},{5,4},{6,7},{7,6},{8,9},{10,11},{11,10},{1... | collective-permute-start | bytes 786440 | tf_op jit(solution)/shard_map/ppermute | solution.py:353
  61.1 3.5 %collective-permute-start.9 = (f32[128,512]{1,0:T(8,128)S(1)}, f32[128,512]{1,0:T(8,128)S(1)}, u32[]{:S(2)}, u32[]{:S(2)}) collective-permute-start(f32[128,512]{1,0:T(8,128)S(1)} %get-tuple-element.195), channel_id=1, source_target_pairs={{0,2},{1,3},{2,4},{3,5},{4,6},{5,7},{8,10},{9,11},{10,12},{11,13},... | collective-permute-start | bytes 786440 | tf_op jit(solution)/shard_map/ppermute | solution.py:352
  66.9 3.3 %collective-permute-start.18 = (f32[128,512]{1,0:T(8,128)S(1)}, f32[128,512]{1,0:T(8,128)S(1)}, u32[]{:S(2)}, u32[]{:S(2)}) collective-permute-start(f32[128,512]{1,0:T(8,128)S(1)} %get-tuple-element.189), channel_id=1, source_target_pairs={{0,2},{1,3},{2,4},{3,5},{4,6},{5,7},{8,10},{9,11},{10,12},{11,13},... | collective-permute-start | bytes 786440 | tf_op jit(solution)/shard_map/ppermute | solution.py:352
  70.7 2.4 %collective-permute-done.19.refs_14_.refs_20_ = f32[128,512]{1,0:T(8,128)S(1)} collective-permute-done((f32[128,512]{1,0:T(8,128)S(1)}, f32[128,512]{1,0:T(8,128)S(1)}, u32[]{:S(2)}, u32[]{:S(2)}) %collective-permute-start.19) | collective-permute-done | bytes 262176 | tf_op jit(solution)/shard_map/ppermute | solution.py:353
  77.4 3.3 %collective-permute-start.21 = (f32[128,512]{1,0:T(8,128)}, f32[128,512]{1,0:T(8,128)}, u32[]{:S(2)}, u32[]{:S(2)}) collective-permute-start(f32[128,512]{1,0:T(8,128)} %get-tuple-element.184), channel_id=1, source_target_pairs={{0,2},{1,3},{2,4},{3,5},{4,6},{5,7},{8,10},{9,11},{10,12},{11,13},... | collective-permute-start | bytes 786440 | tf_op jit(solution)/shard_map/ppermute | solution.py:352
  80.8 2.5 %collective-permute-start.20 = (f32[128,512]{1,0:T(8,128)}, f32[128,512]{1,0:T(8,128)}, u32[]{:S(2)}, u32[]{:S(2)}) collective-permute-start(f32[128,512]{1,0:T(8,128)} %get-tuple-element.185), channel_id=1, source_target_pairs={{0,1},{2,3},{3,2},{4,5},{5,4},{6,7},{7,6},{8,9},{10,11},{11,10},{1... | collective-permute-start | bytes 786440 | tf_op jit(solution)/shard_map/ppermute | solution.py:353
  84.0 2.9 %collective-permute-start.12 = (f32[128,512]{1,0:T(8,128)}, f32[128,512]{1,0:T(8,128)S(1)}, u32[]{:S(2)}, u32[]{:S(2)}) collective-permute-start(f32[128,512]{1,0:T(8,128)} %get-tuple-element.186), channel_id=1, source_target_pairs={{0,2},{1,3},{2,4},{3,5},{4,6},{5,7},{8,10},{9,11},{10,12},{11,13},... | collective-permute-start | bytes 786440 | tf_op jit(solution)/shard_map/ppermute | solution.py:352
  86.9 2.5 %collective-permute-start.13 = (f32[128,512]{1,0:T(8,128)}, f32[128,512]{1,0:T(8,128)S(1)}, u32[]{:S(2)}, u32[]{:S(2)}) collective-permute-start(f32[128,512]{1,0:T(8,128)} %get-tuple-element.187), channel_id=1, source_target_pairs={{0,1},{2,3},{3,2},{4,5},{5,4},{6,7},{7,6},{8,9},{10,11},{11,10},{1... | collective-permute-start | bytes 786440 | tf_op jit(solution)/shard_map/ppermute | solution.py:353
  92.4 2.3 %shard_map.58 = (f32[512,640]{1,0:T(8,128)S(1)}, f32[256,640]{1,0:T(8,128)}) custom-call(s32[2]{0:T(128)S(1)} %copy-done.35, s32[512,128]{1,0:T(8,128)S(1)} %copy-done.33, f32[512,640]{1,0:T(8,128)S(1)} %copy-done.30, f32[256,640]{1,0:T(8,128)S(1)} %collective-permute-done.11.refs_0_, f32[256,640]{1,0:T(8,128)} %collective-permute-done.22.refs_1_), custom_call_target="tpu_custom_call" | custom-call | tf_op jit(solution)/shard_map/pallas_call | solution.py:473
  99.4 3.3 %collective-permute-start.27 = (f32[128,512]{1,0:T(8,128)S(1)}, f32[128,512]{1,0:T(8,128)S(1)}, u32[]{:S(2)}, u32[]{:S(2)}) collective-permute-start(f32[128,512]{1,0:T(8,128)S(1)} %get-tuple-element.182), channel_id=1, source_target_pairs={{0,1},{2,3},{3,2},{4,5},{5,4},{6,7},{7,6},{8,9},{10,11},{11,10},{1... | collective-permute-start | bytes 786440 | tf_op jit(solution)/shard_map/ppermute | solution.py:353
  102.7 3.2 %collective-permute-start.25 = (f32[128,512]{1,0:T(8,128)S(1)}, f32[128,512]{1,0:T(8,128)S(1)}, u32[]{:S(2)}, u32[]{:S(2)}) collective-permute-start(f32[128,512]{1,0:T(8,128)S(1)} %get-tuple-element.183), channel_id=1, source_target_pairs={{0,2},{1,3},{2,4},{3,5},{4,6},{5,7},{8,10},{9,11},{10,12},{11,13},... | collective-permute-start | bytes 786440 | tf_op jit(solution)/shard_map/ppermute | solution.py:352
  107.7 4.4 %collective-permute-done.25.refs_11_ = f32[128,512]{1,0:T(8,128)S(1)} collective-permute-done((f32[128,512]{1,0:T(8,128)S(1)}, f32[128,512]{1,0:T(8,128)S(1)}, u32[]{:S(2)}, u32[]{:S(2)}) %collective-permute-start.25) | collective-permute-done | bytes 262176 | tf_op jit(solution)/shard_map/ppermute | solution.py:352
  120.6 4.1 %collective-permute-start.24 = (f32[128,512]{1,0:T(8,128)S(1)}, f32[128,512]{1,0:T(8,128)S(1)}, u32[]{:S(2)}, u32[]{:S(2)}) collective-permute-start(f32[128,512]{1,0:T(8,128)S(1)} %get-tuple-element.181), channel_id=1, source_target_pairs={{0,1},{2,3},{3,2},{4,5},{5,4},{6,7},{7,6},{8,9},{10,11},{11,10},{1... | collective-permute-start | bytes 786440 | tf_op jit(solution)/shard_map/ppermute | solution.py:353
  126.0 5.1 %shard_map.59 = (f32[512,640]{1,0:T(8,128)S(1)}, f32[512,640]{1,0:T(8,128)S(1)}) custom-call(s32[2]{0:T(128)S(1)} %copy-done.36, f32[512,640]{1,0:T(8,128)S(1)} %get-tuple-element.125.top_in_ref, f32[512,512]{1,0:T(8,128)S(1)} %copy-done.38, f32[512,512]{1,0:T(8,128)S(1)} %copy-done.39), custom_call_target="tpu_custom_call" | custom-call | flops 4026531840 | tf_op jit(solution)/shard_map/pallas_call | solution.py:480
  137.6 3.5 %collective-permute-start.33 = (f32[128,512]{1,0:T(8,128)S(1)}, f32[128,512]{1,0:T(8,128)S(1)}, u32[]{:S(2)}, u32[]{:S(2)}) collective-permute-start(f32[128,512]{1,0:T(8,128)S(1)} %get-tuple-element.175), channel_id=1, source_target_pairs={{0,1},{2,3},{3,2},{4,5},{5,4},{6,7},{7,6},{8,9},{10,11},{11,10},{1... | collective-permute-start | bytes 786440 | tf_op jit(solution)/shard_map/ppermute | solution.py:353
  143.7 4.9 %collective-permute-done.33.refs_29_ = f32[128,512]{1,0:T(8,128)S(1)} collective-permute-done((f32[128,512]{1,0:T(8,128)S(1)}, f32[128,512]{1,0:T(8,128)S(1)}, u32[]{:S(2)}, u32[]{:S(2)}) %collective-permute-start.33) | collective-permute-done | bytes 262176 | tf_op jit(solution)/shard_map/ppermute | solution.py:353
  148.6 5.2 %collective-permute-done.32.refs_28_ = f32[128,512]{1,0:T(8,128)S(1)} collective-permute-done((f32[128,512]{1,0:T(8,128)S(1)}, f32[128,512]{1,0:T(8,128)S(1)}, u32[]{:S(2)}, u32[]{:S(2)}) %collective-permute-start.32) | collective-permute-done | bytes 262176 | tf_op jit(solution)/shard_map/ppermute | solution.py:353
  153.9 10.8 %shard_map.61 = f32[2048,640]{1,0:T(8,128)} custom-call(s32[2]{0:T(128)S(1)} %copy-done.36, s32[8,512]{1,0:T(8,128)S(1)} %get-tuple-element.83.table_ref, s32[16]{0:T(128)S(1)} %dynamic-slice_bitcast_fusion.choice_ref, f32[512,640]{1,0:T(8,128)S(1)} %maximum_select_fusion.displaced_ref, f32[512,640]{1,0:T(8,128)S(1)} %get-tuple-element.128.weights_ref, ...), custom_call_target="tpu_custom_call" | custom-call | flops 4026531840 | bytes 14680064 | tf_op jit(solution)/shard_map/pallas_call | solution.py:492
  (186 shorter events, 48.7 us)
Async XLA Ops:
  3.9 15.3 %collective-permute-start.1 = (f32[128,512]{1,0:T(8,128)S(1)}, f32[128,512]{1,0:T(8,128)S(1)}, u32[]{:S(2)}, u32[]{:S(2)}) collective-permute-start(f32[128,512]{1,0:T(8,128)S(1)} %get-tuple-element.171), channel_id=1, source_target_pairs={{0,1},{2,3},{3,2},{4,5},{5,4},{6,7},{7,6},{8,9},{10,11},{11,10},{1... | collective-permute-start | bytes 786440 | tf_op jit(solution)/shard_map/ppermute | solution.py:353
  7.3 11.8 %collective-permute-start = (f32[128,512]{1,0:T(8,128)S(1)}, f32[128,512]{1,0:T(8,128)S(1)}, u32[]{:S(2)}, u32[]{:S(2)}) collective-permute-start(f32[128,512]{1,0:T(8,128)S(1)} %get-tuple-element.172), channel_id=1, source_target_pairs={{0,2},{1,3},{2,4},{3,5},{4,6},{5,7},{8,10},{9,11},{10,12},{11,13},... | collective-permute-start | bytes 786440 | tf_op jit(solution)/shard_map/ppermute | solution.py:352
  10.8 14.4 %collective-permute-start.3 = (f32[128,512]{1,0:T(8,128)S(1)}, f32[128,512]{1,0:T(8,128)S(1)}, u32[]{:S(2)}, u32[]{:S(2)}) collective-permute-start(f32[128,512]{1,0:T(8,128)S(1)} %get-tuple-element.88), channel_id=1, source_target_pairs={{0,1},{2,3},{3,2},{4,5},{5,4},{6,7},{7,6},{8,9},{10,11},{11,10},{1... | collective-permute-start | bytes 786440 | tf_op jit(solution)/shard_map/ppermute | solution.py:353
  13.2 12.0 %collective-permute-start.2 = (f32[128,512]{1,0:T(8,128)S(1)}, f32[128,512]{1,0:T(8,128)}, u32[]{:S(2)}, u32[]{:S(2)}) collective-permute-start(f32[128,512]{1,0:T(8,128)S(1)} %get-tuple-element.87), channel_id=1, source_target_pairs={{0,2},{1,3},{2,4},{3,5},{4,6},{5,7},{8,10},{9,11},{10,12},{11,13},... | collective-permute-start | bytes 786440 | tf_op jit(solution)/shard_map/ppermute | solution.py:352
  25.3 19.9 %collective-permute-start.6 = (f32[512,640]{1,0:T(8,128)S(1)}, f32[512,640]{1,0:T(8,128)S(1)}, u32[]{:S(2)}, u32[]{:S(2)}) collective-permute-start(f32[512,640]{1,0:T(8,128)S(1)} %shard_map.56.held_ref), channel_id=1, source_target_pairs={{0,8},{8,0},{16,24},{24,16},{1,9},{9,1},{17,25},{25,17},{2,10},{10... | collective-permute-start | bytes 3932168 | tf_op jit(solution)/shard_map/ppermute | solution.py:464
  25.5 13.6 %collective-permute-start.15 = (f32[128,512]{1,0:T(8,128)S(1)}, f32[128,512]{1,0:T(8,128)S(1)}, u32[]{:S(2)}, u32[]{:S(2)}) collective-permute-start(f32[128,512]{1,0:T(8,128)S(1)} %get-tuple-element.192), channel_id=1, source_target_pairs={{0,1},{2,3},{3,2},{4,5},{5,4},{6,7},{7,6},{8,9},{10,11},{11,10},{1... | collective-permute-start | bytes 786440 | tf_op jit(solution)/shard_map/ppermute | solution.py:353
  29.1 10.7 %collective-permute-start.14 = (f32[128,512]{1,0:T(8,128)S(1)}, f32[128,512]{1,0:T(8,128)S(1)}, u32[]{:S(2)}, u32[]{:S(2)}) collective-permute-start(f32[128,512]{1,0:T(8,128)S(1)} %get-tuple-element.193), channel_id=1, source_target_pairs={{0,2},{1,3},{2,4},{3,5},{4,6},{5,7},{8,10},{9,11},{10,12},{11,13},... | collective-permute-start | bytes 786440 | tf_op jit(solution)/shard_map/ppermute | solution.py:352
  32.3 12.1 %collective-permute-start.5 = (f32[128,512]{1,0:T(8,128)S(1)}, f32[128,512]{1,0:T(8,128)S(1)}, u32[]{:S(2)}, u32[]{:S(2)}) collective-permute-start(f32[128,512]{1,0:T(8,128)S(1)} %get-tuple-element.198), channel_id=1, source_target_pairs={{0,1},{2,3},{3,2},{4,5},{5,4},{6,7},{7,6},{8,9},{10,11},{11,10},{1... | collective-permute-start | bytes 786440 | tf_op jit(solution)/shard_map/ppermute | solution.py:353
  34.7 10.5 %collective-permute-start.4 = (f32[128,512]{1,0:T(8,128)S(1)}, f32[128,512]{1,0:T(8,128)S(1)}, u32[]{:S(2)}, u32[]{:S(2)}) collective-permute-start(f32[128,512]{1,0:T(8,128)S(1)} %get-tuple-element.199), channel_id=1, source_target_pairs={{0,2},{1,3},{2,4},{3,5},{4,6},{5,7},{8,10},{9,11},{10,12},{11,13},... | collective-permute-start | bytes 786440 | tf_op jit(solution)/shard_map/ppermute | solution.py:352
  39.9 12.4 %collective-permute-start.17 = (f32[128,512]{1,0:T(8,128)S(1)}, f32[128,512]{1,0:T(8,128)S(1)}, u32[]{:S(2)}, u32[]{:S(2)}) collective-permute-start(f32[128,512]{1,0:T(8,128)S(1)} %get-tuple-element.190), channel_id=1, source_target_pairs={{0,1},{2,3},{3,2},{4,5},{5,4},{6,7},{7,6},{8,9},{10,11},{11,10},{1... | collective-permute-start | bytes 786440 | tf_op jit(solution)/shard_map/ppermute | solution.py:353
  42.1 10.3 %collective-permute-start.16 = (f32[128,512]{1,0:T(8,128)S(1)}, f32[128,512]{1,0:T(8,128)S(1)}, u32[]{:S(2)}, u32[]{:S(2)}) collective-permute-start(f32[128,512]{1,0:T(8,128)S(1)} %get-tuple-element.191), channel_id=1, source_target_pairs={{0,2},{1,3},{2,4},{3,5},{4,6},{5,7},{8,10},{9,11},{10,12},{11,13},... | collective-permute-start | bytes 786440 | tf_op jit(solution)/shard_map/ppermute | solution.py:352
  45.9 9.4 %collective-permute-start.8 = (f32[128,512]{1,0:T(8,128)S(1)}, f32[128,512]{1,0:T(8,128)S(1)}, u32[]{:S(2)}, u32[]{:S(2)}) collective-permute-start(f32[128,512]{1,0:T(8,128)S(1)} %get-tuple-element.196), channel_id=1, source_target_pairs={{0,1},{2,3},{3,2},{4,5},{5,4},{6,7},{7,6},{8,9},{10,11},{11,10},{1... | collective-permute-start | bytes 786440 | tf_op jit(solution)/shard_map/ppermute | solution.py:353
  49.0 9.0 %collective-permute-start.7 = (f32[128,512]{1,0:T(8,128)S(1)}, f32[128,512]{1,0:T(8,128)S(1)}, u32[]{:S(2)}, u32[]{:S(2)}) collective-permute-start(f32[128,512]{1,0:T(8,128)S(1)} %get-tuple-element.197), channel_id=1, source_target_pairs={{0,2},{1,3},{2,4},{3,5},{4,6},{5,7},{8,10},{9,11},{10,12},{11,13},... | collective-permute-start | bytes 786440 | tf_op jit(solution)/shard_map/ppermute | solution.py:352
  53.2 17.5 %collective-permute-start.11 = (f32[256,640]{1,0:T(8,128)S(1)}, f32[256,640]{1,0:T(8,128)S(1)}, u32[]{:S(2)}, u32[]{:S(2)}) collective-permute-start(f32[256,640]{1,0:T(8,128)S(1)} %get-tuple-element.101), channel_id=1, source_target_pairs={{0,16},{8,24},{16,0},{24,8},{1,17},{9,25},{17,1},{25,9},{2,18},{10... | collective-permute-start | bytes 1966088 | tf_op jit(solution)/shard_map/ppermute | solution.py:468
  58.1 12.2 %collective-permute-start.10 = (f32[128,512]{1,0:T(8,128)S(1)}, f32[128,512]{1,0:T(8,128)S(1)}, u32[]{:S(2)}, u32[]{:S(2)}) collective-permute-start(f32[128,512]{1,0:T(8,128)S(1)} %get-tuple-element.194), channel_id=1, source_target_pairs={{0,1},{2,3},{3,2},{4,5},{5,4},{6,7},{7,6},{8,9},{10,11},{11,10},{1... | collective-permute-start | bytes 786440 | tf_op jit(solution)/shard_map/ppermute | solution.py:353
  61.1 9.6 %collective-permute-start.9 = (f32[128,512]{1,0:T(8,128)S(1)}, f32[128,512]{1,0:T(8,128)S(1)}, u32[]{:S(2)}, u32[]{:S(2)}) collective-permute-start(f32[128,512]{1,0:T(8,128)S(1)} %get-tuple-element.195), channel_id=1, source_target_pairs={{0,2},{1,3},{2,4},{3,5},{4,6},{5,7},{8,10},{9,11},{10,12},{11,13},... | collective-permute-start | bytes 786440 | tf_op jit(solution)/shard_map/ppermute | solution.py:352
  70.7 18.8 %collective-permute-start.22 = (f32[256,640]{1,0:T(8,128)S(1)}, f32[256,640]{1,0:T(8,128)}, u32[]{:S(2)}, u32[]{:S(2)}) collective-permute-start(f32[256,640]{1,0:T(8,128)S(1)} %collective-permute-done.11.refs_0_), channel_id=1, source_target_pairs={{0,8},{8,0},{16,24},{24,16},{1,9},{9,1},{17,25},{25,17},{2,10},{10... | collective-permute-start | bytes 1966088 | tf_op jit(solution)/shard_map/ppermute | solution.py:470
  77.4 12.0 %collective-permute-start.21 = (f32[128,512]{1,0:T(8,128)}, f32[128,512]{1,0:T(8,128)}, u32[]{:S(2)}, u32[]{:S(2)}) collective-permute-start(f32[128,512]{1,0:T(8,128)} %get-tuple-element.184), channel_id=1, source_target_pairs={{0,2},{1,3},{2,4},{3,5},{4,6},{5,7},{8,10},{9,11},{10,12},{11,13},... | collective-permute-start | bytes 786440 | tf_op jit(solution)/shard_map/ppermute | solution.py:352
  80.8 8.7 %collective-permute-start.20 = (f32[128,512]{1,0:T(8,128)}, f32[128,512]{1,0:T(8,128)}, u32[]{:S(2)}, u32[]{:S(2)}) collective-permute-start(f32[128,512]{1,0:T(8,128)} %get-tuple-element.185), channel_id=1, source_target_pairs={{0,1},{2,3},{3,2},{4,5},{5,4},{6,7},{7,6},{8,9},{10,11},{11,10},{1... | collective-permute-start | bytes 786440 | tf_op jit(solution)/shard_map/ppermute | solution.py:353
  84.0 12.5 %collective-permute-start.12 = (f32[128,512]{1,0:T(8,128)}, f32[128,512]{1,0:T(8,128)S(1)}, u32[]{:S(2)}, u32[]{:S(2)}) collective-permute-start(f32[128,512]{1,0:T(8,128)} %get-tuple-element.186), channel_id=1, source_target_pairs={{0,2},{1,3},{2,4},{3,5},{4,6},{5,7},{8,10},{9,11},{10,12},{11,13},... | collective-permute-start | bytes 786440 | tf_op jit(solution)/shard_map/ppermute | solution.py:352
  86.9 9.6 %collective-permute-start.13 = (f32[128,512]{1,0:T(8,128)}, f32[128,512]{1,0:T(8,128)S(1)}, u32[]{:S(2)}, u32[]{:S(2)}) collective-permute-start(f32[128,512]{1,0:T(8,128)} %get-tuple-element.187), channel_id=1, source_target_pairs={{0,1},{2,3},{3,2},{4,5},{5,4},{6,7},{7,6},{8,9},{10,11},{11,10},{1... | collective-permute-start | bytes 786440 | tf_op jit(solution)/shard_map/ppermute | solution.py:353
  98.6 13.5 %collective-permute-start.28 = (f32[512,512]{1,0:T(8,128)S(1)}, f32[512,512]{1,0:T(8,128)S(1)}, u32[]{:S(2)}, u32[]{:S(2)}) collective-permute-start(f32[512,512]{1,0:T(8,128)S(1)} %shard_map.60), channel_id=1, source_target_pairs={{0,8},{1,9},{2,10},{3,11},{4,12},{5,13},{6,14},{7,15}} | collective-permute-start | bytes 3145736 | tf_op jit(solution)/shard_map/ppermute | solution.py:433
  102.7 9.4 %collective-permute-start.25 = (f32[128,512]{1,0:T(8,128)S(1)}, f32[128,512]{1,0:T(8,128)S(1)}, u32[]{:S(2)}, u32[]{:S(2)}) collective-permute-start(f32[128,512]{1,0:T(8,128)S(1)} %get-tuple-element.183), channel_id=1, source_target_pairs={{0,2},{1,3},{2,4},{3,5},{4,6},{5,7},{8,10},{9,11},{10,12},{11,13},... | collective-permute-start | bytes 786440 | tf_op jit(solution)/shard_map/ppermute | solution.py:352
  114.6 16.4 %collective-permute-start.31 = (f32[128,512]{1,0:T(8,128)S(1)}, f32[128,512]{1,0:T(8,128)S(1)}, u32[]{:S(2)}, u32[]{:S(2)}) collective-permute-start(f32[128,512]{1,0:T(8,128)S(1)} %get-tuple-element.178), channel_id=1, source_target_pairs={{0,1},{2,3},{3,2},{4,5},{5,4},{6,7},{7,6},{8,9},{10,11},{11,10},{1... | collective-permute-start | bytes 786440 | tf_op jit(solution)/shard_map/ppermute | solution.py:353
  116.6 14.5 %collective-permute-start.29 = (f32[128,512]{1,0:T(8,128)S(1)}, f32[128,512]{1,0:T(8,128)S(1)}, u32[]{:S(2)}, u32[]{:S(2)}) collective-permute-start(f32[128,512]{1,0:T(8,128)S(1)} %get-tuple-element.179), channel_id=1, source_target_pairs={{0,2},{1,3},{2,4},{3,5},{4,6},{5,7},{8,10},{9,11},{10,12},{11,13},... | collective-permute-start | bytes 786440 | tf_op jit(solution)/shard_map/ppermute | solution.py:352
  118.6 12.5 %collective-permute-start.23 = (f32[128,512]{1,0:T(8,128)S(1)}, f32[128,512]{1,0:T(8,128)S(1)}, u32[]{:S(2)}, u32[]{:S(2)}) collective-permute-start(f32[128,512]{1,0:T(8,128)S(1)} %get-tuple-element.180), channel_id=1, source_target_pairs={{0,2},{1,3},{2,4},{3,5},{4,6},{5,7},{8,10},{9,11},{10,12},{11,13},... | collective-permute-start | bytes 786440 | tf_op jit(solution)/shard_map/ppermute | solution.py:352
  120.6 10.5 %collective-permute-start.24 = (f32[128,512]{1,0:T(8,128)S(1)}, f32[128,512]{1,0:T(8,128)S(1)}, u32[]{:S(2)}, u32[]{:S(2)}) collective-permute-start(f32[128,512]{1,0:T(8,128)S(1)} %get-tuple-element.181), channel_id=1, source_target_pairs={{0,1},{2,3},{3,2},{4,5},{5,4},{6,7},{7,6},{8,9},{10,11},{11,10},{1... | collective-permute-start | bytes 786440 | tf_op jit(solution)/shard_map/ppermute | solution.py:353
  124.6 11.1 %collective-permute-start.34 = (f32[256,512]{1,0:T(8,128)S(1)}, f32[256,512]{1,0:T(8,128)S(1)}, u32[]{:S(2)}, u32[]{:S(2)}) collective-permute-start(f32[256,512]{1,0:T(8,128)S(1)} %slice_select_fusion), channel_id=1, source_target_pairs={{0,16},{8,24},{1,17},{9,25},{2,18},{10,26},{3,19},{11,27},{4,20},{... | collective-permute-start | bytes 1572872 | tf_op jit(solution)/shard_map/ppermute | solution.py:438
  131.2 9.9 %collective-permute-start.26 = (f32[128,512]{1,0:T(8,128)S(1)}, f32[128,512]{1,0:T(8,128)S(1)}, u32[]{:S(2)}, u32[]{:S(2)}) collective-permute-start(f32[128,512]{1,0:T(8,128)S(1)} %get-tuple-element.176), channel_id=1, source_target_pairs={{0,2},{1,3},{2,4},{3,5},{4,6},{5,7},{8,10},{9,11},{10,12},{11,13},... | collective-permute-start | bytes 786440 | tf_op jit(solution)/shard_map/ppermute | solution.py:352
  135.7 18.1 %collective-permute-start.35 = (f32[256,512]{1,0:T(8,128)S(1)}, f32[256,512]{1,0:T(8,128)S(1)}, u32[]{:S(2)}, u32[]{:S(2)}) collective-permute-start(f32[256,512]{1,0:T(8,128)S(1)} %collective-permute-done.34.refs_31_), channel_id=1, source_target_pairs={{16,24},{24,16},{17,25},{25,17},{18,26},{26,18},{19,27},{27,19},{2... | collective-permute-start | bytes 1572872 | tf_op jit(solution)/shard_map/ppermute | solution.py:439
  137.6 11.0 %collective-permute-start.33 = (f32[128,512]{1,0:T(8,128)S(1)}, f32[128,512]{1,0:T(8,128)S(1)}, u32[]{:S(2)}, u32[]{:S(2)}) collective-permute-start(f32[128,512]{1,0:T(8,128)S(1)} %get-tuple-element.175), channel_id=1, source_target_pairs={{0,1},{2,3},{3,2},{4,5},{5,4},{6,7},{7,6},{8,9},{10,11},{11,10},{1... | collective-permute-start | bytes 786440 | tf_op jit(solution)/shard_map/ppermute | solution.py:353
  141.5 12.4 %collective-permute-start.32 = (f32[128,512]{1,0:T(8,128)S(1)}, f32[128,512]{1,0:T(8,128)S(1)}, u32[]{:S(2)}, u32[]{:S(2)}) collective-permute-start(f32[128,512]{1,0:T(8,128)S(1)} %broadcast_select_fusion.4), channel_id=1, source_target_pairs={{0,1},{2,3},{3,2},{4,5},{5,4},{6,7},{7,6},{8,9},{10,11},{11,10},{1... | collective-permute-start | bytes 786440 | tf_op jit(solution)/shard_map/ppermute | solution.py:353
  (64 other events, 451.8 us)

commit v16 on v15

--- a/solution.py
+++ b/solution.py
@@ -492,7 +492,7 @@
     return call(
         functools.partial(
             final_kernel, n_bufs=len(bufs), n_tops=len(tops), n_cols=n_cols, parts=parts,
-            block=256,
+            block=512,
         ),
         jax.ShapeDtypeStruct(matrix.shape, f32),
         [SMEM, SMEM, SMEM, VMEM, VMEM, VMEM, ANY] + [ANY] * (len(bufs) + len(tops)),

time: 166 us -> 166 us (level)
  no operation moved by 1% of the time
where the time goes in v16:
time: 166 us; the launch traced here: 165 us
  starting transfers between devices  90.1 us (54%)
  waiting for transfers between devices  27.7 us (17%)
  Pallas kernels  25 us (15%)
  local copies, waits for them, and re-layouts  13.8 us (8%)
  other arithmetic  7.25 us (4%)
    ppermute x16, starting transfers between devices, spread(): cross.append(lax.ppermute(aside, 'pcol', across))  44.2 us
    ppermute x14, starting transfers between devices, spread(): chain.append(lax.ppermute(ahead, 'pcol', along))  41.3 us
    ppermute x16, waiting for transfers between devices, spread(): cross.append(lax.ppermute(aside, 'pcol', across))  16.1 us
    pallas_call x1, Pallas kernels, local(): call(functools.partial(final_kernel, n_bufs=len(bufs), n_tops=len(tops),...  11.1 us
    ppermute x14, waiting for transfers between devices, spread(): chain.append(lax.ppermute(ahead, 'pcol', along))  11 us
    unnamed x120, local copies, waits for them, and re-layouts  9.3 us
    pallas_call x1, Pallas kernels, exchange_rider(): call(factor_kernel, (slot, slot), [SMEM, VMEM, VMEM, VMEM], (VMEM, VMEM),...  5.09 us
    slice x1, local copies, waits for them, and re-layouts, local(): lax.slice(matrix, (k * chunk, 0), ((k + 1) * chunk, nb))  3.84 us
  transfers between devices with their start and end apart: 36, of which 14 were waited for; matrix products, arithmetic and copies ran while one was open for 4% of the time, Pallas kernels for 8%

profile of v16, /device:TPU:10, one launch (start us, length us, event | category | flops | bytes accessed | tf_op | source)
XLA Modules:
  0.0 165.1 jit_solution(2953171055728384439)
XLA Ops:
  0.0 3.8 %fusion = (f32[128,512]{1,0:T(8,128)}, f32[128,512]{1,0:T(8,128)}, f32[128,512]{1,0:T(8,128)}, f32[128,512]{1,0:T(8,128)}, f32[128,512]{1,0:T(8,128)}, /*index=5...) fusion(f32[2048,640]{1,0:T(8,128)} %matrix_ref.5), kind=kLoop, calls=%fused_computation.33 | loop fusion | bytes 8388608 | tf_op jit(solution)/shard_map/slice | solution.py:387
  3.9 3.4 %collective-permute-start.1 = (f32[128,512]{1,0:T(8,128)S(1)}, f32[128,512]{1,0:T(8,128)S(1)}, u32[]{:S(2)}, u32[]{:S(2)}) collective-permute-start(f32[128,512]{1,0:T(8,128)S(1)} %get-tuple-element.171), channel_id=1, source_target_pairs={{0,1},{2,3},{3,2},{4,5},{5,4},{6,7},{7,6},{8,9},{10,11},{11,10},{1... | collective-permute-start | bytes 786440 | tf_op jit(solution)/shard_map/ppermute | solution.py:353
  7.3 3.5 %collective-permute-start = (f32[128,512]{1,0:T(8,128)S(1)}, f32[128,512]{1,0:T(8,128)S(1)}, u32[]{:S(2)}, u32[]{:S(2)}) collective-permute-start(f32[128,512]{1,0:T(8,128)S(1)} %get-tuple-element.172), channel_id=1, source_target_pairs={{0,2},{1,3},{2,4},{3,5},{4,6},{5,7},{8,10},{9,11},{10,12},{11,13},... | collective-permute-start | bytes 786440 | tf_op jit(solution)/shard_map/ppermute | solution.py:352
  10.8 2.4 %collective-permute-start.3 = (f32[128,512]{1,0:T(8,128)S(1)}, f32[128,512]{1,0:T(8,128)S(1)}, u32[]{:S(2)}, u32[]{:S(2)}) collective-permute-start(f32[128,512]{1,0:T(8,128)S(1)} %get-tuple-element.88), channel_id=1, source_target_pairs={{0,1},{2,3},{3,2},{4,5},{5,4},{6,7},{7,6},{8,9},{10,11},{11,10},{1... | collective-permute-start | bytes 786440 | tf_op jit(solution)/shard_map/ppermute | solution.py:353
  13.2 3.5 %collective-permute-start.2 = (f32[128,512]{1,0:T(8,128)S(1)}, f32[128,512]{1,0:T(8,128)}, u32[]{:S(2)}, u32[]{:S(2)}) collective-permute-start(f32[128,512]{1,0:T(8,128)S(1)} %get-tuple-element.87), channel_id=1, source_target_pairs={{0,2},{1,3},{2,4},{3,5},{4,6},{5,7},{8,10},{9,11},{10,12},{11,13},... | collective-permute-start | bytes 786440 | tf_op jit(solution)/shard_map/ppermute | solution.py:352
  19.1 2.6 %copy-done = f32[2048,640]{1,0:T(8,128)S(1)} copy-done((f32[2048,640]{1,0:T(8,128)S(1)}, f32[2048,640]{1,0:T(8,128)}, u32[]{:S(2)}) %copy-start) | copy-done | bytes 5242904
  21.7 3.5 %shard_map.56.held_ref = f32[512,640]{1,0:T(8,128)S(1)} custom-call(s32[8,512]{1,0:T(8,128)S(1)} %get-tuple-element.83.table_ref, f32[2048,640]{1,0:T(8,128)S(1)} %copy-done), custom_call_target="tpu_custom_call" | custom-call | tf_op jit(solution)/shard_map/pallas_call | solution.py:455
  25.5 3.6 %collective-permute-start.15 = (f32[128,512]{1,0:T(8,128)S(1)}, f32[128,512]{1,0:T(8,128)S(1)}, u32[]{:S(2)}, u32[]{:S(2)}) collective-permute-start(f32[128,512]{1,0:T(8,128)S(1)} %get-tuple-element.192), channel_id=1, source_target_pairs={{0,1},{2,3},{3,2},{4,5},{5,4},{6,7},{7,6},{8,9},{10,11},{11,10},{1... | collective-permute-start | bytes 786440 | tf_op jit(solution)/shard_map/ppermute | solution.py:353
  32.3 2.4 %collective-permute-start.5 = (f32[128,512]{1,0:T(8,128)S(1)}, f32[128,512]{1,0:T(8,128)S(1)}, u32[]{:S(2)}, u32[]{:S(2)}) collective-permute-start(f32[128,512]{1,0:T(8,128)S(1)} %get-tuple-element.198), channel_id=1, source_target_pairs={{0,1},{2,3},{3,2},{4,5},{5,4},{6,7},{7,6},{8,9},{10,11},{11,10},{1... | collective-permute-start | bytes 786440 | tf_op jit(solution)/shard_map/ppermute | solution.py:353
  34.7 4.5 %collective-permute-start.4 = (f32[128,512]{1,0:T(8,128)S(1)}, f32[128,512]{1,0:T(8,128)S(1)}, u32[]{:S(2)}, u32[]{:S(2)}) collective-permute-start(f32[128,512]{1,0:T(8,128)S(1)} %get-tuple-element.199), channel_id=1, source_target_pairs={{0,2},{1,3},{2,4},{3,5},{4,6},{5,7},{8,10},{9,11},{10,12},{11,13},... | collective-permute-start | bytes 786440 | tf_op jit(solution)/shard_map/ppermute | solution.py:352
  42.1 2.3 %collective-permute-start.16 = (f32[128,512]{1,0:T(8,128)S(1)}, f32[128,512]{1,0:T(8,128)S(1)}, u32[]{:S(2)}, u32[]{:S(2)}) collective-permute-start(f32[128,512]{1,0:T(8,128)S(1)} %get-tuple-element.191), channel_id=1, source_target_pairs={{0,2},{1,3},{2,4},{3,5},{4,6},{5,7},{8,10},{9,11},{10,12},{11,13},... | collective-permute-start | bytes 786440 | tf_op jit(solution)/shard_map/ppermute | solution.py:352
  45.9 3.1 %collective-permute-start.8 = (f32[128,512]{1,0:T(8,128)S(1)}, f32[128,512]{1,0:T(8,128)S(1)}, u32[]{:S(2)}, u32[]{:S(2)}) collective-permute-start(f32[128,512]{1,0:T(8,128)S(1)} %get-tuple-element.196), channel_id=1, source_target_pairs={{0,1},{2,3},{3,2},{4,5},{5,4},{6,7},{7,6},{8,9},{10,11},{11,10},{1... | collective-permute-start | bytes 786440 | tf_op jit(solution)/shard_map/ppermute | solution.py:353
  49.0 3.3 %collective-permute-start.7 = (f32[128,512]{1,0:T(8,128)S(1)}, f32[128,512]{1,0:T(8,128)S(1)}, u32[]{:S(2)}, u32[]{:S(2)}) collective-permute-start(f32[128,512]{1,0:T(8,128)S(1)} %get-tuple-element.197), channel_id=1, source_target_pairs={{0,2},{1,3},{2,4},{3,5},{4,6},{5,7},{8,10},{9,11},{10,12},{11,13},... | collective-permute-start | bytes 786440 | tf_op jit(solution)/shard_map/ppermute | solution.py:352
  55.3 2.7 %collective-permute-done.7.refs_5_ = f32[128,512]{1,0:T(8,128)S(1)} collective-permute-done((f32[128,512]{1,0:T(8,128)S(1)}, f32[128,512]{1,0:T(8,128)S(1)}, u32[]{:S(2)}, u32[]{:S(2)}) %collective-permute-start.7) | collective-permute-done | bytes 262176 | tf_op jit(solution)/shard_map/ppermute | solution.py:352
  58.1 3.0 %collective-permute-start.10 = (f32[128,512]{1,0:T(8,128)S(1)}, f32[128,512]{1,0:T(8,128)S(1)}, u32[]{:S(2)}, u32[]{:S(2)}) collective-permute-start(f32[128,512]{1,0:T(8,128)S(1)} %get-tuple-element.194), channel_id=1, source_target_pairs={{0,1},{2,3},{3,2},{4,5},{5,4},{6,7},{7,6},{8,9},{10,11},{11,10},{1... | collective-permute-start | bytes 786440 | tf_op jit(solution)/shard_map/ppermute | solution.py:353
  61.1 3.5 %collective-permute-start.9 = (f32[128,512]{1,0:T(8,128)S(1)}, f32[128,512]{1,0:T(8,128)S(1)}, u32[]{:S(2)}, u32[]{:S(2)}) collective-permute-start(f32[128,512]{1,0:T(8,128)S(1)} %get-tuple-element.195), channel_id=1, source_target_pairs={{0,2},{1,3},{2,4},{3,5},{4,6},{5,7},{8,10},{9,11},{10,12},{11,13},... | collective-permute-start | bytes 786440 | tf_op jit(solution)/shard_map/ppermute | solution.py:352
  66.9 3.3 %collective-permute-start.18 = (f32[128,512]{1,0:T(8,128)S(1)}, f32[128,512]{1,0:T(8,128)S(1)}, u32[]{:S(2)}, u32[]{:S(2)}) collective-permute-start(f32[128,512]{1,0:T(8,128)S(1)} %get-tuple-element.189), channel_id=1, source_target_pairs={{0,2},{1,3},{2,4},{3,5},{4,6},{5,7},{8,10},{9,11},{10,12},{11,13},... | collective-permute-start | bytes 786440 | tf_op jit(solution)/shard_map/ppermute | solution.py:352
  70.7 2.4 %collective-permute-done.19.refs_14_.refs_20_ = f32[128,512]{1,0:T(8,128)S(1)} collective-permute-done((f32[128,512]{1,0:T(8,128)S(1)}, f32[128,512]{1,0:T(8,128)S(1)}, u32[]{:S(2)}, u32[]{:S(2)}) %collective-permute-start.19) | collective-permute-done | bytes 262176 | tf_op jit(solution)/shard_map/ppermute | solution.py:353
  77.4 3.3 %collective-permute-start.21 = (f32[128,512]{1,0:T(8,128)}, f32[128,512]{1,0:T(8,128)}, u32[]{:S(2)}, u32[]{:S(2)}) collective-permute-start(f32[128,512]{1,0:T(8,128)} %get-tuple-element.184), channel_id=1, source_target_pairs={{0,2},{1,3},{2,4},{3,5},{4,6},{5,7},{8,10},{9,11},{10,12},{11,13},... | collective-permute-start | bytes 786440 | tf_op jit(solution)/shard_map/ppermute | solution.py:352
  80.8 2.5 %collective-permute-start.20 = (f32[128,512]{1,0:T(8,128)}, f32[128,512]{1,0:T(8,128)}, u32[]{:S(2)}, u32[]{:S(2)}) collective-permute-start(f32[128,512]{1,0:T(8,128)} %get-tuple-element.185), channel_id=1, source_target_pairs={{0,1},{2,3},{3,2},{4,5},{5,4},{6,7},{7,6},{8,9},{10,11},{11,10},{1... | collective-permute-start | bytes 786440 | tf_op jit(solution)/shard_map/ppermute | solution.py:353
  84.0 2.9 %collective-permute-start.12 = (f32[128,512]{1,0:T(8,128)}, f32[128,512]{1,0:T(8,128)S(1)}, u32[]{:S(2)}, u32[]{:S(2)}) collective-permute-start(f32[128,512]{1,0:T(8,128)} %get-tuple-element.186), channel_id=1, source_target_pairs={{0,2},{1,3},{2,4},{3,5},{4,6},{5,7},{8,10},{9,11},{10,12},{11,13},... | collective-permute-start | bytes 786440 | tf_op jit(solution)/shard_map/ppermute | solution.py:352
  86.9 2.5 %collective-permute-start.13 = (f32[128,512]{1,0:T(8,128)}, f32[128,512]{1,0:T(8,128)S(1)}, u32[]{:S(2)}, u32[]{:S(2)}) collective-permute-start(f32[128,512]{1,0:T(8,128)} %get-tuple-element.187), channel_id=1, source_target_pairs={{0,1},{2,3},{3,2},{4,5},{5,4},{6,7},{7,6},{8,9},{10,11},{11,10},{1... | collective-permute-start | bytes 786440 | tf_op jit(solution)/shard_map/ppermute | solution.py:353
  92.4 2.3 %shard_map.58 = (f32[512,640]{1,0:T(8,128)S(1)}, f32[256,640]{1,0:T(8,128)}) custom-call(s32[2]{0:T(128)S(1)} %copy-done.35, s32[512,128]{1,0:T(8,128)S(1)} %copy-done.33, f32[512,640]{1,0:T(8,128)S(1)} %copy-done.30, f32[256,640]{1,0:T(8,128)S(1)} %collective-permute-done.11.refs_0_, f32[256,640]{1,0:T(8,128)} %collective-permute-done.22.refs_1_), custom_call_target="tpu_custom_call" | custom-call | tf_op jit(solution)/shard_map/pallas_call | solution.py:473
  99.4 3.3 %collective-permute-start.27 = (f32[128,512]{1,0:T(8,128)S(1)}, f32[128,512]{1,0:T(8,128)S(1)}, u32[]{:S(2)}, u32[]{:S(2)}) collective-permute-start(f32[128,512]{1,0:T(8,128)S(1)} %get-tuple-element.182), channel_id=1, source_target_pairs={{0,1},{2,3},{3,2},{4,5},{5,4},{6,7},{7,6},{8,9},{10,11},{11,10},{1... | collective-permute-start | bytes 786440 | tf_op jit(solution)/shard_map/ppermute | solution.py:353
  102.7 3.2 %collective-permute-start.25 = (f32[128,512]{1,0:T(8,128)S(1)}, f32[128,512]{1,0:T(8,128)S(1)}, u32[]{:S(2)}, u32[]{:S(2)}) collective-permute-start(f32[128,512]{1,0:T(8,128)S(1)} %get-tuple-element.183), channel_id=1, source_target_pairs={{0,2},{1,3},{2,4},{3,5},{4,6},{5,7},{8,10},{9,11},{10,12},{11,13},... | collective-permute-start | bytes 786440 | tf_op jit(solution)/shard_map/ppermute | solution.py:352
  107.7 4.4 %collective-permute-done.25.refs_11_ = f32[128,512]{1,0:T(8,128)S(1)} collective-permute-done((f32[128,512]{1,0:T(8,128)S(1)}, f32[128,512]{1,0:T(8,128)S(1)}, u32[]{:S(2)}, u32[]{:S(2)}) %collective-permute-start.25) | collective-permute-done | bytes 262176 | tf_op jit(solution)/shard_map/ppermute | solution.py:352
  120.6 4.1 %collective-permute-start.24 = (f32[128,512]{1,0:T(8,128)S(1)}, f32[128,512]{1,0:T(8,128)S(1)}, u32[]{:S(2)}, u32[]{:S(2)}) collective-permute-start(f32[128,512]{1,0:T(8,128)S(1)} %get-tuple-element.181), channel_id=1, source_target_pairs={{0,1},{2,3},{3,2},{4,5},{5,4},{6,7},{7,6},{8,9},{10,11},{11,10},{1... | collective-permute-start | bytes 786440 | tf_op jit(solution)/shard_map/ppermute | solution.py:353
  126.0 5.1 %shard_map.59 = (f32[512,640]{1,0:T(8,128)S(1)}, f32[512,640]{1,0:T(8,128)S(1)}) custom-call(s32[2]{0:T(128)S(1)} %copy-done.36, f32[512,640]{1,0:T(8,128)S(1)} %get-tuple-element.125.top_in_ref, f32[512,512]{1,0:T(8,128)S(1)} %copy-done.38, f32[512,512]{1,0:T(8,128)S(1)} %copy-done.39), custom_call_target="tpu_custom_call" | custom-call | flops 4026531840 | tf_op jit(solution)/shard_map/pallas_call | solution.py:480
  137.6 3.5 %collective-permute-start.33 = (f32[128,512]{1,0:T(8,128)S(1)}, f32[128,512]{1,0:T(8,128)S(1)}, u32[]{:S(2)}, u32[]{:S(2)}) collective-permute-start(f32[128,512]{1,0:T(8,128)S(1)} %get-tuple-element.175), channel_id=1, source_target_pairs={{0,1},{2,3},{3,2},{4,5},{5,4},{6,7},{7,6},{8,9},{10,11},{11,10},{1... | collective-permute-start | bytes 786440 | tf_op jit(solution)/shard_map/ppermute | solution.py:353
  143.7 4.9 %collective-permute-done.33.refs_29_ = f32[128,512]{1,0:T(8,128)S(1)} collective-permute-done((f32[128,512]{1,0:T(8,128)S(1)}, f32[128,512]{1,0:T(8,128)S(1)}, u32[]{:S(2)}, u32[]{:S(2)}) %collective-permute-start.33) | collective-permute-done | bytes 262176 | tf_op jit(solution)/shard_map/ppermute | solution.py:353
  148.6 5.2 %collective-permute-done.32.refs_28_ = f32[128,512]{1,0:T(8,128)S(1)} collective-permute-done((f32[128,512]{1,0:T(8,128)S(1)}, f32[128,512]{1,0:T(8,128)S(1)}, u32[]{:S(2)}, u32[]{:S(2)}) %collective-permute-start.32) | collective-permute-done | bytes 262176 | tf_op jit(solution)/shard_map/ppermute | solution.py:353
  153.9 11.1 %shard_map.61 = f32[2048,640]{1,0:T(8,128)} custom-call(s32[2]{0:T(128)S(1)} %copy-done.36, s32[8,512]{1,0:T(8,128)S(1)} %get-tuple-element.83.table_ref, s32[16]{0:T(128)S(1)} %dynamic-slice_bitcast_fusion.choice_ref, f32[512,640]{1,0:T(8,128)S(1)} %maximum_select_fusion.displaced_ref, f32[512,640]{1,0:T(8,128)S(1)} %get-tuple-element.128.weights_ref, ...), custom_call_target="tpu_custom_call" | custom-call | flops 4026531840 | bytes 14680064 | tf_op jit(solution)/shard_map/pallas_call | solution.py:492
  (186 shorter events, 48.7 us)
Async XLA Ops:
  3.9 15.3 %collective-permute-start.1 = (f32[128,512]{1,0:T(8,128)S(1)}, f32[128,512]{1,0:T(8,128)S(1)}, u32[]{:S(2)}, u32[]{:S(2)}) collective-permute-start(f32[128,512]{1,0:T(8,128)S(1)} %get-tuple-element.171), channel_id=1, source_target_pairs={{0,1},{2,3},{3,2},{4,5},{5,4},{6,7},{7,6},{8,9},{10,11},{11,10},{1... | collective-permute-start | bytes 786440 | tf_op jit(solution)/shard_map/ppermute | solution.py:353
  7.3 11.8 %collective-permute-start = (f32[128,512]{1,0:T(8,128)S(1)}, f32[128,512]{1,0:T(8,128)S(1)}, u32[]{:S(2)}, u32[]{:S(2)}) collective-permute-start(f32[128,512]{1,0:T(8,128)S(1)} %get-tuple-element.172), channel_id=1, source_target_pairs={{0,2},{1,3},{2,4},{3,5},{4,6},{5,7},{8,10},{9,11},{10,12},{11,13},... | collective-permute-start | bytes 786440 | tf_op jit(solution)/shard_map/ppermute | solution.py:352
  10.8 14.4 %collective-permute-start.3 = (f32[128,512]{1,0:T(8,128)S(1)}, f32[128,512]{1,0:T(8,128)S(1)}, u32[]{:S(2)}, u32[]{:S(2)}) collective-permute-start(f32[128,512]{1,0:T(8,128)S(1)} %get-tuple-element.88), channel_id=1, source_target_pairs={{0,1},{2,3},{3,2},{4,5},{5,4},{6,7},{7,6},{8,9},{10,11},{11,10},{1... | collective-permute-start | bytes 786440 | tf_op jit(solution)/shard_map/ppermute | solution.py:353
  13.2 12.0 %collective-permute-start.2 = (f32[128,512]{1,0:T(8,128)S(1)}, f32[128,512]{1,0:T(8,128)}, u32[]{:S(2)}, u32[]{:S(2)}) collective-permute-start(f32[128,512]{1,0:T(8,128)S(1)} %get-tuple-element.87), channel_id=1, source_target_pairs={{0,2},{1,3},{2,4},{3,5},{4,6},{5,7},{8,10},{9,11},{10,12},{11,13},... | collective-permute-start | bytes 786440 | tf_op jit(solution)/shard_map/ppermute | solution.py:352
  25.3 19.9 %collective-permute-start.6 = (f32[512,640]{1,0:T(8,128)S(1)}, f32[512,640]{1,0:T(8,128)S(1)}, u32[]{:S(2)}, u32[]{:S(2)}) collective-permute-start(f32[512,640]{1,0:T(8,128)S(1)} %shard_map.56.held_ref), channel_id=1, source_target_pairs={{0,8},{8,0},{16,24},{24,16},{1,9},{9,1},{17,25},{25,17},{2,10},{10... | collective-permute-start | bytes 3932168 | tf_op jit(solution)/shard_map/ppermute | solution.py:464
  25.5 13.6 %collective-permute-start.15 = (f32[128,512]{1,0:T(8,128)S(1)}, f32[128,512]{1,0:T(8,128)S(1)}, u32[]{:S(2)}, u32[]{:S(2)}) collective-permute-start(f32[128,512]{1,0:T(8,128)S(1)} %get-tuple-element.192), channel_id=1, source_target_pairs={{0,1},{2,3},{3,2},{4,5},{5,4},{6,7},{7,6},{8,9},{10,11},{11,10},{1... | collective-permute-start | bytes 786440 | tf_op jit(solution)/shard_map/ppermute | solution.py:353
  29.1 10.7 %collective-permute-start.14 = (f32[128,512]{1,0:T(8,128)S(1)}, f32[128,512]{1,0:T(8,128)S(1)}, u32[]{:S(2)}, u32[]{:S(2)}) collective-permute-start(f32[128,512]{1,0:T(8,128)S(1)} %get-tuple-element.193), channel_id=1, source_target_pairs={{0,2},{1,3},{2,4},{3,5},{4,6},{5,7},{8,10},{9,11},{10,12},{11,13},... | collective-permute-start | bytes 786440 | tf_op jit(solution)/shard_map/ppermute | solution.py:352
  32.3 12.1 %collective-permute-start.5 = (f32[128,512]{1,0:T(8,128)S(1)}, f32[128,512]{1,0:T(8,128)S(1)}, u32[]{:S(2)}, u32[]{:S(2)}) collective-permute-start(f32[128,512]{1,0:T(8,128)S(1)} %get-tuple-element.198), channel_id=1, source_target_pairs={{0,1},{2,3},{3,2},{4,5},{5,4},{6,7},{7,6},{8,9},{10,11},{11,10},{1... | collective-permute-start | bytes 786440 | tf_op jit(solution)/shard_map/ppermute | solution.py:353
  34.7 10.5 %collective-permute-start.4 = (f32[128,512]{1,0:T(8,128)S(1)}, f32[128,512]{1,0:T(8,128)S(1)}, u32[]{:S(2)}, u32[]{:S(2)}) collective-permute-start(f32[128,512]{1,0:T(8,128)S(1)} %get-tuple-element.199), channel_id=1, source_target_pairs={{0,2},{1,3},{2,4},{3,5},{4,6},{5,7},{8,10},{9,11},{10,12},{11,13},... | collective-permute-start | bytes 786440 | tf_op jit(solution)/shard_map/ppermute | solution.py:352
  39.9 12.4 %collective-permute-start.17 = (f32[128,512]{1,0:T(8,128)S(1)}, f32[128,512]{1,0:T(8,128)S(1)}, u32[]{:S(2)}, u32[]{:S(2)}) collective-permute-start(f32[128,512]{1,0:T(8,128)S(1)} %get-tuple-element.190), channel_id=1, source_target_pairs={{0,1},{2,3},{3,2},{4,5},{5,4},{6,7},{7,6},{8,9},{10,11},{11,10},{1... | collective-permute-start | bytes 786440 | tf_op jit(solution)/shard_map/ppermute | solution.py:353
  42.1 10.3 %collective-permute-start.16 = (f32[128,512]{1,0:T(8,128)S(1)}, f32[128,512]{1,0:T(8,128)S(1)}, u32[]{:S(2)}, u32[]{:S(2)}) collective-permute-start(f32[128,512]{1,0:T(8,128)S(1)} %get-tuple-element.191), channel_id=1, source_target_pairs={{0,2},{1,3},{2,4},{3,5},{4,6},{5,7},{8,10},{9,11},{10,12},{11,13},... | collective-permute-start | bytes 786440 | tf_op jit(solution)/shard_map/ppermute | solution.py:352
  45.9 9.4 %collective-permute-start.8 = (f32[128,512]{1,0:T(8,128)S(1)}, f32[128,512]{1,0:T(8,128)S(1)}, u32[]{:S(2)}, u32[]{:S(2)}) collective-permute-start(f32[128,512]{1,0:T(8,128)S(1)} %get-tuple-element.196), channel_id=1, source_target_pairs={{0,1},{2,3},{3,2},{4,5},{5,4},{6,7},{7,6},{8,9},{10,11},{11,10},{1... | collective-permute-start | bytes 786440 | tf_op jit(solution)/shard_map/ppermute | solution.py:353
  49.0 9.0 %collective-permute-start.7 = (f32[128,512]{1,0:T(8,128)S(1)}, f32[128,512]{1,0:T(8,128)S(1)}, u32[]{:S(2)}, u32[]{:S(2)}) collective-permute-start(f32[128,512]{1,0:T(8,128)S(1)} %get-tuple-element.197), channel_id=1, source_target_pairs={{0,2},{1,3},{2,4},{3,5},{4,6},{5,7},{8,10},{9,11},{10,12},{11,13},... | collective-permute-start | bytes 786440 | tf_op jit(solution)/shard_map/ppermute | solution.py:352
  53.2 17.5 %collective-permute-start.11 = (f32[256,640]{1,0:T(8,128)S(1)}, f32[256,640]{1,0:T(8,128)S(1)}, u32[]{:S(2)}, u32[]{:S(2)}) collective-permute-start(f32[256,640]{1,0:T(8,128)S(1)} %get-tuple-element.101), channel_id=1, source_target_pairs={{0,16},{8,24},{16,0},{24,8},{1,17},{9,25},{17,1},{25,9},{2,18},{10... | collective-permute-start | bytes 1966088 | tf_op jit(solution)/shard_map/ppermute | solution.py:468
  58.1 12.2 %collective-permute-start.10 = (f32[128,512]{1,0:T(8,128)S(1)}, f32[128,512]{1,0:T(8,128)S(1)}, u32[]{:S(2)}, u32[]{:S(2)}) collective-permute-start(f32[128,512]{1,0:T(8,128)S(1)} %get-tuple-element.194), channel_id=1, source_target_pairs={{0,1},{2,3},{3,2},{4,5},{5,4},{6,7},{7,6},{8,9},{10,11},{11,10},{1... | collective-permute-start | bytes 786440 | tf_op jit(solution)/shard_map/ppermute | solution.py:353
  61.1 9.6 %collective-permute-start.9 = (f32[128,512]{1,0:T(8,128)S(1)}, f32[128,512]{1,0:T(8,128)S(1)}, u32[]{:S(2)}, u32[]{:S(2)}) collective-permute-start(f32[128,512]{1,0:T(8,128)S(1)} %get-tuple-element.195), channel_id=1, source_target_pairs={{0,2},{1,3},{2,4},{3,5},{4,6},{5,7},{8,10},{9,11},{10,12},{11,13},... | collective-permute-start | bytes 786440 | tf_op jit(solution)/shard_map/ppermute | solution.py:352
  70.7 18.8 %collective-permute-start.22 = (f32[256,640]{1,0:T(8,128)S(1)}, f32[256,640]{1,0:T(8,128)}, u32[]{:S(2)}, u32[]{:S(2)}) collective-permute-start(f32[256,640]{1,0:T(8,128)S(1)} %collective-permute-done.11.refs_0_), channel_id=1, source_target_pairs={{0,8},{8,0},{16,24},{24,16},{1,9},{9,1},{17,25},{25,17},{2,10},{10... | collective-permute-start | bytes 1966088 | tf_op jit(solution)/shard_map/ppermute | solution.py:470
  77.4 12.0 %collective-permute-start.21 = (f32[128,512]{1,0:T(8,128)}, f32[128,512]{1,0:T(8,128)}, u32[]{:S(2)}, u32[]{:S(2)}) collective-permute-start(f32[128,512]{1,0:T(8,128)} %get-tuple-element.184), channel_id=1, source_target_pairs={{0,2},{1,3},{2,4},{3,5},{4,6},{5,7},{8,10},{9,11},{10,12},{11,13},... | collective-permute-start | bytes 786440 | tf_op jit(solution)/shard_map/ppermute | solution.py:352
  80.8 8.7 %collective-permute-start.20 = (f32[128,512]{1,0:T(8,128)}, f32[128,512]{1,0:T(8,128)}, u32[]{:S(2)}, u32[]{:S(2)}) collective-permute-start(f32[128,512]{1,0:T(8,128)} %get-tuple-element.185), channel_id=1, source_target_pairs={{0,1},{2,3},{3,2},{4,5},{5,4},{6,7},{7,6},{8,9},{10,11},{11,10},{1... | collective-permute-start | bytes 786440 | tf_op jit(solution)/shard_map/ppermute | solution.py:353
  84.0 12.5 %collective-permute-start.12 = (f32[128,512]{1,0:T(8,128)}, f32[128,512]{1,0:T(8,128)S(1)}, u32[]{:S(2)}, u32[]{:S(2)}) collective-permute-start(f32[128,512]{1,0:T(8,128)} %get-tuple-element.186), channel_id=1, source_target_pairs={{0,2},{1,3},{2,4},{3,5},{4,6},{5,7},{8,10},{9,11},{10,12},{11,13},... | collective-permute-start | bytes 786440 | tf_op jit(solution)/shard_map/ppermute | solution.py:352
  86.9 9.6 %collective-permute-start.13 = (f32[128,512]{1,0:T(8,128)}, f32[128,512]{1,0:T(8,128)S(1)}, u32[]{:S(2)}, u32[]{:S(2)}) collective-permute-start(f32[128,512]{1,0:T(8,128)} %get-tuple-element.187), channel_id=1, source_target_pairs={{0,1},{2,3},{3,2},{4,5},{5,4},{6,7},{7,6},{8,9},{10,11},{11,10},{1... | collective-permute-start | bytes 786440 | tf_op jit(solution)/shard_map/ppermute | solution.py:353
  98.6 13.5 %collective-permute-start.28 = (f32[512,512]{1,0:T(8,128)S(1)}, f32[512,512]{1,0:T(8,128)S(1)}, u32[]{:S(2)}, u32[]{:S(2)}) collective-permute-start(f32[512,512]{1,0:T(8,128)S(1)} %shard_map.60), channel_id=1, source_target_pairs={{0,8},{1,9},{2,10},{3,11},{4,12},{5,13},{6,14},{7,15}} | collective-permute-start | bytes 3145736 | tf_op jit(solution)/shard_map/ppermute | solution.py:433
  102.7 9.4 %collective-permute-start.25 = (f32[128,512]{1,0:T(8,128)S(1)}, f32[128,512]{1,0:T(8,128)S(1)}, u32[]{:S(2)}, u32[]{:S(2)}) collective-permute-start(f32[128,512]{1,0:T(8,128)S(1)} %get-tuple-element.183), channel_id=1, source_target_pairs={{0,2},{1,3},{2,4},{3,5},{4,6},{5,7},{8,10},{9,11},{10,12},{11,13},... | collective-permute-start | bytes 786440 | tf_op jit(solution)/shard_map/ppermute | solution.py:352
  114.6 16.4 %collective-permute-start.31 = (f32[128,512]{1,0:T(8,128)S(1)}, f32[128,512]{1,0:T(8,128)S(1)}, u32[]{:S(2)}, u32[]{:S(2)}) collective-permute-start(f32[128,512]{1,0:T(8,128)S(1)} %get-tuple-element.178), channel_id=1, source_target_pairs={{0,1},{2,3},{3,2},{4,5},{5,4},{6,7},{7,6},{8,9},{10,11},{11,10},{1... | collective-permute-start | bytes 786440 | tf_op jit(solution)/shard_map/ppermute | solution.py:353
  116.6 14.5 %collective-permute-start.29 = (f32[128,512]{1,0:T(8,128)S(1)}, f32[128,512]{1,0:T(8,128)S(1)}, u32[]{:S(2)}, u32[]{:S(2)}) collective-permute-start(f32[128,512]{1,0:T(8,128)S(1)} %get-tuple-element.179), channel_id=1, source_target_pairs={{0,2},{1,3},{2,4},{3,5},{4,6},{5,7},{8,10},{9,11},{10,12},{11,13},... | collective-permute-start | bytes 786440 | tf_op jit(solution)/shard_map/ppermute | solution.py:352
  118.6 12.5 %collective-permute-start.23 = (f32[128,512]{1,0:T(8,128)S(1)}, f32[128,512]{1,0:T(8,128)S(1)}, u32[]{:S(2)}, u32[]{:S(2)}) collective-permute-start(f32[128,512]{1,0:T(8,128)S(1)} %get-tuple-element.180), channel_id=1, source_target_pairs={{0,2},{1,3},{2,4},{3,5},{4,6},{5,7},{8,10},{9,11},{10,12},{11,13},... | collective-permute-start | bytes 786440 | tf_op jit(solution)/shard_map/ppermute | solution.py:352
  120.6 10.5 %collective-permute-start.24 = (f32[128,512]{1,0:T(8,128)S(1)}, f32[128,512]{1,0:T(8,128)S(1)}, u32[]{:S(2)}, u32[]{:S(2)}) collective-permute-start(f32[128,512]{1,0:T(8,128)S(1)} %get-tuple-element.181), channel_id=1, source_target_pairs={{0,1},{2,3},{3,2},{4,5},{5,4},{6,7},{7,6},{8,9},{10,11},{11,10},{1... | collective-permute-start | bytes 786440 | tf_op jit(solution)/shard_map/ppermute | solution.py:353
  124.6 11.1 %collective-permute-start.34 = (f32[256,512]{1,0:T(8,128)S(1)}, f32[256,512]{1,0:T(8,128)S(1)}, u32[]{:S(2)}, u32[]{:S(2)}) collective-permute-start(f32[256,512]{1,0:T(8,128)S(1)} %slice_select_fusion), channel_id=1, source_target_pairs={{0,16},{8,24},{1,17},{9,25},{2,18},{10,26},{3,19},{11,27},{4,20},{... | collective-permute-start | bytes 1572872 | tf_op jit(solution)/shard_map/ppermute | solution.py:438
  131.2 9.9 %collective-permute-start.26 = (f32[128,512]{1,0:T(8,128)S(1)}, f32[128,512]{1,0:T(8,128)S(1)}, u32[]{:S(2)}, u32[]{:S(2)}) collective-permute-start(f32[128,512]{1,0:T(8,128)S(1)} %get-tuple-element.176), channel_id=1, source_target_pairs={{0,2},{1,3},{2,4},{3,5},{4,6},{5,7},{8,10},{9,11},{10,12},{11,13},... | collective-permute-start | bytes 786440 | tf_op jit(solution)/shard_map/ppermute | solution.py:352
  135.7 18.1 %collective-permute-start.35 = (f32[256,512]{1,0:T(8,128)S(1)}, f32[256,512]{1,0:T(8,128)S(1)}, u32[]{:S(2)}, u32[]{:S(2)}) collective-permute-start(f32[256,512]{1,0:T(8,128)S(1)} %collective-permute-done.34.refs_31_), channel_id=1, source_target_pairs={{16,24},{24,16},{17,25},{25,17},{18,26},{26,18},{19,27},{27,19},{2... | collective-permute-start | bytes 1572872 | tf_op jit(solution)/shard_map/ppermute | solution.py:439
  137.6 11.0 %collective-permute-start.33 = (f32[128,512]{1,0:T(8,128)S(1)}, f32[128,512]{1,0:T(8,128)S(1)}, u32[]{:S(2)}, u32[]{:S(2)}) collective-permute-start(f32[128,512]{1,0:T(8,128)S(1)} %get-tuple-element.175), channel_id=1, source_target_pairs={{0,1},{2,3},{3,2},{4,5},{5,4},{6,7},{7,6},{8,9},{10,11},{11,10},{1... | collective-permute-start | bytes 786440 | tf_op jit(solution)/shard_map/ppermute | solution.py:353
  141.5 12.4 %collective-permute-start.32 = (f32[128,512]{1,0:T(8,128)S(1)}, f32[128,512]{1,0:T(8,128)S(1)}, u32[]{:S(2)}, u32[]{:S(2)}) collective-permute-start(f32[128,512]{1,0:T(8,128)S(1)} %broadcast_select_fusion.4), channel_id=1, source_target_pairs={{0,1},{2,3},{3,2},{4,5},{5,4},{6,7},{7,6},{8,9},{10,11},{11,10},{1... | collective-permute-start | bytes 786440 | tf_op jit(solution)/shard_map/ppermute | solution.py:353
  (64 other events, 451.8 us)
